TPU v7x, 32 devices: a whole 2x2x4 slice. The times are simulated.
32 devices in a mesh: dp: 8 (over y, x, core), section: 4 (over z).
Axes of the slice: x: 2, y: 2, z: 4, core: 2. Of those that a mesh axis runs over, the one named last changes fastest.
Arguments:
- saved_inputs: bfloat16 [4, 8, 2, 384, 2048], P('section', 'dp'), may hold values from -6 to 6
- hidden_grads: bfloat16 [4, 8, 2, 384, 256], P('section', 'dp'), may hold values from -0.029907227 to 0.029907227
- block_expert: int32 [4, 8, 2, 3], P('section', 'dp'), may hold values from 0 to 1, as said below
- live_counts: int32 [4, 8, 2, 2], P('section', 'dp'), may hold values from 0 to 384, as said below
- first_moment: float32 [4, 2048, 2, 256], P('section', 'dp'), may hold values from -3 to 3
- second_moment: float32 [4, 2048, 2, 256], P('section', 'dp'), may hold values from 0.05 to 2
Outputs:
- grad_total: float32 [4, 2048, 2, 256], P('section', 'dp')
- new_first: float32 [4, 2048, 2, 256], P('section', 'dp')
- new_second: float32 [4, 2048, 2, 256], P('section', 'dp')
- step_direction: float32 [4, 2048, 2, 256], P('section', 'dp')
Inputs may be any that keep to these rules, and one draw needn't show every extreme that they name: block_expert[p, d, k, b] names the expert of rows b * 128 to (b + 1) * 128 - 1 of that device's direction-k rows. live_counts[p, d, k, e] is 0 when no block of that direction names expert e; for n such blocks it lies between 128 * (n - 1) + 1 and 128 * n. On every device one of the two directions has all its blocks on one expert with all 384 rows live.
All inputs are finite; a program needn't handle non-finite values.
Results may differ from a plain program's by a relative error of at most 0.0021.
Values may be sent and summed in bfloat16 or wider, within the bound.
No kernel may reach another device: no remote copies, remote signals or barrier semaphores. Data moves between devices by JAX's collectives and lax.ppermute only.
A program may use at most 64 MiB of HBM per device.

v0:
```python
import jax
import jax.numpy as jnp
from jax import lax
from jax.sharding import PartitionSpec as P

EXPERTS = 2
BLOCK = 128
NBLK = 3


beta_one = 0.9
beta_two = 0.95
adam_epsilon = 1e-08
bias_first = 1.0 - 0.9**50
bias_second = 1.0 - 0.95**50


def shifted(value, axis, steps):
    count = lax.axis_size(axis)
    pairs = [(source, (source + steps) % count) for source in range(count)]
    return lax.ppermute(value, axis, pairs)


def route_select(block_expert, live_counts):
    experts = jnp.arange(EXPERTS, dtype=jnp.int32)
    onehot = (block_expert[..., :, None] == experts).astype(jnp.int32)
    earlier = jnp.cumsum(onehot, axis=-2) - onehot
    before = jnp.sum(earlier * onehot, axis=-1)
    limits = jnp.sum(live_counts[..., None, :] * onehot, axis=-1)
    offsets = jnp.arange(BLOCK, dtype=jnp.int32)
    positions = before[..., None] * BLOCK + offsets
    live_rows = positions < limits[..., None]
    return (live_rows, onehot)


def per_device(saved_inputs, hidden_grads, block_expert, live_counts, first_moment, second_moment):
    model_width = saved_inputs.shape[4]
    hidden = hidden_grads.shape[4]
    live_rows, onehot = route_select(block_expert.reshape(2, NBLK), live_counts.reshape(2, EXPERTS))
    weights = onehot.astype(jnp.float32)
    inputs = saved_inputs.reshape(2, NBLK, BLOCK, model_width)
    masked = hidden_grads.reshape(2, NBLK, BLOCK, hidden) * live_rows[..., None].astype(
        jnp.bfloat16
    )
    half_span = lax.axis_size("section") // 2

    def direction_part(direction):
        columns = inputs[direction]
        blocks = jnp.einsum(
            "brd,brf->bdf", columns, masked[direction], preferred_element_type=jnp.float32
        )
        return jnp.einsum(
            "bdf,be->def", blocks, weights[direction], precision=lax.Precision.HIGHEST
        )

    own_part = direction_part(0)
    sent_part = lax.optimization_barrier(direction_part(1).astype(jnp.bfloat16)).astype(jnp.float32)
    summed = lax.psum_scatter(
        jnp.stack([own_part, sent_part], axis=1), "dp", scatter_dimension=0, tiled=True
    )
    partner = shifted(summed[:, 1], "section", half_span)
    grad_total = summed[:, 0] + partner
    moment_one = first_moment[0]
    moment_two = second_moment[0]
    new_first = beta_one * moment_one + (1.0 - beta_one) * grad_total
    new_second = beta_two * moment_two + (1.0 - beta_two) * grad_total * grad_total
    step_direction = new_first / bias_first / (jnp.sqrt(new_second / bias_second) + adam_epsilon)
    return (grad_total[None], new_first[None], new_second[None], step_direction[None])


def solution(mesh):
    in_specs = (
        P("section", "dp", None, None, None),
        P("section", "dp", None, None, None),
        P("section", "dp", None, None),
        P("section", "dp", None, None),
        P("section", "dp", None, None),
        P("section", "dp", None, None),
    )
    out_specs = (
        P("section", "dp", None, None),
        P("section", "dp", None, None),
        P("section", "dp", None, None),
        P("section", "dp", None, None),
    )
    return jax.shard_map(
        per_device, mesh=mesh, in_specs=in_specs, out_specs=out_specs, check_vma=False
    )
```

profile of v0, /device:TPU:0, one launch (start us, length us, event | category | flops | bytes accessed | tf_op | source)
XLA Modules:
  0.0 210.0 jit_solution(8174226185561573289)
XLA Ops:
  7.2 0.0 copy-start.4
  7.2 0.0 reduce-scatter.5.cloned.1.call-start
  7.2 0.7 fusion.20
  7.9 0.3 reduce_window_sum.11
  8.3 0.8 select_reduce_fusion.1
  9.1 2.2 %fusion.24 = (bf16[1,1,1,384,2048]{4,3,2,1,0:T(8,128)(2,1)S(1)}, bf16[1,1,1,384,2048]{4,3,2,1,0:T(8,128)(2,1)S(1)}) fusion(bf16[1,1,2,384,2048]{4,3,2,1,0:T(8,128)(2,1)} %param.6), kind=kLoop, calls=%fused_computation.34 | loop fusion | bytes 6291456 | tf_op jit(solution)/shard_map/slice | solution.py:48
  11.3 0.1 fusion.18
  11.4 0.0 copy-done.4
  11.4 0.2 broadcast_multiply_fusion
  11.5 3.7 %fusion.16 = f32[3,256,2048]{2,1,0:T(8,128)} fusion(bf16[3,128,2048]{2,1,0:T(8,128)(2,1)S(1)} %bitcast.76, bf16[2,3,128,256]{3,2,1,0:T(8,128)(2,1)S(1)} %broadcast_multiply_fusion), kind=kOutput, calls=%fused_computation.18 | convolution fusion | flops 402653184 | bytes 8060928 | tf_op jit(solution)/shard_map/brd,brf->bdf/dot_general | solution.py:49
  15.3 9.1 %copy.11 = f32[3,256,2048]{1,0,2:T(4,128)} copy(f32[3,256,2048]{2,1,0:T(8,128)} %fusion.16) | data formatting | bytes 12582912 | tf_op jit(solution)/shard_map/brd,brf->bdf/dot_general | solution.py:49
  24.3 17.4 %fusion.10 = bf16[2048,2,256]{2,1,0:T(2,128)(2,1)S(1)} fusion(f32[3,256,2048]{1,0,2:T(4,128)} %copy.11, f32[2,3,2]{1,2,0:T(2,128)S(1)} %get-tuple-element.12), kind=kOutput, calls=%fused_computation.7 | convolution fusion | flops 38797312 | bytes 8389632 | tf_op jit(solution)/shard_map/bdf,be->def/dot_general | solution.py:52
  41.7 3.1 %bitcast_convert_fusion = f32[2048,1,2,256]{3,2,0,1:T(2,128)} fusion(bf16[2048,2,256]{2,1,0:T(2,128)(2,1)S(1)} %fusion.10), kind=kLoop, calls=%fused_computation.8 | loop fusion | flops 1048576 | bytes 6291456 | tf_op jit(solution)/shard_map/stack | solution.py:59
  44.9 3.7 %fusion.17 = f32[3,256,2048]{2,1,0:T(8,128)} fusion(bf16[3,128,2048]{2,1,0:T(8,128)(2,1)S(1)} %bitcast.75, bf16[2,3,128,256]{3,2,1,0:T(8,128)(2,1)S(1)} %broadcast_multiply_fusion), kind=kOutput, calls=%fused_computation.20 | convolution fusion | flops 402653184 | bytes 8060928 | tf_op jit(solution)/shard_map/brd,brf->bdf/dot_general | solution.py:49
  48.6 9.1 %copy.10 = f32[3,256,2048]{1,0,2:T(4,128)} copy(f32[3,256,2048]{2,1,0:T(8,128)} %fusion.17) | data formatting | bytes 12582912 | tf_op jit(solution)/shard_map/brd,brf->bdf/dot_general | solution.py:49
  57.7 0.0 copy-start
  57.7 17.3 %fusion.4 = f32[2048,1,2,256]{3,2,0,1:T(2,128)S(1)} fusion(f32[3,256,2048]{1,0,2:T(4,128)} %copy.10, f32[2,3,2]{1,2,0:T(2,128)S(1)} %get-tuple-element.12), kind=kOutput, calls=%fused_computation.5 | convolution fusion | flops 37748736 | bytes 10486784 | tf_op jit(solution)/shard_map/bdf,be->def/dot_general | solution.py:52
  75.0 0.0 copy-done
  75.0 4.5 %pad_maximum_fusion = f32[2048,2,2,256]{3,2,0,1:T(2,128)S(1)} fusion(f32[2048,1,2,256]{3,2,0,1:T(2,128)S(1)} %copy-done, f32[2048,1,2,256]{3,2,0,1:T(2,128)S(1)} %fusion.4), kind=kLoop, calls=%fused_computation | loop fusion | flops 2097152 | bytes 16777216 | tf_op jit(solution)/shard_map/stack | solution.py:59
  79.5 5.9 %copy.12 = f32[2048,2,2,256]{3,2,1,0:T(2,128)} copy(f32[2048,2,2,256]{3,2,0,1:T(2,128)S(1)} %pad_maximum_fusion) | data formatting | bytes 16777216
  85.4 11.5 %reshape.37 = f32[2048,1024]{1,0:T(8,128)} reshape(f32[2048,2,2,256]{3,2,1,0:T(2,128)} %copy.12) | data formatting | bytes 16777216
  96.9 0.0 copy-start.1
  96.9 0.0 copy-start.2
  96.9 0.0 reduce-scatter.5.cloned.1.call-update
  96.9 74.1 %reduce-scatter.5.cloned.1.call-done = f32[256,1024]{1,0:T(8,128)} async-done(((f32[2048,1024]{1,0:T(8,128)}), f32[256,1024]{1,0:T(8,128)}) %reduce-scatter.5.cloned.1.call-update) | async-done | bytes 1048592
  171.0 2.1 %reshape.38 = f32[256,2,2,256]{3,2,1,0:T(2,128)S(1)} reshape(f32[256,1024]{1,0:T(8,128)} %reduce-scatter.5.cloned.1.call-done) | data formatting | bytes 2097152
  173.1 0.2 slice_bitcast_fusion
  173.3 2.5 %collective-permute-start = (f32[256,2,256]{2,1,0:T(2,128)S(1)}, f32[256,2,256]{2,1,0:T(2,128)S(1)}, u32[]{:S(2)}, u32[]{:S(2)}) collective-permute-start(f32[256,2,256]{2,1,0:T(2,128)S(1)} %slice_bitcast_fusion), channel_id=1, source_target_pairs={{0,2},{1,3},{2,0},{3,1},{4,6},{5,7},{6,4},{7,5},{8,10},{9,11},{10,... | collective-permute-start | bytes 1572872 | tf_op jit(solution)/shard_map/ppermute | solution.py:21
  175.8 23.4 %collective-permute-done = f32[256,2,256]{2,1,0:T(2,128)S(1)} collective-permute-done((f32[256,2,256]{2,1,0:T(2,128)S(1)}, f32[256,2,256]{2,1,0:T(2,128)S(1)}, u32[]{:S(2)}, u32[]{:S(2)}) %collective-permute-start) | collective-permute-done | bytes 524320 | tf_op jit(solution)/shard_map/ppermute | solution.py:21
  199.2 0.0 copy-done.1
  199.2 0.0 copy-done.2
  199.2 2.2 %fusion.15 = (f32[1,256,2,256]{3,2,1,0:T(2,128)}, f32[256,2,256]{2,1,0:T(2,128)S(1)}) fusion(f32[1,256,2,256]{3,2,1,0:T(2,128)S(1)} %copy-done.1, f32[1,256,2,256]{3,2,1,0:T(2,128)S(1)} %copy-done.2, f32[256,2,256]{2,1,0:T(2,128)S(1)} %collective-permute-done, f32[256,2,2,256]{3,2,1,0:T(2,128)S(1)} %reshape.38), kind=kLoop, calls=%fused_computation.16 | loop fusion | flops 1572864 | bytes 3145728 | tf_op jit(solution)/shard_map/broadcast_in_dim | solution.py:68
  201.3 0.0 copy-start.3
  201.3 1.8 fusion.22
  203.1 0.0 copy-done.3
  (1 shorter events, 0.0 us)
Async XLA Ops:
  7.2 4.2 %copy-start.4 = (bf16[1,1,2,384,256]{4,3,2,1,0:T(8,128)(2,1)S(1)}, bf16[1,1,2,384,256]{4,3,2,1,0:T(8,128)(2,1)}, u32[]{:S(2)}) copy-start(bf16[1,1,2,384,256]{4,3,2,1,0:T(8,128)(2,1)} %param.7) | copy-start | bytes 1179652
  7.2 163.8 %reduce-scatter.5.cloned.1.call-start = ((), (), s32[]{:S(2)}) async-start(), calls=%async_computation.1 | async-start | bytes 9437184
  57.7 17.4 %copy-start = (f32[2048,1,2,256]{3,2,0,1:T(2,128)S(1)}, f32[2048,1,2,256]{3,2,0,1:T(2,128)}, u32[]{:S(2)}) copy-start(f32[2048,1,2,256]{3,2,0,1:T(2,128)} %bitcast_convert_fusion) | copy-start | bytes 12582916
  96.9 102.3 %copy-start.1 = (f32[1,256,2,256]{3,2,1,0:T(2,128)S(1)}, f32[1,256,2,256]{3,2,1,0:T(2,128)}, u32[]{:S(2)}) copy-start(f32[1,256,2,256]{3,2,1,0:T(2,128)} %param.10) | copy-start | bytes 1572868
  96.9 102.3 %copy-start.2 = (f32[1,256,2,256]{3,2,1,0:T(2,128)S(1)}, f32[1,256,2,256]{3,2,1,0:T(2,128)}, u32[]{:S(2)}) copy-start(f32[1,256,2,256]{3,2,1,0:T(2,128)} %param.11) | copy-start | bytes 1572868
  173.3 25.9 %collective-permute-start = (f32[256,2,256]{2,1,0:T(2,128)S(1)}, f32[256,2,256]{2,1,0:T(2,128)S(1)}, u32[]{:S(2)}, u32[]{:S(2)}) collective-permute-start(f32[256,2,256]{2,1,0:T(2,128)S(1)} %slice_bitcast_fusion), channel_id=1, source_target_pairs={{0,2},{1,3},{2,0},{3,1},{4,6},{5,7},{6,4},{7,5},{8,10},{9,11},{10,... | collective-permute-start | bytes 1572872 | tf_op jit(solution)/shard_map/ppermute | solution.py:21
  201.3 1.8 copy-start.3
Sparse Core Ops, SparseCore 0:
  97.0 73.9 reduce-scatter.4
where the time goes:
time: 211 us; the launch traced here: 210 us
  waiting for transfers between devices  97.5 us (46%)
  matrix products  42.1 us (20%)
  local copies, waits for them, and re-layouts  40 us (19%)
  between operations  14.1 us (7%)
  other arithmetic  13.6 us (6%)
  starting transfers between devices  2.51 us (1%)
    unnamed x2, waiting for transfers between devices  74.1 us
    dot_general x2, matrix products, direction_part(): jnp.einsum('bdf,be->def', blocks, weights[direction], precision=lax.Preci...  34.7 us
    ppermute x1, waiting for transfers between devices, shifted(): return lax.ppermute(value, axis, pairs)  23.4 us
    unnamed x13, local copies, waits for them, and re-layouts  19.5 us
    dot_general x2, local copies, waits for them, and re-layouts, direction_part(): jnp.einsum('brd,brf->bdf', columns, masked[direction], preferred_element_...  18.2 us
    another operation x2, other arithmetic, per_device(): jnp.stack([own_part, sent_part], axis=1)  7.6 us
    dot_general x2, matrix products, direction_part(): jnp.einsum('brd,brf->bdf', columns, masked[direction], preferred_element_...  7.43 us
  transfers between devices with their start and end apart: 2, of which 2 were waited for; matrix products, arithmetic and copies ran while one was open for 0% of the time, Pallas kernels for 0%

commit v1 on v0

v1 whole, which is shorter than its diff:
```python
import functools

import jax
import jax.numpy as jnp
from jax import lax
from jax.experimental import pallas as pl
from jax.experimental.pallas import tpu as pltpu
from jax.sharding import PartitionSpec as P

beta_one = 0.9
beta_two = 0.95
adam_epsilon = 1e-08
bias_first = 1.0 - 0.9**50
bias_second = 1.0 - 0.95**50

LANES = 128


def exchanged(value, axis, mask):
    count = lax.axis_size(axis)
    return lax.ppermute(value, axis, [(source, source ^ mask) for source in range(count)])


def mirrored(value):
    count = lax.axis_size("section")
    pairs = [(source, (source + count // 2) % count) for source in range(count)]
    return lax.ppermute(value, "section", pairs)


def expand_hidden(route, counts, direction, hidden, wide, blocks, experts):
    rows, width = hidden.shape
    block = rows // blocks
    seen = [jnp.int32(0) for _ in range(experts)]
    place = lax.broadcasted_iota(jnp.int32, (block, width), 0)
    for b in range(blocks):
        expert = route[direction, b]
        values = hidden[b * block : (b + 1) * block, :].astype(jnp.float32)
        for e in range(experts):
            named = expert == e
            limit = jnp.where(named, counts[direction, e] - seen[e] * block, 0)
            kept = jnp.where(place < limit, values, 0.0)
            wide[b * block : (b + 1) * block, e * width : (e + 1) * width] = kept.astype(wide.dtype)
            seen[e] = seen[e] + named.astype(jnp.int32)


def product_kernel(direction, blocks, experts, place, route, counts, inputs, hidden, out, wide):
    @pl.when(pl.program_id(0) == 0)
    def _():
        expand_hidden(route, counts, direction, hidden, wide, blocks, experts)

    product = lax.dot_general(
        inputs[...], wide[...], (((0,), (0,)), ((), ())), preferred_element_type=jnp.float32
    )
    out[...] = product.astype(out.dtype)


def products(direction, sibling, place, route, counts, inputs, hidden, share, chips, experts, dtype):
    _, rows, _ = inputs.shape
    width = hidden.shape[2]
    blocks = route.shape[1]
    columns = experts * width

    def column(k, place, route, counts):
        chip = place[0] ^ k
        core = place[1] ^ (1 if sibling else 0)
        return (direction, 0, chip * 2 + core)

    return pl.pallas_call(
        functools.partial(product_kernel, direction, blocks, experts),
        grid_spec=pltpu.PrefetchScalarGridSpec(
            num_scalar_prefetch=3,
            grid=(chips,),
            in_specs=[
                pl.BlockSpec((None, rows, share), column),
                pl.BlockSpec((None, rows, width), lambda k, *_: (direction, 0, 0)),
            ],
            out_specs=pl.BlockSpec((None, share, columns), lambda k, *_: (k, 0, 0)),
            scratch_shapes=[pltpu.VMEM((rows, columns), jnp.bfloat16)],
        ),
        out_shape=jax.ShapeDtypeStruct((chips, share, columns), dtype),
        cost_estimate=pl.CostEstimate(
            flops=2 * rows * chips * share * columns,
            bytes_accessed=2 * rows * (chips * share + width)
            + chips * share * columns * jnp.dtype(dtype).itemsize,
            transcendentals=0,
        ),
    )(place, route, counts, inputs, hidden)


def join_kernel(own, received, kept, *sent):
    total = own[...].astype(jnp.float32) + received[...].astype(jnp.float32)
    kept[...] = total[0]
    for k, out in enumerate(sent):
        out[...] = total[k + 1].astype(out.dtype)


def joined(own, received):
    chips, share, columns = own.shape
    rows = share // 2
    piece = pl.BlockSpec((rows, columns), lambda i: (i, 0))
    whole = pl.BlockSpec((chips, rows, columns), lambda i: (0, i, 0))
    return pl.pallas_call(
        join_kernel,
        grid=(2,),
        in_specs=[whole, whole],
        out_specs=[piece] * chips,
        out_shape=[jax.ShapeDtypeStruct((share, columns), jnp.float32)]
        + [jax.ShapeDtypeStruct((share, columns), jnp.bfloat16)] * (chips - 1),
        cost_estimate=pl.CostEstimate(
            flops=own.size,
            bytes_accessed=own.nbytes + received.nbytes + share * columns * (4 + 2 * (chips - 1)),
            transcendentals=0,
        ),
    )(own, received)


def total_kernel(kept, *refs):
    *received, out = refs
    total = kept[...]
    for part in received:
        total = total + part[...].astype(jnp.float32)
    out[...] = total.astype(out.dtype)


def totalled(kept, received, dtype):
    return pl.pallas_call(
        total_kernel,
        out_shape=jax.ShapeDtypeStruct(kept.shape, dtype),
        cost_estimate=pl.CostEstimate(
            flops=kept.size * len(received),
            bytes_accessed=kept.nbytes + sum(part.nbytes for part in received),
            transcendentals=0,
        ),
    )(kept, *received)


def update_kernel(experts, received_count, *refs):
    kept = refs[0]
    received = refs[1 : 1 + received_count]
    first, second = refs[1 + received_count : 3 + received_count]
    grad_out, first_out, second_out, step_out = refs[3 + received_count :]
    width = first.shape[2]
    for e in range(experts):
        columns = slice(e * width, (e + 1) * width)
        grad = kept[:, columns]
        for part in received:
            grad = grad + part[:, columns].astype(jnp.float32)
        new_first = beta_one * first[:, e, :] + (1.0 - beta_one) * grad
        new_second = beta_two * second[:, e, :] + (1.0 - beta_two) * grad * grad
        grad_out[:, e, :] = grad
        first_out[:, e, :] = new_first
        second_out[:, e, :] = new_second
        step_out[:, e, :] = (
            new_first / bias_first / (jnp.sqrt(new_second / bias_second) + adam_epsilon)
        )


def updated(kept, received, first, second):
    share, experts, width = first.shape
    rows = share // 2
    flat = pl.BlockSpec((rows, experts * width), lambda i: (i, 0))
    moment = pl.BlockSpec((rows, experts, width), lambda i: (i, 0, 0))
    return pl.pallas_call(
        functools.partial(update_kernel, experts, len(received)),
        grid=(2,),
        in_specs=[flat] * (1 + len(received)) + [moment] * 2,
        out_specs=[moment] * 4,
        out_shape=[jax.ShapeDtypeStruct(first.shape, jnp.float32)] * 4,
        cost_estimate=pl.CostEstimate(
            flops=20 * first.size,
            bytes_accessed=7 * first.nbytes + sum(part.nbytes for part in received),
            transcendentals=2 * first.size,
        ),
    )(kept, *received, first, second)


def fast_device(saved_inputs, hidden_grads, block_expert, live_counts, first_moment, second_moment):
    ranks = lax.axis_size("dp")
    chips = ranks // 2
    me = lax.axis_index("dp")
    place = jnp.stack([me // 2, me % 2]).astype(jnp.int32)
    inputs = saved_inputs[0, 0]
    hidden = hidden_grads[0, 0]
    route = block_expert[0, 0]
    counts = live_counts[0, 0]
    share, experts = first_moment.shape[1:3]
    product = functools.partial(
        products,
        place=place,
        route=route,
        counts=counts,
        inputs=inputs,
        hidden=hidden,
        share=share,
        chips=chips,
        experts=experts,
    )

    def direction_part(direction, dtype):
        other = exchanged(product(direction, True, dtype=dtype), "dp", 1)
        kept, *sent = joined(product(direction, False, dtype=dtype), other)
        return kept, [exchanged(part, "dp", 2 * (k + 1)) for k, part in enumerate(sent)]

    kept_one, received_one = direction_part(1, jnp.bfloat16)
    partner = mirrored(totalled(kept_one, received_one, jnp.bfloat16))
    kept_zero, received_zero = direction_part(0, jnp.float32)
    outs = updated(kept_zero, received_zero + [partner], first_moment[0], second_moment[0])
    return tuple(out[None] for out in outs)


def route_select(block_expert, live_counts, block):
    experts = jnp.arange(live_counts.shape[-1], dtype=jnp.int32)
    onehot = (block_expert[..., :, None] == experts).astype(jnp.int32)
    earlier = jnp.cumsum(onehot, axis=-2) - onehot
    before = jnp.sum(earlier * onehot, axis=-1)
    limits = jnp.sum(live_counts[..., None, :] * onehot, axis=-1)
    positions = before[..., None] * block + jnp.arange(block, dtype=jnp.int32)
    return positions < limits[..., None], onehot


def plain_device(saved_inputs, hidden_grads, block_expert, live_counts, first_moment, second_moment):
    _, _, _, rows, model_width = saved_inputs.shape
    hidden = hidden_grads.shape[4]
    blocks = block_expert.shape[3]
    block = rows // blocks
    live_rows, onehot = route_select(block_expert[0, 0], live_counts[0, 0], block)
    masked = hidden_grads.reshape(2, blocks, block, hidden) * live_rows[..., None].astype(
        jnp.bfloat16
    )
    wide = masked[:, :, :, None, :] * onehot[:, :, None, :, None].astype(jnp.bfloat16)
    wide = wide.reshape(2, rows, -1)
    parts = jnp.einsum(
        "krd,krc->kdc", saved_inputs[0, 0], wide, preferred_element_type=jnp.float32
    )
    sent = lax.optimization_barrier(parts[1].astype(jnp.bfloat16)).astype(jnp.float32)
    summed = lax.psum_scatter(
        jnp.stack([parts[0], sent], axis=1), "dp", scatter_dimension=0, tiled=True
    )
    grad_total = (summed[:, 0] + mirrored(summed[:, 1])).reshape(first_moment.shape[1:])
    new_first = beta_one * first_moment[0] + (1.0 - beta_one) * grad_total
    new_second = beta_two * second_moment[0] + (1.0 - beta_two) * grad_total * grad_total
    step_direction = new_first / bias_first / (jnp.sqrt(new_second / bias_second) + adam_epsilon)
    return (grad_total[None], new_first[None], new_second[None], step_direction[None])


def solution(mesh):
    in_specs = (
        P("section", "dp", None, None, None),
        P("section", "dp", None, None, None),
        P("section", "dp", None, None),
        P("section", "dp", None, None),
        P("section", "dp", None, None),
        P("section", "dp", None, None),
    )
    out_specs = (P("section", "dp", None, None),) * 4

    def run(*arrays):
        ranks = mesh.shape["dp"]
        paired = ranks % 2 == 0 and ranks & (ranks - 1) == 0
        per_device = fast_device if paired and arrays[4].shape[1] // ranks % LANES == 0 else plain_device
        return jax.shard_map(
            per_device, mesh=mesh, in_specs=in_specs, out_specs=out_specs, check_vma=False
        )(*arrays)

    return run
```

time: 211 us -> 65.3 us (0.31)
  waiting for transfers between devices: 97.5 us -> 17.5 us
  matrix products: 42.1 us -> 0 us
  local copies, waits for them, and re-layouts: 40 us -> 3.9 us
  Pallas kernels: 0 us -> 30.9 us
  between operations: 14.1 us -> 0.69 us
  other arithmetic: 13.6 us -> 0.65 us
  starting transfers between devices: 2.51 us -> 11.1 us
    unnamed x2 -> x0, waiting for transfers between devices: 74.1 us -> none
    dot_general x4 -> x0, matrix products: 42.1 us -> none  [the longest x2 34.7 us: direction_part(): jnp.einsum('bdf,be->def', blocks, weights[direction], precision=lax.Preci...]
    pallas_call x0 -> x8, Pallas kernels: none -> 30.9 us  [the longest x4 19.7 us: products(): pl.pallas_call(functools.partial(product_kernel, direction, blocks, exper...]
    dot_general x2 -> x0, local copies, waits for them, and re-layouts: 18.2 us -> none  [direction_part(): jnp.einsum('brd,brf->bdf', columns, masked[direction], preferred_element_...]
    unnamed x13 -> x18, local copies, waits for them, and re-layouts: 19.5 us -> 3.9 us
    ppermute x1 -> x9, starting transfers between devices: 2.47 us -> 11.1 us  [the longest x8 8.47 us: exchanged(): lax.ppermute(value, axis, [(source, source ^ mask) for source in range(co...]
    another operation x3 -> x1, other arithmetic: 7.95 us -> 0.65 us  [fast_device(): place = jnp.stack([me // 2, me % 2]).astype(jnp.int32)]
    ppermute x1 -> x9, waiting for transfers between devices: 23.4 us -> 17.5 us  [the longest x8 14.2 us: exchanged(): lax.ppermute(value, axis, [(source, source ^ mask) for source in range(co...]
  transfers between devices with their start and end apart: 2 -> 9, of which waited for: 2 -> 5; matrix products, arithmetic and copies ran while one was open for 0% -> 0% of each run, Pallas kernels for 0% -> 34%
where the time goes in v1:
time: 65.3 us; the launch traced here: 64.8 us
  Pallas kernels  30.9 us (47%)
  waiting for transfers between devices  17.5 us (27%)
  starting transfers between devices  11.1 us (17%)
  local copies, waits for them, and re-layouts  3.9 us (6%)
  between operations  0.69 us (1%)
    pallas_call x4, Pallas kernels, products(): pl.pallas_call(functools.partial(product_kernel, direction, blocks, exper...  19.7 us
    ppermute x8, waiting for transfers between devices, exchanged(): lax.ppermute(value, axis, [(source, source ^ mask) for source in range(co...  14.2 us
    ppermute x8, starting transfers between devices, exchanged(): lax.ppermute(value, axis, [(source, source ^ mask) for source in range(co...  8.47 us
    pallas_call x2, Pallas kernels, joined(): pl.pallas_call(join_kernel, grid=(2,), in_specs=[whole, whole], out_specs...  5.5 us
    unnamed x18, local copies, waits for them, and re-layouts  3.9 us
    pallas_call x1, Pallas kernels, updated(): pl.pallas_call(functools.partial(update_kernel, experts, len(received)),...  3.65 us
    ppermute x1, waiting for transfers between devices, mirrored(): return lax.ppermute(value, 'section', pairs)  3.27 us
    ppermute x1, starting transfers between devices, mirrored(): return lax.ppermute(value, 'section', pairs)  2.59 us
  transfers between devices with their start and end apart: 9, of which 5 were waited for; matrix products, arithmetic and copies ran while one was open for 0% of the time, Pallas kernels for 34%

profile of v1, /device:TPU:0, one launch (start us, length us, event | category | flops | bytes accessed | tf_op | source)
XLA Modules:
  0.0 64.8 jit_solution(1970560724996504833)
XLA Ops:
  0.6 0.7 %pad_add_fusion.place = s32[2]{0:T(128)} fusion(s32[1]{0:T(128)} %bitcast.1, s32[1]{0:T(128)} %bitcast), kind=kLoop, calls=%fused_computation | loop fusion | flops 2 | bytes 16 | tf_op jit(solution)/shard_map/stack | solution.py:181
  1.3 5.0 %shard_map.94 = f32[4,256,512]{2,1,0:T(8,128)} custom-call(s32[2]{0:T(128)} %pad_add_fusion.place, s32[2,3]{1,0:T(2,128)} %bitcast.22, s32[2,2]{1,0:T(2,128)} %bitcast.26, bf16[2,384,2048]{2,1,0:T(8,128)(2,1)} %bitcast.12, bf16[2,384,256]{2,1,0:T(8,128)(2,1)} %bitcast.16), custom_call_target="tpu_custom_call" | custom-call | flops 402653184 | bytes 3080192 | tf_op jit(solution)/shard_map/pallas_call | solution.py:68
  6.3 0.5 collective-permute-start
  6.8 4.8 %shard_map.97 = bf16[4,256,512]{2,1,0:T(8,128)(2,1)} custom-call(s32[2]{0:T(128)} %pad_add_fusion.place, s32[2,3]{1,0:T(2,128)} %bitcast.23, s32[2,2]{1,0:T(2,128)} %bitcast.27, bf16[2,384,2048]{2,1,0:T(8,128)(2,1)} %bitcast.13, bf16[2,384,256]{2,1,0:T(8,128)(2,1)} %bitcast.17), custom_call_target="tpu_custom_call" | custom-call | flops 402653184 | bytes 2031616 | tf_op jit(solution)/shard_map/pallas_call | solution.py:68
  11.6 0.1 collective-permute-start.4
  11.7 4.8 %shard_map.96.own = bf16[4,256,512]{2,1,0:T(8,128)(2,1)} custom-call(s32[2]{0:T(128)} %pad_add_fusion.place, s32[2,3]{1,0:T(2,128)} %bitcast.24, s32[2,2]{1,0:T(2,128)} %bitcast.28, bf16[2,384,2048]{2,1,0:T(8,128)(2,1)} %bitcast.14, bf16[2,384,256]{2,1,0:T(8,128)(2,1)} %bitcast.18), custom_call_target="tpu_custom_call" | custom-call | flops 402653184 | bytes 2031616 | tf_op jit(solution)/shard_map/pallas_call | solution.py:68
  16.5 0.0 collective-permute-done.4.received
  16.5 0.0 copy-start.1
  16.5 1.0 %copy-done.1 = bf16[4,256,512]{2,1,0:T(8,128)(2,1)} copy-done((bf16[4,256,512]{2,1,0:T(8,128)(2,1)}, bf16[4,256,512]{2,1,0:T(8,128)(2,1)S(1)}, u32[]{:S(2)}) %copy-start.1) | copy-done | bytes 1048600
  17.5 2.4 %shard_map.98 = (f32[256,512]{1,0:T(8,128)}, bf16[256,512]{1,0:T(8,128)(2,1)}, bf16[256,512]{1,0:T(8,128)(2,1)}, bf16[256,512]{1,0:T(8,128)(2,1)}) custom-call(bf16[4,256,512]{2,1,0:T(8,128)(2,1)} %shard_map.96.own, bf16[4,256,512]{2,1,0:T(8,128)(2,1)} %copy-done.1), custom_call_target="tpu_custom_call" | custom-call | flops 524288 | bytes 3407872 | tf_op jit(solution)/shard_map/pallas_call | solution.py:102
  19.9 2.9 %collective-permute-start.5 = (bf16[256,512]{1,0:T(8,128)(2,1)}, bf16[256,512]{1,0:T(8,128)(2,1)S(1)}, u32[]{:S(2)}, u32[]{:S(2)}) collective-permute-start(bf16[256,512]{1,0:T(8,128)(2,1)} %get-tuple-element.21), channel_id=1, source_target_pairs={{0,8},{4,12},{8,0},{12,4},{16,24},{20,28},{24,16},{28,20},{1,9},{5... | collective-permute-start | bytes 786440 | tf_op jit(solution)/shard_map/ppermute | solution.py:21
  22.8 1.5 %collective-permute-start.6 = (bf16[256,512]{1,0:T(8,128)(2,1)}, bf16[256,512]{1,0:T(8,128)(2,1)S(1)}, u32[]{:S(2)}, u32[]{:S(2)}) collective-permute-start(bf16[256,512]{1,0:T(8,128)(2,1)} %get-tuple-element.22), channel_id=1, source_target_pairs={{0,16},{4,20},{8,24},{12,28},{16,0},{20,4},{24,8},{28,12},{1,17},{... | collective-permute-start | bytes 786440 | tf_op jit(solution)/shard_map/ppermute | solution.py:21
  24.4 0.0 collective-permute-start.7
  24.4 5.0 %shard_map.93.own = f32[4,256,512]{2,1,0:T(8,128)} custom-call(s32[2]{0:T(128)} %pad_add_fusion.place, s32[2,3]{1,0:T(2,128)} %bitcast.25, s32[2,2]{1,0:T(2,128)} %bitcast.29, bf16[2,384,2048]{2,1,0:T(8,128)(2,1)} %bitcast.15, bf16[2,384,256]{2,1,0:T(8,128)(2,1)} %bitcast.19), custom_call_target="tpu_custom_call" | custom-call | flops 402653184 | bytes 3080192 | tf_op jit(solution)/shard_map/pallas_call | solution.py:68
  29.4 0.8 %collective-permute-done.5.refs_0_ = bf16[256,512]{1,0:T(8,128)(2,1)S(1)} collective-permute-done((bf16[256,512]{1,0:T(8,128)(2,1)}, bf16[256,512]{1,0:T(8,128)(2,1)S(1)}, u32[]{:S(2)}, u32[]{:S(2)}) %collective-permute-start.5) | collective-permute-done | bytes 262176 | tf_op jit(solution)/shard_map/ppermute | solution.py:21
  30.2 0.0 copy-start.6
  30.2 6.4 %collective-permute-done.6.refs_1_ = bf16[256,512]{1,0:T(8,128)(2,1)S(1)} collective-permute-done((bf16[256,512]{1,0:T(8,128)(2,1)}, bf16[256,512]{1,0:T(8,128)(2,1)S(1)}, u32[]{:S(2)}, u32[]{:S(2)}) %collective-permute-start.6) | collective-permute-done | bytes 262176 | tf_op jit(solution)/shard_map/ppermute | solution.py:21
  36.6 0.0 copy-start.7
  36.6 0.0 collective-permute-done.7.refs_2_
  36.6 0.0 copy-start.8
  36.6 0.0 copy-done.6
  36.6 0.7 %copy-done.7 = bf16[256,512]{1,0:T(8,128)(2,1)} copy-done((bf16[256,512]{1,0:T(8,128)(2,1)}, bf16[256,512]{1,0:T(8,128)(2,1)S(1)}, u32[]{:S(2)}) %copy-start.7) | copy-done | bytes 262168
  37.3 0.1 copy-done.8
  37.4 2.1 %shard_map.99 = bf16[256,512]{1,0:T(8,128)(2,1)} custom-call(f32[256,512]{1,0:T(8,128)} %get-tuple-element.20.kept, bf16[256,512]{1,0:T(8,128)(2,1)} %copy-done.6, bf16[256,512]{1,0:T(8,128)(2,1)} %copy-done.7, bf16[256,512]{1,0:T(8,128)(2,1)} %copy-done.8), custom_call_target="tpu_custom_call" | custom-call | flops 393216 | bytes 1310720 | tf_op jit(solution)/shard_map/pallas_call | solution.py:126
  39.5 2.6 %collective-permute-start.8 = (bf16[256,512]{1,0:T(8,128)(2,1)}, bf16[256,512]{1,0:T(8,128)(2,1)S(1)}, u32[]{:S(2)}, u32[]{:S(2)}) collective-permute-start(bf16[256,512]{1,0:T(8,128)(2,1)} %shard_map.99), channel_id=1, source_target_pairs={{0,2},{1,3},{2,0},{3,1},{4,6},{5,7},{6,4},{7,5},{8,10},{9,11},{10,... | collective-permute-start | bytes 786440 | tf_op jit(solution)/shard_map/ppermute | solution.py:27
  42.1 0.0 collective-permute-done.received
  42.1 0.0 copy-start
  42.1 1.3 %copy-done = f32[4,256,512]{2,1,0:T(8,128)} copy-done((f32[4,256,512]{2,1,0:T(8,128)}, f32[4,256,512]{2,1,0:T(8,128)S(1)}, u32[]{:S(2)}) %copy-start) | copy-done | bytes 2097176
  43.4 3.1 %shard_map.95 = (f32[256,512]{1,0:T(8,128)}, bf16[256,512]{1,0:T(8,128)(2,1)}, bf16[256,512]{1,0:T(8,128)(2,1)}, bf16[256,512]{1,0:T(8,128)(2,1)}) custom-call(f32[4,256,512]{2,1,0:T(8,128)} %shard_map.93.own, f32[4,256,512]{2,1,0:T(8,128)} %copy-done), custom_call_target="tpu_custom_call" | custom-call | flops 524288 | bytes 5505024 | tf_op jit(solution)/shard_map/pallas_call | solution.py:102
  46.5 1.1 %collective-permute-start.1 = (bf16[256,512]{1,0:T(8,128)(2,1)}, bf16[256,512]{1,0:T(8,128)(2,1)S(1)}, u32[]{:S(2)}, u32[]{:S(2)}) collective-permute-start(bf16[256,512]{1,0:T(8,128)(2,1)} %get-tuple-element.17), channel_id=1, source_target_pairs={{0,8},{4,12},{8,0},{12,4},{16,24},{20,28},{24,16},{28,20},{1,9},{5... | collective-permute-start | bytes 786440 | tf_op jit(solution)/shard_map/ppermute | solution.py:21
  47.7 0.9 %collective-permute-start.2 = (bf16[256,512]{1,0:T(8,128)(2,1)}, bf16[256,512]{1,0:T(8,128)(2,1)S(1)}, u32[]{:S(2)}, u32[]{:S(2)}) collective-permute-start(bf16[256,512]{1,0:T(8,128)(2,1)} %get-tuple-element.18), channel_id=1, source_target_pairs={{0,16},{4,20},{8,24},{12,28},{16,0},{20,4},{24,8},{28,12},{1,17},{... | collective-permute-start | bytes 786440 | tf_op jit(solution)/shard_map/ppermute | solution.py:21
  48.6 1.4 %collective-permute-start.3 = (bf16[256,512]{1,0:T(8,128)(2,1)}, bf16[256,512]{1,0:T(8,128)(2,1)S(1)}, u32[]{:S(2)}, u32[]{:S(2)}) collective-permute-start(bf16[256,512]{1,0:T(8,128)(2,1)} %get-tuple-element.19), channel_id=1, source_target_pairs={{0,24},{4,28},{8,16},{12,20},{16,8},{20,12},{24,0},{28,4},{1,25},{... | collective-permute-start | bytes 786440 | tf_op jit(solution)/shard_map/ppermute | solution.py:21
  50.0 3.3 %collective-permute-done.8.refs_4_ = bf16[256,512]{1,0:T(8,128)(2,1)S(1)} collective-permute-done((bf16[256,512]{1,0:T(8,128)(2,1)}, bf16[256,512]{1,0:T(8,128)(2,1)S(1)}, u32[]{:S(2)}, u32[]{:S(2)}) %collective-permute-start.8) | collective-permute-done | bytes 262176 | tf_op jit(solution)/shard_map/ppermute | solution.py:27
  53.3 0.0 copy-start.2
  53.3 2.7 %collective-permute-done.1.refs_1_ = bf16[256,512]{1,0:T(8,128)(2,1)S(1)} collective-permute-done((bf16[256,512]{1,0:T(8,128)(2,1)}, bf16[256,512]{1,0:T(8,128)(2,1)S(1)}, u32[]{:S(2)}, u32[]{:S(2)}) %collective-permute-start.1) | collective-permute-done | bytes 262176 | tf_op jit(solution)/shard_map/ppermute | solution.py:21
  56.0 0.0 copy-start.3
  56.0 4.3 %collective-permute-done.2.refs_2_ = bf16[256,512]{1,0:T(8,128)(2,1)S(1)} collective-permute-done((bf16[256,512]{1,0:T(8,128)(2,1)}, bf16[256,512]{1,0:T(8,128)(2,1)S(1)}, u32[]{:S(2)}, u32[]{:S(2)}) %collective-permute-start.2) | collective-permute-done | bytes 262176 | tf_op jit(solution)/shard_map/ppermute | solution.py:21
  60.3 0.0 copy-start.4
  60.3 0.0 collective-permute-done.3.refs_3_
  60.3 0.0 copy-start.5
  60.3 0.0 copy-done.2
  60.3 0.0 copy-done.3
  60.3 0.7 %copy-done.4 = bf16[256,512]{1,0:T(8,128)(2,1)} copy-done((bf16[256,512]{1,0:T(8,128)(2,1)}, bf16[256,512]{1,0:T(8,128)(2,1)S(1)}, u32[]{:S(2)}) %copy-start.4) | copy-done | bytes 262168
  61.0 0.1 copy-done.5
  61.1 3.7 %shard_map.100 = (f32[256,2,256]{2,1,0:T(2,128)}, f32[256,2,256]{2,1,0:T(2,128)}, f32[256,2,256]{2,1,0:T(2,128)}, f32[256,2,256]{2,1,0:T(2,128)}) custom-call(f32[256,512]{1,0:T(8,128)} %get-tuple-element.16.refs_0_, bf16[256,512]{1,0:T(8,128)(2,1)} %copy-done.3, bf16[256,512]{1,0:T(8,128)(2,1)} %copy-done.4, bf16[256,512]{1,0:T(8,128)(2,1)} %copy-done.5, ...), custom_call_target="tpu_custom_call" | custom-call | flops 2621440 | bytes 4718592 | tf_op jit(solution)/shard_map/pallas_call | solution.py:163
Async XLA Ops:
  6.3 35.7 %collective-permute-start = (f32[4,256,512]{2,1,0:T(8,128)}, f32[4,256,512]{2,1,0:T(8,128)S(1)}, u32[]{:S(2)}, u32[]{:S(2)}) collective-permute-start(f32[4,256,512]{2,1,0:T(8,128)} %shard_map.94), channel_id=1, source_target_pairs={{0,4},{4,0},{8,12},{12,8},{16,20},{20,16},{24,28},{28,24},{1,5},{5... | collective-permute-start | bytes 6291464 | tf_op jit(solution)/shard_map/ppermute | solution.py:21
  11.6 4.9 %collective-permute-start.4 = (bf16[4,256,512]{2,1,0:T(8,128)(2,1)}, bf16[4,256,512]{2,1,0:T(8,128)(2,1)S(1)}, u32[]{:S(2)}, u32[]{:S(2)}) collective-permute-start(bf16[4,256,512]{2,1,0:T(8,128)(2,1)} %shard_map.97), channel_id=1, source_target_pairs={{0,4},{4,0},{8,12},{12,8},{16,20},{20,16},{24,28},{28,24},{1,5},{5... | collective-permute-start | bytes 3145736 | tf_op jit(solution)/shard_map/ppermute | solution.py:21
  16.5 1.0 %copy-start.1 = (bf16[4,256,512]{2,1,0:T(8,128)(2,1)}, bf16[4,256,512]{2,1,0:T(8,128)(2,1)S(1)}, u32[]{:S(2)}) copy-start(bf16[4,256,512]{2,1,0:T(8,128)(2,1)S(1)} %collective-permute-done.4.received) | copy-start | bytes 3145732
  19.9 10.3 %collective-permute-start.5 = (bf16[256,512]{1,0:T(8,128)(2,1)}, bf16[256,512]{1,0:T(8,128)(2,1)S(1)}, u32[]{:S(2)}, u32[]{:S(2)}) collective-permute-start(bf16[256,512]{1,0:T(8,128)(2,1)} %get-tuple-element.21), channel_id=1, source_target_pairs={{0,8},{4,12},{8,0},{12,4},{16,24},{20,28},{24,16},{28,20},{1,9},{5... | collective-permute-start | bytes 786440 | tf_op jit(solution)/shard_map/ppermute | solution.py:21
  22.8 13.8 %collective-permute-start.6 = (bf16[256,512]{1,0:T(8,128)(2,1)}, bf16[256,512]{1,0:T(8,128)(2,1)S(1)}, u32[]{:S(2)}, u32[]{:S(2)}) collective-permute-start(bf16[256,512]{1,0:T(8,128)(2,1)} %get-tuple-element.22), channel_id=1, source_target_pairs={{0,16},{4,20},{8,24},{12,28},{16,0},{20,4},{24,8},{28,12},{1,17},{... | collective-permute-start | bytes 786440 | tf_op jit(solution)/shard_map/ppermute | solution.py:21
  24.4 12.2 %collective-permute-start.7 = (bf16[256,512]{1,0:T(8,128)(2,1)}, bf16[256,512]{1,0:T(8,128)(2,1)S(1)}, u32[]{:S(2)}, u32[]{:S(2)}) collective-permute-start(bf16[256,512]{1,0:T(8,128)(2,1)} %get-tuple-element.23), channel_id=1, source_target_pairs={{0,24},{4,28},{8,16},{12,20},{16,8},{20,12},{24,0},{28,4},{1,25},{... | collective-permute-start | bytes 786440 | tf_op jit(solution)/shard_map/ppermute | solution.py:21
  30.2 6.4 %copy-start.6 = (bf16[256,512]{1,0:T(8,128)(2,1)}, bf16[256,512]{1,0:T(8,128)(2,1)S(1)}, u32[]{:S(2)}) copy-start(bf16[256,512]{1,0:T(8,128)(2,1)S(1)} %collective-permute-done.5.refs_0_) | copy-start | bytes 786436
  36.6 0.7 %copy-start.7 = (bf16[256,512]{1,0:T(8,128)(2,1)}, bf16[256,512]{1,0:T(8,128)(2,1)S(1)}, u32[]{:S(2)}) copy-start(bf16[256,512]{1,0:T(8,128)(2,1)S(1)} %collective-permute-done.6.refs_1_) | copy-start | bytes 786436
  36.6 0.8 %copy-start.8 = (bf16[256,512]{1,0:T(8,128)(2,1)}, bf16[256,512]{1,0:T(8,128)(2,1)S(1)}, u32[]{:S(2)}) copy-start(bf16[256,512]{1,0:T(8,128)(2,1)S(1)} %collective-permute-done.7.refs_2_) | copy-start | bytes 786436
  39.5 13.8 %collective-permute-start.8 = (bf16[256,512]{1,0:T(8,128)(2,1)}, bf16[256,512]{1,0:T(8,128)(2,1)S(1)}, u32[]{:S(2)}, u32[]{:S(2)}) collective-permute-start(bf16[256,512]{1,0:T(8,128)(2,1)} %shard_map.99), channel_id=1, source_target_pairs={{0,2},{1,3},{2,0},{3,1},{4,6},{5,7},{6,4},{7,5},{8,10},{9,11},{10,... | collective-permute-start | bytes 786440 | tf_op jit(solution)/shard_map/ppermute | solution.py:27
  42.1 1.3 %copy-start = (f32[4,256,512]{2,1,0:T(8,128)}, f32[4,256,512]{2,1,0:T(8,128)S(1)}, u32[]{:S(2)}) copy-start(f32[4,256,512]{2,1,0:T(8,128)S(1)} %collective-permute-done.received) | copy-start | bytes 6291460
  46.5 9.5 %collective-permute-start.1 = (bf16[256,512]{1,0:T(8,128)(2,1)}, bf16[256,512]{1,0:T(8,128)(2,1)S(1)}, u32[]{:S(2)}, u32[]{:S(2)}) collective-permute-start(bf16[256,512]{1,0:T(8,128)(2,1)} %get-tuple-element.17), channel_id=1, source_target_pairs={{0,8},{4,12},{8,0},{12,4},{16,24},{20,28},{24,16},{28,20},{1,9},{5... | collective-permute-start | bytes 786440 | tf_op jit(solution)/shard_map/ppermute | solution.py:21
  47.7 12.6 %collective-permute-start.2 = (bf16[256,512]{1,0:T(8,128)(2,1)}, bf16[256,512]{1,0:T(8,128)(2,1)S(1)}, u32[]{:S(2)}, u32[]{:S(2)}) collective-permute-start(bf16[256,512]{1,0:T(8,128)(2,1)} %get-tuple-element.18), channel_id=1, source_target_pairs={{0,16},{4,20},{8,24},{12,28},{16,0},{20,4},{24,8},{28,12},{1,17},{... | collective-permute-start | bytes 786440 | tf_op jit(solution)/shard_map/ppermute | solution.py:21
  48.6 11.7 %collective-permute-start.3 = (bf16[256,512]{1,0:T(8,128)(2,1)}, bf16[256,512]{1,0:T(8,128)(2,1)S(1)}, u32[]{:S(2)}, u32[]{:S(2)}) collective-permute-start(bf16[256,512]{1,0:T(8,128)(2,1)} %get-tuple-element.19), channel_id=1, source_target_pairs={{0,24},{4,28},{8,16},{12,20},{16,8},{20,12},{24,0},{28,4},{1,25},{... | collective-permute-start | bytes 786440 | tf_op jit(solution)/shard_map/ppermute | solution.py:21
  53.3 7.0 %copy-start.2 = (bf16[256,512]{1,0:T(8,128)(2,1)}, bf16[256,512]{1,0:T(8,128)(2,1)S(1)}, u32[]{:S(2)}) copy-start(bf16[256,512]{1,0:T(8,128)(2,1)S(1)} %collective-permute-done.8.refs_4_) | copy-start | bytes 786436
  56.0 4.3 %copy-start.3 = (bf16[256,512]{1,0:T(8,128)(2,1)}, bf16[256,512]{1,0:T(8,128)(2,1)S(1)}, u32[]{:S(2)}) copy-start(bf16[256,512]{1,0:T(8,128)(2,1)S(1)} %collective-permute-done.1.refs_1_) | copy-start | bytes 786436
  60.3 0.7 %copy-start.4 = (bf16[256,512]{1,0:T(8,128)(2,1)}, bf16[256,512]{1,0:T(8,128)(2,1)S(1)}, u32[]{:S(2)}) copy-start(bf16[256,512]{1,0:T(8,128)(2,1)S(1)} %collective-permute-done.2.refs_2_) | copy-start | bytes 786436
  60.3 0.8 %copy-start.5 = (bf16[256,512]{1,0:T(8,128)(2,1)}, bf16[256,512]{1,0:T(8,128)(2,1)S(1)}, u32[]{:S(2)}) copy-start(bf16[256,512]{1,0:T(8,128)(2,1)S(1)} %collective-permute-done.3.refs_3_) | copy-start | bytes 786436

commit v2 on v1

v2 whole, which is shorter than its diff:
```python
import functools

import jax
import jax.numpy as jnp
from jax import lax
from jax.experimental import pallas as pl
from jax.experimental.pallas import tpu as pltpu
from jax.sharding import PartitionSpec as P

beta_one = 0.9
beta_two = 0.95
adam_epsilon = 1e-08
bias_first = 1.0 - 0.9**50
bias_second = 1.0 - 0.95**50

LANES = 128


def exchanged(value, axis, mask):
    count = lax.axis_size(axis)
    return lax.ppermute(value, axis, [(source, source ^ mask) for source in range(count)])


def mirrored(value):
    count = lax.axis_size("section")
    pairs = [(source, (source + count // 2) % count) for source in range(count)]
    return lax.ppermute(value, "section", pairs)


def expand_hidden(route, counts, direction, hidden, wide, blocks, experts):
    rows, width = hidden.shape
    block = rows // blocks
    seen = [jnp.int32(0) for _ in range(experts)]
    place = lax.broadcasted_iota(jnp.int32, (block, width), 0)
    for b in range(blocks):
        expert = route[direction, b]
        values = hidden[b * block : (b + 1) * block, :].astype(jnp.float32)
        for e in range(experts):
            named = expert == e
            limit = jnp.where(named, counts[direction, e] - seen[e] * block, 0)
            kept = jnp.where(place < limit, values, 0.0)
            wide[b * block : (b + 1) * block, e * width : (e + 1) * width] = kept.astype(wide.dtype)
            seen[e] = seen[e] + named.astype(jnp.int32)


VMEM_BYTES = 16 << 20
ANYWHERE = pl.BlockSpec(memory_space=pl.ANY)
IN_VMEM = pl.BlockSpec(memory_space=pltpu.VMEM)
IN_SMEM = pl.BlockSpec(memory_space=pltpu.SMEM)
PARAMS = pltpu.CompilerParams(vmem_limit_bytes=VMEM_BYTES)


def held(value):
    return pltpu.with_memory_space_constraint(value, pltpu.VMEM)


def product_kernel(
    direction, sibling, experts, route, counts, inputs, hidden, *refs
):
    out, wide, columns, rows, column_sems, row_sem = refs[-6:]
    chips, _, share = columns.shape
    me = lax.axis_index("dp")
    chip, core = me // 2, me % 2
    if sibling:
        core = 1 - core
    row_copy = pltpu.make_async_copy(hidden.at[direction], rows, row_sem)
    row_copy.start()
    copies = []
    for k in range(chips):
        begin = pl.multiple_of((lax.bitwise_xor(chip, k) * 2 + core) * share, share)
        copy = pltpu.make_async_copy(
            inputs.at[direction, :, pl.ds(begin, share)], columns.at[k], column_sems.at[k]
        )
        copy.start()
        copies.append(copy)
    row_copy.wait()
    expand_hidden(route, counts, direction, rows, wide, route.shape[1], experts)
    for k in range(chips):
        copies[k].wait()
        product = lax.dot_general(
            columns[k], wide[...], (((0,), (0,)), ((), ())), preferred_element_type=jnp.float32
        )
        out[k] = product.astype(out.dtype)


def products(direction, sibling, after, route, counts, inputs, hidden, share, chips, experts, dtype):
    _, rows, _ = inputs.shape
    width = hidden.shape[2]
    columns = experts * width
    return pl.pallas_call(
        functools.partial(product_kernel, direction, sibling, experts),
        in_specs=[IN_SMEM, IN_SMEM, ANYWHERE, ANYWHERE] + [ANYWHERE] * len(after),
        out_specs=IN_VMEM,
        out_shape=pltpu.VMEM((chips, share, columns), dtype),
        scratch_shapes=[
            pltpu.VMEM((rows, columns), jnp.bfloat16),
            pltpu.VMEM((chips, rows, share), jnp.bfloat16),
            pltpu.VMEM((rows, width), jnp.bfloat16),
            pltpu.SemaphoreType.DMA((chips,)),
            pltpu.SemaphoreType.DMA,
        ],
        compiler_params=PARAMS,
        cost_estimate=pl.CostEstimate(
            flops=2 * rows * chips * share * columns,
            bytes_accessed=2 * rows * (chips * share + width),
            transcendentals=0,
        ),
    )(
        route,
        counts,
        pltpu.with_memory_space_constraint(inputs, pltpu.HBM),
        pltpu.with_memory_space_constraint(hidden, pltpu.HBM),
        *after,
    )


def join_kernel(own, received, kept, *sent):
    kept[...] = own[0].astype(jnp.float32) + received[0].astype(jnp.float32)
    for k, out in enumerate(sent):
        total = own[k + 1].astype(jnp.float32) + received[k + 1].astype(jnp.float32)
        out[...] = total.astype(out.dtype)


def joined(own, received):
    chips, share, columns = own.shape
    return pl.pallas_call(
        join_kernel,
        in_specs=[IN_VMEM, IN_VMEM],
        out_specs=[IN_VMEM] * chips,
        out_shape=[pltpu.VMEM((share, columns), jnp.float32)]
        + [pltpu.VMEM((share, columns), jnp.bfloat16)] * (chips - 1),
        compiler_params=PARAMS,
        cost_estimate=pl.CostEstimate(
            flops=own.size, bytes_accessed=own.nbytes, transcendentals=0
        ),
    )(held(own), held(received))


def total_kernel(count, kept, *refs):
    total = kept[...]
    for part in refs[:count]:
        total = total + part[...].astype(jnp.float32)
    out = refs[-1]
    out[...] = total.astype(out.dtype)


def totalled(kept, received, after, dtype):
    count = len(received)
    return pl.pallas_call(
        functools.partial(total_kernel, count),
        in_specs=[IN_VMEM] * (1 + count) + [ANYWHERE] * len(after),
        out_specs=IN_VMEM,
        out_shape=pltpu.VMEM(kept.shape, dtype),
        compiler_params=PARAMS,
        cost_estimate=pl.CostEstimate(
            flops=kept.size * count, bytes_accessed=kept.nbytes, transcendentals=0
        ),
    )(held(kept), *map(held, received), *after)


def update_kernel(experts, count, steps, *refs):
    kept = refs[0]
    received = refs[1 : 1 + count]
    first, second = refs[1 + count : 3 + count]
    outs = refs[3 + count : 7 + count]
    grad_out, first_out, second_out, step_out, sems = refs[7 + count :]
    share, _, width = first.shape
    rows = share // steps
    copies = []
    for i in range(steps):
        some = slice(i * rows, (i + 1) * rows)
        for e in range(experts):
            columns = slice(e * width, (e + 1) * width)
            grad = kept[some, columns]
            for part in received:
                grad = grad + part[some, columns].astype(jnp.float32)
            new_first = beta_one * first[some, e, :] + (1.0 - beta_one) * grad
            new_second = beta_two * second[some, e, :] + (1.0 - beta_two) * grad * grad
            grad_out[some, e, :] = grad
            first_out[some, e, :] = new_first
            second_out[some, e, :] = new_second
            step_out[some, e, :] = (
                new_first / bias_first / (jnp.sqrt(new_second / bias_second) + adam_epsilon)
            )
        for j, (source, target) in enumerate(
            zip((grad_out, first_out, second_out, step_out), outs)
        ):
            copy = pltpu.make_async_copy(
                source.at[pl.ds(i * rows, rows)], target.at[pl.ds(i * rows, rows)], sems.at[i, j]
            )
            copy.start()
            copies.append(copy)
    for copy in copies:
        copy.wait()


def updated(kept, received, first, second):
    _, experts, _ = first.shape
    count, steps = len(received), 4
    return pl.pallas_call(
        functools.partial(update_kernel, experts, count, steps),
        in_specs=[IN_VMEM] * (3 + count),
        out_specs=[ANYWHERE] * 4,
        out_shape=[jax.ShapeDtypeStruct(first.shape, jnp.float32)] * 4,
        scratch_shapes=[pltpu.VMEM(first.shape, jnp.float32)] * 4
        + [pltpu.SemaphoreType.DMA((steps, 4))],
        compiler_params=PARAMS,
        cost_estimate=pl.CostEstimate(
            flops=20 * first.size,
            bytes_accessed=4 * first.nbytes,
            transcendentals=2 * first.size,
        ),
    )(held(kept), *map(held, received), held(first), held(second))


def fast_device(saved_inputs, hidden_grads, block_expert, live_counts, first_moment, second_moment):
    chips = lax.axis_size("dp") // 2
    share, experts = first_moment.shape[1:3]
    product = functools.partial(
        products,
        route=block_expert[0, 0],
        counts=live_counts[0, 0],
        inputs=saved_inputs[0, 0],
        hidden=hidden_grads[0, 0],
        share=share,
        chips=chips,
        experts=experts,
    )

    def direction_part(direction, after, dtype):
        sibling = product(direction, True, after, dtype=dtype)
        other = exchanged(sibling, "dp", 1)
        kept, *sent = joined(product(direction, False, [sibling], dtype=dtype), other)
        return kept, [exchanged(part, "dp", 2 * (k + 1)) for k, part in enumerate(sent)]

    kept_one, received_one = direction_part(1, [], jnp.bfloat16)
    kept_zero, received_zero = direction_part(0, [kept_one], jnp.float32)
    partner = mirrored(totalled(kept_one, received_one, [kept_zero], jnp.bfloat16))
    outs = updated(kept_zero, received_zero + [partner], first_moment[0], second_moment[0])
    return tuple(out[None] for out in outs)


def route_select(block_expert, live_counts, block):
    experts = jnp.arange(live_counts.shape[-1], dtype=jnp.int32)
    onehot = (block_expert[..., :, None] == experts).astype(jnp.int32)
    earlier = jnp.cumsum(onehot, axis=-2) - onehot
    before = jnp.sum(earlier * onehot, axis=-1)
    limits = jnp.sum(live_counts[..., None, :] * onehot, axis=-1)
    positions = before[..., None] * block + jnp.arange(block, dtype=jnp.int32)
    return positions < limits[..., None], onehot


def plain_device(saved_inputs, hidden_grads, block_expert, live_counts, first_moment, second_moment):
    _, _, _, rows, model_width = saved_inputs.shape
    hidden = hidden_grads.shape[4]
    blocks = block_expert.shape[3]
    block = rows // blocks
    live_rows, onehot = route_select(block_expert[0, 0], live_counts[0, 0], block)
    masked = hidden_grads.reshape(2, blocks, block, hidden) * live_rows[..., None].astype(
        jnp.bfloat16
    )
    wide = masked[:, :, :, None, :] * onehot[:, :, None, :, None].astype(jnp.bfloat16)
    wide = wide.reshape(2, rows, -1)
    parts = jnp.einsum(
        "krd,krc->kdc", saved_inputs[0, 0], wide, preferred_element_type=jnp.float32
    )
    sent = lax.optimization_barrier(parts[1].astype(jnp.bfloat16)).astype(jnp.float32)
    summed = lax.psum_scatter(
        jnp.stack([parts[0], sent], axis=1), "dp", scatter_dimension=0, tiled=True
    )
    grad_total = (summed[:, 0] + mirrored(summed[:, 1])).reshape(first_moment.shape[1:])
    new_first = beta_one * first_moment[0] + (1.0 - beta_one) * grad_total
    new_second = beta_two * second_moment[0] + (1.0 - beta_two) * grad_total * grad_total
    step_direction = new_first / bias_first / (jnp.sqrt(new_second / bias_second) + adam_epsilon)
    return (grad_total[None], new_first[None], new_second[None], step_direction[None])


def solution(mesh):
    in_specs = (
        P("section", "dp", None, None, None),
        P("section", "dp", None, None, None),
        P("section", "dp", None, None),
        P("section", "dp", None, None),
        P("section", "dp", None, None),
        P("section", "dp", None, None),
    )
    out_specs = (P("section", "dp", None, None),) * 4

    def run(*arrays):
        ranks = mesh.shape["dp"]
        paired = ranks % 2 == 0 and ranks & (ranks - 1) == 0
        per_device = fast_device if paired and arrays[4].shape[1] // ranks % LANES == 0 else plain_device
        return jax.shard_map(
            per_device, mesh=mesh, in_specs=in_specs, out_specs=out_specs, check_vma=False
        )(*arrays)

    return run
```

time: 65.3 us -> 47.3 us (0.72)
  Pallas kernels: 30.9 us -> 14.5 us
  local copies, waits for them, and re-layouts: 3.9 us -> 1.36 us
  waiting for transfers between devices: 17.5 us -> 19.2 us
    pallas_call x8, Pallas kernels: 30.9 us -> 14.5 us  [the longest x4 11.6 us: products(): pl.pallas_call(functools.partial(product_kernel, direction, sibling, expe...]
    ppermute x1, waiting for transfers between devices: 3.27 us -> 7.67 us  [mirrored(): return lax.ppermute(value, 'section', pairs)]
    ppermute x8, waiting for transfers between devices: 14.2 us -> 11.5 us  [exchanged(): lax.ppermute(value, axis, [(source, source ^ mask) for source in range(co...]
    unnamed x18 -> x8, local copies, waits for them, and re-layouts: 3.9 us -> 1.36 us
    another operation x1 -> x0, other arithmetic: 0.65 us -> none  [fast_device(): place = jnp.stack([me // 2, me % 2]).astype(jnp.int32)]
  transfers between devices with their start and end apart: 9 -> 9, of which waited for: 5 -> 4; matrix products, arithmetic and copies ran while one was open for 0% -> 0% of each run, Pallas kernels for 34% -> 13%
where the time goes in v2:
time: 47.3 us; the launch traced here: 47.1 us
  waiting for transfers between devices  19.2 us (41%)
  Pallas kernels  14.5 us (31%)
  starting transfers between devices  11.2 us (24%)
  local copies, waits for them, and re-layouts  1.36 us (3%)
  between operations  0.73 us (2%)
    pallas_call x4, Pallas kernels, products(): pl.pallas_call(functools.partial(product_kernel, direction, sibling, expe...  11.6 us
    ppermute x8, waiting for transfers between devices, exchanged(): lax.ppermute(value, axis, [(source, source ^ mask) for source in range(co...  11.5 us
    ppermute x8, starting transfers between devices, exchanged(): lax.ppermute(value, axis, [(source, source ^ mask) for source in range(co...  8.59 us
    ppermute x1, waiting for transfers between devices, mirrored(): return lax.ppermute(value, 'section', pairs)  7.67 us
    ppermute x1, starting transfers between devices, mirrored(): return lax.ppermute(value, 'section', pairs)  2.66 us
    pallas_call x1, Pallas kernels, updated(): pl.pallas_call(functools.partial(update_kernel, experts, count, steps), i...  2.35 us
    unnamed x8, local copies, waits for them, and re-layouts  1.36 us
  transfers between devices with their start and end apart: 9, of which 4 were waited for; matrix products, arithmetic and copies ran while one was open for 0% of the time, Pallas kernels for 13%

profile of v2, /device:TPU:0, one launch (start us, length us, event | category | flops | bytes accessed | tf_op | source)
XLA Modules:
  0.0 47.1 jit_solution(13890573680857596054)
XLA Ops:
  0.6 0.0 copy-start.2
  0.6 0.7 %copy-done.2 = s32[1,1,2,3]{3,2,1,0:T(2,128)S(1)} copy-done((s32[1,1,2,3]{3,2,1,0:T(2,128)S(1)}, s32[1,1,2,3]{3,2,1,0:T(2,128)}, u32[]{:S(2)}) %copy-start.2) | copy-done | bytes 48
  1.3 0.0 copy-start.3
  1.3 0.7 %copy-done.3 = s32[1,1,2,2]{3,2,1,0:T(2,128)S(1)} copy-done((s32[1,1,2,2]{3,2,1,0:T(2,128)S(1)}, s32[1,1,2,2]{3,2,1,0:T(2,128)}, u32[]{:S(2)}) %copy-start.3) | copy-done | bytes 40
  2.0 2.9 %shard_map.93.refs_0_ = bf16[4,256,512]{2,1,0:T(8,128)(2,1)S(1)} custom-call(s32[2,3]{1,0:T(2,128)S(1)} %bitcast.12, s32[2,2]{1,0:T(2,128)S(1)} %bitcast.16, bf16[2,384,2048]{2,1,0:T(8,128)(2,1)} %bitcast.20, bf16[2,384,256]{2,1,0:T(8,128)(2,1)} %bitcast.24), custom_call_target="tpu_custom_call" | custom-call | flops 402653184 | bytes 983040 | tf_op jit(solution)/shard_map/pallas_call | solution.py:90
  4.9 0.5 %collective-permute-start = (bf16[4,256,512]{2,1,0:T(8,128)(2,1)S(1)}, bf16[4,256,512]{2,1,0:T(8,128)(2,1)S(1)}, u32[]{:S(2)}, u32[]{:S(2)}) collective-permute-start(bf16[4,256,512]{2,1,0:T(8,128)(2,1)S(1)} %shard_map.93.refs_0_), channel_id=1, source_target_pairs={{0,4},{4,0},{8,12},{12,8},{16,20},{20,16},{24,28},{28,24},{1,5},{5... | collective-permute-start | bytes 3145736 | tf_op jit(solution)/shard_map/ppermute | solution.py:21
  5.4 2.9 %shard_map.94.own = bf16[4,256,512]{2,1,0:T(8,128)(2,1)S(1)} custom-call(s32[2,3]{1,0:T(2,128)S(1)} %bitcast.13, s32[2,2]{1,0:T(2,128)S(1)} %bitcast.17, bf16[2,384,2048]{2,1,0:T(8,128)(2,1)} %bitcast.21, bf16[2,384,256]{2,1,0:T(8,128)(2,1)} %bitcast.25, bf16[4,256,512]{2,1,0:T(8,128)(2,1)S(1)} %shard_map.93.refs_0_), custom_call_target="tpu_custom_call" | custom-call | flops 402653184 | bytes 983040 | tf_op jit(solution)/shard_map/pallas_call | solution.py:90
  8.3 0.0 collective-permute-done.received
  8.4 0.2 shard_map.95
  8.6 2.9 %shard_map.96.refs_0_ = f32[4,256,512]{2,1,0:T(8,128)S(1)} custom-call(s32[2,3]{1,0:T(2,128)S(1)} %bitcast.14, s32[2,2]{1,0:T(2,128)S(1)} %bitcast.18, bf16[2,384,2048]{2,1,0:T(8,128)(2,1)} %bitcast.22, bf16[2,384,256]{2,1,0:T(8,128)(2,1)} %bitcast.26, f32[256,512]{1,0:T(8,128)S(1)} %get-tuple-element.16.refs_0_.kept), custom_call_target="tpu_custom_call" | custom-call | flops 402653184 | bytes 983040 | tf_op jit(solution)/shard_map/pallas_call | solution.py:90
  11.5 0.1 collective-permute-start.1
  11.6 2.9 %collective-permute-start.5 = (bf16[256,512]{1,0:T(8,128)(2,1)S(1)}, bf16[256,512]{1,0:T(8,128)(2,1)S(1)}, u32[]{:S(2)}, u32[]{:S(2)}) collective-permute-start(bf16[256,512]{1,0:T(8,128)(2,1)S(1)} %get-tuple-element.21), channel_id=1, source_target_pairs={{0,8},{4,12},{8,0},{12,4},{16,24},{20,28},{24,16},{28,20},{1,9},{5... | collective-permute-start | bytes 786440 | tf_op jit(solution)/shard_map/ppermute | solution.py:21
  14.6 1.5 %collective-permute-start.6 = (bf16[256,512]{1,0:T(8,128)(2,1)S(1)}, bf16[256,512]{1,0:T(8,128)(2,1)S(1)}, u32[]{:S(2)}, u32[]{:S(2)}) collective-permute-start(bf16[256,512]{1,0:T(8,128)(2,1)S(1)} %get-tuple-element.22), channel_id=1, source_target_pairs={{0,16},{4,20},{8,24},{12,28},{16,0},{20,4},{24,8},{28,12},{1,17},{... | collective-permute-start | bytes 786440 | tf_op jit(solution)/shard_map/ppermute | solution.py:21
  16.1 0.0 collective-permute-start.7
  16.1 2.9 %shard_map.97.own = f32[4,256,512]{2,1,0:T(8,128)S(1)} custom-call(s32[2,3]{1,0:T(2,128)S(1)} %bitcast.15, s32[2,2]{1,0:T(2,128)S(1)} %bitcast.19, bf16[2,384,2048]{2,1,0:T(8,128)(2,1)} %bitcast.23, bf16[2,384,256]{2,1,0:T(8,128)(2,1)} %bitcast.27, f32[4,256,512]{2,1,0:T(8,128)S(1)} %shard_map.96.refs_0_), custom_call_target="tpu_custom_call" | custom-call | flops 402653184 | bytes 983040 | tf_op jit(solution)/shard_map/pallas_call | solution.py:90
  19.0 0.0 collective-permute-done.1.received
  19.0 0.2 shard_map.98
  19.2 0.0 copy-start
  19.2 0.0 copy-start.1
  19.3 2.4 %collective-permute-done.5.refs_0_ = bf16[256,512]{1,0:T(8,128)(2,1)S(1)} collective-permute-done((bf16[256,512]{1,0:T(8,128)(2,1)S(1)}, bf16[256,512]{1,0:T(8,128)(2,1)S(1)}, u32[]{:S(2)}, u32[]{:S(2)}) %collective-permute-start.5) | collective-permute-done | bytes 262176 | tf_op jit(solution)/shard_map/ppermute | solution.py:21
  21.7 6.5 %collective-permute-done.6.refs_1_ = bf16[256,512]{1,0:T(8,128)(2,1)S(1)} collective-permute-done((bf16[256,512]{1,0:T(8,128)(2,1)S(1)}, bf16[256,512]{1,0:T(8,128)(2,1)S(1)}, u32[]{:S(2)}, u32[]{:S(2)}) %collective-permute-start.6) | collective-permute-done | bytes 262176 | tf_op jit(solution)/shard_map/ppermute | solution.py:21
  28.2 0.0 collective-permute-done.7.refs_2_
  28.2 0.1 shard_map.99
  28.3 2.7 %collective-permute-start.8 = (bf16[256,512]{1,0:T(8,128)(2,1)S(1)}, bf16[256,512]{1,0:T(8,128)(2,1)S(1)}, u32[]{:S(2)}, u32[]{:S(2)}) collective-permute-start(bf16[256,512]{1,0:T(8,128)(2,1)S(1)} %shard_map.99), channel_id=1, source_target_pairs={{0,2},{1,3},{2,0},{3,1},{4,6},{5,7},{6,4},{7,5},{8,10},{9,11},{10,... | collective-permute-start | bytes 786440 | tf_op jit(solution)/shard_map/ppermute | solution.py:27
  31.0 1.2 %collective-permute-start.2 = (bf16[256,512]{1,0:T(8,128)(2,1)S(1)}, bf16[256,512]{1,0:T(8,128)(2,1)S(1)}, u32[]{:S(2)}, u32[]{:S(2)}) collective-permute-start(bf16[256,512]{1,0:T(8,128)(2,1)S(1)} %get-tuple-element.18), channel_id=1, source_target_pairs={{0,8},{4,12},{8,0},{12,4},{16,24},{20,28},{24,16},{28,20},{1,9},{5... | collective-permute-start | bytes 786440 | tf_op jit(solution)/shard_map/ppermute | solution.py:21
  32.2 0.8 %collective-permute-start.3 = (bf16[256,512]{1,0:T(8,128)(2,1)S(1)}, bf16[256,512]{1,0:T(8,128)(2,1)S(1)}, u32[]{:S(2)}, u32[]{:S(2)}) collective-permute-start(bf16[256,512]{1,0:T(8,128)(2,1)S(1)} %get-tuple-element.19), channel_id=1, source_target_pairs={{0,16},{4,20},{8,24},{12,28},{16,0},{20,4},{24,8},{28,12},{1,17},{... | collective-permute-start | bytes 786440 | tf_op jit(solution)/shard_map/ppermute | solution.py:21
  33.0 1.4 %collective-permute-start.4 = (bf16[256,512]{1,0:T(8,128)(2,1)S(1)}, bf16[256,512]{1,0:T(8,128)(2,1)S(1)}, u32[]{:S(2)}, u32[]{:S(2)}) collective-permute-start(bf16[256,512]{1,0:T(8,128)(2,1)S(1)} %get-tuple-element.20), channel_id=1, source_target_pairs={{0,24},{4,28},{8,16},{12,20},{16,8},{20,12},{24,0},{28,4},{1,25},{... | collective-permute-start | bytes 786440 | tf_op jit(solution)/shard_map/ppermute | solution.py:21
  34.5 7.7 %collective-permute-done.8.refs_4_ = bf16[256,512]{1,0:T(8,128)(2,1)S(1)} collective-permute-done((bf16[256,512]{1,0:T(8,128)(2,1)S(1)}, bf16[256,512]{1,0:T(8,128)(2,1)S(1)}, u32[]{:S(2)}, u32[]{:S(2)}) %collective-permute-start.8) | collective-permute-done | bytes 262176 | tf_op jit(solution)/shard_map/ppermute | solution.py:27
  42.1 0.0 collective-permute-done.2.refs_1_
  42.2 2.6 %collective-permute-done.3.refs_2_ = bf16[256,512]{1,0:T(8,128)(2,1)S(1)} collective-permute-done((bf16[256,512]{1,0:T(8,128)(2,1)S(1)}, bf16[256,512]{1,0:T(8,128)(2,1)S(1)}, u32[]{:S(2)}, u32[]{:S(2)}) %collective-permute-start.3) | collective-permute-done | bytes 262176 | tf_op jit(solution)/shard_map/ppermute | solution.py:21
  44.7 0.0 collective-permute-done.4.refs_3_
  44.7 0.0 copy-done
  44.7 0.0 copy-done.1
  44.7 2.4 %shard_map.100 = (f32[256,2,256]{2,1,0:T(2,128)}, f32[256,2,256]{2,1,0:T(2,128)}, f32[256,2,256]{2,1,0:T(2,128)}, f32[256,2,256]{2,1,0:T(2,128)}) custom-call(f32[256,512]{1,0:T(8,128)S(1)} %get-tuple-element.17.refs_3_.refs_0_, bf16[256,512]{1,0:T(8,128)(2,1)S(1)} %collective-permute-done.2.refs_1_, bf16[256,512]{1,0:T(8,128)(2,1)S(1)} %collective-permute-done.3.refs_2_, ...), custom_call_target="tpu_custom_call" | custom-call | flops 2621440 | bytes 2097152 | tf_op jit(solution)/shard_map/pallas_call | solution.py:200
Async XLA Ops:
  0.6 0.7 %copy-start.2 = (s32[1,1,2,3]{3,2,1,0:T(2,128)S(1)}, s32[1,1,2,3]{3,2,1,0:T(2,128)}, u32[]{:S(2)}) copy-start(s32[1,1,2,3]{3,2,1,0:T(2,128)} %param.8) | copy-start | bytes 76
  1.3 0.7 %copy-start.3 = (s32[1,1,2,2]{3,2,1,0:T(2,128)S(1)}, s32[1,1,2,2]{3,2,1,0:T(2,128)}, u32[]{:S(2)}) copy-start(s32[1,1,2,2]{3,2,1,0:T(2,128)} %param.9) | copy-start | bytes 52
  4.9 3.4 %collective-permute-start = (bf16[4,256,512]{2,1,0:T(8,128)(2,1)S(1)}, bf16[4,256,512]{2,1,0:T(8,128)(2,1)S(1)}, u32[]{:S(2)}, u32[]{:S(2)}) collective-permute-start(bf16[4,256,512]{2,1,0:T(8,128)(2,1)S(1)} %shard_map.93.refs_0_), channel_id=1, source_target_pairs={{0,4},{4,0},{8,12},{12,8},{16,20},{20,16},{24,28},{28,24},{1,5},{5... | collective-permute-start | bytes 3145736 | tf_op jit(solution)/shard_map/ppermute | solution.py:21
  11.5 7.5 %collective-permute-start.1 = (f32[4,256,512]{2,1,0:T(8,128)S(1)}, f32[4,256,512]{2,1,0:T(8,128)S(1)}, u32[]{:S(2)}, u32[]{:S(2)}) collective-permute-start(f32[4,256,512]{2,1,0:T(8,128)S(1)} %shard_map.96.refs_0_), channel_id=1, source_target_pairs={{0,4},{4,0},{8,12},{12,8},{16,20},{20,16},{24,28},{28,24},{1,5},{5... | collective-permute-start | bytes 6291464 | tf_op jit(solution)/shard_map/ppermute | solution.py:21
  11.6 10.0 %collective-permute-start.5 = (bf16[256,512]{1,0:T(8,128)(2,1)S(1)}, bf16[256,512]{1,0:T(8,128)(2,1)S(1)}, u32[]{:S(2)}, u32[]{:S(2)}) collective-permute-start(bf16[256,512]{1,0:T(8,128)(2,1)S(1)} %get-tuple-element.21), channel_id=1, source_target_pairs={{0,8},{4,12},{8,0},{12,4},{16,24},{20,28},{24,16},{28,20},{1,9},{5... | collective-permute-start | bytes 786440 | tf_op jit(solution)/shard_map/ppermute | solution.py:21
  14.6 13.6 %collective-permute-start.6 = (bf16[256,512]{1,0:T(8,128)(2,1)S(1)}, bf16[256,512]{1,0:T(8,128)(2,1)S(1)}, u32[]{:S(2)}, u32[]{:S(2)}) collective-permute-start(bf16[256,512]{1,0:T(8,128)(2,1)S(1)} %get-tuple-element.22), channel_id=1, source_target_pairs={{0,16},{4,20},{8,24},{12,28},{16,0},{20,4},{24,8},{28,12},{1,17},{... | collective-permute-start | bytes 786440 | tf_op jit(solution)/shard_map/ppermute | solution.py:21
  16.1 12.1 %collective-permute-start.7 = (bf16[256,512]{1,0:T(8,128)(2,1)S(1)}, bf16[256,512]{1,0:T(8,128)(2,1)S(1)}, u32[]{:S(2)}, u32[]{:S(2)}) collective-permute-start(bf16[256,512]{1,0:T(8,128)(2,1)S(1)} %get-tuple-element.23), channel_id=1, source_target_pairs={{0,24},{4,28},{8,16},{12,20},{16,8},{20,12},{24,0},{28,4},{1,25},{... | collective-permute-start | bytes 786440 | tf_op jit(solution)/shard_map/ppermute | solution.py:21
  19.2 25.5 %copy-start = (f32[1,256,2,256]{3,2,1,0:T(2,128)S(1)}, f32[1,256,2,256]{3,2,1,0:T(2,128)}, u32[]{:S(2)}) copy-start(f32[1,256,2,256]{3,2,1,0:T(2,128)} %param.10) | copy-start | bytes 1572868
  19.2 25.5 %copy-start.1 = (f32[1,256,2,256]{3,2,1,0:T(2,128)S(1)}, f32[1,256,2,256]{3,2,1,0:T(2,128)}, u32[]{:S(2)}) copy-start(f32[1,256,2,256]{3,2,1,0:T(2,128)} %param.11) | copy-start | bytes 1572868
  28.3 13.8 %collective-permute-start.8 = (bf16[256,512]{1,0:T(8,128)(2,1)S(1)}, bf16[256,512]{1,0:T(8,128)(2,1)S(1)}, u32[]{:S(2)}, u32[]{:S(2)}) collective-permute-start(bf16[256,512]{1,0:T(8,128)(2,1)S(1)} %shard_map.99), channel_id=1, source_target_pairs={{0,2},{1,3},{2,0},{3,1},{4,6},{5,7},{6,4},{7,5},{8,10},{9,11},{10,... | collective-permute-start | bytes 786440 | tf_op jit(solution)/shard_map/ppermute | solution.py:27
  31.0 11.2 %collective-permute-start.2 = (bf16[256,512]{1,0:T(8,128)(2,1)S(1)}, bf16[256,512]{1,0:T(8,128)(2,1)S(1)}, u32[]{:S(2)}, u32[]{:S(2)}) collective-permute-start(bf16[256,512]{1,0:T(8,128)(2,1)S(1)} %get-tuple-element.18), channel_id=1, source_target_pairs={{0,8},{4,12},{8,0},{12,4},{16,24},{20,28},{24,16},{28,20},{1,9},{5... | collective-permute-start | bytes 786440 | tf_op jit(solution)/shard_map/ppermute | solution.py:21
  32.2 12.5 %collective-permute-start.3 = (bf16[256,512]{1,0:T(8,128)(2,1)S(1)}, bf16[256,512]{1,0:T(8,128)(2,1)S(1)}, u32[]{:S(2)}, u32[]{:S(2)}) collective-permute-start(bf16[256,512]{1,0:T(8,128)(2,1)S(1)} %get-tuple-element.19), channel_id=1, source_target_pairs={{0,16},{4,20},{8,24},{12,28},{16,0},{20,4},{24,8},{28,12},{1,17},{... | collective-permute-start | bytes 786440 | tf_op jit(solution)/shard_map/ppermute | solution.py:21
  33.0 11.7 %collective-permute-start.4 = (bf16[256,512]{1,0:T(8,128)(2,1)S(1)}, bf16[256,512]{1,0:T(8,128)(2,1)S(1)}, u32[]{:S(2)}, u32[]{:S(2)}) collective-permute-start(bf16[256,512]{1,0:T(8,128)(2,1)S(1)} %get-tuple-element.20), channel_id=1, source_target_pairs={{0,24},{4,28},{8,16},{12,20},{16,8},{20,12},{24,0},{28,4},{1,25},{... | collective-permute-start | bytes 786440 | tf_op jit(solution)/shard_map/ppermute | solution.py:21

commit v3 on v2

--- a/solution.py
+++ b/solution.py
@@ -46,7 +46,6 @@
 VMEM_BYTES = 16 << 20
 ANYWHERE = pl.BlockSpec(memory_space=pl.ANY)
 IN_VMEM = pl.BlockSpec(memory_space=pltpu.VMEM)
-IN_SMEM = pl.BlockSpec(memory_space=pltpu.SMEM)
 PARAMS = pltpu.CompilerParams(vmem_limit_bytes=VMEM_BYTES)
 
 
@@ -54,86 +53,139 @@
     return pltpu.with_memory_space_constraint(value, pltpu.VMEM)
 
 
-def product_kernel(
-    direction, sibling, experts, route, counts, inputs, hidden, *refs
-):
-    out, wide, columns, rows, column_sems, row_sem = refs[-6:]
-    chips, _, share = columns.shape
+def routed_copies(route, counts, route_now, counts_now, sems):
+    return [
+        pltpu.make_async_copy(route, route_now, sems.at[0]),
+        pltpu.make_async_copy(counts, counts_now, sems.at[1]),
+    ]
+
+
+def column_copies(inputs, direction, sibling, target, share, sem):
     me = lax.axis_index("dp")
     chip, core = me // 2, me % 2
     if sibling:
         core = 1 - core
-    row_copy = pltpu.make_async_copy(hidden.at[direction], rows, row_sem)
-    row_copy.start()
     copies = []
-    for k in range(chips):
+    for k in range(target.shape[1] // share):
         begin = pl.multiple_of((lax.bitwise_xor(chip, k) * 2 + core) * share, share)
-        copy = pltpu.make_async_copy(
-            inputs.at[direction, :, pl.ds(begin, share)], columns.at[k], column_sems.at[k]
+        copies.append(
+            pltpu.make_async_copy(
+                inputs.at[direction, :, pl.ds(begin, share)],
+                target.at[:, pl.ds(k * share, share)],
+                sem.at[k],
+            )
         )
+    return copies
+
+
+def contracted(columns, wide):
+    return lax.dot_general(
+        columns, wide, (((0,), (0,)), ((), ())), preferred_element_type=jnp.float32
+    )
+
+
+def product_kernel(sibling, experts, count, route, counts, inputs, hidden, *refs):
+    out, wide, columns, rows, route_now, counts_now, column_sems, sems = refs[-8:]
+    share = out.shape[1]
+    copies = routed_copies(route, counts, route_now, counts_now, sems)
+    copies.append(pltpu.make_async_copy(hidden.at[1], rows.at[0], sems.at[2]))
+    first = column_copies(inputs, 1, sibling, columns, share, column_sems.at[0])
+    later = []
+    if not sibling:
+        ahead, mine, ahead_wide = refs[count : count + 3]
+        later = column_copies(inputs, 0, True, ahead, share, column_sems.at[1])
+        later += column_copies(inputs, 0, False, mine, share, column_sems.at[2])
+        later.append(pltpu.make_async_copy(hidden.at[0], rows.at[1], sems.at[3]))
+    for copy in copies + first + later:
         copy.start()
-        copies.append(copy)
-    row_copy.wait()
-    expand_hidden(route, counts, direction, rows, wide, route.shape[1], experts)
-    for k in range(chips):
-        copies[k].wait()
-        product = lax.dot_general(
-            columns[k], wide[...], (((0,), (0,)), ((), ())), preferred_element_type=jnp.float32
-        )
-        out[k] = product.astype(out.dtype)
-
-
-def products(direction, sibling, after, route, counts, inputs, hidden, share, chips, experts, dtype):
+    for copy in copies:
+        copy.wait()
+    blocks = route.shape[1]
+    expand_hidden(route_now, counts_now, 1, rows.at[0], wide, blocks, experts)
+    for copy in first:
+        copy.wait()
+    out[...] = contracted(columns[...], wide[...]).astype(out.dtype).reshape(out.shape)
+    for copy in later:
+        copy.wait()
+    if not sibling:
+        expand_hidden(route_now, counts_now, 0, rows.at[1], ahead_wide, blocks, experts)
+
+
+def products(sibling, after, route, counts, inputs, hidden, share, chips, experts):
     _, rows, _ = inputs.shape
     width = hidden.shape[2]
-    columns = experts * width
+    wide = pltpu.VMEM((rows, experts * width), jnp.bfloat16)
+    columns = pltpu.VMEM((rows, chips * share), jnp.bfloat16)
+    extra = [] if sibling else [columns, columns, wide]
+    outs = extra + [pltpu.VMEM((chips, share, experts * width), jnp.bfloat16)]
     return pl.pallas_call(
-        functools.partial(product_kernel, direction, sibling, experts),
-        in_specs=[IN_SMEM, IN_SMEM, ANYWHERE, ANYWHERE] + [ANYWHERE] * len(after),
-        out_specs=IN_VMEM,
-        out_shape=pltpu.VMEM((chips, share, columns), dtype),
+        functools.partial(product_kernel, sibling, experts, len(after)),
+        in_specs=[ANYWHERE] * (4 + len(after)),
+        out_specs=[IN_VMEM] * len(outs),
+        out_shape=outs,
         scratch_shapes=[
-            pltpu.VMEM((rows, columns), jnp.bfloat16),
-            pltpu.VMEM((chips, rows, share), jnp.bfloat16),
-            pltpu.VMEM((rows, width), jnp.bfloat16),
-            pltpu.SemaphoreType.DMA((chips,)),
-            pltpu.SemaphoreType.DMA,
+            wide,
+            columns,
+            pltpu.VMEM((2, rows, width), jnp.bfloat16),
+            pltpu.SMEM(route.shape, jnp.int32),
+            pltpu.SMEM(counts.shape, jnp.int32),
+            pltpu.SemaphoreType.DMA((3, chips)),
+            pltpu.SemaphoreType.DMA((4,)),
         ],
         compiler_params=PARAMS,
-        cost_estimate=pl.CostEstimate(
-            flops=2 * rows * chips * share * columns,
-            bytes_accessed=2 * rows * (chips * share + width),
-            transcendentals=0,
-        ),
+        cost_estimate=pl.CostEstimate(flops=1, bytes_accessed=1, transcendentals=0),
     )(
-        route,
-        counts,
-        pltpu.with_memory_space_constraint(inputs, pltpu.HBM),
-        pltpu.with_memory_space_constraint(hidden, pltpu.HBM),
+        *(pltpu.with_memory_space_constraint(x, pltpu.HBM) for x in (route, counts, inputs, hidden)),
         *after,
     )
 
 
-def join_kernel(own, received, kept, *sent):
-    kept[...] = own[0].astype(jnp.float32) + received[0].astype(jnp.float32)
+def join_kernel(parts, own, received, *outs):
+    chips, share, _ = own.shape
+    rows = share // parts
+    for i in range(parts):
+        some = slice(i * rows, (i + 1) * rows)
+        for k in range(chips):
+            out = outs[i * chips + k]
+            total = own[k, some].astype(jnp.float32) + received[k, some].astype(jnp.float32)
+            out[...] = total.astype(out.dtype)
+
+
+def joined(own, received, parts):
+    chips, share, columns = own.shape
+    shape = (share // parts, columns)
+    outs = [pltpu.VMEM(shape, jnp.float32)] + [pltpu.VMEM(shape, jnp.bfloat16)] * (chips - 1)
+    flat = pl.pallas_call(
+        functools.partial(join_kernel, parts),
+        in_specs=[IN_VMEM, IN_VMEM],
+        out_specs=[IN_VMEM] * (chips * parts),
+        out_shape=outs * parts,
+        compiler_params=PARAMS,
+        cost_estimate=pl.CostEstimate(flops=1, bytes_accessed=1, transcendentals=0),
+    )(held(own), held(received))
+    return [flat[i * chips : (i + 1) * chips] for i in range(parts)]
+
+
+def pair_kernel(mine, wide, other, other_wide, kept, *sent):
+    total = contracted(mine[...], wide[...]) + contracted(other[...], other_wide[...])
+    total = total.reshape(1 + len(sent), *kept.shape)
+    kept[...] = total[0]
     for k, out in enumerate(sent):
-        total = own[k + 1].astype(jnp.float32) + received[k + 1].astype(jnp.float32)
-        out[...] = total.astype(out.dtype)
-
-
-def joined(own, received):
-    chips, share, columns = own.shape
+        out[...] = total[k + 1].astype(out.dtype)
+
+
+def paired(mine, wide, other, other_wide, share):
+    chips, columns = mine.shape[1] // share, wide.shape[1]
+    shape = (share, columns)
     return pl.pallas_call(
-        join_kernel,
-        in_specs=[IN_VMEM, IN_VMEM],
+        pair_kernel,
+        in_specs=[IN_VMEM] * 4,
         out_specs=[IN_VMEM] * chips,
-        out_shape=[pltpu.VMEM((share, columns), jnp.float32)]
-        + [pltpu.VMEM((share, columns), jnp.bfloat16)] * (chips - 1),
-        compiler_params=PARAMS,
-        cost_estimate=pl.CostEstimate(
-            flops=own.size, bytes_accessed=own.nbytes, transcendentals=0
-        ),
-    )(held(own), held(received))
+        out_shape=[pltpu.VMEM(shape, jnp.float32)]
+        + [pltpu.VMEM(shape, jnp.bfloat16)] * (chips - 1),
+        compiler_params=PARAMS,
+        cost_estimate=pl.CostEstimate(flops=1, bytes_accessed=1, transcendentals=0),
+    )(held(mine), held(wide), held(other), held(other_wide))
 
 
 def total_kernel(count, kept, *refs):
@@ -153,17 +205,16 @@
         out_shape=pltpu.VMEM(kept.shape, dtype),
         compiler_params=PARAMS,
         cost_estimate=pl.CostEstimate(
-            flops=kept.size * count, bytes_accessed=kept.nbytes, transcendentals=0
+            flops=1, bytes_accessed=1, transcendentals=0
         ),
     )(held(kept), *map(held, received), *after)
 
 
-def update_kernel(experts, count, steps, *refs):
-    kept = refs[0]
-    received = refs[1 : 1 + count]
-    first, second = refs[1 + count : 3 + count]
-    outs = refs[3 + count : 7 + count]
-    grad_out, first_out, second_out, step_out, sems = refs[7 + count :]
+def update_kernel(experts, count, steps, kept, *refs):
+    received, partners = refs[:count], refs[count : count + steps]
+    first, second = refs[count + steps : count + steps + 2]
+    outs = refs[count + steps + 2 : count + steps + 6]
+    grad_out, first_out, second_out, step_out, sems = refs[count + steps + 6 :]
     share, _, width = first.shape
     rows = share // steps
     copies = []
@@ -174,6 +225,7 @@
             grad = kept[some, columns]
             for part in received:
                 grad = grad + part[some, columns].astype(jnp.float32)
+            grad = grad + partners[i][:, columns].astype(jnp.float32)
             new_first = beta_one * first[some, e, :] + (1.0 - beta_one) * grad
             new_second = beta_two * second[some, e, :] + (1.0 - beta_two) * grad * grad
             grad_out[some, e, :] = grad
@@ -194,23 +246,22 @@
         copy.wait()
 
 
-def updated(kept, received, first, second):
+def updated(kept, received, partners, first, second):
     _, experts, _ = first.shape
-    count, steps = len(received), 4
+    count, steps = len(received), len(partners)
     return pl.pallas_call(
         functools.partial(update_kernel, experts, count, steps),
-        in_specs=[IN_VMEM] * (3 + count),
+        in_specs=[IN_VMEM] * (3 + count + steps),
         out_specs=[ANYWHERE] * 4,
         out_shape=[jax.ShapeDtypeStruct(first.shape, jnp.float32)] * 4,
         scratch_shapes=[pltpu.VMEM(first.shape, jnp.float32)] * 4
         + [pltpu.SemaphoreType.DMA((steps, 4))],
         compiler_params=PARAMS,
-        cost_estimate=pl.CostEstimate(
-            flops=20 * first.size,
-            bytes_accessed=4 * first.nbytes,
-            transcendentals=2 * first.size,
-        ),
-    )(held(kept), *map(held, received), held(first), held(second))
+        cost_estimate=pl.CostEstimate(flops=1, bytes_accessed=1, transcendentals=0),
+    )(*map(held, (kept, *received, *partners, first, second)))
+
+
+PARTS = 1
 
 
 def fast_device(saved_inputs, hidden_grads, block_expert, live_counts, first_moment, second_moment):
@@ -227,16 +278,21 @@
         experts=experts,
     )
 
-    def direction_part(direction, after, dtype):
-        sibling = product(direction, True, after, dtype=dtype)
-        other = exchanged(sibling, "dp", 1)
-        kept, *sent = joined(product(direction, False, [sibling], dtype=dtype), other)
-        return kept, [exchanged(part, "dp", 2 * (k + 1)) for k, part in enumerate(sent)]
-
-    kept_one, received_one = direction_part(1, [], jnp.bfloat16)
-    kept_zero, received_zero = direction_part(0, [kept_one], jnp.float32)
-    partner = mirrored(totalled(kept_one, received_one, [kept_zero], jnp.bfloat16))
-    outs = updated(kept_zero, received_zero + [partner], first_moment[0], second_moment[0])
+    def to_owners(pieces):
+        return [exchanged(piece, "dp", 2 * (k + 1)) for k, piece in enumerate(pieces)]
+
+    (sibling,) = product(True, [])
+    other = exchanged(sibling, "dp", 1)
+    ahead, mine, wide, own = product(False, [sibling])
+    parts = [(kept, to_owners(sent)) for kept, *sent in joined(own, other, PARTS)]
+    kept_zero, *sent_zero = paired(
+        mine, wide, exchanged(ahead, "dp", 1), exchanged(wide, "dp", 1), share
+    )
+    received_zero = to_owners(sent_zero)
+    partners = [
+        mirrored(totalled(kept, received, [kept_zero], jnp.bfloat16)) for kept, received in parts
+    ]
+    outs = updated(kept_zero, received_zero, partners, first_moment[0], second_moment[0])
     return tuple(out[None] for out in outs)
 
 

time: 47.3 us -> 40.4 us (0.85)
  Pallas kernels: 14.5 us -> 8.87 us
  starting transfers between devices: 11.2 us -> 14.4 us
  waiting for transfers between devices: 19.2 us -> 16.3 us
  local copies, waits for them, and re-layouts: 1.36 us -> 0.01 us
    pallas_call x6 -> x4, Pallas kernels: 12.1 us -> 6.39 us  [the longest x2 4.88 us: products(): pl.pallas_call(functools.partial(product_kernel, sibling, experts, len(af...]
    ppermute x1, waiting for transfers between devices: 7.67 us -> 3.12 us  [mirrored(): return lax.ppermute(value, 'section', pairs)]
    ppermute x8 -> x9, starting transfers between devices: 8.59 us -> 11.7 us  [exchanged(): lax.ppermute(value, axis, [(source, source ^ mask) for source in range(co...]
    ppermute x8 -> x9, waiting for transfers between devices: 11.5 us -> 13.2 us  [exchanged(): lax.ppermute(value, axis, [(source, source ^ mask) for source in range(co...]
    unnamed x8 -> x4, local copies, waits for them, and re-layouts: 1.36 us -> 0.01 us
  transfers between devices with their start and end apart: 9 -> 10, of which waited for: 4 -> 5; matrix products, arithmetic and copies ran while one was open for 0% -> 0% of each run, Pallas kernels for 13% -> 11%
where the time goes in v3:
time: 40.4 us; the launch traced here: 40.2 us
  waiting for transfers between devices  16.3 us (40%)
  starting transfers between devices  14.4 us (36%)
  Pallas kernels  8.87 us (22%)
  between operations  0.67 us (2%)
    ppermute x9, waiting for transfers between devices, exchanged(): lax.ppermute(value, axis, [(source, source ^ mask) for source in range(co...  13.2 us
    ppermute x9, starting transfers between devices, exchanged(): lax.ppermute(value, axis, [(source, source ^ mask) for source in range(co...  11.7 us
    pallas_call x2, Pallas kernels, products(): pl.pallas_call(functools.partial(product_kernel, sibling, experts, len(af...  4.88 us
    ppermute x1, waiting for transfers between devices, mirrored(): return lax.ppermute(value, 'section', pairs)  3.12 us
    ppermute x1, starting transfers between devices, mirrored(): return lax.ppermute(value, 'section', pairs)  2.67 us
    pallas_call x1, Pallas kernels, updated(): pl.pallas_call(functools.partial(update_kernel, experts, count, steps), i...  2.37 us
    pallas_call x1, Pallas kernels, paired(): pl.pallas_call(pair_kernel, in_specs=[IN_VMEM] * 4, out_specs=[IN_VMEM] *...  1.28 us
  transfers between devices with their start and end apart: 10, of which 5 were waited for; matrix products, arithmetic and copies ran while one was open for 0% of the time, Pallas kernels for 11%

profile of v3, /device:TPU:0, one launch (start us, length us, event | category | flops | bytes accessed | tf_op | source)
XLA Modules:
  0.0 40.2 jit_solution(7165455251218506658)
XLA Ops:
  0.6 2.2 %shard_map.93.refs_0_ = bf16[4,256,512]{2,1,0:T(8,128)(2,1)S(1)} custom-call(s32[2,3]{1,0:T(2,128)} %bitcast.16, s32[2,2]{1,0:T(2,128)} %bitcast.18, bf16[2,384,2048]{2,1,0:T(8,128)(2,1)} %bitcast.12, bf16[2,384,256]{2,1,0:T(8,128)(2,1)} %bitcast.14), custom_call_target="tpu_custom_call" | custom-call | flops 1 | bytes 1 | tf_op jit(solution)/shard_map/pallas_call | solution.py:121
  2.8 0.5 %collective-permute-start.5 = (bf16[4,256,512]{2,1,0:T(8,128)(2,1)S(1)}, bf16[4,256,512]{2,1,0:T(8,128)(2,1)S(1)}, u32[]{:S(2)}, u32[]{:S(2)}) collective-permute-start(bf16[4,256,512]{2,1,0:T(8,128)(2,1)S(1)} %shard_map.93.refs_0_), channel_id=1, source_target_pairs={{0,4},{4,0},{8,12},{12,8},{16,20},{20,16},{24,28},{28,24},{1,5},{5... | collective-permute-start | bytes 3145736 | tf_op jit(solution)/shard_map/ppermute | solution.py:21
  3.4 2.7 %shard_map.94 = (bf16[384,1024]{1,0:T(8,128)(2,1)S(1)}, bf16[384,1024]{1,0:T(8,128)(2,1)S(1)}, bf16[384,512]{1,0:T(8,128)(2,1)S(1)}, bf16[4,256,512]{2,1,0:T(8,128)(2,1)S(1)}) custom-call(s32[2,3]{1,0:T(2,128)} %bitcast.17, s32[2,2]{1,0:T(2,128)} %bitcast.19, bf16[2,384,2048]{2,1,0:T(8,128)(2,1)} %bitcast.13, bf16[2,384,256]{2,1,0:T(8,128)(2,1)} %bitcast.15, ...), custom_call_target="tpu_custom_call" | custom-call | flops 1 | bytes 1 | tf_op jit(solution)/shard_map/pallas_call | solution.py:121
  6.0 0.1 collective-permute-start
  6.2 0.5 %collective-permute-start.1 = (bf16[384,512]{1,0:T(8,128)(2,1)S(1)}, bf16[384,512]{1,0:T(8,128)(2,1)S(1)}, u32[]{:S(2)}, u32[]{:S(2)}) collective-permute-start(bf16[384,512]{1,0:T(8,128)(2,1)S(1)} %get-tuple-element.21.wide), channel_id=1, source_target_pairs={{0,4},{4,0},{8,12},{12,8},{16,20},{20,16},{24,28},{28,24},{1,5},{5... | collective-permute-start | bytes 1179656 | tf_op jit(solution)/shard_map/ppermute | solution.py:21
  6.6 0.0 collective-permute-done.5.received
  6.6 0.0 copy-start
  6.6 0.0 copy-start.1
  6.6 0.2 shard_map.96
  6.9 2.6 %collective-permute-start.6 = (bf16[256,512]{1,0:T(8,128)(2,1)S(1)}, bf16[256,512]{1,0:T(8,128)(2,1)S(1)}, u32[]{:S(2)}, u32[]{:S(2)}) collective-permute-start(bf16[256,512]{1,0:T(8,128)(2,1)S(1)} %get-tuple-element.29), channel_id=1, source_target_pairs={{0,8},{4,12},{8,0},{12,4},{16,24},{20,28},{24,16},{28,20},{1,9},{5... | collective-permute-start | bytes 786440 | tf_op jit(solution)/shard_map/ppermute | solution.py:21
  9.5 1.5 %collective-permute-start.7 = (bf16[256,512]{1,0:T(8,128)(2,1)S(1)}, bf16[256,512]{1,0:T(8,128)(2,1)S(1)}, u32[]{:S(2)}, u32[]{:S(2)}) collective-permute-start(bf16[256,512]{1,0:T(8,128)(2,1)S(1)} %get-tuple-element.30), channel_id=1, source_target_pairs={{0,16},{4,20},{8,24},{12,28},{16,0},{20,4},{24,8},{28,12},{1,17},{... | collective-permute-start | bytes 786440 | tf_op jit(solution)/shard_map/ppermute | solution.py:21
  11.0 0.0 collective-permute-start.8
  11.0 0.0 collective-permute-done.1.other_wide
  11.0 0.0 collective-permute-done.other
  11.0 1.3 %shard_map.95 = (f32[256,512]{1,0:T(8,128)S(1)}, bf16[256,512]{1,0:T(8,128)(2,1)S(1)}, bf16[256,512]{1,0:T(8,128)(2,1)S(1)}, bf16[256,512]{1,0:T(8,128)(2,1)S(1)}) custom-call(bf16[384,1024]{1,0:T(8,128)(2,1)S(1)} %get-tuple-element.20.mine, bf16[384,512]{1,0:T(8,128)(2,1)S(1)} %get-tuple-element.21.wide, bf16[384,1024]{1,0:T(8,128)(2,1)S(1)} %collective-permute-done.other, ...), custom_call_target="tpu_custom_call" | custom-call | flops 1 | bytes 1 | tf_op jit(solution)/shard_map/pallas_call | solution.py:180
  12.3 2.0 %collective-permute-start.2 = (bf16[256,512]{1,0:T(8,128)(2,1)S(1)}, bf16[256,512]{1,0:T(8,128)(2,1)S(1)}, u32[]{:S(2)}, u32[]{:S(2)}) collective-permute-start(bf16[256,512]{1,0:T(8,128)(2,1)S(1)} %get-tuple-element.24), channel_id=1, source_target_pairs={{0,8},{4,12},{8,0},{12,4},{16,24},{20,28},{24,16},{28,20},{1,9},{5... | collective-permute-start | bytes 786440 | tf_op jit(solution)/shard_map/ppermute | solution.py:21
  14.3 1.5 %collective-permute-start.3 = (bf16[256,512]{1,0:T(8,128)(2,1)S(1)}, bf16[256,512]{1,0:T(8,128)(2,1)S(1)}, u32[]{:S(2)}, u32[]{:S(2)}) collective-permute-start(bf16[256,512]{1,0:T(8,128)(2,1)S(1)} %get-tuple-element.25), channel_id=1, source_target_pairs={{0,16},{4,20},{8,24},{12,28},{16,0},{20,4},{24,8},{28,12},{1,17},{... | collective-permute-start | bytes 786440 | tf_op jit(solution)/shard_map/ppermute | solution.py:21
  15.9 0.8 %collective-permute-done.6.refs_0_ = bf16[256,512]{1,0:T(8,128)(2,1)S(1)} collective-permute-done((bf16[256,512]{1,0:T(8,128)(2,1)S(1)}, bf16[256,512]{1,0:T(8,128)(2,1)S(1)}, u32[]{:S(2)}, u32[]{:S(2)}) %collective-permute-start.6) | collective-permute-done | bytes 262176 | tf_op jit(solution)/shard_map/ppermute | solution.py:21
  16.6 2.9 %collective-permute-start.4 = (bf16[256,512]{1,0:T(8,128)(2,1)S(1)}, bf16[256,512]{1,0:T(8,128)(2,1)S(1)}, u32[]{:S(2)}, u32[]{:S(2)}) collective-permute-start(bf16[256,512]{1,0:T(8,128)(2,1)S(1)} %get-tuple-element.26), channel_id=1, source_target_pairs={{0,24},{4,28},{8,16},{12,20},{16,8},{20,12},{24,0},{28,4},{1,25},{... | collective-permute-start | bytes 786440 | tf_op jit(solution)/shard_map/ppermute | solution.py:21
  19.6 4.7 %collective-permute-done.7.refs_1_ = bf16[256,512]{1,0:T(8,128)(2,1)S(1)} collective-permute-done((bf16[256,512]{1,0:T(8,128)(2,1)S(1)}, bf16[256,512]{1,0:T(8,128)(2,1)S(1)}, u32[]{:S(2)}, u32[]{:S(2)}) %collective-permute-start.7) | collective-permute-done | bytes 262176 | tf_op jit(solution)/shard_map/ppermute | solution.py:21
  24.3 0.0 collective-permute-done.8.refs_2_
  24.3 0.1 shard_map.97
  24.4 2.7 %collective-permute-start.9 = (bf16[256,512]{1,0:T(8,128)(2,1)S(1)}, bf16[256,512]{1,0:T(8,128)(2,1)S(1)}, u32[]{:S(2)}, u32[]{:S(2)}) collective-permute-start(bf16[256,512]{1,0:T(8,128)(2,1)S(1)} %shard_map.97), channel_id=1, source_target_pairs={{0,2},{1,3},{2,0},{3,1},{4,6},{5,7},{6,4},{7,5},{8,10},{9,11},{10,... | collective-permute-start | bytes 786440 | tf_op jit(solution)/shard_map/ppermute | solution.py:27
  27.0 0.9 %collective-permute-done.2.refs_0_ = bf16[256,512]{1,0:T(8,128)(2,1)S(1)} collective-permute-done((bf16[256,512]{1,0:T(8,128)(2,1)S(1)}, bf16[256,512]{1,0:T(8,128)(2,1)S(1)}, u32[]{:S(2)}, u32[]{:S(2)}) %collective-permute-start.2) | collective-permute-done | bytes 262176 | tf_op jit(solution)/shard_map/ppermute | solution.py:21
  27.9 6.8 %collective-permute-done.3.refs_1_ = bf16[256,512]{1,0:T(8,128)(2,1)S(1)} collective-permute-done((bf16[256,512]{1,0:T(8,128)(2,1)S(1)}, bf16[256,512]{1,0:T(8,128)(2,1)S(1)}, u32[]{:S(2)}, u32[]{:S(2)}) %collective-permute-start.3) | collective-permute-done | bytes 262176 | tf_op jit(solution)/shard_map/ppermute | solution.py:21
  34.7 0.0 collective-permute-done.4.refs_2_
  34.7 3.1 %collective-permute-done.9.refs_3_ = bf16[256,512]{1,0:T(8,128)(2,1)S(1)} collective-permute-done((bf16[256,512]{1,0:T(8,128)(2,1)S(1)}, bf16[256,512]{1,0:T(8,128)(2,1)S(1)}, u32[]{:S(2)}, u32[]{:S(2)}) %collective-permute-start.9) | collective-permute-done | bytes 262176 | tf_op jit(solution)/shard_map/ppermute | solution.py:27
  37.8 0.0 copy-done
  37.8 0.0 copy-done.1
  37.8 2.4 %shard_map.98 = (f32[256,2,256]{2,1,0:T(2,128)}, f32[256,2,256]{2,1,0:T(2,128)}, f32[256,2,256]{2,1,0:T(2,128)}, f32[256,2,256]{2,1,0:T(2,128)}) custom-call(f32[256,512]{1,0:T(8,128)S(1)} %get-tuple-element.23.refs_3_.kept, bf16[256,512]{1,0:T(8,128)(2,1)S(1)} %collective-permute-done.2.refs_0_, bf16[256,512]{1,0:T(8,128)(2,1)S(1)} %collective-permute-done.3.refs_1_, ...), custom_call_target="tpu_custom_call" | custom-call | flops 1 | bytes 1 | tf_op jit(solution)/shard_map/pallas_call | solution.py:252
Async XLA Ops:
  2.8 3.8 %collective-permute-start.5 = (bf16[4,256,512]{2,1,0:T(8,128)(2,1)S(1)}, bf16[4,256,512]{2,1,0:T(8,128)(2,1)S(1)}, u32[]{:S(2)}, u32[]{:S(2)}) collective-permute-start(bf16[4,256,512]{2,1,0:T(8,128)(2,1)S(1)} %shard_map.93.refs_0_), channel_id=1, source_target_pairs={{0,4},{4,0},{8,12},{12,8},{16,20},{20,16},{24,28},{28,24},{1,5},{5... | collective-permute-start | bytes 3145736 | tf_op jit(solution)/shard_map/ppermute | solution.py:21
  6.0 5.0 %collective-permute-start = (bf16[384,1024]{1,0:T(8,128)(2,1)S(1)}, bf16[384,1024]{1,0:T(8,128)(2,1)S(1)}, u32[]{:S(2)}, u32[]{:S(2)}) collective-permute-start(bf16[384,1024]{1,0:T(8,128)(2,1)S(1)} %get-tuple-element.22), channel_id=1, source_target_pairs={{0,4},{4,0},{8,12},{12,8},{16,20},{20,16},{24,28},{28,24},{1,5},{5... | collective-permute-start | bytes 2359304 | tf_op jit(solution)/shard_map/ppermute | solution.py:21
  6.2 4.9 %collective-permute-start.1 = (bf16[384,512]{1,0:T(8,128)(2,1)S(1)}, bf16[384,512]{1,0:T(8,128)(2,1)S(1)}, u32[]{:S(2)}, u32[]{:S(2)}) collective-permute-start(bf16[384,512]{1,0:T(8,128)(2,1)S(1)} %get-tuple-element.21.wide), channel_id=1, source_target_pairs={{0,4},{4,0},{8,12},{12,8},{16,20},{20,16},{24,28},{28,24},{1,5},{5... | collective-permute-start | bytes 1179656 | tf_op jit(solution)/shard_map/ppermute | solution.py:21
  6.6 31.2 %copy-start = (f32[1,256,2,256]{3,2,1,0:T(2,128)S(1)}, f32[1,256,2,256]{3,2,1,0:T(2,128)}, u32[]{:S(2)}) copy-start(f32[1,256,2,256]{3,2,1,0:T(2,128)} %param.10) | copy-start | bytes 1572868
  6.6 31.2 %copy-start.1 = (f32[1,256,2,256]{3,2,1,0:T(2,128)S(1)}, f32[1,256,2,256]{3,2,1,0:T(2,128)}, u32[]{:S(2)}) copy-start(f32[1,256,2,256]{3,2,1,0:T(2,128)} %param.11) | copy-start | bytes 1572868
  6.9 9.8 %collective-permute-start.6 = (bf16[256,512]{1,0:T(8,128)(2,1)S(1)}, bf16[256,512]{1,0:T(8,128)(2,1)S(1)}, u32[]{:S(2)}, u32[]{:S(2)}) collective-permute-start(bf16[256,512]{1,0:T(8,128)(2,1)S(1)} %get-tuple-element.29), channel_id=1, source_target_pairs={{0,8},{4,12},{8,0},{12,4},{16,24},{20,28},{24,16},{28,20},{1,9},{5... | collective-permute-start | bytes 786440 | tf_op jit(solution)/shard_map/ppermute | solution.py:21
  9.5 14.8 %collective-permute-start.7 = (bf16[256,512]{1,0:T(8,128)(2,1)S(1)}, bf16[256,512]{1,0:T(8,128)(2,1)S(1)}, u32[]{:S(2)}, u32[]{:S(2)}) collective-permute-start(bf16[256,512]{1,0:T(8,128)(2,1)S(1)} %get-tuple-element.30), channel_id=1, source_target_pairs={{0,16},{4,20},{8,24},{12,28},{16,0},{20,4},{24,8},{28,12},{1,17},{... | collective-permute-start | bytes 786440 | tf_op jit(solution)/shard_map/ppermute | solution.py:21
  11.0 13.2 %collective-permute-start.8 = (bf16[256,512]{1,0:T(8,128)(2,1)S(1)}, bf16[256,512]{1,0:T(8,128)(2,1)S(1)}, u32[]{:S(2)}, u32[]{:S(2)}) collective-permute-start(bf16[256,512]{1,0:T(8,128)(2,1)S(1)} %get-tuple-element.31), channel_id=1, source_target_pairs={{0,24},{4,28},{8,16},{12,20},{16,8},{20,12},{24,0},{28,4},{1,25},{... | collective-permute-start | bytes 786440 | tf_op jit(solution)/shard_map/ppermute | solution.py:21
  12.3 15.6 %collective-permute-start.2 = (bf16[256,512]{1,0:T(8,128)(2,1)S(1)}, bf16[256,512]{1,0:T(8,128)(2,1)S(1)}, u32[]{:S(2)}, u32[]{:S(2)}) collective-permute-start(bf16[256,512]{1,0:T(8,128)(2,1)S(1)} %get-tuple-element.24), channel_id=1, source_target_pairs={{0,8},{4,12},{8,0},{12,4},{16,24},{20,28},{24,16},{28,20},{1,9},{5... | collective-permute-start | bytes 786440 | tf_op jit(solution)/shard_map/ppermute | solution.py:21
  14.3 20.4 %collective-permute-start.3 = (bf16[256,512]{1,0:T(8,128)(2,1)S(1)}, bf16[256,512]{1,0:T(8,128)(2,1)S(1)}, u32[]{:S(2)}, u32[]{:S(2)}) collective-permute-start(bf16[256,512]{1,0:T(8,128)(2,1)S(1)} %get-tuple-element.25), channel_id=1, source_target_pairs={{0,16},{4,20},{8,24},{12,28},{16,0},{20,4},{24,8},{28,12},{1,17},{... | collective-permute-start | bytes 786440 | tf_op jit(solution)/shard_map/ppermute | solution.py:21
  16.6 18.1 %collective-permute-start.4 = (bf16[256,512]{1,0:T(8,128)(2,1)S(1)}, bf16[256,512]{1,0:T(8,128)(2,1)S(1)}, u32[]{:S(2)}, u32[]{:S(2)}) collective-permute-start(bf16[256,512]{1,0:T(8,128)(2,1)S(1)} %get-tuple-element.26), channel_id=1, source_target_pairs={{0,24},{4,28},{8,16},{12,20},{16,8},{20,12},{24,0},{28,4},{1,25},{... | collective-permute-start | bytes 786440 | tf_op jit(solution)/shard_map/ppermute | solution.py:21
  24.4 13.5 %collective-permute-start.9 = (bf16[256,512]{1,0:T(8,128)(2,1)S(1)}, bf16[256,512]{1,0:T(8,128)(2,1)S(1)}, u32[]{:S(2)}, u32[]{:S(2)}) collective-permute-start(bf16[256,512]{1,0:T(8,128)(2,1)S(1)} %shard_map.97), channel_id=1, source_target_pairs={{0,2},{1,3},{2,0},{3,1},{4,6},{5,7},{6,4},{7,5},{8,10},{9,11},{10,... | collective-permute-start | bytes 786440 | tf_op jit(solution)/shard_map/ppermute | solution.py:27

commit v4 on v3

--- a/solution.py
+++ b/solution.py
@@ -16,15 +16,17 @@
 LANES = 128
 
 
-def exchanged(value, axis, mask):
+def exchanged(value, axis, mask, name):
     count = lax.axis_size(axis)
-    return lax.ppermute(value, axis, [(source, source ^ mask) for source in range(count)])
-
-
-def mirrored(value):
+    with jax.named_scope(name):
+        return lax.ppermute(value, axis, [(source, source ^ mask) for source in range(count)])
+
+
+def mirrored(value, name="mirror"):
     count = lax.axis_size("section")
     pairs = [(source, (source + count // 2) % count) for source in range(count)]
-    return lax.ppermute(value, "section", pairs)
+    with jax.named_scope(name):
+        return lax.ppermute(value, "section", pairs)
 
 
 def expand_hidden(route, counts, direction, hidden, wide, blocks, experts):
@@ -47,6 +49,7 @@
 ANYWHERE = pl.BlockSpec(memory_space=pl.ANY)
 IN_VMEM = pl.BlockSpec(memory_space=pltpu.VMEM)
 PARAMS = pltpu.CompilerParams(vmem_limit_bytes=VMEM_BYTES)
+SMALL = pl.CostEstimate(flops=1, bytes_accessed=1, transcendentals=0)
 
 
 def held(value):
@@ -92,23 +95,25 @@
     first = column_copies(inputs, 1, sibling, columns, share, column_sems.at[0])
     later = []
     if not sibling:
-        ahead, mine, ahead_wide = refs[count : count + 3]
-        later = column_copies(inputs, 0, True, ahead, share, column_sems.at[1])
+        ahead, mine = refs[count : count + 2]
+        ahead_wide = ahead.at[:, columns.shape[1] :]
+        copies.append(pltpu.make_async_copy(hidden.at[0], rows.at[1], sems.at[3]))
+        span = columns.shape[1]
+        later = column_copies(inputs, 0, True, ahead.at[:, :span], share, column_sems.at[1])
         later += column_copies(inputs, 0, False, mine, share, column_sems.at[2])
-        later.append(pltpu.make_async_copy(hidden.at[0], rows.at[1], sems.at[3]))
     for copy in copies + first + later:
         copy.start()
     for copy in copies:
         copy.wait()
     blocks = route.shape[1]
     expand_hidden(route_now, counts_now, 1, rows.at[0], wide, blocks, experts)
+    if not sibling:
+        expand_hidden(route_now, counts_now, 0, rows.at[1], ahead_wide, blocks, experts)
     for copy in first:
         copy.wait()
     out[...] = contracted(columns[...], wide[...]).astype(out.dtype).reshape(out.shape)
     for copy in later:
         copy.wait()
-    if not sibling:
-        expand_hidden(route_now, counts_now, 0, rows.at[1], ahead_wide, blocks, experts)
 
 
 def products(sibling, after, route, counts, inputs, hidden, share, chips, experts):
@@ -116,7 +121,8 @@
     width = hidden.shape[2]
     wide = pltpu.VMEM((rows, experts * width), jnp.bfloat16)
     columns = pltpu.VMEM((rows, chips * share), jnp.bfloat16)
-    extra = [] if sibling else [columns, columns, wide]
+    both = pltpu.VMEM((rows, chips * share + experts * width), jnp.bfloat16)
+    extra = [] if sibling else [both, columns]
     outs = extra + [pltpu.VMEM((chips, share, experts * width), jnp.bfloat16)]
     return pl.pallas_call(
         functools.partial(product_kernel, sibling, experts, len(after)),
@@ -133,7 +139,7 @@
             pltpu.SemaphoreType.DMA((4,)),
         ],
         compiler_params=PARAMS,
-        cost_estimate=pl.CostEstimate(flops=1, bytes_accessed=1, transcendentals=0),
+        cost_estimate=SMALL,
     )(
         *(pltpu.with_memory_space_constraint(x, pltpu.HBM) for x in (route, counts, inputs, hidden)),
         *after,
@@ -161,31 +167,34 @@
         out_specs=[IN_VMEM] * (chips * parts),
         out_shape=outs * parts,
         compiler_params=PARAMS,
-        cost_estimate=pl.CostEstimate(flops=1, bytes_accessed=1, transcendentals=0),
+        cost_estimate=SMALL,
     )(held(own), held(received))
     return [flat[i * chips : (i + 1) * chips] for i in range(parts)]
 
 
-def pair_kernel(mine, wide, other, other_wide, kept, *sent):
-    total = contracted(mine[...], wide[...]) + contracted(other[...], other_wide[...])
+def pair_kernel(count, mine, ahead, other, *refs):
+    kept, *sent = refs[count:]
+    span = mine.shape[1]
+    total = contracted(mine[...], ahead[:, span:]) + contracted(other[:, :span], other[:, span:])
     total = total.reshape(1 + len(sent), *kept.shape)
     kept[...] = total[0]
     for k, out in enumerate(sent):
         out[...] = total[k + 1].astype(out.dtype)
 
 
-def paired(mine, wide, other, other_wide, share):
-    chips, columns = mine.shape[1] // share, wide.shape[1]
+def paired(mine, ahead, other, after, share):
+    span = mine.shape[1]
+    chips, columns = span // share, ahead.shape[1] - span
     shape = (share, columns)
     return pl.pallas_call(
-        pair_kernel,
-        in_specs=[IN_VMEM] * 4,
+        functools.partial(pair_kernel, len(after)),
+        in_specs=[IN_VMEM] * 3 + [ANYWHERE] * len(after),
         out_specs=[IN_VMEM] * chips,
         out_shape=[pltpu.VMEM(shape, jnp.float32)]
         + [pltpu.VMEM(shape, jnp.bfloat16)] * (chips - 1),
         compiler_params=PARAMS,
-        cost_estimate=pl.CostEstimate(flops=1, bytes_accessed=1, transcendentals=0),
-    )(held(mine), held(wide), held(other), held(other_wide))
+        cost_estimate=SMALL,
+    )(held(mine), held(ahead), held(other), *after)
 
 
 def total_kernel(count, kept, *refs):
@@ -204,9 +213,7 @@
         out_specs=IN_VMEM,
         out_shape=pltpu.VMEM(kept.shape, dtype),
         compiler_params=PARAMS,
-        cost_estimate=pl.CostEstimate(
-            flops=1, bytes_accessed=1, transcendentals=0
-        ),
+        cost_estimate=SMALL,
     )(held(kept), *map(held, received), *after)
 
 
@@ -257,11 +264,11 @@
         scratch_shapes=[pltpu.VMEM(first.shape, jnp.float32)] * 4
         + [pltpu.SemaphoreType.DMA((steps, 4))],
         compiler_params=PARAMS,
-        cost_estimate=pl.CostEstimate(flops=1, bytes_accessed=1, transcendentals=0),
+        cost_estimate=SMALL,
     )(*map(held, (kept, *received, *partners, first, second)))
 
 
-PARTS = 1
+PARTS = 2
 
 
 def fast_device(saved_inputs, hidden_grads, block_expert, live_counts, first_moment, second_moment):
@@ -278,21 +285,33 @@
         experts=experts,
     )
 
-    def to_owners(pieces):
-        return [exchanged(piece, "dp", 2 * (k + 1)) for k, piece in enumerate(pieces)]
-
-    (sibling,) = product(True, [])
-    other = exchanged(sibling, "dp", 1)
-    ahead, mine, wide, own = product(False, [sibling])
-    parts = [(kept, to_owners(sent)) for kept, *sent in joined(own, other, PARTS)]
-    kept_zero, *sent_zero = paired(
-        mine, wide, exchanged(ahead, "dp", 1), exchanged(wide, "dp", 1), share
-    )
-    received_zero = to_owners(sent_zero)
-    partners = [
-        mirrored(totalled(kept, received, [kept_zero], jnp.bfloat16)) for kept, received in parts
-    ]
-    outs = updated(kept_zero, received_zero, partners, first_moment[0], second_moment[0])
+    def to_owners(pieces, name):
+        return [
+            exchanged(piece, "dp", 2 * (k + 1), f"{name}_to_chip_{k + 1}")
+            for k, piece in enumerate(pieces)
+        ]
+
+    with jax.named_scope("sibling_products"):
+        (sibling,) = product(True, [])
+    other = exchanged(sibling, "dp", 1, "sibling_exchange")
+    with jax.named_scope("own_products"):
+        ahead, mine, own = product(False, [sibling])
+    other_ahead = exchanged(ahead, "dp", 1, "operand_exchange")
+    with jax.named_scope("join"):
+        pieces = joined(own, other, PARTS)
+    parts = [(kept, to_owners(sent, f"one_part_{i}")) for i, (kept, *sent) in enumerate(pieces)]
+    with jax.named_scope("total_0"):
+        first_total = totalled(*parts[0], [], jnp.bfloat16)
+    with jax.named_scope("pair"):
+        kept_zero, *sent_zero = paired(mine, ahead, other_ahead, [parts[0][1][1]], share)
+    received_zero = to_owners(sent_zero, "zero")
+    partners = [mirrored(first_total, "mirror_0")]
+    for i, (kept, received) in enumerate(parts[1:]):
+        with jax.named_scope(f"total_{i + 1}"):
+            total = totalled(kept, received, [kept_zero], jnp.bfloat16)
+        partners.append(mirrored(total, f"mirror_{i + 1}"))
+    with jax.named_scope("update"):
+        outs = updated(kept_zero, received_zero, partners, first_moment[0], second_moment[0])
     return tuple(out[None] for out in outs)
 
 

time: 40.4 us -> 38 us (0.941)
  waiting for transfers between devices: 16.3 us -> 10.5 us
  starting transfers between devices: 14.4 us -> 17.6 us
    ppermute x9 -> x11, waiting for transfers between devices: 13.2 us -> 1.87 us  [exchanged(): lax.ppermute(value, axis, [(source, source ^ mask) for source in range(co...]
    ppermute x1 -> x2, waiting for transfers between devices: 3.12 us -> 8.66 us  [mirrored(): return lax.ppermute(value, 'section', pairs)]
    ppermute x9 -> x11, starting transfers between devices: 11.7 us -> 14 us  [exchanged(): lax.ppermute(value, axis, [(source, source ^ mask) for source in range(co...]
    ppermute x1 -> x2, starting transfers between devices: 2.67 us -> 3.66 us  [mirrored(): return lax.ppermute(value, 'section', pairs)]
  transfers between devices with their start and end apart: 10 -> 13, of which waited for: 5 -> 5; matrix products, arithmetic and copies ran while one was open for 0% -> 0% of each run, Pallas kernels for 11% -> 12%
where the time goes in v4:
time: 38 us; the launch traced here: 37.9 us
  starting transfers between devices  17.6 us (46%)
  waiting for transfers between devices  10.5 us (28%)
  Pallas kernels  8.97 us (24%)
  between operations  0.73 us (2%)
    ppermute x11, starting transfers between devices, exchanged(): lax.ppermute(value, axis, [(source, source ^ mask) for source in range(co...  14 us
    ppermute x2, waiting for transfers between devices, mirrored(): return lax.ppermute(value, 'section', pairs)  8.66 us
    pallas_call x2, Pallas kernels, products(): pl.pallas_call(functools.partial(product_kernel, sibling, experts, len(af...  5.01 us
    ppermute x2, starting transfers between devices, mirrored(): return lax.ppermute(value, 'section', pairs)  3.66 us
    pallas_call x1, Pallas kernels, updated(): pl.pallas_call(functools.partial(update_kernel, experts, count, steps), i...  2.33 us
    ppermute x11, waiting for transfers between devices, exchanged(): lax.ppermute(value, axis, [(source, source ^ mask) for source in range(co...  1.87 us
    pallas_call x1, Pallas kernels, paired(): pl.pallas_call(functools.partial(pair_kernel, len(after)), in_specs=[IN_V...  1.27 us
  transfers between devices with their start and end apart: 13, of which 5 were waited for; matrix products, arithmetic and copies ran while one was open for 0% of the time, Pallas kernels for 12%

profile of v4, /device:TPU:0, one launch (start us, length us, event | category | flops | bytes accessed | tf_op | source)
XLA Modules:
  0.0 37.9 jit_solution(3020864113370361080)
XLA Ops:
  0.6 2.2 %sibling_products.1.refs_0_ = bf16[4,256,512]{2,1,0:T(8,128)(2,1)S(1)} custom-call(s32[2,3]{1,0:T(2,128)} %bitcast.16, s32[2,2]{1,0:T(2,128)} %bitcast.18, bf16[2,384,2048]{2,1,0:T(8,128)(2,1)} %bitcast.12, bf16[2,384,256]{2,1,0:T(8,128)(2,1)} %bitcast.14), custom_call_target="tpu_custom_call" | custom-call | flops 1 | bytes 1 | tf_op jit(solution)/shard_map/sibling_products/pallas_call | solution.py:127
  2.8 0.5 %collective-permute-start.1 = (bf16[4,256,512]{2,1,0:T(8,128)(2,1)S(1)}, bf16[4,256,512]{2,1,0:T(8,128)(2,1)S(1)}, u32[]{:S(2)}, u32[]{:S(2)}) collective-permute-start(bf16[4,256,512]{2,1,0:T(8,128)(2,1)S(1)} %sibling_products.1.refs_0_), channel_id=1, source_target_pairs={{0,4},{4,0},{8,12},{12,8},{16,20},{20,16},{24,28},{28,24},{1,5},{5... | collective-permute-start | bytes 3145736 | tf_op jit(solution)/shard_map/sibling_exchange/ppermute | solution.py:22
  3.4 2.8 %own_products.1 = (bf16[384,1536]{1,0:T(8,128)(2,1)S(1)}, bf16[384,1024]{1,0:T(8,128)(2,1)S(1)}, bf16[4,256,512]{2,1,0:T(8,128)(2,1)S(1)}) custom-call(s32[2,3]{1,0:T(2,128)} %bitcast.17, s32[2,2]{1,0:T(2,128)} %bitcast.19, bf16[2,384,2048]{2,1,0:T(8,128)(2,1)} %bitcast.13, bf16[2,384,256]{2,1,0:T(8,128)(2,1)} %bitcast.15, ...), custom_call_target="tpu_custom_call" | custom-call | flops 1 | bytes 1 | tf_op jit(solution)/shard_map/own_products/pallas_call | solution.py:127
  6.2 0.1 collective-permute-start
  6.3 0.0 collective-permute-done.1.received
  6.3 0.2 join.1
  6.5 3.0 %collective-permute-start.2 = (bf16[128,512]{1,0:T(8,128)(2,1)S(1)}, bf16[128,512]{1,0:T(8,128)(2,1)S(1)}, u32[]{:S(2)}, u32[]{:S(2)}) collective-permute-start(bf16[128,512]{1,0:T(8,128)(2,1)S(1)} %get-tuple-element.26), channel_id=1, source_target_pairs={{0,16},{4,20},{8,24},{12,28},{16,0},{20,4},{24,8},{28,12},{1,17},{... | collective-permute-start | bytes 393224 | tf_op jit(solution)/shard_map/one_part_0_to_chip_2/ppermute | solution.py:22
  9.6 1.5 %collective-permute-start.6 = (bf16[128,512]{1,0:T(8,128)(2,1)S(1)}, bf16[128,512]{1,0:T(8,128)(2,1)S(1)}, u32[]{:S(2)}, u32[]{:S(2)}) collective-permute-start(bf16[128,512]{1,0:T(8,128)(2,1)S(1)} %get-tuple-element.32), channel_id=1, source_target_pairs={{0,8},{4,12},{8,0},{12,4},{16,24},{20,28},{24,16},{28,20},{1,9},{5... | collective-permute-start | bytes 393224 | tf_op jit(solution)/shard_map/one_part_0_to_chip_1/ppermute | solution.py:22
  11.1 0.0 collective-permute-start.7
  11.1 1.9 %collective-permute-start.9 = (bf16[128,512]{1,0:T(8,128)(2,1)S(1)}, bf16[128,512]{1,0:T(8,128)(2,1)S(1)}, u32[]{:S(2)}, u32[]{:S(2)}) collective-permute-start(bf16[128,512]{1,0:T(8,128)(2,1)S(1)} %get-tuple-element.35), channel_id=1, source_target_pairs={{0,8},{4,12},{8,0},{12,4},{16,24},{20,28},{24,16},{28,20},{1,9},{5... | collective-permute-start | bytes 393224 | tf_op jit(solution)/shard_map/one_part_1_to_chip_1/ppermute | solution.py:22
  13.0 0.2 collective-permute-done.2.refs_0_.refs_1_
  13.3 1.8 %collective-permute-start.10 = (bf16[128,512]{1,0:T(8,128)(2,1)S(1)}, bf16[128,512]{1,0:T(8,128)(2,1)S(1)}, u32[]{:S(2)}, u32[]{:S(2)}) collective-permute-start(bf16[128,512]{1,0:T(8,128)(2,1)S(1)} %get-tuple-element.36), channel_id=1, source_target_pairs={{0,16},{4,20},{8,24},{12,28},{16,0},{20,4},{24,8},{28,12},{1,17},{... | collective-permute-start | bytes 393224 | tf_op jit(solution)/shard_map/one_part_1_to_chip_2/ppermute | solution.py:22
  15.1 0.0 collective-permute-done.other
  15.1 1.4 %collective-permute-start.11 = (bf16[128,512]{1,0:T(8,128)(2,1)S(1)}, bf16[128,512]{1,0:T(8,128)(2,1)S(1)}, u32[]{:S(2)}, u32[]{:S(2)}) collective-permute-start(bf16[128,512]{1,0:T(8,128)(2,1)S(1)} %get-tuple-element.37), channel_id=1, source_target_pairs={{0,24},{4,28},{8,16},{12,20},{16,8},{20,12},{24,0},{28,4},{1,25},{... | collective-permute-start | bytes 393224 | tf_op jit(solution)/shard_map/one_part_1_to_chip_3/ppermute | solution.py:22
  16.5 1.3 %pair.1 = (f32[256,512]{1,0:T(8,128)S(1)}, bf16[256,512]{1,0:T(8,128)(2,1)S(1)}, bf16[256,512]{1,0:T(8,128)(2,1)S(1)}, bf16[256,512]{1,0:T(8,128)(2,1)S(1)}) custom-call(bf16[384,1024]{1,0:T(8,128)(2,1)S(1)} %get-tuple-element.23.mine, bf16[384,1536]{1,0:T(8,128)(2,1)S(1)} %get-tuple-element.24.ahead, bf16[384,1536]{1,0:T(8,128)(2,1)S(1)} %collective-permute-done.other, ...), custom_call_target="tpu_custom_call" | custom-call | flops 1 | bytes 1 | tf_op jit(solution)/shard_map/pair/pallas_call | solution.py:189
  17.8 0.0 copy-start
  17.8 0.0 copy-start.1
  17.8 0.0 collective-permute-done.6.refs_0_
  17.8 0.3 collective-permute-start.3
  18.1 0.3 collective-permute-done.7.refs_2_
  18.4 1.8 %collective-permute-start.4 = (bf16[256,512]{1,0:T(8,128)(2,1)S(1)}, bf16[256,512]{1,0:T(8,128)(2,1)S(1)}, u32[]{:S(2)}, u32[]{:S(2)}) collective-permute-start(bf16[256,512]{1,0:T(8,128)(2,1)S(1)} %get-tuple-element.29), channel_id=1, source_target_pairs={{0,16},{4,20},{8,24},{12,28},{16,0},{20,4},{24,8},{28,12},{1,17},{... | collective-permute-start | bytes 786440 | tf_op jit(solution)/shard_map/zero_to_chip_2/ppermute | solution.py:22
  20.2 1.3 %collective-permute-done.9.refs_0_ = bf16[128,512]{1,0:T(8,128)(2,1)S(1)} collective-permute-done((bf16[128,512]{1,0:T(8,128)(2,1)S(1)}, bf16[128,512]{1,0:T(8,128)(2,1)S(1)}, u32[]{:S(2)}, u32[]{:S(2)}) %collective-permute-start.9) | collective-permute-done | bytes 131104 | tf_op jit(solution)/shard_map/one_part_1_to_chip_1/ppermute | solution.py:22
  21.6 1.4 %collective-permute-start.5 = (bf16[256,512]{1,0:T(8,128)(2,1)S(1)}, bf16[256,512]{1,0:T(8,128)(2,1)S(1)}, u32[]{:S(2)}, u32[]{:S(2)}) collective-permute-start(bf16[256,512]{1,0:T(8,128)(2,1)S(1)} %get-tuple-element.30), channel_id=1, source_target_pairs={{0,24},{4,28},{8,16},{12,20},{16,8},{20,12},{24,0},{28,4},{1,25},{... | collective-permute-start | bytes 786440 | tf_op jit(solution)/shard_map/zero_to_chip_3/ppermute | solution.py:22
  23.0 0.1 total_0.1
  23.1 0.0 collective-permute-done.10.refs_1_
  23.1 2.7 %collective-permute-start.8 = (bf16[128,512]{1,0:T(8,128)(2,1)S(1)}, bf16[128,512]{1,0:T(8,128)(2,1)S(1)}, u32[]{:S(2)}, u32[]{:S(2)}) collective-permute-start(bf16[128,512]{1,0:T(8,128)(2,1)S(1)} %total_0.1), channel_id=1, source_target_pairs={{0,2},{1,3},{2,0},{3,1},{4,6},{5,7},{6,4},{7,5},{8,10},{9,11},{10,... | collective-permute-start | bytes 393224 | tf_op jit(solution)/shard_map/mirror_0/ppermute | solution.py:29
  25.8 0.0 collective-permute-done.11.refs_2_
  25.8 0.1 total_1.1
  25.8 1.0 %collective-permute-start.12 = (bf16[128,512]{1,0:T(8,128)(2,1)S(1)}, bf16[128,512]{1,0:T(8,128)(2,1)S(1)}, u32[]{:S(2)}, u32[]{:S(2)}) collective-permute-start(bf16[128,512]{1,0:T(8,128)(2,1)S(1)} %total_1.1), channel_id=1, source_target_pairs={{0,2},{1,3},{2,0},{3,1},{4,6},{5,7},{6,4},{7,5},{8,10},{9,11},{10,... | collective-permute-start | bytes 393224 | tf_op jit(solution)/shard_map/mirror_1/ppermute | solution.py:29
  26.8 7.3 %collective-permute-done.8.refs_3_ = bf16[128,512]{1,0:T(8,128)(2,1)S(1)} collective-permute-done((bf16[128,512]{1,0:T(8,128)(2,1)S(1)}, bf16[128,512]{1,0:T(8,128)(2,1)S(1)}, u32[]{:S(2)}, u32[]{:S(2)}) %collective-permute-start.8) | collective-permute-done | bytes 131104 | tf_op jit(solution)/shard_map/mirror_0/ppermute | solution.py:29
  34.1 1.4 %collective-permute-done.12.refs_4_ = bf16[128,512]{1,0:T(8,128)(2,1)S(1)} collective-permute-done((bf16[128,512]{1,0:T(8,128)(2,1)S(1)}, bf16[128,512]{1,0:T(8,128)(2,1)S(1)}, u32[]{:S(2)}, u32[]{:S(2)}) %collective-permute-start.12) | collective-permute-done | bytes 131104 | tf_op jit(solution)/shard_map/mirror_1/ppermute | solution.py:29
  35.5 0.0 collective-permute-done.3.refs_0_
  35.5 0.0 collective-permute-done.4.refs_1_
  35.5 0.0 collective-permute-done.5.refs_2_
  35.5 0.0 copy-done
  35.5 0.0 copy-done.1
  35.5 2.3 %update.1 = (f32[256,2,256]{2,1,0:T(2,128)}, f32[256,2,256]{2,1,0:T(2,128)}, f32[256,2,256]{2,1,0:T(2,128)}, f32[256,2,256]{2,1,0:T(2,128)}) custom-call(f32[256,512]{1,0:T(8,128)S(1)} %get-tuple-element.27.refs_3_.kept, bf16[256,512]{1,0:T(8,128)(2,1)S(1)} %collective-permute-done.3.refs_0_, bf16[256,512]{1,0:T(8,128)(2,1)S(1)} %collective-permute-done.4.refs_1_, ...), custom_call_target="tpu_custom_call" | custom-call | flops 1 | bytes 1 | tf_op jit(solution)/shard_map/update/pallas_call | solution.py:259
Async XLA Ops:
  2.8 3.5 %collective-permute-start.1 = (bf16[4,256,512]{2,1,0:T(8,128)(2,1)S(1)}, bf16[4,256,512]{2,1,0:T(8,128)(2,1)S(1)}, u32[]{:S(2)}, u32[]{:S(2)}) collective-permute-start(bf16[4,256,512]{2,1,0:T(8,128)(2,1)S(1)} %sibling_products.1.refs_0_), channel_id=1, source_target_pairs={{0,4},{4,0},{8,12},{12,8},{16,20},{20,16},{24,28},{28,24},{1,5},{5... | collective-permute-start | bytes 3145736 | tf_op jit(solution)/shard_map/sibling_exchange/ppermute | solution.py:22
  6.2 8.9 %collective-permute-start = (bf16[384,1536]{1,0:T(8,128)(2,1)S(1)}, bf16[384,1536]{1,0:T(8,128)(2,1)S(1)}, u32[]{:S(2)}, u32[]{:S(2)}) collective-permute-start(bf16[384,1536]{1,0:T(8,128)(2,1)S(1)} %get-tuple-element.24.ahead), channel_id=1, source_target_pairs={{0,4},{4,0},{8,12},{12,8},{16,20},{20,16},{24,28},{28,24},{1,5},{5... | collective-permute-start | bytes 3538952 | tf_op jit(solution)/shard_map/operand_exchange/ppermute | solution.py:22
  6.5 6.7 %collective-permute-start.2 = (bf16[128,512]{1,0:T(8,128)(2,1)S(1)}, bf16[128,512]{1,0:T(8,128)(2,1)S(1)}, u32[]{:S(2)}, u32[]{:S(2)}) collective-permute-start(bf16[128,512]{1,0:T(8,128)(2,1)S(1)} %get-tuple-element.26), channel_id=1, source_target_pairs={{0,16},{4,20},{8,24},{12,28},{16,0},{20,4},{24,8},{28,12},{1,17},{... | collective-permute-start | bytes 393224 | tf_op jit(solution)/shard_map/one_part_0_to_chip_2/ppermute | solution.py:22
  9.6 8.2 %collective-permute-start.6 = (bf16[128,512]{1,0:T(8,128)(2,1)S(1)}, bf16[128,512]{1,0:T(8,128)(2,1)S(1)}, u32[]{:S(2)}, u32[]{:S(2)}) collective-permute-start(bf16[128,512]{1,0:T(8,128)(2,1)S(1)} %get-tuple-element.32), channel_id=1, source_target_pairs={{0,8},{4,12},{8,0},{12,4},{16,24},{20,28},{24,16},{28,20},{1,9},{5... | collective-permute-start | bytes 393224 | tf_op jit(solution)/shard_map/one_part_0_to_chip_1/ppermute | solution.py:22
  11.1 7.3 %collective-permute-start.7 = (bf16[128,512]{1,0:T(8,128)(2,1)S(1)}, bf16[128,512]{1,0:T(8,128)(2,1)S(1)}, u32[]{:S(2)}, u32[]{:S(2)}) collective-permute-start(bf16[128,512]{1,0:T(8,128)(2,1)S(1)} %get-tuple-element.33), channel_id=1, source_target_pairs={{0,24},{4,28},{8,16},{12,20},{16,8},{20,12},{24,0},{28,4},{1,25},{... | collective-permute-start | bytes 393224 | tf_op jit(solution)/shard_map/one_part_0_to_chip_3/ppermute | solution.py:22
  11.1 10.5 %collective-permute-start.9 = (bf16[128,512]{1,0:T(8,128)(2,1)S(1)}, bf16[128,512]{1,0:T(8,128)(2,1)S(1)}, u32[]{:S(2)}, u32[]{:S(2)}) collective-permute-start(bf16[128,512]{1,0:T(8,128)(2,1)S(1)} %get-tuple-element.35), channel_id=1, source_target_pairs={{0,8},{4,12},{8,0},{12,4},{16,24},{20,28},{24,16},{28,20},{1,9},{5... | collective-permute-start | bytes 393224 | tf_op jit(solution)/shard_map/one_part_1_to_chip_1/ppermute | solution.py:22
  13.3 9.8 %collective-permute-start.10 = (bf16[128,512]{1,0:T(8,128)(2,1)S(1)}, bf16[128,512]{1,0:T(8,128)(2,1)S(1)}, u32[]{:S(2)}, u32[]{:S(2)}) collective-permute-start(bf16[128,512]{1,0:T(8,128)(2,1)S(1)} %get-tuple-element.36), channel_id=1, source_target_pairs={{0,16},{4,20},{8,24},{12,28},{16,0},{20,4},{24,8},{28,12},{1,17},{... | collective-permute-start | bytes 393224 | tf_op jit(solution)/shard_map/one_part_1_to_chip_2/ppermute | solution.py:22
  15.1 10.7 %collective-permute-start.11 = (bf16[128,512]{1,0:T(8,128)(2,1)S(1)}, bf16[128,512]{1,0:T(8,128)(2,1)S(1)}, u32[]{:S(2)}, u32[]{:S(2)}) collective-permute-start(bf16[128,512]{1,0:T(8,128)(2,1)S(1)} %get-tuple-element.37), channel_id=1, source_target_pairs={{0,24},{4,28},{8,16},{12,20},{16,8},{20,12},{24,0},{28,4},{1,25},{... | collective-permute-start | bytes 393224 | tf_op jit(solution)/shard_map/one_part_1_to_chip_3/ppermute | solution.py:22
  17.8 17.7 %copy-start = (f32[1,256,2,256]{3,2,1,0:T(2,128)S(1)}, f32[1,256,2,256]{3,2,1,0:T(2,128)}, u32[]{:S(2)}) copy-start(f32[1,256,2,256]{3,2,1,0:T(2,128)} %param.10) | copy-start | bytes 1572868
  17.8 17.7 %copy-start.1 = (f32[1,256,2,256]{3,2,1,0:T(2,128)S(1)}, f32[1,256,2,256]{3,2,1,0:T(2,128)}, u32[]{:S(2)}) copy-start(f32[1,256,2,256]{3,2,1,0:T(2,128)} %param.11) | copy-start | bytes 1572868
  17.8 17.7 %collective-permute-start.3 = (bf16[256,512]{1,0:T(8,128)(2,1)S(1)}, bf16[256,512]{1,0:T(8,128)(2,1)S(1)}, u32[]{:S(2)}, u32[]{:S(2)}) collective-permute-start(bf16[256,512]{1,0:T(8,128)(2,1)S(1)} %get-tuple-element.28), channel_id=1, source_target_pairs={{0,8},{4,12},{8,0},{12,4},{16,24},{20,28},{24,16},{28,20},{1,9},{5... | collective-permute-start | bytes 786440 | tf_op jit(solution)/shard_map/zero_to_chip_1/ppermute | solution.py:22
  18.4 17.1 %collective-permute-start.4 = (bf16[256,512]{1,0:T(8,128)(2,1)S(1)}, bf16[256,512]{1,0:T(8,128)(2,1)S(1)}, u32[]{:S(2)}, u32[]{:S(2)}) collective-permute-start(bf16[256,512]{1,0:T(8,128)(2,1)S(1)} %get-tuple-element.29), channel_id=1, source_target_pairs={{0,16},{4,20},{8,24},{12,28},{16,0},{20,4},{24,8},{28,12},{1,17},{... | collective-permute-start | bytes 786440 | tf_op jit(solution)/shard_map/zero_to_chip_2/ppermute | solution.py:22
  21.6 13.9 %collective-permute-start.5 = (bf16[256,512]{1,0:T(8,128)(2,1)S(1)}, bf16[256,512]{1,0:T(8,128)(2,1)S(1)}, u32[]{:S(2)}, u32[]{:S(2)}) collective-permute-start(bf16[256,512]{1,0:T(8,128)(2,1)S(1)} %get-tuple-element.30), channel_id=1, source_target_pairs={{0,24},{4,28},{8,16},{12,20},{16,8},{20,12},{24,0},{28,4},{1,25},{... | collective-permute-start | bytes 786440 | tf_op jit(solution)/shard_map/zero_to_chip_3/ppermute | solution.py:22
  23.1 11.0 %collective-permute-start.8 = (bf16[128,512]{1,0:T(8,128)(2,1)S(1)}, bf16[128,512]{1,0:T(8,128)(2,1)S(1)}, u32[]{:S(2)}, u32[]{:S(2)}) collective-permute-start(bf16[128,512]{1,0:T(8,128)(2,1)S(1)} %total_0.1), channel_id=1, source_target_pairs={{0,2},{1,3},{2,0},{3,1},{4,6},{5,7},{6,4},{7,5},{8,10},{9,11},{10,... | collective-permute-start | bytes 393224 | tf_op jit(solution)/shard_map/mirror_0/ppermute | solution.py:29
  25.8 9.7 %collective-permute-start.12 = (bf16[128,512]{1,0:T(8,128)(2,1)S(1)}, bf16[128,512]{1,0:T(8,128)(2,1)S(1)}, u32[]{:S(2)}, u32[]{:S(2)}) collective-permute-start(bf16[128,512]{1,0:T(8,128)(2,1)S(1)} %total_1.1), channel_id=1, source_target_pairs={{0,2},{1,3},{2,0},{3,1},{4,6},{5,7},{6,4},{7,5},{8,10},{9,11},{10,... | collective-permute-start | bytes 393224 | tf_op jit(solution)/shard_map/mirror_1/ppermute | solution.py:29

commit v5 on v4

--- a/solution.py
+++ b/solution.py
@@ -50,6 +50,11 @@
 IN_VMEM = pl.BlockSpec(memory_space=pltpu.VMEM)
 PARAMS = pltpu.CompilerParams(vmem_limit_bytes=VMEM_BYTES)
 SMALL = pl.CostEstimate(flops=1, bytes_accessed=1, transcendentals=0)
+LARGE = pl.CostEstimate(flops=1 << 33, bytes_accessed=1, transcendentals=0)
+
+
+def in_hbm(values):
+    return [pltpu.with_memory_space_constraint(x, pltpu.HBM) for x in values]
 
 
 def held(value):
@@ -88,27 +93,23 @@
 
 
 def product_kernel(sibling, experts, count, route, counts, inputs, hidden, *refs):
-    out, wide, columns, rows, route_now, counts_now, column_sems, sems = refs[-8:]
-    share = out.shape[1]
+    wide, columns, rows, route_now, counts_now, column_sems, sems = refs[-7:]
+    out, *ahead = refs[count:-7]
+    share, span, blocks = out.shape[1], columns.shape[1], route.shape[1]
     copies = routed_copies(route, counts, route_now, counts_now, sems)
     copies.append(pltpu.make_async_copy(hidden.at[1], rows.at[0], sems.at[2]))
     first = column_copies(inputs, 1, sibling, columns, share, column_sems.at[0])
     later = []
-    if not sibling:
-        ahead, mine = refs[count : count + 2]
-        ahead_wide = ahead.at[:, columns.shape[1] :]
+    for extra in ahead:
         copies.append(pltpu.make_async_copy(hidden.at[0], rows.at[1], sems.at[3]))
-        span = columns.shape[1]
-        later = column_copies(inputs, 0, True, ahead.at[:, :span], share, column_sems.at[1])
-        later += column_copies(inputs, 0, False, mine, share, column_sems.at[2])
+        later = column_copies(inputs, 0, True, extra.at[:, :span], share, column_sems.at[1])
     for copy in copies + first + later:
         copy.start()
     for copy in copies:
         copy.wait()
-    blocks = route.shape[1]
     expand_hidden(route_now, counts_now, 1, rows.at[0], wide, blocks, experts)
-    if not sibling:
-        expand_hidden(route_now, counts_now, 0, rows.at[1], ahead_wide, blocks, experts)
+    for extra in ahead:
+        expand_hidden(route_now, counts_now, 0, rows.at[1], extra.at[:, span:], blocks, experts)
     for copy in first:
         copy.wait()
     out[...] = contracted(columns[...], wide[...]).astype(out.dtype).reshape(out.shape)
@@ -119,82 +120,83 @@
 def products(sibling, after, route, counts, inputs, hidden, share, chips, experts):
     _, rows, _ = inputs.shape
     width = hidden.shape[2]
-    wide = pltpu.VMEM((rows, experts * width), jnp.bfloat16)
-    columns = pltpu.VMEM((rows, chips * share), jnp.bfloat16)
-    both = pltpu.VMEM((rows, chips * share + experts * width), jnp.bfloat16)
-    extra = [] if sibling else [both, columns]
-    outs = extra + [pltpu.VMEM((chips, share, experts * width), jnp.bfloat16)]
+    span, columns = chips * share, experts * width
+    outs = [pltpu.VMEM((chips, share, columns), jnp.bfloat16)]
+    if not sibling:
+        outs.append(pltpu.VMEM((rows, span + columns), jnp.bfloat16))
     return pl.pallas_call(
         functools.partial(product_kernel, sibling, experts, len(after)),
         in_specs=[ANYWHERE] * (4 + len(after)),
         out_specs=[IN_VMEM] * len(outs),
         out_shape=outs,
         scratch_shapes=[
-            wide,
-            columns,
+            pltpu.VMEM((rows, columns), jnp.bfloat16),
+            pltpu.VMEM((rows, span), jnp.bfloat16),
             pltpu.VMEM((2, rows, width), jnp.bfloat16),
             pltpu.SMEM(route.shape, jnp.int32),
             pltpu.SMEM(counts.shape, jnp.int32),
-            pltpu.SemaphoreType.DMA((3, chips)),
+            pltpu.SemaphoreType.DMA((2, chips)),
             pltpu.SemaphoreType.DMA((4,)),
         ],
         compiler_params=PARAMS,
         cost_estimate=SMALL,
-    )(
-        *(pltpu.with_memory_space_constraint(x, pltpu.HBM) for x in (route, counts, inputs, hidden)),
-        *after,
-    )
-
-
-def join_kernel(parts, own, received, *outs):
-    chips, share, _ = own.shape
-    rows = share // parts
-    for i in range(parts):
-        some = slice(i * rows, (i + 1) * rows)
+    )(*in_hbm((route, counts, inputs, hidden)), *after)
+
+
+def join_kernel(cuts, own, received, *outs):
+    chips = own.shape[0]
+    for i, some in enumerate(cuts):
         for k in range(chips):
             out = outs[i * chips + k]
             total = own[k, some].astype(jnp.float32) + received[k, some].astype(jnp.float32)
             out[...] = total.astype(out.dtype)
 
 
-def joined(own, received, parts):
-    chips, share, columns = own.shape
-    shape = (share // parts, columns)
-    outs = [pltpu.VMEM(shape, jnp.float32)] + [pltpu.VMEM(shape, jnp.bfloat16)] * (chips - 1)
+def joined(own, received, cuts):
+    chips, _, columns = own.shape
+    outs = []
+    for some in cuts:
+        shape = (some.stop - some.start, columns)
+        outs += [pltpu.VMEM(shape, jnp.float32)] + [pltpu.VMEM(shape, jnp.bfloat16)] * (chips - 1)
     flat = pl.pallas_call(
-        functools.partial(join_kernel, parts),
+        functools.partial(join_kernel, cuts),
         in_specs=[IN_VMEM, IN_VMEM],
-        out_specs=[IN_VMEM] * (chips * parts),
-        out_shape=outs * parts,
+        out_specs=[IN_VMEM] * len(outs),
+        out_shape=outs,
         compiler_params=PARAMS,
         cost_estimate=SMALL,
     )(held(own), held(received))
-    return [flat[i * chips : (i + 1) * chips] for i in range(parts)]
-
-
-def pair_kernel(count, mine, ahead, other, *refs):
+    return [flat[i * chips : (i + 1) * chips] for i in range(len(cuts))]
+
+
+def pair_kernel(count, messages, inputs, ahead, other, *refs):
     kept, *sent = refs[count:]
-    span = mine.shape[1]
-    total = contracted(mine[...], ahead[:, span:]) + contracted(other[:, :span], other[:, span:])
-    total = total.reshape(1 + len(sent), *kept.shape)
-    kept[...] = total[0]
-    for k, out in enumerate(sent):
-        out[...] = total[k + 1].astype(out.dtype)
-
-
-def paired(mine, ahead, other, after, share):
-    span = mine.shape[1]
-    chips, columns = span // share, ahead.shape[1] - span
-    shape = (share, columns)
+    share = kept.shape[0]
+    span = ahead.shape[1] - kept.shape[1]
+    me = lax.axis_index("dp")
+    for k in range(span // share):
+        begin = pl.multiple_of((lax.bitwise_xor(me // 2, k) * 2 + me % 2) * share, share)
+        total = contracted(inputs[0, :, pl.ds(begin, share)], ahead[:, span:])
+        total = total + contracted(other[:, k * share : (k + 1) * share], other[:, span:])
+        if k == 0:
+            kept[...] = total
+        for (place, some), out in zip(messages, sent):
+            if place == k:
+                out[...] = total[some].astype(out.dtype)
+
+
+def paired(inputs, ahead, other, after, share, chips, messages):
+    columns = ahead.shape[1] - chips * share
+    outs = [pltpu.VMEM((share, columns), jnp.float32)]
+    outs += [pltpu.VMEM((some.stop - some.start, columns), jnp.bfloat16) for _, some in messages]
     return pl.pallas_call(
-        functools.partial(pair_kernel, len(after)),
+        functools.partial(pair_kernel, len(after), messages),
         in_specs=[IN_VMEM] * 3 + [ANYWHERE] * len(after),
-        out_specs=[IN_VMEM] * chips,
-        out_shape=[pltpu.VMEM(shape, jnp.float32)]
-        + [pltpu.VMEM(shape, jnp.bfloat16)] * (chips - 1),
+        out_specs=[IN_VMEM] * len(outs),
+        out_shape=outs,
         compiler_params=PARAMS,
         cost_estimate=SMALL,
-    )(held(mine), held(ahead), held(other), *after)
+    )(*map(held, (inputs, ahead, other)), *after)
 
 
 def total_kernel(count, kept, *refs):
@@ -205,7 +207,7 @@
     out[...] = total.astype(out.dtype)
 
 
-def totalled(kept, received, after, dtype):
+def totalled(kept, received, after, dtype, cost=None):
     count = len(received)
     return pl.pallas_call(
         functools.partial(total_kernel, count),
@@ -213,62 +215,84 @@
         out_specs=IN_VMEM,
         out_shape=pltpu.VMEM(kept.shape, dtype),
         compiler_params=PARAMS,
-        cost_estimate=SMALL,
+        cost_estimate=cost or SMALL,
     )(held(kept), *map(held, received), *after)
 
 
-def update_kernel(experts, count, steps, kept, *refs):
-    received, partners = refs[:count], refs[count : count + steps]
-    first, second = refs[count + steps : count + steps + 2]
-    outs = refs[count + steps + 2 : count + steps + 6]
-    grad_out, first_out, second_out, step_out, sems = refs[count + steps + 6 :]
-    share, _, width = first.shape
-    rows = share // steps
+def update_kernel(experts, cuts, messages, kept, *refs):
+    count, parts = len(messages), len(cuts)
+    received, partners = refs[:count], refs[count : count + parts]
+    first, second, *outs = refs[count + parts : count + parts + 6]
+    grad_out, first_out, second_out, step_out, sems = refs[count + parts + 6 :]
+    share, columns = kept.shape
+    lines = columns // LANES
+    chunks = columns // experts // LANES
+    steps = sorted({0, *(some.stop for some in cuts), *(some.stop for _, some in messages)})
     copies = []
-    for i in range(steps):
-        some = slice(i * rows, (i + 1) * rows)
-        for e in range(experts):
-            columns = slice(e * width, (e + 1) * width)
-            grad = kept[some, columns]
-            for part in received:
-                grad = grad + part[some, columns].astype(jnp.float32)
-            grad = grad + partners[i][:, columns].astype(jnp.float32)
-            new_first = beta_one * first[some, e, :] + (1.0 - beta_one) * grad
-            new_second = beta_two * second[some, e, :] + (1.0 - beta_two) * grad * grad
-            grad_out[some, e, :] = grad
-            first_out[some, e, :] = new_first
-            second_out[some, e, :] = new_second
-            step_out[some, e, :] = (
-                new_first / bias_first / (jnp.sqrt(new_second / bias_second) + adam_epsilon)
-            )
+    for i, (begin, end) in enumerate(zip(steps, steps[1:])):
+        rows = end - begin
+
+        def inside(spans):
+            return [
+                (ref, slice(begin - span.start, end - span.start))
+                for ref, span in spans
+                if span.start <= begin and end <= span.stop
+            ]
+
+        terms = inside(zip(received, (span for _, span in messages)))
+        terms += inside(zip(partners, cuts))
+        for line in range(lines):
+            expert, chunk = line // chunks, line % chunks
+            some = slice(line * LANES, (line + 1) * LANES)
+            grad = kept[begin:end, some]
+            for part, place in terms:
+                grad = grad + part[place, some].astype(jnp.float32)
+            place = begin * lines + chunk * experts + expert
+            grad_out[pl.ds(place, rows, stride=lines), :] = grad
+        some = slice(begin * lines, end * lines)
+        grad = grad_out[some, :]
+        new_first = beta_one * first[some, :] + (1.0 - beta_one) * grad
+        new_second = beta_two * second[some, :] + (1.0 - beta_two) * grad * grad
+        first_out[some, :] = new_first
+        second_out[some, :] = new_second
+        step_out[some, :] = (
+            new_first / bias_first / (jnp.sqrt(new_second / bias_second) + adam_epsilon)
+        )
         for j, (source, target) in enumerate(
             zip((grad_out, first_out, second_out, step_out), outs)
         ):
-            copy = pltpu.make_async_copy(
-                source.at[pl.ds(i * rows, rows)], target.at[pl.ds(i * rows, rows)], sems.at[i, j]
-            )
+            copy = pltpu.make_async_copy(source.at[some], target.at[some], sems.at[i, j])
             copy.start()
             copies.append(copy)
     for copy in copies:
         copy.wait()
 
 
-def updated(kept, received, partners, first, second):
-    _, experts, _ = first.shape
-    count, steps = len(received), len(partners)
-    return pl.pallas_call(
-        functools.partial(update_kernel, experts, count, steps),
-        in_specs=[IN_VMEM] * (3 + count + steps),
+def in_lines(value):
+    rows, experts, width = value.shape
+    value = value.reshape(rows, experts, width // LANES, LANES)
+    return value.transpose(0, 2, 1, 3).reshape(-1, LANES)
+
+
+def from_lines(value, shape):
+    rows, experts, width = shape
+    value = value.reshape(rows, width // LANES, experts, LANES)
+    return value.transpose(0, 2, 1, 3).reshape(shape)
+
+
+def updated(kept, received, partners, first, second, cuts, messages):
+    most = 1 + len(cuts) + len(messages)
+    lines = pltpu.VMEM((first.size // LANES, LANES), jnp.float32)
+    outs = pl.pallas_call(
+        functools.partial(update_kernel, first.shape[1], cuts, messages),
+        in_specs=[IN_VMEM] * (3 + len(received) + len(partners)),
         out_specs=[ANYWHERE] * 4,
-        out_shape=[jax.ShapeDtypeStruct(first.shape, jnp.float32)] * 4,
-        scratch_shapes=[pltpu.VMEM(first.shape, jnp.float32)] * 4
-        + [pltpu.SemaphoreType.DMA((steps, 4))],
+        out_shape=[jax.ShapeDtypeStruct(lines.shape, jnp.float32)] * 4,
+        scratch_shapes=[lines] * 4 + [pltpu.SemaphoreType.DMA((most, 4))],
         compiler_params=PARAMS,
         cost_estimate=SMALL,
-    )(*map(held, (kept, *received, *partners, first, second)))
-
-
-PARTS = 2
+    )(*map(held, (kept, *received, *partners, in_lines(first), in_lines(second))))
+    return [from_lines(out, first.shape) for out in outs]
 
 
 def fast_device(saved_inputs, hidden_grads, block_expert, live_counts, first_moment, second_moment):
@@ -285,33 +309,44 @@
         experts=experts,
     )
 
-    def to_owners(pieces, name):
+    def to_owners(pieces, places, name):
         return [
-            exchanged(piece, "dp", 2 * (k + 1), f"{name}_to_chip_{k + 1}")
-            for k, piece in enumerate(pieces)
+            exchanged(piece, "dp", 2 * k, f"{name}_to_chip_{k}")
+            for piece, k in zip(pieces, places)
         ]
 
+    cut, half = share * 4 // 8, share // 2
+    cuts = [slice(0, cut), slice(cut, share)]
+    halves = [slice(0, half), slice(half, share)]
+    places = range(1, chips)
+    messages = [(k, slice(0, share)) for k in places]
     with jax.named_scope("sibling_products"):
         (sibling,) = product(True, [])
     other = exchanged(sibling, "dp", 1, "sibling_exchange")
     with jax.named_scope("own_products"):
-        ahead, mine, own = product(False, [sibling])
+        own, ahead = product(False, [sibling])
     other_ahead = exchanged(ahead, "dp", 1, "operand_exchange")
     with jax.named_scope("join"):
-        pieces = joined(own, other, PARTS)
-    parts = [(kept, to_owners(sent, f"one_part_{i}")) for i, (kept, *sent) in enumerate(pieces)]
+        pieces = joined(own, other, cuts)
+    parts = [
+        (kept, to_owners(sent, places, f"one_part_{i}")) for i, (kept, *sent) in enumerate(pieces)
+    ]
+    with jax.named_scope("pair"):
+        kept_zero, *sent_zero = paired(
+            saved_inputs[0, 0], ahead, other_ahead, [parts[0][1][1]], share, chips, messages
+        )
+    received_zero = to_owners(sent_zero, [k for k, _ in messages], "zero")
     with jax.named_scope("total_0"):
-        first_total = totalled(*parts[0], [], jnp.bfloat16)
-    with jax.named_scope("pair"):
-        kept_zero, *sent_zero = paired(mine, ahead, other_ahead, [parts[0][1][1]], share)
-    received_zero = to_owners(sent_zero, "zero")
+        first_total = totalled(*parts[0], [kept_zero], jnp.bfloat16)
     partners = [mirrored(first_total, "mirror_0")]
     for i, (kept, received) in enumerate(parts[1:]):
         with jax.named_scope(f"total_{i + 1}"):
-            total = totalled(kept, received, [kept_zero], jnp.bfloat16)
+            total = totalled(kept, received, [kept_zero], jnp.bfloat16, LARGE)
         partners.append(mirrored(total, f"mirror_{i + 1}"))
     with jax.named_scope("update"):
-        outs = updated(kept_zero, received_zero, partners, first_moment[0], second_moment[0])
+        outs = updated(
+            kept_zero, received_zero, partners, first_moment[0], second_moment[0], cuts, messages
+        )
     return tuple(out[None] for out in outs)
 
 

time: 38 us -> 36.2 us (0.953)
  waiting for transfers between devices: 10.5 us -> 8.05 us
  starting transfers between devices: 17.6 us -> 19.1 us
  Pallas kernels: 8.97 us -> 8.19 us
    ppermute x2, waiting for transfers between devices: 8.66 us -> 4.79 us  [mirrored(): return lax.ppermute(value, 'section', pairs)]
    ppermute x2, starting transfers between devices: 3.66 us -> 5.23 us  [mirrored(): return lax.ppermute(value, 'section', pairs)]
    ppermute x11, waiting for transfers between devices: 1.87 us -> 3.26 us  [exchanged(): lax.ppermute(value, axis, [(source, source ^ mask) for source in range(co...]
    pallas_call x3, Pallas kernels: 3.84 us -> 3.24 us  [the longest x1 1.74 us: updated(): pl.pallas_call(functools.partial(update_kernel, first.shape[1], cuts, mes...]
  transfers between devices with their start and end apart: 13 -> 13, of which waited for: 5 -> 4; matrix products, arithmetic and copies ran while one was open for 0% -> 0% of each run, Pallas kernels for 12% -> 12%
where the time goes in v5:
time: 36.2 us; the launch traced here: 36 us
  starting transfers between devices  19.1 us (53%)
  Pallas kernels  8.19 us (23%)
  waiting for transfers between devices  8.05 us (22%)
  between operations  0.69 us (2%)
    ppermute x11, starting transfers between devices, exchanged(): lax.ppermute(value, axis, [(source, source ^ mask) for source in range(co...  13.8 us
    ppermute x2, starting transfers between devices, mirrored(): return lax.ppermute(value, 'section', pairs)  5.23 us
    pallas_call x2, Pallas kernels, products(): pl.pallas_call(functools.partial(product_kernel, sibling, experts, len(af...  4.83 us
    ppermute x2, waiting for transfers between devices, mirrored(): return lax.ppermute(value, 'section', pairs)  4.79 us
    ppermute x11, waiting for transfers between devices, exchanged(): lax.ppermute(value, axis, [(source, source ^ mask) for source in range(co...  3.26 us
    pallas_call x1, Pallas kernels, updated(): pl.pallas_call(functools.partial(update_kernel, first.shape[1], cuts, mes...  1.74 us
    pallas_call x1, Pallas kernels, paired(): pl.pallas_call(functools.partial(pair_kernel, len(after), messages), in_s...  1.26 us
  transfers between devices with their start and end apart: 13, of which 4 were waited for; matrix products, arithmetic and copies ran while one was open for 0% of the time, Pallas kernels for 12%

profile of v5, /device:TPU:0, one launch (start us, length us, event | category | flops | bytes accessed | tf_op | source)
XLA Modules:
  0.0 36.0 jit_solution(9420813951925581935)
XLA Ops:
  0.6 2.2 %sibling_products.1.refs_0_ = bf16[4,256,512]{2,1,0:T(8,128)(2,1)S(1)} custom-call(s32[2,3]{1,0:T(2,128)} %bitcast.41, s32[2,2]{1,0:T(2,128)} %bitcast.43, bf16[2,384,2048]{2,1,0:T(8,128)(2,1)} %bitcast.34, bf16[2,384,256]{2,1,0:T(8,128)(2,1)} %bitcast.39), custom_call_target="tpu_custom_call" | custom-call | flops 1 | bytes 1 | tf_op jit(solution)/shard_map/sibling_products/pallas_call | solution.py:127
  2.8 0.5 %collective-permute-start.1 = (bf16[4,256,512]{2,1,0:T(8,128)(2,1)S(1)}, bf16[4,256,512]{2,1,0:T(8,128)(2,1)S(1)}, u32[]{:S(2)}, u32[]{:S(2)}) collective-permute-start(bf16[4,256,512]{2,1,0:T(8,128)(2,1)S(1)} %sibling_products.1.refs_0_), channel_id=1, source_target_pairs={{0,4},{4,0},{8,12},{12,8},{16,20},{20,16},{24,28},{28,24},{1,5},{5... | collective-permute-start | bytes 3145736 | tf_op jit(solution)/shard_map/sibling_exchange/ppermute | solution.py:22
  3.3 0.0 copy-start
  3.3 2.7 %own_products.1 = (bf16[4,256,512]{2,1,0:T(8,128)(2,1)S(1)}, bf16[384,1536]{1,0:T(8,128)(2,1)S(1)}) custom-call(s32[2,3]{1,0:T(2,128)} %bitcast.42, s32[2,2]{1,0:T(2,128)} %bitcast.44, bf16[2,384,2048]{2,1,0:T(8,128)(2,1)} %bitcast.35, bf16[2,384,256]{2,1,0:T(8,128)(2,1)} %bitcast.40, bf16[4,256,512]{2,1,0:T(8,128)(2,1)S(1)} %sibling_products.1.refs_0_), custom_call_target="tpu_custom_call" | custom-call | flops 1 | bytes 1 | tf_op jit(solution)/shard_map/own_products/pallas_call | solution.py:127
  6.0 0.1 collective-permute-start
  6.1 0.0 collective-permute-done.1.received
  6.1 0.2 join.1
  6.4 3.0 %collective-permute-start.2 = (bf16[128,512]{1,0:T(8,128)(2,1)S(1)}, bf16[128,512]{1,0:T(8,128)(2,1)S(1)}, u32[]{:S(2)}, u32[]{:S(2)}) collective-permute-start(bf16[128,512]{1,0:T(8,128)(2,1)S(1)} %get-tuple-element.24), channel_id=1, source_target_pairs={{0,16},{4,20},{8,24},{12,28},{16,0},{20,4},{24,8},{28,12},{1,17},{... | collective-permute-start | bytes 393224 | tf_op jit(solution)/shard_map/one_part_0_to_chip_2/ppermute | solution.py:22
  9.4 1.5 %collective-permute-start.6 = (bf16[128,512]{1,0:T(8,128)(2,1)S(1)}, bf16[128,512]{1,0:T(8,128)(2,1)S(1)}, u32[]{:S(2)}, u32[]{:S(2)}) collective-permute-start(bf16[128,512]{1,0:T(8,128)(2,1)S(1)} %get-tuple-element.30), channel_id=1, source_target_pairs={{0,8},{4,12},{8,0},{12,4},{16,24},{20,28},{24,16},{28,20},{1,9},{5... | collective-permute-start | bytes 393224 | tf_op jit(solution)/shard_map/one_part_0_to_chip_1/ppermute | solution.py:22
  10.9 0.0 collective-permute-start.7
  10.9 1.9 %collective-permute-start.9 = (bf16[128,512]{1,0:T(8,128)(2,1)S(1)}, bf16[128,512]{1,0:T(8,128)(2,1)S(1)}, u32[]{:S(2)}, u32[]{:S(2)}) collective-permute-start(bf16[128,512]{1,0:T(8,128)(2,1)S(1)} %get-tuple-element.33), channel_id=1, source_target_pairs={{0,8},{4,12},{8,0},{12,4},{16,24},{20,28},{24,16},{28,20},{1,9},{5... | collective-permute-start | bytes 393224 | tf_op jit(solution)/shard_map/one_part_1_to_chip_1/ppermute | solution.py:22
  12.8 0.2 collective-permute-done.2.refs_0_.refs_1_
  13.1 1.8 %collective-permute-start.10 = (bf16[128,512]{1,0:T(8,128)(2,1)S(1)}, bf16[128,512]{1,0:T(8,128)(2,1)S(1)}, u32[]{:S(2)}, u32[]{:S(2)}) collective-permute-start(bf16[128,512]{1,0:T(8,128)(2,1)S(1)} %get-tuple-element.34), channel_id=1, source_target_pairs={{0,16},{4,20},{8,24},{12,28},{16,0},{20,4},{24,8},{28,12},{1,17},{... | collective-permute-start | bytes 393224 | tf_op jit(solution)/shard_map/one_part_1_to_chip_2/ppermute | solution.py:22
  14.9 0.0 collective-permute-done.other
  14.9 1.4 %collective-permute-start.11 = (bf16[128,512]{1,0:T(8,128)(2,1)S(1)}, bf16[128,512]{1,0:T(8,128)(2,1)S(1)}, u32[]{:S(2)}, u32[]{:S(2)}) collective-permute-start(bf16[128,512]{1,0:T(8,128)(2,1)S(1)} %get-tuple-element.35), channel_id=1, source_target_pairs={{0,24},{4,28},{8,16},{12,20},{16,8},{20,12},{24,0},{28,4},{1,25},{... | collective-permute-start | bytes 393224 | tf_op jit(solution)/shard_map/one_part_1_to_chip_3/ppermute | solution.py:22
  16.3 0.0 copy-done
  16.3 1.3 %pair.1 = (f32[256,512]{1,0:T(8,128)S(1)}, bf16[256,512]{1,0:T(8,128)(2,1)S(1)}, bf16[256,512]{1,0:T(8,128)(2,1)S(1)}, bf16[256,512]{1,0:T(8,128)(2,1)S(1)}) custom-call(bf16[2,384,2048]{2,1,0:T(8,128)(2,1)S(1)} %bitcast.36, bf16[384,1536]{1,0:T(8,128)(2,1)S(1)} %get-tuple-element.22.ahead, bf16[384,1536]{1,0:T(8,128)(2,1)S(1)} %collective-permute-done.other, ...), custom_call_target="tpu_custom_call" | custom-call | flops 1 | bytes 1 | tf_op jit(solution)/shard_map/pair/pallas_call | solution.py:192
  17.6 0.0 collective-permute-done.6.refs_0_
  17.6 0.6 %collective-permute-done.7.refs_2_ = bf16[128,512]{1,0:T(8,128)(2,1)S(1)} collective-permute-done((bf16[128,512]{1,0:T(8,128)(2,1)S(1)}, bf16[128,512]{1,0:T(8,128)(2,1)S(1)}, u32[]{:S(2)}, u32[]{:S(2)}) %collective-permute-start.7) | collective-permute-done | bytes 131104 | tf_op jit(solution)/shard_map/one_part_0_to_chip_3/ppermute | solution.py:22
  18.2 0.1 total_0.1
  18.3 2.7 %collective-permute-start.8 = (bf16[128,512]{1,0:T(8,128)(2,1)S(1)}, bf16[128,512]{1,0:T(8,128)(2,1)S(1)}, u32[]{:S(2)}, u32[]{:S(2)}) collective-permute-start(bf16[128,512]{1,0:T(8,128)(2,1)S(1)} %total_0.1), channel_id=1, source_target_pairs={{0,2},{1,3},{2,0},{3,1},{4,6},{5,7},{6,4},{7,5},{8,10},{9,11},{10,... | collective-permute-start | bytes 393224 | tf_op jit(solution)/shard_map/mirror_0/ppermute | solution.py:29
  21.0 1.8 %collective-permute-start.3 = (bf16[256,512]{1,0:T(8,128)(2,1)S(1)}, bf16[256,512]{1,0:T(8,128)(2,1)S(1)}, u32[]{:S(2)}, u32[]{:S(2)}) collective-permute-start(bf16[256,512]{1,0:T(8,128)(2,1)S(1)} %get-tuple-element.26), channel_id=1, source_target_pairs={{0,8},{4,12},{8,0},{12,4},{16,24},{20,28},{24,16},{28,20},{1,9},{5... | collective-permute-start | bytes 786440 | tf_op jit(solution)/shard_map/zero_to_chip_1/ppermute | solution.py:22
  22.8 0.0 collective-permute-done.9.refs_0_
  22.8 1.5 %collective-permute-start.4 = (bf16[256,512]{1,0:T(8,128)(2,1)S(1)}, bf16[256,512]{1,0:T(8,128)(2,1)S(1)}, u32[]{:S(2)}, u32[]{:S(2)}) collective-permute-start(bf16[256,512]{1,0:T(8,128)(2,1)S(1)} %get-tuple-element.27), channel_id=1, source_target_pairs={{0,16},{4,20},{8,24},{12,28},{16,0},{20,4},{24,8},{28,12},{1,17},{... | collective-permute-start | bytes 786440 | tf_op jit(solution)/shard_map/zero_to_chip_2/ppermute | solution.py:22
  24.3 0.0 collective-permute-done.10.refs_1_
  24.3 0.2 collective-permute-start.5
  24.5 0.0 collective-permute-done.11.refs_2_
  24.5 0.0 copy-start.1
  24.5 0.0 copy-start.2
  24.5 0.1 total_1.1
  24.5 2.5 %collective-permute-start.12 = (bf16[128,512]{1,0:T(8,128)(2,1)S(1)}, bf16[128,512]{1,0:T(8,128)(2,1)S(1)}, u32[]{:S(2)}, u32[]{:S(2)}) collective-permute-start(bf16[128,512]{1,0:T(8,128)(2,1)S(1)} %total_1.1), channel_id=1, source_target_pairs={{0,2},{1,3},{2,0},{3,1},{4,6},{5,7},{6,4},{7,5},{8,10},{9,11},{10,... | collective-permute-start | bytes 393224 | tf_op jit(solution)/shard_map/mirror_1/ppermute | solution.py:29
  27.1 0.0 collective-permute-done.8.refs_3_
  27.1 4.8 %collective-permute-done.12.refs_4_ = bf16[128,512]{1,0:T(8,128)(2,1)S(1)} collective-permute-done((bf16[128,512]{1,0:T(8,128)(2,1)S(1)}, bf16[128,512]{1,0:T(8,128)(2,1)S(1)}, u32[]{:S(2)}, u32[]{:S(2)}) %collective-permute-start.12) | collective-permute-done | bytes 131104 | tf_op jit(solution)/shard_map/mirror_1/ppermute | solution.py:29
  31.9 0.0 collective-permute-done.3.refs_0_
  31.9 2.4 %collective-permute-done.4.refs_1_ = bf16[256,512]{1,0:T(8,128)(2,1)S(1)} collective-permute-done((bf16[256,512]{1,0:T(8,128)(2,1)S(1)}, bf16[256,512]{1,0:T(8,128)(2,1)S(1)}, u32[]{:S(2)}, u32[]{:S(2)}) %collective-permute-start.4) | collective-permute-done | bytes 262176 | tf_op jit(solution)/shard_map/zero_to_chip_2/ppermute | solution.py:22
  34.2 0.0 collective-permute-done.5.refs_2_
  34.2 0.0 copy-done.1
  34.3 0.0 copy-done.2
  34.3 1.7 %update.1 = (f32[1024,128]{1,0:T(8,128)}, f32[1024,128]{1,0:T(8,128)}, f32[1024,128]{1,0:T(8,128)}, f32[1024,128]{1,0:T(8,128)}) custom-call(f32[256,512]{1,0:T(8,128)S(1)} %get-tuple-element.25.refs_3_.kept, bf16[256,512]{1,0:T(8,128)(2,1)S(1)} %collective-permute-done.3.refs_0_, bf16[256,512]{1,0:T(8,128)(2,1)S(1)} %collective-permute-done.4.refs_1_, ...), custom_call_target="tpu_custom_call" | custom-call | flops 1 | bytes 1 | tf_op jit(solution)/shard_map/update/pallas_call | solution.py:286
Async XLA Ops:
  2.8 3.3 %collective-permute-start.1 = (bf16[4,256,512]{2,1,0:T(8,128)(2,1)S(1)}, bf16[4,256,512]{2,1,0:T(8,128)(2,1)S(1)}, u32[]{:S(2)}, u32[]{:S(2)}) collective-permute-start(bf16[4,256,512]{2,1,0:T(8,128)(2,1)S(1)} %sibling_products.1.refs_0_), channel_id=1, source_target_pairs={{0,4},{4,0},{8,12},{12,8},{16,20},{20,16},{24,28},{28,24},{1,5},{5... | collective-permute-start | bytes 3145736 | tf_op jit(solution)/shard_map/sibling_exchange/ppermute | solution.py:22
  3.3 13.0 %copy-start = (bf16[1,1,2,384,2048]{4,3,2,1,0:T(8,128)(2,1)S(1)}, bf16[1,1,2,384,2048]{4,3,2,1,0:T(8,128)(2,1)}, u32[]{:S(2)}) copy-start(bf16[1,1,2,384,2048]{4,3,2,1,0:T(8,128)(2,1)} %param.6) | copy-start | bytes 9437188
  6.0 8.9 %collective-permute-start = (bf16[384,1536]{1,0:T(8,128)(2,1)S(1)}, bf16[384,1536]{1,0:T(8,128)(2,1)S(1)}, u32[]{:S(2)}, u32[]{:S(2)}) collective-permute-start(bf16[384,1536]{1,0:T(8,128)(2,1)S(1)} %get-tuple-element.22.ahead), channel_id=1, source_target_pairs={{0,4},{4,0},{8,12},{12,8},{16,20},{20,16},{24,28},{28,24},{1,5},{5... | collective-permute-start | bytes 3538952 | tf_op jit(solution)/shard_map/operand_exchange/ppermute | solution.py:22
  6.4 6.7 %collective-permute-start.2 = (bf16[128,512]{1,0:T(8,128)(2,1)S(1)}, bf16[128,512]{1,0:T(8,128)(2,1)S(1)}, u32[]{:S(2)}, u32[]{:S(2)}) collective-permute-start(bf16[128,512]{1,0:T(8,128)(2,1)S(1)} %get-tuple-element.24), channel_id=1, source_target_pairs={{0,16},{4,20},{8,24},{12,28},{16,0},{20,4},{24,8},{28,12},{1,17},{... | collective-permute-start | bytes 393224 | tf_op jit(solution)/shard_map/one_part_0_to_chip_2/ppermute | solution.py:22
  9.4 8.2 %collective-permute-start.6 = (bf16[128,512]{1,0:T(8,128)(2,1)S(1)}, bf16[128,512]{1,0:T(8,128)(2,1)S(1)}, u32[]{:S(2)}, u32[]{:S(2)}) collective-permute-start(bf16[128,512]{1,0:T(8,128)(2,1)S(1)} %get-tuple-element.30), channel_id=1, source_target_pairs={{0,8},{4,12},{8,0},{12,4},{16,24},{20,28},{24,16},{28,20},{1,9},{5... | collective-permute-start | bytes 393224 | tf_op jit(solution)/shard_map/one_part_0_to_chip_1/ppermute | solution.py:22
  10.9 7.3 %collective-permute-start.7 = (bf16[128,512]{1,0:T(8,128)(2,1)S(1)}, bf16[128,512]{1,0:T(8,128)(2,1)S(1)}, u32[]{:S(2)}, u32[]{:S(2)}) collective-permute-start(bf16[128,512]{1,0:T(8,128)(2,1)S(1)} %get-tuple-element.31), channel_id=1, source_target_pairs={{0,24},{4,28},{8,16},{12,20},{16,8},{20,12},{24,0},{28,4},{1,25},{... | collective-permute-start | bytes 393224 | tf_op jit(solution)/shard_map/one_part_0_to_chip_3/ppermute | solution.py:22
  10.9 11.8 %collective-permute-start.9 = (bf16[128,512]{1,0:T(8,128)(2,1)S(1)}, bf16[128,512]{1,0:T(8,128)(2,1)S(1)}, u32[]{:S(2)}, u32[]{:S(2)}) collective-permute-start(bf16[128,512]{1,0:T(8,128)(2,1)S(1)} %get-tuple-element.33), channel_id=1, source_target_pairs={{0,8},{4,12},{8,0},{12,4},{16,24},{20,28},{24,16},{28,20},{1,9},{5... | collective-permute-start | bytes 393224 | tf_op jit(solution)/shard_map/one_part_1_to_chip_1/ppermute | solution.py:22
  13.1 11.2 %collective-permute-start.10 = (bf16[128,512]{1,0:T(8,128)(2,1)S(1)}, bf16[128,512]{1,0:T(8,128)(2,1)S(1)}, u32[]{:S(2)}, u32[]{:S(2)}) collective-permute-start(bf16[128,512]{1,0:T(8,128)(2,1)S(1)} %get-tuple-element.34), channel_id=1, source_target_pairs={{0,16},{4,20},{8,24},{12,28},{16,0},{20,4},{24,8},{28,12},{1,17},{... | collective-permute-start | bytes 393224 | tf_op jit(solution)/shard_map/one_part_1_to_chip_2/ppermute | solution.py:22
  14.9 9.6 %collective-permute-start.11 = (bf16[128,512]{1,0:T(8,128)(2,1)S(1)}, bf16[128,512]{1,0:T(8,128)(2,1)S(1)}, u32[]{:S(2)}, u32[]{:S(2)}) collective-permute-start(bf16[128,512]{1,0:T(8,128)(2,1)S(1)} %get-tuple-element.35), channel_id=1, source_target_pairs={{0,24},{4,28},{8,16},{12,20},{16,8},{20,12},{24,0},{28,4},{1,25},{... | collective-permute-start | bytes 393224 | tf_op jit(solution)/shard_map/one_part_1_to_chip_3/ppermute | solution.py:22
  18.3 8.8 %collective-permute-start.8 = (bf16[128,512]{1,0:T(8,128)(2,1)S(1)}, bf16[128,512]{1,0:T(8,128)(2,1)S(1)}, u32[]{:S(2)}, u32[]{:S(2)}) collective-permute-start(bf16[128,512]{1,0:T(8,128)(2,1)S(1)} %total_0.1), channel_id=1, source_target_pairs={{0,2},{1,3},{2,0},{3,1},{4,6},{5,7},{6,4},{7,5},{8,10},{9,11},{10,... | collective-permute-start | bytes 393224 | tf_op jit(solution)/shard_map/mirror_0/ppermute | solution.py:29
  21.0 10.9 %collective-permute-start.3 = (bf16[256,512]{1,0:T(8,128)(2,1)S(1)}, bf16[256,512]{1,0:T(8,128)(2,1)S(1)}, u32[]{:S(2)}, u32[]{:S(2)}) collective-permute-start(bf16[256,512]{1,0:T(8,128)(2,1)S(1)} %get-tuple-element.26), channel_id=1, source_target_pairs={{0,8},{4,12},{8,0},{12,4},{16,24},{20,28},{24,16},{28,20},{1,9},{5... | collective-permute-start | bytes 786440 | tf_op jit(solution)/shard_map/zero_to_chip_1/ppermute | solution.py:22
  22.8 11.5 %collective-permute-start.4 = (bf16[256,512]{1,0:T(8,128)(2,1)S(1)}, bf16[256,512]{1,0:T(8,128)(2,1)S(1)}, u32[]{:S(2)}, u32[]{:S(2)}) collective-permute-start(bf16[256,512]{1,0:T(8,128)(2,1)S(1)} %get-tuple-element.27), channel_id=1, source_target_pairs={{0,16},{4,20},{8,24},{12,28},{16,0},{20,4},{24,8},{28,12},{1,17},{... | collective-permute-start | bytes 786440 | tf_op jit(solution)/shard_map/zero_to_chip_2/ppermute | solution.py:22
  24.3 10.0 %collective-permute-start.5 = (bf16[256,512]{1,0:T(8,128)(2,1)S(1)}, bf16[256,512]{1,0:T(8,128)(2,1)S(1)}, u32[]{:S(2)}, u32[]{:S(2)}) collective-permute-start(bf16[256,512]{1,0:T(8,128)(2,1)S(1)} %get-tuple-element.28), channel_id=1, source_target_pairs={{0,24},{4,28},{8,16},{12,20},{16,8},{20,12},{24,0},{28,4},{1,25},{... | collective-permute-start | bytes 786440 | tf_op jit(solution)/shard_map/zero_to_chip_3/ppermute | solution.py:22
  24.5 9.8 %copy-start.1 = (f32[1,256,2,256]{3,2,1,0:T(2,128)S(1)}, f32[1,256,2,256]{3,2,1,0:T(2,128)}, u32[]{:S(2)}) copy-start(f32[1,256,2,256]{3,2,1,0:T(2,128)} %param.10) | copy-start | bytes 1572868
  24.5 9.8 %copy-start.2 = (f32[1,256,2,256]{3,2,1,0:T(2,128)S(1)}, f32[1,256,2,256]{3,2,1,0:T(2,128)}, u32[]{:S(2)}) copy-start(f32[1,256,2,256]{3,2,1,0:T(2,128)} %param.11) | copy-start | bytes 1572868
  24.5 7.3 %collective-permute-start.12 = (bf16[128,512]{1,0:T(8,128)(2,1)S(1)}, bf16[128,512]{1,0:T(8,128)(2,1)S(1)}, u32[]{:S(2)}, u32[]{:S(2)}) collective-permute-start(bf16[128,512]{1,0:T(8,128)(2,1)S(1)} %total_1.1), channel_id=1, source_target_pairs={{0,2},{1,3},{2,0},{3,1},{4,6},{5,7},{6,4},{7,5},{8,10},{9,11},{10,... | collective-permute-start | bytes 393224 | tf_op jit(solution)/shard_map/mirror_1/ppermute | solution.py:29

commit v6 on v5

--- a/solution.py
+++ b/solution.py
@@ -49,6 +49,7 @@
 ANYWHERE = pl.BlockSpec(memory_space=pl.ANY)
 IN_VMEM = pl.BlockSpec(memory_space=pltpu.VMEM)
 PARAMS = pltpu.CompilerParams(vmem_limit_bytes=VMEM_BYTES)
+PIECES = 4
 SMALL = pl.CostEstimate(flops=1, bytes_accessed=1, transcendentals=0)
 LARGE = pl.CostEstimate(flops=1 << 33, bytes_accessed=1, transcendentals=0)
 
@@ -68,22 +69,14 @@
     ]
 
 
-def column_copies(inputs, direction, sibling, target, share, sem):
-    me = lax.axis_index("dp")
-    chip, core = me // 2, me % 2
-    if sibling:
-        core = 1 - core
-    copies = []
-    for k in range(target.shape[1] // share):
-        begin = pl.multiple_of((lax.bitwise_xor(chip, k) * 2 + core) * share, share)
-        copies.append(
-            pltpu.make_async_copy(
-                inputs.at[direction, :, pl.ds(begin, share)],
-                target.at[:, pl.ds(k * share, share)],
-                sem.at[k],
-            )
-        )
-    return copies
+def row_copies(source, target, sems):
+    pieces = sems.shape[0]
+    rows = source.shape[0] // pieces
+    some = [pl.ds(i * rows, rows) for i in range(pieces)]
+    return [
+        pltpu.make_async_copy(source.at[place], target.at[place], sems.at[i])
+        for i, place in enumerate(some)
+    ]
 
 
 def contracted(columns, wide):
@@ -92,111 +85,147 @@
     )
 
 
-def product_kernel(sibling, experts, count, route, counts, inputs, hidden, *refs):
-    wide, columns, rows, route_now, counts_now, column_sems, sems = refs[-7:]
-    out, *ahead = refs[count:-7]
-    share, span, blocks = out.shape[1], columns.shape[1], route.shape[1]
+def owner_columns(k, sibling, share):
+    me = lax.axis_index("dp")
+    core = 1 - me % 2 if sibling else me % 2
+    begin = (lax.bitwise_xor(me // 2, k) * 2 + core) * share
+    return pl.ds(pl.multiple_of(begin, share), share)
+
+
+def sibling_kernel(experts, cuts, route, counts, inputs, hidden, *refs):
+    outs = refs[: len(cuts)]
+    columns, wide, rows, route_now, counts_now, column_sems, sems = refs[len(cuts) :]
     copies = routed_copies(route, counts, route_now, counts_now, sems)
-    copies.append(pltpu.make_async_copy(hidden.at[1], rows.at[0], sems.at[2]))
-    first = column_copies(inputs, 1, sibling, columns, share, column_sems.at[0])
-    later = []
-    for extra in ahead:
-        copies.append(pltpu.make_async_copy(hidden.at[0], rows.at[1], sems.at[3]))
-        later = column_copies(inputs, 0, True, extra.at[:, :span], share, column_sems.at[1])
-    for copy in copies + first + later:
+    copies.append(pltpu.make_async_copy(hidden.at[1], rows, sems.at[2]))
+    column_copies = row_copies(inputs.at[1], columns, column_sems)
+    for copy in copies + column_copies:
         copy.start()
     for copy in copies:
         copy.wait()
-    expand_hidden(route_now, counts_now, 1, rows.at[0], wide, blocks, experts)
-    for extra in ahead:
-        expand_hidden(route_now, counts_now, 0, rows.at[1], extra.at[:, span:], blocks, experts)
-    for copy in first:
+    expand_hidden(route_now, counts_now, 1, rows, wide, route.shape[1], experts)
+    for copy in column_copies:
         copy.wait()
-    out[...] = contracted(columns[...], wide[...]).astype(out.dtype).reshape(out.shape)
-    for copy in later:
-        copy.wait()
-
-
-def products(sibling, after, route, counts, inputs, hidden, share, chips, experts):
-    _, rows, _ = inputs.shape
+    chips, _, _ = outs[0].shape
+    share = cuts[-1].stop
+    for k in range(chips):
+        product = contracted(columns[:, owner_columns(k, True, share)], wide[...])
+        for out, some in zip(outs, cuts):
+            out[k] = product[some].astype(out.dtype)
+
+
+def sibling_products(route, counts, inputs, hidden, chips, experts, cuts):
+    _, rows, model = inputs.shape
     width = hidden.shape[2]
-    span, columns = chips * share, experts * width
-    outs = [pltpu.VMEM((chips, share, columns), jnp.bfloat16)]
-    if not sibling:
-        outs.append(pltpu.VMEM((rows, span + columns), jnp.bfloat16))
+    columns = experts * width
+    outs = [pltpu.VMEM((chips, some.stop - some.start, columns), jnp.bfloat16) for some in cuts]
+    outs += [pltpu.VMEM((rows, model), jnp.bfloat16), pltpu.VMEM((rows, columns), jnp.bfloat16)]
     return pl.pallas_call(
-        functools.partial(product_kernel, sibling, experts, len(after)),
-        in_specs=[ANYWHERE] * (4 + len(after)),
+        functools.partial(sibling_kernel, experts, cuts),
+        in_specs=[ANYWHERE] * 4,
         out_specs=[IN_VMEM] * len(outs),
         out_shape=outs,
         scratch_shapes=[
-            pltpu.VMEM((rows, columns), jnp.bfloat16),
-            pltpu.VMEM((rows, span), jnp.bfloat16),
-            pltpu.VMEM((2, rows, width), jnp.bfloat16),
+            pltpu.VMEM((rows, width), jnp.bfloat16),
             pltpu.SMEM(route.shape, jnp.int32),
             pltpu.SMEM(counts.shape, jnp.int32),
-            pltpu.SemaphoreType.DMA((2, chips)),
-            pltpu.SemaphoreType.DMA((4,)),
+            pltpu.SemaphoreType.DMA((PIECES,)),
+            pltpu.SemaphoreType.DMA((3,)),
         ],
         compiler_params=PARAMS,
         cost_estimate=SMALL,
-    )(*in_hbm((route, counts, inputs, hidden)), *after)
-
-
-def join_kernel(cuts, own, received, *outs):
+    )(*in_hbm((route, counts, inputs, hidden)))
+
+
+def own_kernel(experts, route, counts, inputs, hidden, columns, wide, *refs):
+    out, ahead, rows, route_now, counts_now, column_sems, sems = refs
+    chips, share, _ = out.shape
+    model = columns.shape[1]
+    copies = routed_copies(route, counts, route_now, counts_now, sems)
+    copies.append(pltpu.make_async_copy(hidden.at[0], rows, sems.at[2]))
+    column_copies = row_copies(inputs.at[0], ahead.at[:, :model], column_sems)
+    for copy in copies + column_copies:
+        copy.start()
+    for k in range(chips):
+        product = contracted(columns[:, owner_columns(k, False, share)], wide[...])
+        out[k] = product.astype(out.dtype)
+    for copy in copies:
+        copy.wait()
+    expand_hidden(route_now, counts_now, 0, rows, ahead.at[:, model:], route.shape[1], experts)
+    for copy in column_copies:
+        copy.wait()
+
+
+def own_products(route, counts, inputs, hidden, columns, wide, share, chips, experts):
+    rows, model = columns.shape
+    return pl.pallas_call(
+        functools.partial(own_kernel, experts),
+        in_specs=[ANYWHERE] * 4 + [IN_VMEM] * 2,
+        out_specs=[IN_VMEM] * 2,
+        out_shape=[
+            pltpu.VMEM((chips, share, wide.shape[1]), jnp.bfloat16),
+            pltpu.VMEM((rows, model + wide.shape[1]), jnp.bfloat16),
+        ],
+        scratch_shapes=[
+            pltpu.VMEM(hidden.shape[1:], jnp.bfloat16),
+            pltpu.SMEM(route.shape, jnp.int32),
+            pltpu.SMEM(counts.shape, jnp.int32),
+            pltpu.SemaphoreType.DMA((PIECES,)),
+            pltpu.SemaphoreType.DMA((3,)),
+        ],
+        compiler_params=PARAMS,
+        cost_estimate=SMALL,
+    )(*in_hbm((route, counts, inputs, hidden)), held(columns), held(wide))
+
+
+def join_kernel(some, own, received, *refs):
     chips = own.shape[0]
-    for i, some in enumerate(cuts):
-        for k in range(chips):
-            out = outs[i * chips + k]
-            total = own[k, some].astype(jnp.float32) + received[k, some].astype(jnp.float32)
-            out[...] = total.astype(out.dtype)
-
-
-def joined(own, received, cuts):
-    chips, _, columns = own.shape
-    outs = []
-    for some in cuts:
-        shape = (some.stop - some.start, columns)
-        outs += [pltpu.VMEM(shape, jnp.float32)] + [pltpu.VMEM(shape, jnp.bfloat16)] * (chips - 1)
-    flat = pl.pallas_call(
-        functools.partial(join_kernel, cuts),
-        in_specs=[IN_VMEM, IN_VMEM],
+    for k, out in enumerate(refs[-chips:]):
+        total = own[k, some].astype(jnp.float32) + received[k].astype(jnp.float32)
+        out[...] = total.astype(out.dtype)
+
+
+def joined(own, received, some, passed):
+    chips, rows, columns = received.shape
+    outs = [pltpu.VMEM(x.shape, x.dtype) for x in passed]
+    outs += [pltpu.VMEM((rows, columns), jnp.float32)]
+    outs += [pltpu.VMEM((rows, columns), jnp.bfloat16)] * (chips - 1)
+    return pl.pallas_call(
+        functools.partial(join_kernel, some),
+        in_specs=[IN_VMEM] * (2 + len(passed)),
         out_specs=[IN_VMEM] * len(outs),
         out_shape=outs,
+        input_output_aliases={2 + i: i for i in range(len(passed))},
         compiler_params=PARAMS,
         cost_estimate=SMALL,
-    )(held(own), held(received))
-    return [flat[i * chips : (i + 1) * chips] for i in range(len(cuts))]
-
-
-def pair_kernel(count, messages, inputs, ahead, other, *refs):
+    )(*map(held, (own, received, *passed)))
+
+
+def pair_kernel(count, messages, ahead, other, *refs):
     kept, *sent = refs[count:]
-    share = kept.shape[0]
-    span = ahead.shape[1] - kept.shape[1]
-    me = lax.axis_index("dp")
-    for k in range(span // share):
-        begin = pl.multiple_of((lax.bitwise_xor(me // 2, k) * 2 + me % 2) * share, share)
-        total = contracted(inputs[0, :, pl.ds(begin, share)], ahead[:, span:])
-        total = total + contracted(other[:, k * share : (k + 1) * share], other[:, span:])
+    share, columns = kept.shape
+    model = ahead.shape[1] - columns
+    for k in range(1 + max(place for place, _ in messages)):
+        place = owner_columns(k, False, share)
+        total = contracted(ahead[:, place], ahead[:, model:])
+        total = total + contracted(other[:, place], other[:, model:])
         if k == 0:
             kept[...] = total
-        for (place, some), out in zip(messages, sent):
-            if place == k:
+        for (chip, some), out in zip(messages, sent):
+            if chip == k:
                 out[...] = total[some].astype(out.dtype)
 
 
-def paired(inputs, ahead, other, after, share, chips, messages):
-    columns = ahead.shape[1] - chips * share
+def paired(ahead, other, after, share, columns, messages):
     outs = [pltpu.VMEM((share, columns), jnp.float32)]
     outs += [pltpu.VMEM((some.stop - some.start, columns), jnp.bfloat16) for _, some in messages]
     return pl.pallas_call(
         functools.partial(pair_kernel, len(after), messages),
-        in_specs=[IN_VMEM] * 3 + [ANYWHERE] * len(after),
+        in_specs=[IN_VMEM] * 2 + [ANYWHERE] * len(after),
         out_specs=[IN_VMEM] * len(outs),
         out_shape=outs,
         compiler_params=PARAMS,
         cost_estimate=SMALL,
-    )(*map(held, (inputs, ahead, other)), *after)
+    )(held(ahead), held(other), *after)
 
 
 def total_kernel(count, kept, *refs):
@@ -297,52 +326,42 @@
 
 def fast_device(saved_inputs, hidden_grads, block_expert, live_counts, first_moment, second_moment):
     chips = lax.axis_size("dp") // 2
-    share, experts = first_moment.shape[1:3]
-    product = functools.partial(
-        products,
-        route=block_expert[0, 0],
-        counts=live_counts[0, 0],
-        inputs=saved_inputs[0, 0],
-        hidden=hidden_grads[0, 0],
-        share=share,
-        chips=chips,
-        experts=experts,
-    )
-
-    def to_owners(pieces, places, name):
+    share, experts, width = first_moment.shape[1:]
+    given = (block_expert[0, 0], live_counts[0, 0], saved_inputs[0, 0], hidden_grads[0, 0])
+    cuts = [slice(0, share // 2), slice(share // 2, share)]
+    places = range(1, chips)
+    messages = [(k, slice(0, share)) for k in places]
+
+    def to_owners(pieces, name):
         return [
             exchanged(piece, "dp", 2 * k, f"{name}_to_chip_{k}")
             for piece, k in zip(pieces, places)
         ]
 
-    cut, half = share * 4 // 8, share // 2
-    cuts = [slice(0, cut), slice(cut, share)]
-    halves = [slice(0, half), slice(half, share)]
-    places = range(1, chips)
-    messages = [(k, slice(0, share)) for k in places]
     with jax.named_scope("sibling_products"):
-        (sibling,) = product(True, [])
-    other = exchanged(sibling, "dp", 1, "sibling_exchange")
+        *sibling, columns, wide = sibling_products(*given, chips, experts, cuts)
+    others = [exchanged(part, "dp", 1, f"sibling_{i}") for i, part in enumerate(sibling)]
     with jax.named_scope("own_products"):
-        own, ahead = product(False, [sibling])
+        own, ahead = own_products(*given, columns, wide, share, chips, experts)
+    parts = []
+    for i, (other, some) in enumerate(zip(others, cuts)):
+        with jax.named_scope(f"join_{i}"):
+            if i == 0:
+                ahead, kept, *sent = joined(own, other, some, [ahead])
+            else:
+                kept, *sent = joined(own, other, some, [])
+        parts.append((kept, to_owners(sent, f"one_part_{i}")))
     other_ahead = exchanged(ahead, "dp", 1, "operand_exchange")
-    with jax.named_scope("join"):
-        pieces = joined(own, other, cuts)
-    parts = [
-        (kept, to_owners(sent, places, f"one_part_{i}")) for i, (kept, *sent) in enumerate(pieces)
-    ]
     with jax.named_scope("pair"):
         kept_zero, *sent_zero = paired(
-            saved_inputs[0, 0], ahead, other_ahead, [parts[0][1][1]], share, chips, messages
+            ahead, other_ahead, [parts[0][1][1]], share, experts * width, messages
         )
-    received_zero = to_owners(sent_zero, [k for k, _ in messages], "zero")
-    with jax.named_scope("total_0"):
-        first_total = totalled(*parts[0], [kept_zero], jnp.bfloat16)
-    partners = [mirrored(first_total, "mirror_0")]
-    for i, (kept, received) in enumerate(parts[1:]):
-        with jax.named_scope(f"total_{i + 1}"):
-            total = totalled(kept, received, [kept_zero], jnp.bfloat16, LARGE)
-        partners.append(mirrored(total, f"mirror_{i + 1}"))
+    received_zero = to_owners(sent_zero, "zero")
+    partners = []
+    for i, (kept, received) in enumerate(parts):
+        with jax.named_scope(f"total_{i}"):
+            total = totalled(kept, received, [kept_zero], jnp.bfloat16, LARGE if i else SMALL)
+        partners.append(mirrored(total, f"mirror_{i}"))
     with jax.named_scope("update"):
         outs = updated(
             kept_zero, received_zero, partners, first_moment[0], second_moment[0], cuts, messages

time: 36.2 us -> 35.6 us (0.983)
  Pallas kernels: 8.19 us -> 7.42 us
  starting transfers between devices: 19.1 us -> 19.5 us
    ppermute x11 -> x12, waiting for transfers between devices: 3.26 us -> 2.41 us  [exchanged(): lax.ppermute(value, axis, [(source, source ^ mask) for source in range(co...]
    pallas_call x3 -> x4, Pallas kernels: 5.06 us -> 4.28 us  [the longest x1 2.24 us: sibling_products(): pl.pallas_call(functools.partial(sibling_kernel, experts, cuts), in_specs...]
    ppermute x2, waiting for transfers between devices: 4.79 us -> 5.44 us  [mirrored(): return lax.ppermute(value, 'section', pairs)]
    ppermute x11 -> x12, starting transfers between devices: 13.8 us -> 14.2 us  [exchanged(): lax.ppermute(value, axis, [(source, source ^ mask) for source in range(co...]
  transfers between devices with their start and end apart: 13 -> 14, of which waited for: 4 -> 4; matrix products, arithmetic and copies ran while one was open for 0% -> 0% of each run, Pallas kernels for 12% -> 9%
where the time goes in v6:
time: 35.6 us; the launch traced here: 35.5 us
  starting transfers between devices  19.5 us (55%)
  waiting for transfers between devices  7.85 us (22%)
  Pallas kernels  7.42 us (21%)
  between operations  0.7 us (2%)
    ppermute x12, starting transfers between devices, exchanged(): lax.ppermute(value, axis, [(source, source ^ mask) for source in range(co...  14.2 us
    ppermute x2, waiting for transfers between devices, mirrored(): return lax.ppermute(value, 'section', pairs)  5.44 us
    ppermute x2, starting transfers between devices, mirrored(): return lax.ppermute(value, 'section', pairs)  5.24 us
    ppermute x12, waiting for transfers between devices, exchanged(): lax.ppermute(value, axis, [(source, source ^ mask) for source in range(co...  2.41 us
    pallas_call x1, Pallas kernels, sibling_products(): pl.pallas_call(functools.partial(sibling_kernel, experts, cuts), in_specs...  2.24 us
    pallas_call x1, Pallas kernels, own_products(): pl.pallas_call(functools.partial(own_kernel, experts), in_specs=[ANYWHERE...  1.8 us
    pallas_call x1, Pallas kernels, updated(): pl.pallas_call(functools.partial(update_kernel, first.shape[1], cuts, mes...  1.74 us
    pallas_call x1, Pallas kernels, paired(): pl.pallas_call(functools.partial(pair_kernel, len(after), messages), in_s...  1.28 us
  transfers between devices with their start and end apart: 14, of which 4 were waited for; matrix products, arithmetic and copies ran while one was open for 0% of the time, Pallas kernels for 9%

profile of v6, /device:TPU:0, one launch (start us, length us, event | category | flops | bytes accessed | tf_op | source)
XLA Modules:
  0.0 35.5 jit_solution(4250924782439892203)
XLA Ops:
  0.6 2.2 %sibling_products.1 = (bf16[4,128,512]{2,1,0:T(8,128)(2,1)S(1)}, bf16[4,128,512]{2,1,0:T(8,128)(2,1)S(1)}, bf16[384,2048]{1,0:T(8,128)(2,1)S(1)}, bf16[384,512]{1,0:T(8,128)(2,1)S(1)}) custom-call(s32[2,3]{1,0:T(2,128)} %bitcast.40, s32[2,2]{1,0:T(2,128)} %bitcast.42, bf16[2,384,2048]{2,1,0:T(8,128)(2,1)} %bitcast.36, bf16[2,384,256]{2,1,0:T(8,128)(2,1)} %bitcast.38), custom_call_target="tpu_custom_call" | custom-call | flops 1 | bytes 1 | tf_op jit(solution)/shard_map/sibling_products/pallas_call | solution.py:122
  2.9 0.5 %collective-permute-start = (bf16[4,128,512]{2,1,0:T(8,128)(2,1)S(1)}, bf16[4,128,512]{2,1,0:T(8,128)(2,1)S(1)}, u32[]{:S(2)}, u32[]{:S(2)}) collective-permute-start(bf16[4,128,512]{2,1,0:T(8,128)(2,1)S(1)} %get-tuple-element.30), channel_id=1, source_target_pairs={{0,4},{4,0},{8,12},{12,8},{16,20},{20,16},{24,28},{28,24},{1,5},{5... | collective-permute-start | bytes 1572872 | tf_op jit(solution)/shard_map/sibling_0/ppermute | solution.py:22
  3.4 1.8 %own_products.1 = (bf16[4,256,512]{2,1,0:T(8,128)(2,1)S(1)}, bf16[384,2560]{1,0:T(8,128)(2,1)S(1)}) custom-call(s32[2,3]{1,0:T(2,128)} %bitcast.41, s32[2,2]{1,0:T(2,128)} %bitcast.43, bf16[2,384,2048]{2,1,0:T(8,128)(2,1)} %bitcast.37, bf16[2,384,256]{2,1,0:T(8,128)(2,1)} %bitcast.39, bf16[384,2048]{1,0:T(8,128)(2,1)S(1)} %get-tuple-element.27.columns, ...), custom_call_target="tpu_custom_call" | custom-call | flops 1 | bytes 1 | tf_op jit(solution)/shard_map/own_products/pallas_call | solution.py:160
  5.2 0.0 collective-permute-done.received
  5.2 0.1 join_0.1
  5.3 0.2 collective-permute-start.1
  5.5 0.4 %collective-permute-start.9 = (bf16[4,128,512]{2,1,0:T(8,128)(2,1)S(1)}, bf16[4,128,512]{2,1,0:T(8,128)(2,1)S(1)}, u32[]{:S(2)}, u32[]{:S(2)}) collective-permute-start(bf16[4,128,512]{2,1,0:T(8,128)(2,1)S(1)} %get-tuple-element.41), channel_id=1, source_target_pairs={{0,4},{4,0},{8,12},{12,8},{16,20},{20,16},{24,28},{28,24},{1,5},{5... | collective-permute-start | bytes 1572872 | tf_op jit(solution)/shard_map/sibling_1/ppermute | solution.py:22
  5.9 2.6 %collective-permute-start.2 = (bf16[128,512]{1,0:T(8,128)(2,1)S(1)}, bf16[128,512]{1,0:T(8,128)(2,1)S(1)}, u32[]{:S(2)}, u32[]{:S(2)}) collective-permute-start(bf16[128,512]{1,0:T(8,128)(2,1)S(1)} %get-tuple-element.33), channel_id=1, source_target_pairs={{0,16},{4,20},{8,24},{12,28},{16,0},{20,4},{24,8},{28,12},{1,17},{... | collective-permute-start | bytes 393224 | tf_op jit(solution)/shard_map/one_part_0_to_chip_2/ppermute | solution.py:22
  8.5 1.5 %collective-permute-start.6 = (bf16[128,512]{1,0:T(8,128)(2,1)S(1)}, bf16[128,512]{1,0:T(8,128)(2,1)S(1)}, u32[]{:S(2)}, u32[]{:S(2)}) collective-permute-start(bf16[128,512]{1,0:T(8,128)(2,1)S(1)} %get-tuple-element.39), channel_id=1, source_target_pairs={{0,8},{4,12},{8,0},{12,4},{16,24},{20,28},{24,16},{28,20},{1,9},{5... | collective-permute-start | bytes 393224 | tf_op jit(solution)/shard_map/one_part_0_to_chip_1/ppermute | solution.py:22
  10.0 0.0 collective-permute-start.7
  10.0 0.1 collective-permute-done.9.received
  10.1 0.1 join_1.1
  10.2 2.7 %collective-permute-start.10 = (bf16[128,512]{1,0:T(8,128)(2,1)S(1)}, bf16[128,512]{1,0:T(8,128)(2,1)S(1)}, u32[]{:S(2)}, u32[]{:S(2)}) collective-permute-start(bf16[128,512]{1,0:T(8,128)(2,1)S(1)} %get-tuple-element.43), channel_id=1, source_target_pairs={{0,8},{4,12},{8,0},{12,4},{16,24},{20,28},{24,16},{28,20},{1,9},{5... | collective-permute-start | bytes 393224 | tf_op jit(solution)/shard_map/one_part_1_to_chip_1/ppermute | solution.py:22
  13.0 0.0 collective-permute-done.2.refs_0_.refs_1_
  13.0 1.5 %collective-permute-start.11 = (bf16[128,512]{1,0:T(8,128)(2,1)S(1)}, bf16[128,512]{1,0:T(8,128)(2,1)S(1)}, u32[]{:S(2)}, u32[]{:S(2)}) collective-permute-start(bf16[128,512]{1,0:T(8,128)(2,1)S(1)} %get-tuple-element.44), channel_id=1, source_target_pairs={{0,16},{4,20},{8,24},{12,28},{16,0},{20,4},{24,8},{28,12},{1,17},{... | collective-permute-start | bytes 393224 | tf_op jit(solution)/shard_map/one_part_1_to_chip_2/ppermute | solution.py:22
  14.5 0.0 collective-permute-done.1.other
  14.5 1.3 %collective-permute-start.12 = (bf16[128,512]{1,0:T(8,128)(2,1)S(1)}, bf16[128,512]{1,0:T(8,128)(2,1)S(1)}, u32[]{:S(2)}, u32[]{:S(2)}) collective-permute-start(bf16[128,512]{1,0:T(8,128)(2,1)S(1)} %get-tuple-element.45), channel_id=1, source_target_pairs={{0,24},{4,28},{8,16},{12,20},{16,8},{20,12},{24,0},{28,4},{1,25},{... | collective-permute-start | bytes 393224 | tf_op jit(solution)/shard_map/one_part_1_to_chip_3/ppermute | solution.py:22
  15.8 1.3 %pair.1 = (f32[256,512]{1,0:T(8,128)S(1)}, bf16[256,512]{1,0:T(8,128)(2,1)S(1)}, bf16[256,512]{1,0:T(8,128)(2,1)S(1)}, bf16[256,512]{1,0:T(8,128)(2,1)S(1)}) custom-call(bf16[384,2560]{1,0:T(8,128)(2,1)S(1)} %get-tuple-element.32.ahead, bf16[384,2560]{1,0:T(8,128)(2,1)S(1)} %collective-permute-done.1.other, ...), custom_call_target="tpu_custom_call" | custom-call | flops 1 | bytes 1 | tf_op jit(solution)/shard_map/pair/pallas_call | solution.py:221
  17.1 0.0 collective-permute-done.6.refs_0_
  17.1 0.2 collective-permute-done.7.refs_2_
  17.3 0.1 total_0.1
  17.4 2.8 %collective-permute-start.8 = (bf16[128,512]{1,0:T(8,128)(2,1)S(1)}, bf16[128,512]{1,0:T(8,128)(2,1)S(1)}, u32[]{:S(2)}, u32[]{:S(2)}) collective-permute-start(bf16[128,512]{1,0:T(8,128)(2,1)S(1)} %total_0.1), channel_id=1, source_target_pairs={{0,2},{1,3},{2,0},{3,1},{4,6},{5,7},{6,4},{7,5},{8,10},{9,11},{10,... | collective-permute-start | bytes 393224 | tf_op jit(solution)/shard_map/mirror_0/ppermute | solution.py:29
  20.2 1.7 %collective-permute-start.3 = (bf16[256,512]{1,0:T(8,128)(2,1)S(1)}, bf16[256,512]{1,0:T(8,128)(2,1)S(1)}, u32[]{:S(2)}, u32[]{:S(2)}) collective-permute-start(bf16[256,512]{1,0:T(8,128)(2,1)S(1)} %get-tuple-element.35), channel_id=1, source_target_pairs={{0,8},{4,12},{8,0},{12,4},{16,24},{20,28},{24,16},{28,20},{1,9},{5... | collective-permute-start | bytes 786440 | tf_op jit(solution)/shard_map/zero_to_chip_1/ppermute | solution.py:22
  21.8 0.0 collective-permute-done.10.refs_0_
  21.8 1.5 %collective-permute-start.4 = (bf16[256,512]{1,0:T(8,128)(2,1)S(1)}, bf16[256,512]{1,0:T(8,128)(2,1)S(1)}, u32[]{:S(2)}, u32[]{:S(2)}) collective-permute-start(bf16[256,512]{1,0:T(8,128)(2,1)S(1)} %get-tuple-element.36), channel_id=1, source_target_pairs={{0,16},{4,20},{8,24},{12,28},{16,0},{20,4},{24,8},{28,12},{1,17},{... | collective-permute-start | bytes 786440 | tf_op jit(solution)/shard_map/zero_to_chip_2/ppermute | solution.py:22
  23.3 0.0 collective-permute-done.11.refs_1_
  23.4 0.3 collective-permute-start.5
  23.6 0.0 collective-permute-done.12.refs_2_
  23.7 0.0 copy-start
  23.7 0.0 copy-start.1
  23.7 0.1 total_1.1
  23.7 2.4 %collective-permute-start.13 = (bf16[128,512]{1,0:T(8,128)(2,1)S(1)}, bf16[128,512]{1,0:T(8,128)(2,1)S(1)}, u32[]{:S(2)}, u32[]{:S(2)}) collective-permute-start(bf16[128,512]{1,0:T(8,128)(2,1)S(1)} %total_1.1), channel_id=1, source_target_pairs={{0,2},{1,3},{2,0},{3,1},{4,6},{5,7},{6,4},{7,5},{8,10},{9,11},{10,... | collective-permute-start | bytes 393224 | tf_op jit(solution)/shard_map/mirror_1/ppermute | solution.py:29
  26.2 0.0 collective-permute-done.8.refs_3_
  26.2 5.4 %collective-permute-done.13.refs_4_ = bf16[128,512]{1,0:T(8,128)(2,1)S(1)} collective-permute-done((bf16[128,512]{1,0:T(8,128)(2,1)S(1)}, bf16[128,512]{1,0:T(8,128)(2,1)S(1)}, u32[]{:S(2)}, u32[]{:S(2)}) %collective-permute-start.13) | collective-permute-done | bytes 131104 | tf_op jit(solution)/shard_map/mirror_1/ppermute | solution.py:29
  31.6 0.0 collective-permute-done.3.refs_0_
  31.6 2.1 %collective-permute-done.4.refs_1_ = bf16[256,512]{1,0:T(8,128)(2,1)S(1)} collective-permute-done((bf16[256,512]{1,0:T(8,128)(2,1)S(1)}, bf16[256,512]{1,0:T(8,128)(2,1)S(1)}, u32[]{:S(2)}, u32[]{:S(2)}) %collective-permute-start.4) | collective-permute-done | bytes 262176 | tf_op jit(solution)/shard_map/zero_to_chip_2/ppermute | solution.py:22
  33.7 0.0 collective-permute-done.5.refs_2_
  33.7 0.0 copy-done
  33.7 0.0 copy-done.1
  33.7 1.7 %update.1 = (f32[1024,128]{1,0:T(8,128)}, f32[1024,128]{1,0:T(8,128)}, f32[1024,128]{1,0:T(8,128)}, f32[1024,128]{1,0:T(8,128)}) custom-call(f32[256,512]{1,0:T(8,128)S(1)} %get-tuple-element.34.refs_3_.kept, bf16[256,512]{1,0:T(8,128)(2,1)S(1)} %collective-permute-done.3.refs_0_, bf16[256,512]{1,0:T(8,128)(2,1)S(1)} %collective-permute-done.4.refs_1_, ...), custom_call_target="tpu_custom_call" | custom-call | flops 1 | bytes 1 | tf_op jit(solution)/shard_map/update/pallas_call | solution.py:315
Async XLA Ops:
  2.9 2.3 %collective-permute-start = (bf16[4,128,512]{2,1,0:T(8,128)(2,1)S(1)}, bf16[4,128,512]{2,1,0:T(8,128)(2,1)S(1)}, u32[]{:S(2)}, u32[]{:S(2)}) collective-permute-start(bf16[4,128,512]{2,1,0:T(8,128)(2,1)S(1)} %get-tuple-element.30), channel_id=1, source_target_pairs={{0,4},{4,0},{8,12},{12,8},{16,20},{20,16},{24,28},{28,24},{1,5},{5... | collective-permute-start | bytes 1572872 | tf_op jit(solution)/shard_map/sibling_0/ppermute | solution.py:22
  5.3 9.2 %collective-permute-start.1 = (bf16[384,2560]{1,0:T(8,128)(2,1)S(1)}, bf16[384,2560]{1,0:T(8,128)(2,1)S(1)}, u32[]{:S(2)}, u32[]{:S(2)}) collective-permute-start(bf16[384,2560]{1,0:T(8,128)(2,1)S(1)} %get-tuple-element.32.ahead), channel_id=1, source_target_pairs={{0,4},{4,0},{8,12},{12,8},{16,20},{20,16},{24,28},{28,24},{1,5},{5... | collective-permute-start | bytes 5898248 | tf_op jit(solution)/shard_map/operand_exchange/ppermute | solution.py:22
  5.5 4.6 %collective-permute-start.9 = (bf16[4,128,512]{2,1,0:T(8,128)(2,1)S(1)}, bf16[4,128,512]{2,1,0:T(8,128)(2,1)S(1)}, u32[]{:S(2)}, u32[]{:S(2)}) collective-permute-start(bf16[4,128,512]{2,1,0:T(8,128)(2,1)S(1)} %get-tuple-element.41), channel_id=1, source_target_pairs={{0,4},{4,0},{8,12},{12,8},{16,20},{20,16},{24,28},{28,24},{1,5},{5... | collective-permute-start | bytes 1572872 | tf_op jit(solution)/shard_map/sibling_1/ppermute | solution.py:22
  5.9 7.1 %collective-permute-start.2 = (bf16[128,512]{1,0:T(8,128)(2,1)S(1)}, bf16[128,512]{1,0:T(8,128)(2,1)S(1)}, u32[]{:S(2)}, u32[]{:S(2)}) collective-permute-start(bf16[128,512]{1,0:T(8,128)(2,1)S(1)} %get-tuple-element.33), channel_id=1, source_target_pairs={{0,16},{4,20},{8,24},{12,28},{16,0},{20,4},{24,8},{28,12},{1,17},{... | collective-permute-start | bytes 393224 | tf_op jit(solution)/shard_map/one_part_0_to_chip_2/ppermute | solution.py:22
  8.5 8.6 %collective-permute-start.6 = (bf16[128,512]{1,0:T(8,128)(2,1)S(1)}, bf16[128,512]{1,0:T(8,128)(2,1)S(1)}, u32[]{:S(2)}, u32[]{:S(2)}) collective-permute-start(bf16[128,512]{1,0:T(8,128)(2,1)S(1)} %get-tuple-element.39), channel_id=1, source_target_pairs={{0,8},{4,12},{8,0},{12,4},{16,24},{20,28},{24,16},{28,20},{1,9},{5... | collective-permute-start | bytes 393224 | tf_op jit(solution)/shard_map/one_part_0_to_chip_1/ppermute | solution.py:22
  10.0 7.3 %collective-permute-start.7 = (bf16[128,512]{1,0:T(8,128)(2,1)S(1)}, bf16[128,512]{1,0:T(8,128)(2,1)S(1)}, u32[]{:S(2)}, u32[]{:S(2)}) collective-permute-start(bf16[128,512]{1,0:T(8,128)(2,1)S(1)} %get-tuple-element.40), channel_id=1, source_target_pairs={{0,24},{4,28},{8,16},{12,20},{16,8},{20,12},{24,0},{28,4},{1,25},{... | collective-permute-start | bytes 393224 | tf_op jit(solution)/shard_map/one_part_0_to_chip_3/ppermute | solution.py:22
  10.2 11.6 %collective-permute-start.10 = (bf16[128,512]{1,0:T(8,128)(2,1)S(1)}, bf16[128,512]{1,0:T(8,128)(2,1)S(1)}, u32[]{:S(2)}, u32[]{:S(2)}) collective-permute-start(bf16[128,512]{1,0:T(8,128)(2,1)S(1)} %get-tuple-element.43), channel_id=1, source_target_pairs={{0,8},{4,12},{8,0},{12,4},{16,24},{20,28},{24,16},{28,20},{1,9},{5... | collective-permute-start | bytes 393224 | tf_op jit(solution)/shard_map/one_part_1_to_chip_1/ppermute | solution.py:22
  13.0 10.4 %collective-permute-start.11 = (bf16[128,512]{1,0:T(8,128)(2,1)S(1)}, bf16[128,512]{1,0:T(8,128)(2,1)S(1)}, u32[]{:S(2)}, u32[]{:S(2)}) collective-permute-start(bf16[128,512]{1,0:T(8,128)(2,1)S(1)} %get-tuple-element.44), channel_id=1, source_target_pairs={{0,16},{4,20},{8,24},{12,28},{16,0},{20,4},{24,8},{28,12},{1,17},{... | collective-permute-start | bytes 393224 | tf_op jit(solution)/shard_map/one_part_1_to_chip_2/ppermute | solution.py:22
  14.5 9.2 %collective-permute-start.12 = (bf16[128,512]{1,0:T(8,128)(2,1)S(1)}, bf16[128,512]{1,0:T(8,128)(2,1)S(1)}, u32[]{:S(2)}, u32[]{:S(2)}) collective-permute-start(bf16[128,512]{1,0:T(8,128)(2,1)S(1)} %get-tuple-element.45), channel_id=1, source_target_pairs={{0,24},{4,28},{8,16},{12,20},{16,8},{20,12},{24,0},{28,4},{1,25},{... | collective-permute-start | bytes 393224 | tf_op jit(solution)/shard_map/one_part_1_to_chip_3/ppermute | solution.py:22
  17.4 8.8 %collective-permute-start.8 = (bf16[128,512]{1,0:T(8,128)(2,1)S(1)}, bf16[128,512]{1,0:T(8,128)(2,1)S(1)}, u32[]{:S(2)}, u32[]{:S(2)}) collective-permute-start(bf16[128,512]{1,0:T(8,128)(2,1)S(1)} %total_0.1), channel_id=1, source_target_pairs={{0,2},{1,3},{2,0},{3,1},{4,6},{5,7},{6,4},{7,5},{8,10},{9,11},{10,... | collective-permute-start | bytes 393224 | tf_op jit(solution)/shard_map/mirror_0/ppermute | solution.py:29
  20.2 11.5 %collective-permute-start.3 = (bf16[256,512]{1,0:T(8,128)(2,1)S(1)}, bf16[256,512]{1,0:T(8,128)(2,1)S(1)}, u32[]{:S(2)}, u32[]{:S(2)}) collective-permute-start(bf16[256,512]{1,0:T(8,128)(2,1)S(1)} %get-tuple-element.35), channel_id=1, source_target_pairs={{0,8},{4,12},{8,0},{12,4},{16,24},{20,28},{24,16},{28,20},{1,9},{5... | collective-permute-start | bytes 786440 | tf_op jit(solution)/shard_map/zero_to_chip_1/ppermute | solution.py:22
  21.8 11.9 %collective-permute-start.4 = (bf16[256,512]{1,0:T(8,128)(2,1)S(1)}, bf16[256,512]{1,0:T(8,128)(2,1)S(1)}, u32[]{:S(2)}, u32[]{:S(2)}) collective-permute-start(bf16[256,512]{1,0:T(8,128)(2,1)S(1)} %get-tuple-element.36), channel_id=1, source_target_pairs={{0,16},{4,20},{8,24},{12,28},{16,0},{20,4},{24,8},{28,12},{1,17},{... | collective-permute-start | bytes 786440 | tf_op jit(solution)/shard_map/zero_to_chip_2/ppermute | solution.py:22
  23.4 10.4 %collective-permute-start.5 = (bf16[256,512]{1,0:T(8,128)(2,1)S(1)}, bf16[256,512]{1,0:T(8,128)(2,1)S(1)}, u32[]{:S(2)}, u32[]{:S(2)}) collective-permute-start(bf16[256,512]{1,0:T(8,128)(2,1)S(1)} %get-tuple-element.37), channel_id=1, source_target_pairs={{0,24},{4,28},{8,16},{12,20},{16,8},{20,12},{24,0},{28,4},{1,25},{... | collective-permute-start | bytes 786440 | tf_op jit(solution)/shard_map/zero_to_chip_3/ppermute | solution.py:22
  23.7 10.1 %copy-start = (f32[1,256,2,256]{3,2,1,0:T(2,128)S(1)}, f32[1,256,2,256]{3,2,1,0:T(2,128)}, u32[]{:S(2)}) copy-start(f32[1,256,2,256]{3,2,1,0:T(2,128)} %param.10) | copy-start | bytes 1572868
  23.7 10.1 %copy-start.1 = (f32[1,256,2,256]{3,2,1,0:T(2,128)S(1)}, f32[1,256,2,256]{3,2,1,0:T(2,128)}, u32[]{:S(2)}) copy-start(f32[1,256,2,256]{3,2,1,0:T(2,128)} %param.11) | copy-start | bytes 1572868
  23.7 7.9 %collective-permute-start.13 = (bf16[128,512]{1,0:T(8,128)(2,1)S(1)}, bf16[128,512]{1,0:T(8,128)(2,1)S(1)}, u32[]{:S(2)}, u32[]{:S(2)}) collective-permute-start(bf16[128,512]{1,0:T(8,128)(2,1)S(1)} %total_1.1), channel_id=1, source_target_pairs={{0,2},{1,3},{2,0},{3,1},{4,6},{5,7},{6,4},{7,5},{8,10},{9,11},{10,... | collective-permute-start | bytes 393224 | tf_op jit(solution)/shard_map/mirror_1/ppermute | solution.py:29

commit v7 on v6

--- a/solution.py
+++ b/solution.py
@@ -16,10 +16,16 @@
 LANES = 128
 
 
-def exchanged(value, axis, mask, name):
+def neighbour(piece, core, chips, crossed):
+    if crossed and piece in (1, 2) and chips > 2:
+        return 1 + core if piece == 1 else 2 - core
+    return piece
+
+
+def exchanged(value, axis, mask_of, name):
     count = lax.axis_size(axis)
     with jax.named_scope(name):
-        return lax.ppermute(value, axis, [(source, source ^ mask) for source in range(count)])
+        return lax.ppermute(value, axis, [(i, i ^ mask_of(i)) for i in range(count)])
 
 
 def mirrored(value, name="mirror"):
@@ -85,10 +91,10 @@
     )
 
 
-def owner_columns(k, sibling, share):
+def owner_columns(chip, sibling, share):
     me = lax.axis_index("dp")
     core = 1 - me % 2 if sibling else me % 2
-    begin = (lax.bitwise_xor(me // 2, k) * 2 + core) * share
+    begin = (lax.bitwise_xor(me // 2, chip) * 2 + core) * share
     return pl.ds(pl.multiple_of(begin, share), share)
 
 
@@ -145,9 +151,13 @@
     column_copies = row_copies(inputs.at[0], ahead.at[:, :model], column_sems)
     for copy in copies + column_copies:
         copy.start()
-    for k in range(chips):
+
+    def step(k, carry):
         product = contracted(columns[:, owner_columns(k, False, share)], wide[...])
         out[k] = product.astype(out.dtype)
+        return carry
+
+    lax.fori_loop(0, chips, step, 0)
     for copy in copies:
         copy.wait()
     expand_hidden(route_now, counts_now, 0, rows, ahead.at[:, model:], route.shape[1], experts)
@@ -177,20 +187,22 @@
     )(*in_hbm((route, counts, inputs, hidden)), held(columns), held(wide))
 
 
-def join_kernel(some, own, received, *refs):
+def join_kernel(some, crossed, own, received, *refs):
     chips = own.shape[0]
-    for k, out in enumerate(refs[-chips:]):
+    core = lax.axis_index("dp") % 2
+    for piece, out in enumerate(refs[-chips:]):
+        k = neighbour(piece, core, chips, crossed)
         total = own[k, some].astype(jnp.float32) + received[k].astype(jnp.float32)
         out[...] = total.astype(out.dtype)
 
 
-def joined(own, received, some, passed):
+def joined(own, received, some, passed, crossed):
     chips, rows, columns = received.shape
     outs = [pltpu.VMEM(x.shape, x.dtype) for x in passed]
     outs += [pltpu.VMEM((rows, columns), jnp.float32)]
     outs += [pltpu.VMEM((rows, columns), jnp.bfloat16)] * (chips - 1)
     return pl.pallas_call(
-        functools.partial(join_kernel, some),
+        functools.partial(join_kernel, some, crossed),
         in_specs=[IN_VMEM] * (2 + len(passed)),
         out_specs=[IN_VMEM] * len(outs),
         out_shape=outs,
@@ -204,8 +216,10 @@
     kept, *sent = refs[count:]
     share, columns = kept.shape
     model = ahead.shape[1] - columns
-    for k in range(1 + max(place for place, _ in messages)):
-        place = owner_columns(k, False, share)
+    chips = 1 + max(place for place, _ in messages)
+    for k in range(chips):
+        chip = neighbour(k, lax.axis_index("dp") % 2, chips, True)
+        place = owner_columns(chip, False, share)
         total = contracted(ahead[:, place], ahead[:, model:])
         total = total + contracted(other[:, place], other[:, model:])
         if k == 0:
@@ -332,31 +346,32 @@
     places = range(1, chips)
     messages = [(k, slice(0, share)) for k in places]
 
-    def to_owners(pieces, name):
-        return [
-            exchanged(piece, "dp", 2 * k, f"{name}_to_chip_{k}")
-            for piece, k in zip(pieces, places)
-        ]
+    def to_owners(pieces, name, crossed):
+        sent = []
+        for piece, k in zip(pieces, places):
+            chip = functools.partial(neighbour, k, chips=chips, crossed=crossed)
+            sent.append(exchanged(piece, "dp", lambda i: 2 * chip(i % 2), f"{name}_to_chip_{k}"))
+        return sent
 
     with jax.named_scope("sibling_products"):
         *sibling, columns, wide = sibling_products(*given, chips, experts, cuts)
-    others = [exchanged(part, "dp", 1, f"sibling_{i}") for i, part in enumerate(sibling)]
+    others = [exchanged(part, "dp", lambda i: 1, f"sibling_{i}") for i, part in enumerate(sibling)]
     with jax.named_scope("own_products"):
         own, ahead = own_products(*given, columns, wide, share, chips, experts)
     parts = []
     for i, (other, some) in enumerate(zip(others, cuts)):
         with jax.named_scope(f"join_{i}"):
             if i == 0:
-                ahead, kept, *sent = joined(own, other, some, [ahead])
+                ahead, kept, *sent = joined(own, other, some, [ahead], True)
             else:
-                kept, *sent = joined(own, other, some, [])
-        parts.append((kept, to_owners(sent, f"one_part_{i}")))
-    other_ahead = exchanged(ahead, "dp", 1, "operand_exchange")
+                kept, *sent = joined(own, other, some, [], False)
+        parts.append((kept, to_owners(sent, f"one_part_{i}", False if i else True)))
+    other_ahead = exchanged(ahead, "dp", lambda i: 1, "operand_exchange")
     with jax.named_scope("pair"):
         kept_zero, *sent_zero = paired(
             ahead, other_ahead, [parts[0][1][1]], share, experts * width, messages
         )
-    received_zero = to_owners(sent_zero, "zero")
+    received_zero = to_owners(sent_zero, "zero", True)
     partners = []
     for i, (kept, received) in enumerate(parts):
         with jax.named_scope(f"total_{i}"):

time: 35.6 us -> 35.1 us (0.986)
  waiting for transfers between devices: 7.85 us -> 4.73 us
  starting transfers between devices: 19.5 us -> 22.3 us
    ppermute x12, starting transfers between devices: 14.2 us -> 16.5 us  [exchanged(): lax.ppermute(value, axis, [(i, i ^ mask_of(i)) for i in range(count)])]
    ppermute x12, waiting for transfers between devices: 2.41 us -> 0.38 us  [exchanged(): lax.ppermute(value, axis, [(i, i ^ mask_of(i)) for i in range(count)])]
    ppermute x2, waiting for transfers between devices: 5.44 us -> 4.35 us  [mirrored(): return lax.ppermute(value, 'section', pairs)]
    ppermute x2, starting transfers between devices: 5.24 us -> 5.85 us  [mirrored(): return lax.ppermute(value, 'section', pairs)]
  transfers between devices with their start and end apart: 14 -> 14, of which waited for: 4 -> 2; matrix products, arithmetic and copies ran while one was open for 0% -> 0% of each run, Pallas kernels for 9% -> 9%
where the time goes in v7:
time: 35.1 us; the launch traced here: 35 us
  starting transfers between devices  22.3 us (64%)
  Pallas kernels  7.16 us (20%)
  waiting for transfers between devices  4.73 us (13%)
  between operations  0.71 us (2%)
    ppermute x12, starting transfers between devices, exchanged(): lax.ppermute(value, axis, [(i, i ^ mask_of(i)) for i in range(count)])  16.5 us
    ppermute x2, starting transfers between devices, mirrored(): return lax.ppermute(value, 'section', pairs)  5.85 us
    ppermute x2, waiting for transfers between devices, mirrored(): return lax.ppermute(value, 'section', pairs)  4.35 us
    pallas_call x1, Pallas kernels, sibling_products(): pl.pallas_call(functools.partial(sibling_kernel, experts, cuts), in_specs...  2.24 us
    pallas_call x1, Pallas kernels, updated(): pl.pallas_call(functools.partial(update_kernel, first.shape[1], cuts, mes...  1.74 us
    pallas_call x1, Pallas kernels, own_products(): pl.pallas_call(functools.partial(own_kernel, experts), in_specs=[ANYWHERE...  1.54 us
    pallas_call x1, Pallas kernels, paired(): pl.pallas_call(functools.partial(pair_kernel, len(after), messages), in_s...  1.28 us
  transfers between devices with their start and end apart: 14, of which 2 were waited for; matrix products, arithmetic and copies ran while one was open for 0% of the time, Pallas kernels for 9%

profile of v7, /device:TPU:0, one launch (start us, length us, event | category | flops | bytes accessed | tf_op | source)
XLA Modules:
  0.0 35.0 jit_solution(1907425799210746713)
XLA Ops:
  0.6 2.2 %sibling_products.1 = (bf16[4,128,512]{2,1,0:T(8,128)(2,1)S(1)}, bf16[4,128,512]{2,1,0:T(8,128)(2,1)S(1)}, bf16[384,2048]{1,0:T(8,128)(2,1)S(1)}, bf16[384,512]{1,0:T(8,128)(2,1)S(1)}) custom-call(s32[2,3]{1,0:T(2,128)} %bitcast.40, s32[2,2]{1,0:T(2,128)} %bitcast.42, bf16[2,384,2048]{2,1,0:T(8,128)(2,1)} %bitcast.36, bf16[2,384,256]{2,1,0:T(8,128)(2,1)} %bitcast.38), custom_call_target="tpu_custom_call" | custom-call | flops 1 | bytes 1 | tf_op jit(solution)/shard_map/sibling_products/pallas_call | solution.py:128
  2.9 0.5 %collective-permute-start = (bf16[4,128,512]{2,1,0:T(8,128)(2,1)S(1)}, bf16[4,128,512]{2,1,0:T(8,128)(2,1)S(1)}, u32[]{:S(2)}, u32[]{:S(2)}) collective-permute-start(bf16[4,128,512]{2,1,0:T(8,128)(2,1)S(1)} %get-tuple-element.30), channel_id=1, source_target_pairs={{0,4},{4,0},{8,12},{12,8},{16,20},{20,16},{24,28},{28,24},{1,5},{5... | collective-permute-start | bytes 1572872 | tf_op jit(solution)/shard_map/sibling_0/ppermute | solution.py:28
  3.4 1.5 %own_products.1 = (bf16[4,256,512]{2,1,0:T(8,128)(2,1)S(1)}, bf16[384,2560]{1,0:T(8,128)(2,1)S(1)}) custom-call(s32[2,3]{1,0:T(2,128)} %bitcast.41, s32[2,2]{1,0:T(2,128)} %bitcast.43, bf16[2,384,2048]{2,1,0:T(8,128)(2,1)} %bitcast.37, bf16[2,384,256]{2,1,0:T(8,128)(2,1)} %bitcast.39, bf16[384,2048]{1,0:T(8,128)(2,1)S(1)} %get-tuple-element.27.columns, ...), custom_call_target="tpu_custom_call" | custom-call | flops 1 | bytes 1 | tf_op jit(solution)/shard_map/own_products/pallas_call | solution.py:170
  4.9 0.0 collective-permute-done.received
  4.9 0.1 join_0.1
  5.1 0.4 %collective-permute-start.1 = (bf16[384,2560]{1,0:T(8,128)(2,1)S(1)}, bf16[384,2560]{1,0:T(8,128)(2,1)S(1)}, u32[]{:S(2)}, u32[]{:S(2)}) collective-permute-start(bf16[384,2560]{1,0:T(8,128)(2,1)S(1)} %get-tuple-element.32.ahead), channel_id=1, source_target_pairs={{0,4},{4,0},{8,12},{12,8},{16,20},{20,16},{24,28},{28,24},{1,5},{5... | collective-permute-start | bytes 5898248 | tf_op jit(solution)/shard_map/operand_exchange/ppermute | solution.py:28
  5.5 0.2 collective-permute-start.9
  5.7 2.9 %collective-permute-start.2 = (bf16[128,512]{1,0:T(8,128)(2,1)S(1)}, bf16[128,512]{1,0:T(8,128)(2,1)S(1)}, u32[]{:S(2)}, u32[]{:S(2)}) collective-permute-start(bf16[128,512]{1,0:T(8,128)(2,1)S(1)} %get-tuple-element.33), channel_id=1, source_target_pairs={{0,16},{4,12},{8,24},{12,4},{16,0},{20,28},{24,8},{28,20},{1,17},{... | collective-permute-start | bytes 393224 | tf_op jit(solution)/shard_map/one_part_0_to_chip_2/ppermute | solution.py:28
  8.5 1.5 %collective-permute-start.6 = (bf16[128,512]{1,0:T(8,128)(2,1)S(1)}, bf16[128,512]{1,0:T(8,128)(2,1)S(1)}, u32[]{:S(2)}, u32[]{:S(2)}) collective-permute-start(bf16[128,512]{1,0:T(8,128)(2,1)S(1)} %get-tuple-element.39), channel_id=1, source_target_pairs={{0,8},{4,20},{8,0},{12,28},{16,24},{20,4},{24,16},{28,12},{1,9},{5... | collective-permute-start | bytes 393224 | tf_op jit(solution)/shard_map/one_part_0_to_chip_1/ppermute | solution.py:28
  10.0 0.0 collective-permute-start.7
  10.0 0.0 collective-permute-done.9.received
  10.0 0.1 join_1.1
  10.1 2.7 %collective-permute-start.10 = (bf16[128,512]{1,0:T(8,128)(2,1)S(1)}, bf16[128,512]{1,0:T(8,128)(2,1)S(1)}, u32[]{:S(2)}, u32[]{:S(2)}) collective-permute-start(bf16[128,512]{1,0:T(8,128)(2,1)S(1)} %get-tuple-element.43), channel_id=1, source_target_pairs={{0,8},{4,12},{8,0},{12,4},{16,24},{20,28},{24,16},{28,20},{1,9},{5... | collective-permute-start | bytes 393224 | tf_op jit(solution)/shard_map/one_part_1_to_chip_1/ppermute | solution.py:28
  12.9 0.0 collective-permute-done.2.refs_0_.refs_1_
  12.9 2.6 %collective-permute-start.11 = (bf16[128,512]{1,0:T(8,128)(2,1)S(1)}, bf16[128,512]{1,0:T(8,128)(2,1)S(1)}, u32[]{:S(2)}, u32[]{:S(2)}) collective-permute-start(bf16[128,512]{1,0:T(8,128)(2,1)S(1)} %get-tuple-element.44), channel_id=1, source_target_pairs={{0,16},{4,20},{8,24},{12,28},{16,0},{20,4},{24,8},{28,12},{1,17},{... | collective-permute-start | bytes 393224 | tf_op jit(solution)/shard_map/one_part_1_to_chip_2/ppermute | solution.py:28
  15.5 0.0 collective-permute-done.1.other
  15.5 1.9 %collective-permute-start.12 = (bf16[128,512]{1,0:T(8,128)(2,1)S(1)}, bf16[128,512]{1,0:T(8,128)(2,1)S(1)}, u32[]{:S(2)}, u32[]{:S(2)}) collective-permute-start(bf16[128,512]{1,0:T(8,128)(2,1)S(1)} %get-tuple-element.45), channel_id=1, source_target_pairs={{0,24},{4,28},{8,16},{12,20},{16,8},{20,12},{24,0},{28,4},{1,25},{... | collective-permute-start | bytes 393224 | tf_op jit(solution)/shard_map/one_part_1_to_chip_3/ppermute | solution.py:28
  17.4 1.3 %pair.1 = (f32[256,512]{1,0:T(8,128)S(1)}, bf16[256,512]{1,0:T(8,128)(2,1)S(1)}, bf16[256,512]{1,0:T(8,128)(2,1)S(1)}, bf16[256,512]{1,0:T(8,128)(2,1)S(1)}) custom-call(bf16[384,2560]{1,0:T(8,128)(2,1)S(1)} %get-tuple-element.32.ahead, bf16[384,2560]{1,0:T(8,128)(2,1)S(1)} %collective-permute-done.1.other, ...), custom_call_target="tpu_custom_call" | custom-call | flops 1 | bytes 1 | tf_op jit(solution)/shard_map/pair/pallas_call | solution.py:235
  18.7 0.0 collective-permute-done.6.refs_0_
  18.7 0.0 collective-permute-done.7.refs_2_
  18.7 0.1 total_0.1
  18.7 2.6 %collective-permute-start.8 = (bf16[128,512]{1,0:T(8,128)(2,1)S(1)}, bf16[128,512]{1,0:T(8,128)(2,1)S(1)}, u32[]{:S(2)}, u32[]{:S(2)}) collective-permute-start(bf16[128,512]{1,0:T(8,128)(2,1)S(1)} %total_0.1), channel_id=1, source_target_pairs={{0,2},{1,3},{2,0},{3,1},{4,6},{5,7},{6,4},{7,5},{8,10},{9,11},{10,... | collective-permute-start | bytes 393224 | tf_op jit(solution)/shard_map/mirror_0/ppermute | solution.py:35
  21.4 0.6 %collective-permute-start.3 = (bf16[256,512]{1,0:T(8,128)(2,1)S(1)}, bf16[256,512]{1,0:T(8,128)(2,1)S(1)}, u32[]{:S(2)}, u32[]{:S(2)}) collective-permute-start(bf16[256,512]{1,0:T(8,128)(2,1)S(1)} %get-tuple-element.35), channel_id=1, source_target_pairs={{0,8},{4,20},{8,0},{12,28},{16,24},{20,4},{24,16},{28,12},{1,9},{5... | collective-permute-start | bytes 786440 | tf_op jit(solution)/shard_map/zero_to_chip_1/ppermute | solution.py:28
  21.9 0.0 collective-permute-done.10.refs_0_
  21.9 1.5 %collective-permute-start.4 = (bf16[256,512]{1,0:T(8,128)(2,1)S(1)}, bf16[256,512]{1,0:T(8,128)(2,1)S(1)}, u32[]{:S(2)}, u32[]{:S(2)}) collective-permute-start(bf16[256,512]{1,0:T(8,128)(2,1)S(1)} %get-tuple-element.36), channel_id=1, source_target_pairs={{0,16},{4,12},{8,24},{12,4},{16,0},{20,28},{24,8},{28,20},{1,17},{... | collective-permute-start | bytes 786440 | tf_op jit(solution)/shard_map/zero_to_chip_2/ppermute | solution.py:28
  23.4 0.0 collective-permute-done.11.refs_1_
  23.4 1.8 %collective-permute-start.5 = (bf16[256,512]{1,0:T(8,128)(2,1)S(1)}, bf16[256,512]{1,0:T(8,128)(2,1)S(1)}, u32[]{:S(2)}, u32[]{:S(2)}) collective-permute-start(bf16[256,512]{1,0:T(8,128)(2,1)S(1)} %get-tuple-element.37), channel_id=1, source_target_pairs={{0,24},{4,28},{8,16},{12,20},{16,8},{20,12},{24,0},{28,4},{1,25},{... | collective-permute-start | bytes 786440 | tf_op jit(solution)/shard_map/zero_to_chip_3/ppermute | solution.py:28
  25.2 0.0 collective-permute-done.12.refs_2_
  25.2 0.0 copy-start
  25.2 0.0 copy-start.1
  25.2 0.1 total_1.1
  25.3 3.2 %collective-permute-start.13 = (bf16[128,512]{1,0:T(8,128)(2,1)S(1)}, bf16[128,512]{1,0:T(8,128)(2,1)S(1)}, u32[]{:S(2)}, u32[]{:S(2)}) collective-permute-start(bf16[128,512]{1,0:T(8,128)(2,1)S(1)} %total_1.1), channel_id=1, source_target_pairs={{0,2},{1,3},{2,0},{3,1},{4,6},{5,7},{6,4},{7,5},{8,10},{9,11},{10,... | collective-permute-start | bytes 393224 | tf_op jit(solution)/shard_map/mirror_1/ppermute | solution.py:35
  28.5 0.0 collective-permute-done.8.refs_3_
  28.5 4.3 %collective-permute-done.13.refs_4_ = bf16[128,512]{1,0:T(8,128)(2,1)S(1)} collective-permute-done((bf16[128,512]{1,0:T(8,128)(2,1)S(1)}, bf16[128,512]{1,0:T(8,128)(2,1)S(1)}, u32[]{:S(2)}, u32[]{:S(2)}) %collective-permute-start.13) | collective-permute-done | bytes 131104 | tf_op jit(solution)/shard_map/mirror_1/ppermute | solution.py:35
  32.9 0.0 collective-permute-done.3.refs_0_
  32.9 0.0 collective-permute-done.4.refs_1_
  32.9 0.3 collective-permute-done.5.refs_2_
  33.2 0.0 copy-done
  33.2 0.0 copy-done.1
  33.2 1.7 %update.1 = (f32[1024,128]{1,0:T(8,128)}, f32[1024,128]{1,0:T(8,128)}, f32[1024,128]{1,0:T(8,128)}, f32[1024,128]{1,0:T(8,128)}) custom-call(f32[256,512]{1,0:T(8,128)S(1)} %get-tuple-element.34.refs_3_.kept, bf16[256,512]{1,0:T(8,128)(2,1)S(1)} %collective-permute-done.3.refs_0_, bf16[256,512]{1,0:T(8,128)(2,1)S(1)} %collective-permute-done.4.refs_1_, ...), custom_call_target="tpu_custom_call" | custom-call | flops 1 | bytes 1 | tf_op jit(solution)/shard_map/update/pallas_call | solution.py:329
Async XLA Ops:
  2.9 2.1 %collective-permute-start = (bf16[4,128,512]{2,1,0:T(8,128)(2,1)S(1)}, bf16[4,128,512]{2,1,0:T(8,128)(2,1)S(1)}, u32[]{:S(2)}, u32[]{:S(2)}) collective-permute-start(bf16[4,128,512]{2,1,0:T(8,128)(2,1)S(1)} %get-tuple-element.30), channel_id=1, source_target_pairs={{0,4},{4,0},{8,12},{12,8},{16,20},{20,16},{24,28},{28,24},{1,5},{5... | collective-permute-start | bytes 1572872 | tf_op jit(solution)/shard_map/sibling_0/ppermute | solution.py:28
  5.1 10.4 %collective-permute-start.1 = (bf16[384,2560]{1,0:T(8,128)(2,1)S(1)}, bf16[384,2560]{1,0:T(8,128)(2,1)S(1)}, u32[]{:S(2)}, u32[]{:S(2)}) collective-permute-start(bf16[384,2560]{1,0:T(8,128)(2,1)S(1)} %get-tuple-element.32.ahead), channel_id=1, source_target_pairs={{0,4},{4,0},{8,12},{12,8},{16,20},{20,16},{24,28},{28,24},{1,5},{5... | collective-permute-start | bytes 5898248 | tf_op jit(solution)/shard_map/operand_exchange/ppermute | solution.py:28
  5.5 4.5 %collective-permute-start.9 = (bf16[4,128,512]{2,1,0:T(8,128)(2,1)S(1)}, bf16[4,128,512]{2,1,0:T(8,128)(2,1)S(1)}, u32[]{:S(2)}, u32[]{:S(2)}) collective-permute-start(bf16[4,128,512]{2,1,0:T(8,128)(2,1)S(1)} %get-tuple-element.41), channel_id=1, source_target_pairs={{0,4},{4,0},{8,12},{12,8},{16,20},{20,16},{24,28},{28,24},{1,5},{5... | collective-permute-start | bytes 1572872 | tf_op jit(solution)/shard_map/sibling_1/ppermute | solution.py:28
  5.7 7.2 %collective-permute-start.2 = (bf16[128,512]{1,0:T(8,128)(2,1)S(1)}, bf16[128,512]{1,0:T(8,128)(2,1)S(1)}, u32[]{:S(2)}, u32[]{:S(2)}) collective-permute-start(bf16[128,512]{1,0:T(8,128)(2,1)S(1)} %get-tuple-element.33), channel_id=1, source_target_pairs={{0,16},{4,12},{8,24},{12,4},{16,0},{20,28},{24,8},{28,20},{1,17},{... | collective-permute-start | bytes 393224 | tf_op jit(solution)/shard_map/one_part_0_to_chip_2/ppermute | solution.py:28
  8.5 10.1 %collective-permute-start.6 = (bf16[128,512]{1,0:T(8,128)(2,1)S(1)}, bf16[128,512]{1,0:T(8,128)(2,1)S(1)}, u32[]{:S(2)}, u32[]{:S(2)}) collective-permute-start(bf16[128,512]{1,0:T(8,128)(2,1)S(1)} %get-tuple-element.39), channel_id=1, source_target_pairs={{0,8},{4,20},{8,0},{12,28},{16,24},{20,4},{24,16},{28,12},{1,9},{5... | collective-permute-start | bytes 393224 | tf_op jit(solution)/shard_map/one_part_0_to_chip_1/ppermute | solution.py:28
  10.0 8.7 %collective-permute-start.7 = (bf16[128,512]{1,0:T(8,128)(2,1)S(1)}, bf16[128,512]{1,0:T(8,128)(2,1)S(1)}, u32[]{:S(2)}, u32[]{:S(2)}) collective-permute-start(bf16[128,512]{1,0:T(8,128)(2,1)S(1)} %get-tuple-element.40), channel_id=1, source_target_pairs={{0,24},{4,28},{8,16},{12,20},{16,8},{20,12},{24,0},{28,4},{1,25},{... | collective-permute-start | bytes 393224 | tf_op jit(solution)/shard_map/one_part_0_to_chip_3/ppermute | solution.py:28
  10.1 11.8 %collective-permute-start.10 = (bf16[128,512]{1,0:T(8,128)(2,1)S(1)}, bf16[128,512]{1,0:T(8,128)(2,1)S(1)}, u32[]{:S(2)}, u32[]{:S(2)}) collective-permute-start(bf16[128,512]{1,0:T(8,128)(2,1)S(1)} %get-tuple-element.43), channel_id=1, source_target_pairs={{0,8},{4,12},{8,0},{12,4},{16,24},{20,28},{24,16},{28,20},{1,9},{5... | collective-permute-start | bytes 393224 | tf_op jit(solution)/shard_map/one_part_1_to_chip_1/ppermute | solution.py:28
  12.9 10.5 %collective-permute-start.11 = (bf16[128,512]{1,0:T(8,128)(2,1)S(1)}, bf16[128,512]{1,0:T(8,128)(2,1)S(1)}, u32[]{:S(2)}, u32[]{:S(2)}) collective-permute-start(bf16[128,512]{1,0:T(8,128)(2,1)S(1)} %get-tuple-element.44), channel_id=1, source_target_pairs={{0,16},{4,20},{8,24},{12,28},{16,0},{20,4},{24,8},{28,12},{1,17},{... | collective-permute-start | bytes 393224 | tf_op jit(solution)/shard_map/one_part_1_to_chip_2/ppermute | solution.py:28
  15.5 9.7 %collective-permute-start.12 = (bf16[128,512]{1,0:T(8,128)(2,1)S(1)}, bf16[128,512]{1,0:T(8,128)(2,1)S(1)}, u32[]{:S(2)}, u32[]{:S(2)}) collective-permute-start(bf16[128,512]{1,0:T(8,128)(2,1)S(1)} %get-tuple-element.45), channel_id=1, source_target_pairs={{0,24},{4,28},{8,16},{12,20},{16,8},{20,12},{24,0},{28,4},{1,25},{... | collective-permute-start | bytes 393224 | tf_op jit(solution)/shard_map/one_part_1_to_chip_3/ppermute | solution.py:28
  18.7 9.8 %collective-permute-start.8 = (bf16[128,512]{1,0:T(8,128)(2,1)S(1)}, bf16[128,512]{1,0:T(8,128)(2,1)S(1)}, u32[]{:S(2)}, u32[]{:S(2)}) collective-permute-start(bf16[128,512]{1,0:T(8,128)(2,1)S(1)} %total_0.1), channel_id=1, source_target_pairs={{0,2},{1,3},{2,0},{3,1},{4,6},{5,7},{6,4},{7,5},{8,10},{9,11},{10,... | collective-permute-start | bytes 393224 | tf_op jit(solution)/shard_map/mirror_0/ppermute | solution.py:35
  21.4 11.5 %collective-permute-start.3 = (bf16[256,512]{1,0:T(8,128)(2,1)S(1)}, bf16[256,512]{1,0:T(8,128)(2,1)S(1)}, u32[]{:S(2)}, u32[]{:S(2)}) collective-permute-start(bf16[256,512]{1,0:T(8,128)(2,1)S(1)} %get-tuple-element.35), channel_id=1, source_target_pairs={{0,8},{4,20},{8,0},{12,28},{16,24},{20,4},{24,16},{28,12},{1,9},{5... | collective-permute-start | bytes 786440 | tf_op jit(solution)/shard_map/zero_to_chip_1/ppermute | solution.py:28
  21.9 10.9 %collective-permute-start.4 = (bf16[256,512]{1,0:T(8,128)(2,1)S(1)}, bf16[256,512]{1,0:T(8,128)(2,1)S(1)}, u32[]{:S(2)}, u32[]{:S(2)}) collective-permute-start(bf16[256,512]{1,0:T(8,128)(2,1)S(1)} %get-tuple-element.36), channel_id=1, source_target_pairs={{0,16},{4,12},{8,24},{12,4},{16,0},{20,28},{24,8},{28,20},{1,17},{... | collective-permute-start | bytes 786440 | tf_op jit(solution)/shard_map/zero_to_chip_2/ppermute | solution.py:28
  23.4 9.8 %collective-permute-start.5 = (bf16[256,512]{1,0:T(8,128)(2,1)S(1)}, bf16[256,512]{1,0:T(8,128)(2,1)S(1)}, u32[]{:S(2)}, u32[]{:S(2)}) collective-permute-start(bf16[256,512]{1,0:T(8,128)(2,1)S(1)} %get-tuple-element.37), channel_id=1, source_target_pairs={{0,24},{4,28},{8,16},{12,20},{16,8},{20,12},{24,0},{28,4},{1,25},{... | collective-permute-start | bytes 786440 | tf_op jit(solution)/shard_map/zero_to_chip_3/ppermute | solution.py:28
  25.2 8.0 %copy-start = (f32[1,256,2,256]{3,2,1,0:T(2,128)S(1)}, f32[1,256,2,256]{3,2,1,0:T(2,128)}, u32[]{:S(2)}) copy-start(f32[1,256,2,256]{3,2,1,0:T(2,128)} %param.10) | copy-start | bytes 1572868
  25.2 8.0 %copy-start.1 = (f32[1,256,2,256]{3,2,1,0:T(2,128)S(1)}, f32[1,256,2,256]{3,2,1,0:T(2,128)}, u32[]{:S(2)}) copy-start(f32[1,256,2,256]{3,2,1,0:T(2,128)} %param.11) | copy-start | bytes 1572868
  25.3 7.6 %collective-permute-start.13 = (bf16[128,512]{1,0:T(8,128)(2,1)S(1)}, bf16[128,512]{1,0:T(8,128)(2,1)S(1)}, u32[]{:S(2)}, u32[]{:S(2)}) collective-permute-start(bf16[128,512]{1,0:T(8,128)(2,1)S(1)} %total_1.1), channel_id=1, source_target_pairs={{0,2},{1,3},{2,0},{3,1},{4,6},{5,7},{6,4},{7,5},{8,10},{9,11},{10,... | collective-permute-start | bytes 393224 | tf_op jit(solution)/shard_map/mirror_1/ppermute | solution.py:35

commit v8 on v7

--- a/solution.py
+++ b/solution.py
@@ -331,7 +331,9 @@
         in_specs=[IN_VMEM] * (3 + len(received) + len(partners)),
         out_specs=[ANYWHERE] * 4,
         out_shape=[jax.ShapeDtypeStruct(lines.shape, jnp.float32)] * 4,
-        scratch_shapes=[lines] * 4 + [pltpu.SemaphoreType.DMA((most, 4))],
+        scratch_shapes=[pltpu.VMEM((first.size // LANES + 8, LANES), jnp.float32)]
+        + [lines] * 3
+        + [pltpu.SemaphoreType.DMA((most, 4))],
         compiler_params=PARAMS,
         cost_estimate=SMALL,
     )(*map(held, (kept, *received, *partners, in_lines(first), in_lines(second))))
@@ -432,7 +434,7 @@
 
     def run(*arrays):
         ranks = mesh.shape["dp"]
-        paired = ranks % 2 == 0 and ranks & (ranks - 1) == 0
+        paired = ranks > 2 and ranks & (ranks - 1) == 0
         per_device = fast_device if paired and arrays[4].shape[1] // ranks % LANES == 0 else plain_device
         return jax.shard_map(
             per_device, mesh=mesh, in_specs=in_specs, out_specs=out_specs, check_vma=False

time: 35.1 us -> 35.1 us (level)
  no operation moved by 1% of the time
where the time goes in v8:
time: 35.1 us; the launch traced here: 35 us
  starting transfers between devices  22.3 us (64%)
  Pallas kernels  7.17 us (20%)
  waiting for transfers between devices  4.73 us (13%)
  between operations  0.71 us (2%)
    ppermute x12, starting transfers between devices, exchanged(): lax.ppermute(value, axis, [(i, i ^ mask_of(i)) for i in range(count)])  16.5 us
    ppermute x2, starting transfers between devices, mirrored(): return lax.ppermute(value, 'section', pairs)  5.85 us
    ppermute x2, waiting for transfers between devices, mirrored(): return lax.ppermute(value, 'section', pairs)  4.35 us
    pallas_call x1, Pallas kernels, sibling_products(): pl.pallas_call(functools.partial(sibling_kernel, experts, cuts), in_specs...  2.24 us
    pallas_call x1, Pallas kernels, updated(): pl.pallas_call(functools.partial(update_kernel, first.shape[1], cuts, mes...  1.74 us
    pallas_call x1, Pallas kernels, own_products(): pl.pallas_call(functools.partial(own_kernel, experts), in_specs=[ANYWHERE...  1.54 us
    pallas_call x1, Pallas kernels, paired(): pl.pallas_call(functools.partial(pair_kernel, len(after), messages), in_s...  1.28 us
  transfers between devices with their start and end apart: 14, of which 2 were waited for; matrix products, arithmetic and copies ran while one was open for 0% of the time, Pallas kernels for 9%

profile of v8, /device:TPU:0, one launch (start us, length us, event | category | flops | bytes accessed | tf_op | source)
XLA Modules:
  0.0 35.0 jit_solution(8675680513142695532)
XLA Ops:
  0.6 2.2 %sibling_products.1 = (bf16[4,128,512]{2,1,0:T(8,128)(2,1)S(1)}, bf16[4,128,512]{2,1,0:T(8,128)(2,1)S(1)}, bf16[384,2048]{1,0:T(8,128)(2,1)S(1)}, bf16[384,512]{1,0:T(8,128)(2,1)S(1)}) custom-call(s32[2,3]{1,0:T(2,128)} %bitcast.40, s32[2,2]{1,0:T(2,128)} %bitcast.42, bf16[2,384,2048]{2,1,0:T(8,128)(2,1)} %bitcast.36, bf16[2,384,256]{2,1,0:T(8,128)(2,1)} %bitcast.38), custom_call_target="tpu_custom_call" | custom-call | flops 1 | bytes 1 | tf_op jit(solution)/shard_map/sibling_products/pallas_call | solution.py:128
  2.9 0.5 %collective-permute-start = (bf16[4,128,512]{2,1,0:T(8,128)(2,1)S(1)}, bf16[4,128,512]{2,1,0:T(8,128)(2,1)S(1)}, u32[]{:S(2)}, u32[]{:S(2)}) collective-permute-start(bf16[4,128,512]{2,1,0:T(8,128)(2,1)S(1)} %get-tuple-element.30), channel_id=1, source_target_pairs={{0,4},{4,0},{8,12},{12,8},{16,20},{20,16},{24,28},{28,24},{1,5},{5... | collective-permute-start | bytes 1572872 | tf_op jit(solution)/shard_map/sibling_0/ppermute | solution.py:28
  3.4 1.5 %own_products.1 = (bf16[4,256,512]{2,1,0:T(8,128)(2,1)S(1)}, bf16[384,2560]{1,0:T(8,128)(2,1)S(1)}) custom-call(s32[2,3]{1,0:T(2,128)} %bitcast.41, s32[2,2]{1,0:T(2,128)} %bitcast.43, bf16[2,384,2048]{2,1,0:T(8,128)(2,1)} %bitcast.37, bf16[2,384,256]{2,1,0:T(8,128)(2,1)} %bitcast.39, bf16[384,2048]{1,0:T(8,128)(2,1)S(1)} %get-tuple-element.27.columns, ...), custom_call_target="tpu_custom_call" | custom-call | flops 1 | bytes 1 | tf_op jit(solution)/shard_map/own_products/pallas_call | solution.py:170
  4.9 0.0 collective-permute-done.received
  4.9 0.1 join_0.1
  5.1 0.4 %collective-permute-start.1 = (bf16[384,2560]{1,0:T(8,128)(2,1)S(1)}, bf16[384,2560]{1,0:T(8,128)(2,1)S(1)}, u32[]{:S(2)}, u32[]{:S(2)}) collective-permute-start(bf16[384,2560]{1,0:T(8,128)(2,1)S(1)} %get-tuple-element.32.ahead), channel_id=1, source_target_pairs={{0,4},{4,0},{8,12},{12,8},{16,20},{20,16},{24,28},{28,24},{1,5},{5... | collective-permute-start | bytes 5898248 | tf_op jit(solution)/shard_map/operand_exchange/ppermute | solution.py:28
  5.5 0.2 collective-permute-start.9
  5.7 2.9 %collective-permute-start.2 = (bf16[128,512]{1,0:T(8,128)(2,1)S(1)}, bf16[128,512]{1,0:T(8,128)(2,1)S(1)}, u32[]{:S(2)}, u32[]{:S(2)}) collective-permute-start(bf16[128,512]{1,0:T(8,128)(2,1)S(1)} %get-tuple-element.33), channel_id=1, source_target_pairs={{0,16},{4,12},{8,24},{12,4},{16,0},{20,28},{24,8},{28,20},{1,17},{... | collective-permute-start | bytes 393224 | tf_op jit(solution)/shard_map/one_part_0_to_chip_2/ppermute | solution.py:28
  8.5 1.5 %collective-permute-start.6 = (bf16[128,512]{1,0:T(8,128)(2,1)S(1)}, bf16[128,512]{1,0:T(8,128)(2,1)S(1)}, u32[]{:S(2)}, u32[]{:S(2)}) collective-permute-start(bf16[128,512]{1,0:T(8,128)(2,1)S(1)} %get-tuple-element.39), channel_id=1, source_target_pairs={{0,8},{4,20},{8,0},{12,28},{16,24},{20,4},{24,16},{28,12},{1,9},{5... | collective-permute-start | bytes 393224 | tf_op jit(solution)/shard_map/one_part_0_to_chip_1/ppermute | solution.py:28
  10.0 0.0 collective-permute-start.7
  10.0 0.0 collective-permute-done.9.received
  10.0 0.1 join_1.1
  10.1 2.7 %collective-permute-start.10 = (bf16[128,512]{1,0:T(8,128)(2,1)S(1)}, bf16[128,512]{1,0:T(8,128)(2,1)S(1)}, u32[]{:S(2)}, u32[]{:S(2)}) collective-permute-start(bf16[128,512]{1,0:T(8,128)(2,1)S(1)} %get-tuple-element.43), channel_id=1, source_target_pairs={{0,8},{4,12},{8,0},{12,4},{16,24},{20,28},{24,16},{28,20},{1,9},{5... | collective-permute-start | bytes 393224 | tf_op jit(solution)/shard_map/one_part_1_to_chip_1/ppermute | solution.py:28
  12.9 0.0 collective-permute-done.2.refs_0_.refs_1_
  12.9 2.6 %collective-permute-start.11 = (bf16[128,512]{1,0:T(8,128)(2,1)S(1)}, bf16[128,512]{1,0:T(8,128)(2,1)S(1)}, u32[]{:S(2)}, u32[]{:S(2)}) collective-permute-start(bf16[128,512]{1,0:T(8,128)(2,1)S(1)} %get-tuple-element.44), channel_id=1, source_target_pairs={{0,16},{4,20},{8,24},{12,28},{16,0},{20,4},{24,8},{28,12},{1,17},{... | collective-permute-start | bytes 393224 | tf_op jit(solution)/shard_map/one_part_1_to_chip_2/ppermute | solution.py:28
  15.5 0.0 collective-permute-done.1.other
  15.5 1.9 %collective-permute-start.12 = (bf16[128,512]{1,0:T(8,128)(2,1)S(1)}, bf16[128,512]{1,0:T(8,128)(2,1)S(1)}, u32[]{:S(2)}, u32[]{:S(2)}) collective-permute-start(bf16[128,512]{1,0:T(8,128)(2,1)S(1)} %get-tuple-element.45), channel_id=1, source_target_pairs={{0,24},{4,28},{8,16},{12,20},{16,8},{20,12},{24,0},{28,4},{1,25},{... | collective-permute-start | bytes 393224 | tf_op jit(solution)/shard_map/one_part_1_to_chip_3/ppermute | solution.py:28
  17.4 1.3 %pair.1 = (f32[256,512]{1,0:T(8,128)S(1)}, bf16[256,512]{1,0:T(8,128)(2,1)S(1)}, bf16[256,512]{1,0:T(8,128)(2,1)S(1)}, bf16[256,512]{1,0:T(8,128)(2,1)S(1)}) custom-call(bf16[384,2560]{1,0:T(8,128)(2,1)S(1)} %get-tuple-element.32.ahead, bf16[384,2560]{1,0:T(8,128)(2,1)S(1)} %collective-permute-done.1.other, ...), custom_call_target="tpu_custom_call" | custom-call | flops 1 | bytes 1 | tf_op jit(solution)/shard_map/pair/pallas_call | solution.py:235
  18.7 0.0 collective-permute-done.6.refs_0_
  18.7 0.0 collective-permute-done.7.refs_2_
  18.7 0.1 total_0.1
  18.7 2.6 %collective-permute-start.8 = (bf16[128,512]{1,0:T(8,128)(2,1)S(1)}, bf16[128,512]{1,0:T(8,128)(2,1)S(1)}, u32[]{:S(2)}, u32[]{:S(2)}) collective-permute-start(bf16[128,512]{1,0:T(8,128)(2,1)S(1)} %total_0.1), channel_id=1, source_target_pairs={{0,2},{1,3},{2,0},{3,1},{4,6},{5,7},{6,4},{7,5},{8,10},{9,11},{10,... | collective-permute-start | bytes 393224 | tf_op jit(solution)/shard_map/mirror_0/ppermute | solution.py:35
  21.4 0.6 %collective-permute-start.3 = (bf16[256,512]{1,0:T(8,128)(2,1)S(1)}, bf16[256,512]{1,0:T(8,128)(2,1)S(1)}, u32[]{:S(2)}, u32[]{:S(2)}) collective-permute-start(bf16[256,512]{1,0:T(8,128)(2,1)S(1)} %get-tuple-element.35), channel_id=1, source_target_pairs={{0,8},{4,20},{8,0},{12,28},{16,24},{20,4},{24,16},{28,12},{1,9},{5... | collective-permute-start | bytes 786440 | tf_op jit(solution)/shard_map/zero_to_chip_1/ppermute | solution.py:28
  21.9 0.0 collective-permute-done.10.refs_0_
  21.9 1.5 %collective-permute-start.4 = (bf16[256,512]{1,0:T(8,128)(2,1)S(1)}, bf16[256,512]{1,0:T(8,128)(2,1)S(1)}, u32[]{:S(2)}, u32[]{:S(2)}) collective-permute-start(bf16[256,512]{1,0:T(8,128)(2,1)S(1)} %get-tuple-element.36), channel_id=1, source_target_pairs={{0,16},{4,12},{8,24},{12,4},{16,0},{20,28},{24,8},{28,20},{1,17},{... | collective-permute-start | bytes 786440 | tf_op jit(solution)/shard_map/zero_to_chip_2/ppermute | solution.py:28
  23.4 0.0 collective-permute-done.11.refs_1_
  23.4 1.8 %collective-permute-start.5 = (bf16[256,512]{1,0:T(8,128)(2,1)S(1)}, bf16[256,512]{1,0:T(8,128)(2,1)S(1)}, u32[]{:S(2)}, u32[]{:S(2)}) collective-permute-start(bf16[256,512]{1,0:T(8,128)(2,1)S(1)} %get-tuple-element.37), channel_id=1, source_target_pairs={{0,24},{4,28},{8,16},{12,20},{16,8},{20,12},{24,0},{28,4},{1,25},{... | collective-permute-start | bytes 786440 | tf_op jit(solution)/shard_map/zero_to_chip_3/ppermute | solution.py:28
  25.2 0.0 collective-permute-done.12.refs_2_
  25.2 0.0 copy-start
  25.2 0.0 copy-start.1
  25.2 0.1 total_1.1
  25.3 3.2 %collective-permute-start.13 = (bf16[128,512]{1,0:T(8,128)(2,1)S(1)}, bf16[128,512]{1,0:T(8,128)(2,1)S(1)}, u32[]{:S(2)}, u32[]{:S(2)}) collective-permute-start(bf16[128,512]{1,0:T(8,128)(2,1)S(1)} %total_1.1), channel_id=1, source_target_pairs={{0,2},{1,3},{2,0},{3,1},{4,6},{5,7},{6,4},{7,5},{8,10},{9,11},{10,... | collective-permute-start | bytes 393224 | tf_op jit(solution)/shard_map/mirror_1/ppermute | solution.py:35
  28.5 0.0 collective-permute-done.8.refs_3_
  28.5 4.3 %collective-permute-done.13.refs_4_ = bf16[128,512]{1,0:T(8,128)(2,1)S(1)} collective-permute-done((bf16[128,512]{1,0:T(8,128)(2,1)S(1)}, bf16[128,512]{1,0:T(8,128)(2,1)S(1)}, u32[]{:S(2)}, u32[]{:S(2)}) %collective-permute-start.13) | collective-permute-done | bytes 131104 | tf_op jit(solution)/shard_map/mirror_1/ppermute | solution.py:35
  32.9 0.0 collective-permute-done.3.refs_0_
  32.9 0.0 collective-permute-done.4.refs_1_
  32.9 0.3 collective-permute-done.5.refs_2_
  33.2 0.0 copy-done
  33.2 0.0 copy-done.1
  33.2 1.7 %update.1 = (f32[1024,128]{1,0:T(8,128)}, f32[1024,128]{1,0:T(8,128)}, f32[1024,128]{1,0:T(8,128)}, f32[1024,128]{1,0:T(8,128)}) custom-call(f32[256,512]{1,0:T(8,128)S(1)} %get-tuple-element.34.refs_3_.kept, bf16[256,512]{1,0:T(8,128)(2,1)S(1)} %collective-permute-done.3.refs_0_, bf16[256,512]{1,0:T(8,128)(2,1)S(1)} %collective-permute-done.4.refs_1_, ...), custom_call_target="tpu_custom_call" | custom-call | flops 1 | bytes 1 | tf_op jit(solution)/shard_map/update/pallas_call | solution.py:329
Async XLA Ops:
  2.9 2.1 %collective-permute-start = (bf16[4,128,512]{2,1,0:T(8,128)(2,1)S(1)}, bf16[4,128,512]{2,1,0:T(8,128)(2,1)S(1)}, u32[]{:S(2)}, u32[]{:S(2)}) collective-permute-start(bf16[4,128,512]{2,1,0:T(8,128)(2,1)S(1)} %get-tuple-element.30), channel_id=1, source_target_pairs={{0,4},{4,0},{8,12},{12,8},{16,20},{20,16},{24,28},{28,24},{1,5},{5... | collective-permute-start | bytes 1572872 | tf_op jit(solution)/shard_map/sibling_0/ppermute | solution.py:28
  5.1 10.4 %collective-permute-start.1 = (bf16[384,2560]{1,0:T(8,128)(2,1)S(1)}, bf16[384,2560]{1,0:T(8,128)(2,1)S(1)}, u32[]{:S(2)}, u32[]{:S(2)}) collective-permute-start(bf16[384,2560]{1,0:T(8,128)(2,1)S(1)} %get-tuple-element.32.ahead), channel_id=1, source_target_pairs={{0,4},{4,0},{8,12},{12,8},{16,20},{20,16},{24,28},{28,24},{1,5},{5... | collective-permute-start | bytes 5898248 | tf_op jit(solution)/shard_map/operand_exchange/ppermute | solution.py:28
  5.5 4.5 %collective-permute-start.9 = (bf16[4,128,512]{2,1,0:T(8,128)(2,1)S(1)}, bf16[4,128,512]{2,1,0:T(8,128)(2,1)S(1)}, u32[]{:S(2)}, u32[]{:S(2)}) collective-permute-start(bf16[4,128,512]{2,1,0:T(8,128)(2,1)S(1)} %get-tuple-element.41), channel_id=1, source_target_pairs={{0,4},{4,0},{8,12},{12,8},{16,20},{20,16},{24,28},{28,24},{1,5},{5... | collective-permute-start | bytes 1572872 | tf_op jit(solution)/shard_map/sibling_1/ppermute | solution.py:28
  5.7 7.2 %collective-permute-start.2 = (bf16[128,512]{1,0:T(8,128)(2,1)S(1)}, bf16[128,512]{1,0:T(8,128)(2,1)S(1)}, u32[]{:S(2)}, u32[]{:S(2)}) collective-permute-start(bf16[128,512]{1,0:T(8,128)(2,1)S(1)} %get-tuple-element.33), channel_id=1, source_target_pairs={{0,16},{4,12},{8,24},{12,4},{16,0},{20,28},{24,8},{28,20},{1,17},{... | collective-permute-start | bytes 393224 | tf_op jit(solution)/shard_map/one_part_0_to_chip_2/ppermute | solution.py:28
  8.5 10.1 %collective-permute-start.6 = (bf16[128,512]{1,0:T(8,128)(2,1)S(1)}, bf16[128,512]{1,0:T(8,128)(2,1)S(1)}, u32[]{:S(2)}, u32[]{:S(2)}) collective-permute-start(bf16[128,512]{1,0:T(8,128)(2,1)S(1)} %get-tuple-element.39), channel_id=1, source_target_pairs={{0,8},{4,20},{8,0},{12,28},{16,24},{20,4},{24,16},{28,12},{1,9},{5... | collective-permute-start | bytes 393224 | tf_op jit(solution)/shard_map/one_part_0_to_chip_1/ppermute | solution.py:28
  10.0 8.7 %collective-permute-start.7 = (bf16[128,512]{1,0:T(8,128)(2,1)S(1)}, bf16[128,512]{1,0:T(8,128)(2,1)S(1)}, u32[]{:S(2)}, u32[]{:S(2)}) collective-permute-start(bf16[128,512]{1,0:T(8,128)(2,1)S(1)} %get-tuple-element.40), channel_id=1, source_target_pairs={{0,24},{4,28},{8,16},{12,20},{16,8},{20,12},{24,0},{28,4},{1,25},{... | collective-permute-start | bytes 393224 | tf_op jit(solution)/shard_map/one_part_0_to_chip_3/ppermute | solution.py:28
  10.1 11.8 %collective-permute-start.10 = (bf16[128,512]{1,0:T(8,128)(2,1)S(1)}, bf16[128,512]{1,0:T(8,128)(2,1)S(1)}, u32[]{:S(2)}, u32[]{:S(2)}) collective-permute-start(bf16[128,512]{1,0:T(8,128)(2,1)S(1)} %get-tuple-element.43), channel_id=1, source_target_pairs={{0,8},{4,12},{8,0},{12,4},{16,24},{20,28},{24,16},{28,20},{1,9},{5... | collective-permute-start | bytes 393224 | tf_op jit(solution)/shard_map/one_part_1_to_chip_1/ppermute | solution.py:28
  12.9 10.5 %collective-permute-start.11 = (bf16[128,512]{1,0:T(8,128)(2,1)S(1)}, bf16[128,512]{1,0:T(8,128)(2,1)S(1)}, u32[]{:S(2)}, u32[]{:S(2)}) collective-permute-start(bf16[128,512]{1,0:T(8,128)(2,1)S(1)} %get-tuple-element.44), channel_id=1, source_target_pairs={{0,16},{4,20},{8,24},{12,28},{16,0},{20,4},{24,8},{28,12},{1,17},{... | collective-permute-start | bytes 393224 | tf_op jit(solution)/shard_map/one_part_1_to_chip_2/ppermute | solution.py:28
  15.5 9.7 %collective-permute-start.12 = (bf16[128,512]{1,0:T(8,128)(2,1)S(1)}, bf16[128,512]{1,0:T(8,128)(2,1)S(1)}, u32[]{:S(2)}, u32[]{:S(2)}) collective-permute-start(bf16[128,512]{1,0:T(8,128)(2,1)S(1)} %get-tuple-element.45), channel_id=1, source_target_pairs={{0,24},{4,28},{8,16},{12,20},{16,8},{20,12},{24,0},{28,4},{1,25},{... | collective-permute-start | bytes 393224 | tf_op jit(solution)/shard_map/one_part_1_to_chip_3/ppermute | solution.py:28
  18.7 9.8 %collective-permute-start.8 = (bf16[128,512]{1,0:T(8,128)(2,1)S(1)}, bf16[128,512]{1,0:T(8,128)(2,1)S(1)}, u32[]{:S(2)}, u32[]{:S(2)}) collective-permute-start(bf16[128,512]{1,0:T(8,128)(2,1)S(1)} %total_0.1), channel_id=1, source_target_pairs={{0,2},{1,3},{2,0},{3,1},{4,6},{5,7},{6,4},{7,5},{8,10},{9,11},{10,... | collective-permute-start | bytes 393224 | tf_op jit(solution)/shard_map/mirror_0/ppermute | solution.py:35
  21.4 11.5 %collective-permute-start.3 = (bf16[256,512]{1,0:T(8,128)(2,1)S(1)}, bf16[256,512]{1,0:T(8,128)(2,1)S(1)}, u32[]{:S(2)}, u32[]{:S(2)}) collective-permute-start(bf16[256,512]{1,0:T(8,128)(2,1)S(1)} %get-tuple-element.35), channel_id=1, source_target_pairs={{0,8},{4,20},{8,0},{12,28},{16,24},{20,4},{24,16},{28,12},{1,9},{5... | collective-permute-start | bytes 786440 | tf_op jit(solution)/shard_map/zero_to_chip_1/ppermute | solution.py:28
  21.9 10.9 %collective-permute-start.4 = (bf16[256,512]{1,0:T(8,128)(2,1)S(1)}, bf16[256,512]{1,0:T(8,128)(2,1)S(1)}, u32[]{:S(2)}, u32[]{:S(2)}) collective-permute-start(bf16[256,512]{1,0:T(8,128)(2,1)S(1)} %get-tuple-element.36), channel_id=1, source_target_pairs={{0,16},{4,12},{8,24},{12,4},{16,0},{20,28},{24,8},{28,20},{1,17},{... | collective-permute-start | bytes 786440 | tf_op jit(solution)/shard_map/zero_to_chip_2/ppermute | solution.py:28
  23.4 9.8 %collective-permute-start.5 = (bf16[256,512]{1,0:T(8,128)(2,1)S(1)}, bf16[256,512]{1,0:T(8,128)(2,1)S(1)}, u32[]{:S(2)}, u32[]{:S(2)}) collective-permute-start(bf16[256,512]{1,0:T(8,128)(2,1)S(1)} %get-tuple-element.37), channel_id=1, source_target_pairs={{0,24},{4,28},{8,16},{12,20},{16,8},{20,12},{24,0},{28,4},{1,25},{... | collective-permute-start | bytes 786440 | tf_op jit(solution)/shard_map/zero_to_chip_3/ppermute | solution.py:28
  25.2 8.0 %copy-start = (f32[1,256,2,256]{3,2,1,0:T(2,128)S(1)}, f32[1,256,2,256]{3,2,1,0:T(2,128)}, u32[]{:S(2)}) copy-start(f32[1,256,2,256]{3,2,1,0:T(2,128)} %param.10) | copy-start | bytes 1572868
  25.2 8.0 %copy-start.1 = (f32[1,256,2,256]{3,2,1,0:T(2,128)S(1)}, f32[1,256,2,256]{3,2,1,0:T(2,128)}, u32[]{:S(2)}) copy-start(f32[1,256,2,256]{3,2,1,0:T(2,128)} %param.11) | copy-start | bytes 1572868
  25.3 7.6 %collective-permute-start.13 = (bf16[128,512]{1,0:T(8,128)(2,1)S(1)}, bf16[128,512]{1,0:T(8,128)(2,1)S(1)}, u32[]{:S(2)}, u32[]{:S(2)}) collective-permute-start(bf16[128,512]{1,0:T(8,128)(2,1)S(1)} %total_1.1), channel_id=1, source_target_pairs={{0,2},{1,3},{2,0},{3,1},{4,6},{5,7},{6,4},{7,5},{8,10},{9,11},{10,... | collective-permute-start | bytes 393224 | tf_op jit(solution)/shard_map/mirror_1/ppermute | solution.py:35

commit v9 on v8

--- a/solution.py
+++ b/solution.py
@@ -56,6 +56,7 @@
 IN_VMEM = pl.BlockSpec(memory_space=pltpu.VMEM)
 PARAMS = pltpu.CompilerParams(vmem_limit_bytes=VMEM_BYTES)
 PIECES = 4
+STEPS = 4
 SMALL = pl.CostEstimate(flops=1, bytes_accessed=1, transcendentals=0)
 LARGE = pl.CostEstimate(flops=1 << 33, bytes_accessed=1, transcendentals=0)
 
@@ -103,20 +104,28 @@
     columns, wide, rows, route_now, counts_now, column_sems, sems = refs[len(cuts) :]
     copies = routed_copies(route, counts, route_now, counts_now, sems)
     copies.append(pltpu.make_async_copy(hidden.at[1], rows, sems.at[2]))
-    column_copies = row_copies(inputs.at[1], columns, column_sems)
-    for copy in copies + column_copies:
+    chips, _, _ = outs[0].shape
+    share = cuts[-1].stop
+    column_copies = []
+    for sibling in (True, False):
+        for k in range(chips):
+            place = owner_columns(k, sibling, share)
+            sem = column_sems.at[k + (0 if sibling else chips)]
+            copy = pltpu.make_async_copy(inputs.at[1, :, place], columns.at[:, place], sem)
+            column_copies.append(copy)
+    for copy in copies[2:] + column_copies[:chips] + copies[:2] + column_copies[chips:]:
         copy.start()
     for copy in copies:
         copy.wait()
     expand_hidden(route_now, counts_now, 1, rows, wide, route.shape[1], experts)
-    for copy in column_copies:
-        copy.wait()
-    chips, _, _ = outs[0].shape
-    share = cuts[-1].stop
+    for copy in column_copies[:chips]:
+        copy.wait()
     for k in range(chips):
         product = contracted(columns[:, owner_columns(k, True, share)], wide[...])
         for out, some in zip(outs, cuts):
             out[k] = product[some].astype(out.dtype)
+    for copy in column_copies[chips:]:
+        copy.wait()
 
 
 def sibling_products(route, counts, inputs, hidden, chips, experts, cuts):
@@ -134,7 +143,7 @@
             pltpu.VMEM((rows, width), jnp.bfloat16),
             pltpu.SMEM(route.shape, jnp.int32),
             pltpu.SMEM(counts.shape, jnp.int32),
-            pltpu.SemaphoreType.DMA((PIECES,)),
+            pltpu.SemaphoreType.DMA((2 * chips,)),
             pltpu.SemaphoreType.DMA((3,)),
         ],
         compiler_params=PARAMS,
@@ -270,7 +279,7 @@
     share, columns = kept.shape
     lines = columns // LANES
     chunks = columns // experts // LANES
-    steps = sorted({0, *(some.stop for some in cuts), *(some.stop for _, some in messages)})
+    steps = range(0, share + 1, share // STEPS)
     copies = []
     for i, (begin, end) in enumerate(zip(steps, steps[1:])):
         rows = end - begin
@@ -324,7 +333,6 @@
 
 
 def updated(kept, received, partners, first, second, cuts, messages):
-    most = 1 + len(cuts) + len(messages)
     lines = pltpu.VMEM((first.size // LANES, LANES), jnp.float32)
     outs = pl.pallas_call(
         functools.partial(update_kernel, first.shape[1], cuts, messages),
@@ -333,7 +341,7 @@
         out_shape=[jax.ShapeDtypeStruct(lines.shape, jnp.float32)] * 4,
         scratch_shapes=[pltpu.VMEM((first.size // LANES + 8, LANES), jnp.float32)]
         + [lines] * 3
-        + [pltpu.SemaphoreType.DMA((most, 4))],
+        + [pltpu.SemaphoreType.DMA((STEPS, 4))],
         compiler_params=PARAMS,
         cost_estimate=SMALL,
     )(*map(held, (kept, *received, *partners, in_lines(first), in_lines(second))))

time: 35.1 us -> 34.8 us (level)
  no operation moved by 1% of the time
where the time goes in v9:
time: 34.8 us; the launch traced here: 34.7 us
  starting transfers between devices  22.3 us (64%)
  Pallas kernels  6.87 us (20%)
  waiting for transfers between devices  4.73 us (14%)
  between operations  0.71 us (2%)
    ppermute x12, starting transfers between devices, exchanged(): lax.ppermute(value, axis, [(i, i ^ mask_of(i)) for i in range(count)])  16.5 us
    ppermute x2, starting transfers between devices, mirrored(): return lax.ppermute(value, 'section', pairs)  5.85 us
    ppermute x2, waiting for transfers between devices, mirrored(): return lax.ppermute(value, 'section', pairs)  4.35 us
    pallas_call x1, Pallas kernels, sibling_products(): pl.pallas_call(functools.partial(sibling_kernel, experts, cuts), in_specs...  2.16 us
    pallas_call x1, Pallas kernels, own_products(): pl.pallas_call(functools.partial(own_kernel, experts), in_specs=[ANYWHERE...  1.54 us
    pallas_call x1, Pallas kernels, updated(): pl.pallas_call(functools.partial(update_kernel, first.shape[1], cuts, mes...  1.53 us
    pallas_call x1, Pallas kernels, paired(): pl.pallas_call(functools.partial(pair_kernel, len(after), messages), in_s...  1.28 us
  transfers between devices with their start and end apart: 14, of which 2 were waited for; matrix products, arithmetic and copies ran while one was open for 0% of the time, Pallas kernels for 9%

profile of v9, /device:TPU:0, one launch (start us, length us, event | category | flops | bytes accessed | tf_op | source)
XLA Modules:
  0.0 34.7 jit_solution(18222254649300429156)
XLA Ops:
  0.6 2.2 %sibling_products.1 = (bf16[4,128,512]{2,1,0:T(8,128)(2,1)S(1)}, bf16[4,128,512]{2,1,0:T(8,128)(2,1)S(1)}, bf16[384,2048]{1,0:T(8,128)(2,1)S(1)}, bf16[384,512]{1,0:T(8,128)(2,1)S(1)}) custom-call(s32[2,3]{1,0:T(2,128)} %bitcast.40, s32[2,2]{1,0:T(2,128)} %bitcast.42, bf16[2,384,2048]{2,1,0:T(8,128)(2,1)} %bitcast.36, bf16[2,384,256]{2,1,0:T(8,128)(2,1)} %bitcast.38), custom_call_target="tpu_custom_call" | custom-call | flops 1 | bytes 1 | tf_op jit(solution)/shard_map/sibling_products/pallas_call | solution.py:137
  2.8 0.5 %collective-permute-start = (bf16[4,128,512]{2,1,0:T(8,128)(2,1)S(1)}, bf16[4,128,512]{2,1,0:T(8,128)(2,1)S(1)}, u32[]{:S(2)}, u32[]{:S(2)}) collective-permute-start(bf16[4,128,512]{2,1,0:T(8,128)(2,1)S(1)} %get-tuple-element.30), channel_id=1, source_target_pairs={{0,4},{4,0},{8,12},{12,8},{16,20},{20,16},{24,28},{28,24},{1,5},{5... | collective-permute-start | bytes 1572872 | tf_op jit(solution)/shard_map/sibling_0/ppermute | solution.py:28
  3.3 1.5 %own_products.1 = (bf16[4,256,512]{2,1,0:T(8,128)(2,1)S(1)}, bf16[384,2560]{1,0:T(8,128)(2,1)S(1)}) custom-call(s32[2,3]{1,0:T(2,128)} %bitcast.41, s32[2,2]{1,0:T(2,128)} %bitcast.43, bf16[2,384,2048]{2,1,0:T(8,128)(2,1)} %bitcast.37, bf16[2,384,256]{2,1,0:T(8,128)(2,1)} %bitcast.39, bf16[384,2048]{1,0:T(8,128)(2,1)S(1)} %get-tuple-element.27.columns, ...), custom_call_target="tpu_custom_call" | custom-call | flops 1 | bytes 1 | tf_op jit(solution)/shard_map/own_products/pallas_call | solution.py:179
  4.8 0.0 collective-permute-done.received
  4.9 0.1 join_0.1
  5.0 0.4 %collective-permute-start.1 = (bf16[384,2560]{1,0:T(8,128)(2,1)S(1)}, bf16[384,2560]{1,0:T(8,128)(2,1)S(1)}, u32[]{:S(2)}, u32[]{:S(2)}) collective-permute-start(bf16[384,2560]{1,0:T(8,128)(2,1)S(1)} %get-tuple-element.32.ahead), channel_id=1, source_target_pairs={{0,4},{4,0},{8,12},{12,8},{16,20},{20,16},{24,28},{28,24},{1,5},{5... | collective-permute-start | bytes 5898248 | tf_op jit(solution)/shard_map/operand_exchange/ppermute | solution.py:28
  5.4 0.2 collective-permute-start.9
  5.6 2.9 %collective-permute-start.2 = (bf16[128,512]{1,0:T(8,128)(2,1)S(1)}, bf16[128,512]{1,0:T(8,128)(2,1)S(1)}, u32[]{:S(2)}, u32[]{:S(2)}) collective-permute-start(bf16[128,512]{1,0:T(8,128)(2,1)S(1)} %get-tuple-element.33), channel_id=1, source_target_pairs={{0,16},{4,12},{8,24},{12,4},{16,0},{20,28},{24,8},{28,20},{1,17},{... | collective-permute-start | bytes 393224 | tf_op jit(solution)/shard_map/one_part_0_to_chip_2/ppermute | solution.py:28
  8.4 1.5 %collective-permute-start.6 = (bf16[128,512]{1,0:T(8,128)(2,1)S(1)}, bf16[128,512]{1,0:T(8,128)(2,1)S(1)}, u32[]{:S(2)}, u32[]{:S(2)}) collective-permute-start(bf16[128,512]{1,0:T(8,128)(2,1)S(1)} %get-tuple-element.39), channel_id=1, source_target_pairs={{0,8},{4,20},{8,0},{12,28},{16,24},{20,4},{24,16},{28,12},{1,9},{5... | collective-permute-start | bytes 393224 | tf_op jit(solution)/shard_map/one_part_0_to_chip_1/ppermute | solution.py:28
  9.9 0.0 collective-permute-start.7
  9.9 0.0 collective-permute-done.9.received
  9.9 0.1 join_1.1
  10.1 2.8 %collective-permute-start.10 = (bf16[128,512]{1,0:T(8,128)(2,1)S(1)}, bf16[128,512]{1,0:T(8,128)(2,1)S(1)}, u32[]{:S(2)}, u32[]{:S(2)}) collective-permute-start(bf16[128,512]{1,0:T(8,128)(2,1)S(1)} %get-tuple-element.43), channel_id=1, source_target_pairs={{0,8},{4,12},{8,0},{12,4},{16,24},{20,28},{24,16},{28,20},{1,9},{5... | collective-permute-start | bytes 393224 | tf_op jit(solution)/shard_map/one_part_1_to_chip_1/ppermute | solution.py:28
  12.8 0.0 collective-permute-done.2.refs_0_.refs_1_
  12.8 2.6 %collective-permute-start.11 = (bf16[128,512]{1,0:T(8,128)(2,1)S(1)}, bf16[128,512]{1,0:T(8,128)(2,1)S(1)}, u32[]{:S(2)}, u32[]{:S(2)}) collective-permute-start(bf16[128,512]{1,0:T(8,128)(2,1)S(1)} %get-tuple-element.44), channel_id=1, source_target_pairs={{0,16},{4,20},{8,24},{12,28},{16,0},{20,4},{24,8},{28,12},{1,17},{... | collective-permute-start | bytes 393224 | tf_op jit(solution)/shard_map/one_part_1_to_chip_2/ppermute | solution.py:28
  15.4 0.0 collective-permute-done.1.other
  15.4 1.9 %collective-permute-start.12 = (bf16[128,512]{1,0:T(8,128)(2,1)S(1)}, bf16[128,512]{1,0:T(8,128)(2,1)S(1)}, u32[]{:S(2)}, u32[]{:S(2)}) collective-permute-start(bf16[128,512]{1,0:T(8,128)(2,1)S(1)} %get-tuple-element.45), channel_id=1, source_target_pairs={{0,24},{4,28},{8,16},{12,20},{16,8},{20,12},{24,0},{28,4},{1,25},{... | collective-permute-start | bytes 393224 | tf_op jit(solution)/shard_map/one_part_1_to_chip_3/ppermute | solution.py:28
  17.3 1.3 %pair.1 = (f32[256,512]{1,0:T(8,128)S(1)}, bf16[256,512]{1,0:T(8,128)(2,1)S(1)}, bf16[256,512]{1,0:T(8,128)(2,1)S(1)}, bf16[256,512]{1,0:T(8,128)(2,1)S(1)}) custom-call(bf16[384,2560]{1,0:T(8,128)(2,1)S(1)} %get-tuple-element.32.ahead, bf16[384,2560]{1,0:T(8,128)(2,1)S(1)} %collective-permute-done.1.other, ...), custom_call_target="tpu_custom_call" | custom-call | flops 1 | bytes 1 | tf_op jit(solution)/shard_map/pair/pallas_call | solution.py:244
  18.6 0.0 collective-permute-done.6.refs_0_
  18.6 0.0 collective-permute-done.7.refs_2_
  18.6 0.1 total_0.1
  18.7 2.6 %collective-permute-start.8 = (bf16[128,512]{1,0:T(8,128)(2,1)S(1)}, bf16[128,512]{1,0:T(8,128)(2,1)S(1)}, u32[]{:S(2)}, u32[]{:S(2)}) collective-permute-start(bf16[128,512]{1,0:T(8,128)(2,1)S(1)} %total_0.1), channel_id=1, source_target_pairs={{0,2},{1,3},{2,0},{3,1},{4,6},{5,7},{6,4},{7,5},{8,10},{9,11},{10,... | collective-permute-start | bytes 393224 | tf_op jit(solution)/shard_map/mirror_0/ppermute | solution.py:35
  21.3 0.6 %collective-permute-start.3 = (bf16[256,512]{1,0:T(8,128)(2,1)S(1)}, bf16[256,512]{1,0:T(8,128)(2,1)S(1)}, u32[]{:S(2)}, u32[]{:S(2)}) collective-permute-start(bf16[256,512]{1,0:T(8,128)(2,1)S(1)} %get-tuple-element.35), channel_id=1, source_target_pairs={{0,8},{4,20},{8,0},{12,28},{16,24},{20,4},{24,16},{28,12},{1,9},{5... | collective-permute-start | bytes 786440 | tf_op jit(solution)/shard_map/zero_to_chip_1/ppermute | solution.py:28
  21.9 0.0 collective-permute-done.10.refs_0_
  21.9 1.5 %collective-permute-start.4 = (bf16[256,512]{1,0:T(8,128)(2,1)S(1)}, bf16[256,512]{1,0:T(8,128)(2,1)S(1)}, u32[]{:S(2)}, u32[]{:S(2)}) collective-permute-start(bf16[256,512]{1,0:T(8,128)(2,1)S(1)} %get-tuple-element.36), channel_id=1, source_target_pairs={{0,16},{4,12},{8,24},{12,4},{16,0},{20,28},{24,8},{28,20},{1,17},{... | collective-permute-start | bytes 786440 | tf_op jit(solution)/shard_map/zero_to_chip_2/ppermute | solution.py:28
  23.3 0.0 collective-permute-done.11.refs_1_
  23.3 1.8 %collective-permute-start.5 = (bf16[256,512]{1,0:T(8,128)(2,1)S(1)}, bf16[256,512]{1,0:T(8,128)(2,1)S(1)}, u32[]{:S(2)}, u32[]{:S(2)}) collective-permute-start(bf16[256,512]{1,0:T(8,128)(2,1)S(1)} %get-tuple-element.37), channel_id=1, source_target_pairs={{0,24},{4,28},{8,16},{12,20},{16,8},{20,12},{24,0},{28,4},{1,25},{... | collective-permute-start | bytes 786440 | tf_op jit(solution)/shard_map/zero_to_chip_3/ppermute | solution.py:28
  25.1 0.0 collective-permute-done.12.refs_2_
  25.1 0.0 copy-start
  25.1 0.0 copy-start.1
  25.1 0.1 total_1.1
  25.2 3.2 %collective-permute-start.13 = (bf16[128,512]{1,0:T(8,128)(2,1)S(1)}, bf16[128,512]{1,0:T(8,128)(2,1)S(1)}, u32[]{:S(2)}, u32[]{:S(2)}) collective-permute-start(bf16[128,512]{1,0:T(8,128)(2,1)S(1)} %total_1.1), channel_id=1, source_target_pairs={{0,2},{1,3},{2,0},{3,1},{4,6},{5,7},{6,4},{7,5},{8,10},{9,11},{10,... | collective-permute-start | bytes 393224 | tf_op jit(solution)/shard_map/mirror_1/ppermute | solution.py:35
  28.4 0.0 collective-permute-done.8.refs_3_
  28.4 4.3 %collective-permute-done.13.refs_4_ = bf16[128,512]{1,0:T(8,128)(2,1)S(1)} collective-permute-done((bf16[128,512]{1,0:T(8,128)(2,1)S(1)}, bf16[128,512]{1,0:T(8,128)(2,1)S(1)}, u32[]{:S(2)}, u32[]{:S(2)}) %collective-permute-start.13) | collective-permute-done | bytes 131104 | tf_op jit(solution)/shard_map/mirror_1/ppermute | solution.py:35
  32.8 0.0 collective-permute-done.3.refs_0_
  32.8 0.0 collective-permute-done.4.refs_1_
  32.8 0.3 %collective-permute-done.5.refs_2_ = bf16[256,512]{1,0:T(8,128)(2,1)S(1)} collective-permute-done((bf16[256,512]{1,0:T(8,128)(2,1)S(1)}, bf16[256,512]{1,0:T(8,128)(2,1)S(1)}, u32[]{:S(2)}, u32[]{:S(2)}) %collective-permute-start.5) | collective-permute-done | bytes 262176 | tf_op jit(solution)/shard_map/zero_to_chip_3/ppermute | solution.py:28
  33.1 0.0 copy-done
  33.1 0.0 copy-done.1
  33.1 1.5 %update.1 = (f32[1024,128]{1,0:T(8,128)}, f32[1024,128]{1,0:T(8,128)}, f32[1024,128]{1,0:T(8,128)}, f32[1024,128]{1,0:T(8,128)}) custom-call(f32[256,512]{1,0:T(8,128)S(1)} %get-tuple-element.34.refs_3_.kept, bf16[256,512]{1,0:T(8,128)(2,1)S(1)} %collective-permute-done.3.refs_0_, bf16[256,512]{1,0:T(8,128)(2,1)S(1)} %collective-permute-done.4.refs_1_, ...), custom_call_target="tpu_custom_call" | custom-call | flops 1 | bytes 1 | tf_op jit(solution)/shard_map/update/pallas_call | solution.py:337
Async XLA Ops:
  2.8 2.1 %collective-permute-start = (bf16[4,128,512]{2,1,0:T(8,128)(2,1)S(1)}, bf16[4,128,512]{2,1,0:T(8,128)(2,1)S(1)}, u32[]{:S(2)}, u32[]{:S(2)}) collective-permute-start(bf16[4,128,512]{2,1,0:T(8,128)(2,1)S(1)} %get-tuple-element.30), channel_id=1, source_target_pairs={{0,4},{4,0},{8,12},{12,8},{16,20},{20,16},{24,28},{28,24},{1,5},{5... | collective-permute-start | bytes 1572872 | tf_op jit(solution)/shard_map/sibling_0/ppermute | solution.py:28
  5.0 10.4 %collective-permute-start.1 = (bf16[384,2560]{1,0:T(8,128)(2,1)S(1)}, bf16[384,2560]{1,0:T(8,128)(2,1)S(1)}, u32[]{:S(2)}, u32[]{:S(2)}) collective-permute-start(bf16[384,2560]{1,0:T(8,128)(2,1)S(1)} %get-tuple-element.32.ahead), channel_id=1, source_target_pairs={{0,4},{4,0},{8,12},{12,8},{16,20},{20,16},{24,28},{28,24},{1,5},{5... | collective-permute-start | bytes 5898248 | tf_op jit(solution)/shard_map/operand_exchange/ppermute | solution.py:28
  5.4 4.5 %collective-permute-start.9 = (bf16[4,128,512]{2,1,0:T(8,128)(2,1)S(1)}, bf16[4,128,512]{2,1,0:T(8,128)(2,1)S(1)}, u32[]{:S(2)}, u32[]{:S(2)}) collective-permute-start(bf16[4,128,512]{2,1,0:T(8,128)(2,1)S(1)} %get-tuple-element.41), channel_id=1, source_target_pairs={{0,4},{4,0},{8,12},{12,8},{16,20},{20,16},{24,28},{28,24},{1,5},{5... | collective-permute-start | bytes 1572872 | tf_op jit(solution)/shard_map/sibling_1/ppermute | solution.py:28
  5.6 7.2 %collective-permute-start.2 = (bf16[128,512]{1,0:T(8,128)(2,1)S(1)}, bf16[128,512]{1,0:T(8,128)(2,1)S(1)}, u32[]{:S(2)}, u32[]{:S(2)}) collective-permute-start(bf16[128,512]{1,0:T(8,128)(2,1)S(1)} %get-tuple-element.33), channel_id=1, source_target_pairs={{0,16},{4,12},{8,24},{12,4},{16,0},{20,28},{24,8},{28,20},{1,17},{... | collective-permute-start | bytes 393224 | tf_op jit(solution)/shard_map/one_part_0_to_chip_2/ppermute | solution.py:28
  8.4 10.1 %collective-permute-start.6 = (bf16[128,512]{1,0:T(8,128)(2,1)S(1)}, bf16[128,512]{1,0:T(8,128)(2,1)S(1)}, u32[]{:S(2)}, u32[]{:S(2)}) collective-permute-start(bf16[128,512]{1,0:T(8,128)(2,1)S(1)} %get-tuple-element.39), channel_id=1, source_target_pairs={{0,8},{4,20},{8,0},{12,28},{16,24},{20,4},{24,16},{28,12},{1,9},{5... | collective-permute-start | bytes 393224 | tf_op jit(solution)/shard_map/one_part_0_to_chip_1/ppermute | solution.py:28
  9.9 8.7 %collective-permute-start.7 = (bf16[128,512]{1,0:T(8,128)(2,1)S(1)}, bf16[128,512]{1,0:T(8,128)(2,1)S(1)}, u32[]{:S(2)}, u32[]{:S(2)}) collective-permute-start(bf16[128,512]{1,0:T(8,128)(2,1)S(1)} %get-tuple-element.40), channel_id=1, source_target_pairs={{0,24},{4,28},{8,16},{12,20},{16,8},{20,12},{24,0},{28,4},{1,25},{... | collective-permute-start | bytes 393224 | tf_op jit(solution)/shard_map/one_part_0_to_chip_3/ppermute | solution.py:28
  10.1 11.8 %collective-permute-start.10 = (bf16[128,512]{1,0:T(8,128)(2,1)S(1)}, bf16[128,512]{1,0:T(8,128)(2,1)S(1)}, u32[]{:S(2)}, u32[]{:S(2)}) collective-permute-start(bf16[128,512]{1,0:T(8,128)(2,1)S(1)} %get-tuple-element.43), channel_id=1, source_target_pairs={{0,8},{4,12},{8,0},{12,4},{16,24},{20,28},{24,16},{28,20},{1,9},{5... | collective-permute-start | bytes 393224 | tf_op jit(solution)/shard_map/one_part_1_to_chip_1/ppermute | solution.py:28
  12.8 10.5 %collective-permute-start.11 = (bf16[128,512]{1,0:T(8,128)(2,1)S(1)}, bf16[128,512]{1,0:T(8,128)(2,1)S(1)}, u32[]{:S(2)}, u32[]{:S(2)}) collective-permute-start(bf16[128,512]{1,0:T(8,128)(2,1)S(1)} %get-tuple-element.44), channel_id=1, source_target_pairs={{0,16},{4,20},{8,24},{12,28},{16,0},{20,4},{24,8},{28,12},{1,17},{... | collective-permute-start | bytes 393224 | tf_op jit(solution)/shard_map/one_part_1_to_chip_2/ppermute | solution.py:28
  15.4 9.7 %collective-permute-start.12 = (bf16[128,512]{1,0:T(8,128)(2,1)S(1)}, bf16[128,512]{1,0:T(8,128)(2,1)S(1)}, u32[]{:S(2)}, u32[]{:S(2)}) collective-permute-start(bf16[128,512]{1,0:T(8,128)(2,1)S(1)} %get-tuple-element.45), channel_id=1, source_target_pairs={{0,24},{4,28},{8,16},{12,20},{16,8},{20,12},{24,0},{28,4},{1,25},{... | collective-permute-start | bytes 393224 | tf_op jit(solution)/shard_map/one_part_1_to_chip_3/ppermute | solution.py:28
  18.7 9.8 %collective-permute-start.8 = (bf16[128,512]{1,0:T(8,128)(2,1)S(1)}, bf16[128,512]{1,0:T(8,128)(2,1)S(1)}, u32[]{:S(2)}, u32[]{:S(2)}) collective-permute-start(bf16[128,512]{1,0:T(8,128)(2,1)S(1)} %total_0.1), channel_id=1, source_target_pairs={{0,2},{1,3},{2,0},{3,1},{4,6},{5,7},{6,4},{7,5},{8,10},{9,11},{10,... | collective-permute-start | bytes 393224 | tf_op jit(solution)/shard_map/mirror_0/ppermute | solution.py:35
  21.3 11.5 %collective-permute-start.3 = (bf16[256,512]{1,0:T(8,128)(2,1)S(1)}, bf16[256,512]{1,0:T(8,128)(2,1)S(1)}, u32[]{:S(2)}, u32[]{:S(2)}) collective-permute-start(bf16[256,512]{1,0:T(8,128)(2,1)S(1)} %get-tuple-element.35), channel_id=1, source_target_pairs={{0,8},{4,20},{8,0},{12,28},{16,24},{20,4},{24,16},{28,12},{1,9},{5... | collective-permute-start | bytes 786440 | tf_op jit(solution)/shard_map/zero_to_chip_1/ppermute | solution.py:28
  21.9 10.9 %collective-permute-start.4 = (bf16[256,512]{1,0:T(8,128)(2,1)S(1)}, bf16[256,512]{1,0:T(8,128)(2,1)S(1)}, u32[]{:S(2)}, u32[]{:S(2)}) collective-permute-start(bf16[256,512]{1,0:T(8,128)(2,1)S(1)} %get-tuple-element.36), channel_id=1, source_target_pairs={{0,16},{4,12},{8,24},{12,4},{16,0},{20,28},{24,8},{28,20},{1,17},{... | collective-permute-start | bytes 786440 | tf_op jit(solution)/shard_map/zero_to_chip_2/ppermute | solution.py:28
  23.3 9.8 %collective-permute-start.5 = (bf16[256,512]{1,0:T(8,128)(2,1)S(1)}, bf16[256,512]{1,0:T(8,128)(2,1)S(1)}, u32[]{:S(2)}, u32[]{:S(2)}) collective-permute-start(bf16[256,512]{1,0:T(8,128)(2,1)S(1)} %get-tuple-element.37), channel_id=1, source_target_pairs={{0,24},{4,28},{8,16},{12,20},{16,8},{20,12},{24,0},{28,4},{1,25},{... | collective-permute-start | bytes 786440 | tf_op jit(solution)/shard_map/zero_to_chip_3/ppermute | solution.py:28
  25.1 8.0 %copy-start = (f32[1,256,2,256]{3,2,1,0:T(2,128)S(1)}, f32[1,256,2,256]{3,2,1,0:T(2,128)}, u32[]{:S(2)}) copy-start(f32[1,256,2,256]{3,2,1,0:T(2,128)} %param.10) | copy-start | bytes 1572868
  25.1 8.0 %copy-start.1 = (f32[1,256,2,256]{3,2,1,0:T(2,128)S(1)}, f32[1,256,2,256]{3,2,1,0:T(2,128)}, u32[]{:S(2)}) copy-start(f32[1,256,2,256]{3,2,1,0:T(2,128)} %param.11) | copy-start | bytes 1572868
  25.2 7.6 %collective-permute-start.13 = (bf16[128,512]{1,0:T(8,128)(2,1)S(1)}, bf16[128,512]{1,0:T(8,128)(2,1)S(1)}, u32[]{:S(2)}, u32[]{:S(2)}) collective-permute-start(bf16[128,512]{1,0:T(8,128)(2,1)S(1)} %total_1.1), channel_id=1, source_target_pairs={{0,2},{1,3},{2,0},{3,1},{4,6},{5,7},{6,4},{7,5},{8,10},{9,11},{10,... | collective-permute-start | bytes 393224 | tf_op jit(solution)/shard_map/mirror_1/ppermute | solution.py:35

commit v10 on v9

--- a/solution.py
+++ b/solution.py
@@ -92,20 +92,20 @@
     )
 
 
-def owner_columns(chip, sibling, share):
+def owner_columns(chip, sibling, share, some=None):
     me = lax.axis_index("dp")
     core = 1 - me % 2 if sibling else me % 2
     begin = (lax.bitwise_xor(me // 2, chip) * 2 + core) * share
-    return pl.ds(pl.multiple_of(begin, share), share)
-
-
-def sibling_kernel(experts, cuts, route, counts, inputs, hidden, *refs):
-    outs = refs[: len(cuts)]
-    columns, wide, rows, route_now, counts_now, column_sems, sems = refs[len(cuts) :]
+    some = some or slice(0, share)
+    width = some.stop - some.start
+    return pl.ds(pl.multiple_of(begin + some.start, width), width)
+
+
+def sibling_kernel(experts, share, route, counts, inputs, hidden, *refs):
+    out, columns, wide, rows, route_now, counts_now, column_sems, sems = refs
     copies = routed_copies(route, counts, route_now, counts_now, sems)
     copies.append(pltpu.make_async_copy(hidden.at[1], rows, sems.at[2]))
-    chips, _, _ = outs[0].shape
-    share = cuts[-1].stop
+    chips, part, _ = out.shape
     column_copies = []
     for sibling in (True, False):
         for k in range(chips):
@@ -121,9 +121,8 @@
     for copy in column_copies[:chips]:
         copy.wait()
     for k in range(chips):
-        product = contracted(columns[:, owner_columns(k, True, share)], wide[...])
-        for out, some in zip(outs, cuts):
-            out[k] = product[some].astype(out.dtype)
+        place = owner_columns(k, True, share, slice(0, part))
+        out[k] = contracted(columns[:, place], wide[...]).astype(out.dtype)
     for copy in column_copies[chips:]:
         copy.wait()
 
@@ -132,10 +131,10 @@
     _, rows, model = inputs.shape
     width = hidden.shape[2]
     columns = experts * width
-    outs = [pltpu.VMEM((chips, some.stop - some.start, columns), jnp.bfloat16) for some in cuts]
+    outs = [pltpu.VMEM((chips, cuts[0].stop, columns), jnp.bfloat16)]
     outs += [pltpu.VMEM((rows, model), jnp.bfloat16), pltpu.VMEM((rows, columns), jnp.bfloat16)]
     return pl.pallas_call(
-        functools.partial(sibling_kernel, experts, cuts),
+        functools.partial(sibling_kernel, experts, cuts[-1].stop),
         in_specs=[ANYWHERE] * 4,
         out_specs=[IN_VMEM] * len(outs),
         out_shape=outs,
@@ -152,8 +151,9 @@
 
 
 def own_kernel(experts, route, counts, inputs, hidden, columns, wide, *refs):
-    out, ahead, rows, route_now, counts_now, column_sems, sems = refs
+    out, later, ahead, rows, route_now, counts_now, column_sems, sems = refs
     chips, share, _ = out.shape
+    part = later.shape[1]
     model = columns.shape[1]
     copies = routed_copies(route, counts, route_now, counts_now, sems)
     copies.append(pltpu.make_async_copy(hidden.at[0], rows, sems.at[2]))
@@ -164,6 +164,8 @@
     def step(k, carry):
         product = contracted(columns[:, owner_columns(k, False, share)], wide[...])
         out[k] = product.astype(out.dtype)
+        place = owner_columns(k, True, share, slice(share - part, share))
+        later[k] = contracted(columns[:, place], wide[...]).astype(later.dtype)
         return carry
 
     lax.fori_loop(0, chips, step, 0)
@@ -174,14 +176,15 @@
         copy.wait()
 
 
-def own_products(route, counts, inputs, hidden, columns, wide, share, chips, experts):
+def own_products(route, counts, inputs, hidden, columns, wide, share, chips, experts, cuts):
     rows, model = columns.shape
     return pl.pallas_call(
         functools.partial(own_kernel, experts),
         in_specs=[ANYWHERE] * 4 + [IN_VMEM] * 2,
-        out_specs=[IN_VMEM] * 2,
+        out_specs=[IN_VMEM] * 3,
         out_shape=[
             pltpu.VMEM((chips, share, wide.shape[1]), jnp.bfloat16),
+            pltpu.VMEM((chips, share - cuts[0].stop, wide.shape[1]), jnp.bfloat16),
             pltpu.VMEM((rows, model + wide.shape[1]), jnp.bfloat16),
         ],
         scratch_shapes=[
@@ -364,10 +367,11 @@
         return sent
 
     with jax.named_scope("sibling_products"):
-        *sibling, columns, wide = sibling_products(*given, chips, experts, cuts)
-    others = [exchanged(part, "dp", lambda i: 1, f"sibling_{i}") for i, part in enumerate(sibling)]
+        sibling, columns, wide = sibling_products(*given, chips, experts, cuts)
+    others = [exchanged(sibling, "dp", lambda i: 1, "sibling_0")]
     with jax.named_scope("own_products"):
-        own, ahead = own_products(*given, columns, wide, share, chips, experts)
+        own, later, ahead = own_products(*given, columns, wide, share, chips, experts, cuts)
+    others.append(exchanged(later, "dp", lambda i: 1, "sibling_1"))
     parts = []
     for i, (other, some) in enumerate(zip(others, cuts)):
         with jax.named_scope(f"join_{i}"):

time: 34.8 us -> 34.8 us (level)
    ppermute x2, starting transfers between devices: 5.85 us -> 5.44 us  [mirrored(): return lax.ppermute(value, 'section', pairs)]
    ppermute x12, starting transfers between devices: 16.5 us -> 16.9 us  [exchanged(): lax.ppermute(value, axis, [(i, i ^ mask_of(i)) for i in range(count)])]
  transfers between devices with their start and end apart: 14 -> 14, of which waited for: 2 -> 3; matrix products, arithmetic and copies ran while one was open for 0% -> 0% of each run, Pallas kernels for 9% -> 10%
where the time goes in v10:
time: 34.8 us; the launch traced here: 34.7 us
  starting transfers between devices  22.3 us (64%)
  Pallas kernels  6.88 us (20%)
  waiting for transfers between devices  4.78 us (14%)
  between operations  0.71 us (2%)
    ppermute x12, starting transfers between devices, exchanged(): lax.ppermute(value, axis, [(i, i ^ mask_of(i)) for i in range(count)])  16.9 us
    ppermute x2, starting transfers between devices, mirrored(): return lax.ppermute(value, 'section', pairs)  5.44 us
    ppermute x2, waiting for transfers between devices, mirrored(): return lax.ppermute(value, 'section', pairs)  4.35 us
    pallas_call x1, Pallas kernels, sibling_products(): pl.pallas_call(functools.partial(sibling_kernel, experts, cuts[-1].stop),...  1.89 us
    pallas_call x1, Pallas kernels, own_products(): pl.pallas_call(functools.partial(own_kernel, experts), in_specs=[ANYWHERE...  1.81 us
    pallas_call x1, Pallas kernels, updated(): pl.pallas_call(functools.partial(update_kernel, first.shape[1], cuts, mes...  1.53 us
    pallas_call x1, Pallas kernels, paired(): pl.pallas_call(functools.partial(pair_kernel, len(after), messages), in_s...  1.28 us
  transfers between devices with their start and end apart: 14, of which 3 were waited for; matrix products, arithmetic and copies ran while one was open for 0% of the time, Pallas kernels for 10%

profile of v10, /device:TPU:0, one launch (start us, length us, event | category | flops | bytes accessed | tf_op | source)
XLA Modules:
  0.0 34.7 jit_solution(1937277998405387630)
XLA Ops:
  0.6 1.9 %sibling_products.1 = (bf16[4,128,512]{2,1,0:T(8,128)(2,1)S(1)}, bf16[384,2048]{1,0:T(8,128)(2,1)S(1)}, bf16[384,512]{1,0:T(8,128)(2,1)S(1)}) custom-call(s32[2,3]{1,0:T(2,128)} %bitcast.40, s32[2,2]{1,0:T(2,128)} %bitcast.42, bf16[2,384,2048]{2,1,0:T(8,128)(2,1)} %bitcast.36, bf16[2,384,256]{2,1,0:T(8,128)(2,1)} %bitcast.38), custom_call_target="tpu_custom_call" | custom-call | flops 1 | bytes 1 | tf_op jit(solution)/shard_map/sibling_products/pallas_call | solution.py:136
  2.5 0.5 %collective-permute-start = (bf16[4,128,512]{2,1,0:T(8,128)(2,1)S(1)}, bf16[4,128,512]{2,1,0:T(8,128)(2,1)S(1)}, u32[]{:S(2)}, u32[]{:S(2)}) collective-permute-start(bf16[4,128,512]{2,1,0:T(8,128)(2,1)S(1)} %get-tuple-element.30), channel_id=1, source_target_pairs={{0,4},{4,0},{8,12},{12,8},{16,20},{20,16},{24,28},{28,24},{1,5},{5... | collective-permute-start | bytes 1572872 | tf_op jit(solution)/shard_map/sibling_0/ppermute | solution.py:28
  3.0 1.8 %own_products.1 = (bf16[4,256,512]{2,1,0:T(8,128)(2,1)S(1)}, bf16[4,128,512]{2,1,0:T(8,128)(2,1)S(1)}, bf16[384,2560]{1,0:T(8,128)(2,1)S(1)}) custom-call(s32[2,3]{1,0:T(2,128)} %bitcast.41, s32[2,2]{1,0:T(2,128)} %bitcast.43, bf16[2,384,2048]{2,1,0:T(8,128)(2,1)} %bitcast.37, bf16[2,384,256]{2,1,0:T(8,128)(2,1)} %bitcast.39, ...), custom_call_target="tpu_custom_call" | custom-call | flops 1 | bytes 1 | tf_op jit(solution)/shard_map/own_products/pallas_call | solution.py:181
  4.8 0.0 collective-permute-done.received
  4.9 0.1 join_0.1
  5.0 0.2 collective-permute-start.1
  5.2 0.4 %collective-permute-start.9 = (bf16[4,128,512]{2,1,0:T(8,128)(2,1)S(1)}, bf16[4,128,512]{2,1,0:T(8,128)(2,1)S(1)}, u32[]{:S(2)}, u32[]{:S(2)}) collective-permute-start(bf16[4,128,512]{2,1,0:T(8,128)(2,1)S(1)} %get-tuple-element.41), channel_id=1, source_target_pairs={{0,4},{4,0},{8,12},{12,8},{16,20},{20,16},{24,28},{28,24},{1,5},{5... | collective-permute-start | bytes 1572872 | tf_op jit(solution)/shard_map/sibling_1/ppermute | solution.py:28
  5.6 2.7 %collective-permute-start.2 = (bf16[128,512]{1,0:T(8,128)(2,1)S(1)}, bf16[128,512]{1,0:T(8,128)(2,1)S(1)}, u32[]{:S(2)}, u32[]{:S(2)}) collective-permute-start(bf16[128,512]{1,0:T(8,128)(2,1)S(1)} %get-tuple-element.33), channel_id=1, source_target_pairs={{0,16},{4,12},{8,24},{12,4},{16,0},{20,28},{24,8},{28,20},{1,17},{... | collective-permute-start | bytes 393224 | tf_op jit(solution)/shard_map/one_part_0_to_chip_2/ppermute | solution.py:28
  8.2 1.5 %collective-permute-start.6 = (bf16[128,512]{1,0:T(8,128)(2,1)S(1)}, bf16[128,512]{1,0:T(8,128)(2,1)S(1)}, u32[]{:S(2)}, u32[]{:S(2)}) collective-permute-start(bf16[128,512]{1,0:T(8,128)(2,1)S(1)} %get-tuple-element.39), channel_id=1, source_target_pairs={{0,8},{4,20},{8,0},{12,28},{16,24},{20,4},{24,16},{28,12},{1,9},{5... | collective-permute-start | bytes 393224 | tf_op jit(solution)/shard_map/one_part_0_to_chip_1/ppermute | solution.py:28
  9.7 0.0 collective-permute-start.7
  9.7 0.1 collective-permute-done.9.received
  9.8 0.1 join_1.1
  9.9 2.8 %collective-permute-start.10 = (bf16[128,512]{1,0:T(8,128)(2,1)S(1)}, bf16[128,512]{1,0:T(8,128)(2,1)S(1)}, u32[]{:S(2)}, u32[]{:S(2)}) collective-permute-start(bf16[128,512]{1,0:T(8,128)(2,1)S(1)} %get-tuple-element.43), channel_id=1, source_target_pairs={{0,8},{4,12},{8,0},{12,4},{16,24},{20,28},{24,16},{28,20},{1,9},{5... | collective-permute-start | bytes 393224 | tf_op jit(solution)/shard_map/one_part_1_to_chip_1/ppermute | solution.py:28
  12.6 0.0 collective-permute-done.2.refs_0_.refs_1_
  12.6 1.7 %collective-permute-start.11 = (bf16[128,512]{1,0:T(8,128)(2,1)S(1)}, bf16[128,512]{1,0:T(8,128)(2,1)S(1)}, u32[]{:S(2)}, u32[]{:S(2)}) collective-permute-start(bf16[128,512]{1,0:T(8,128)(2,1)S(1)} %get-tuple-element.44), channel_id=1, source_target_pairs={{0,16},{4,20},{8,24},{12,28},{16,0},{20,4},{24,8},{28,12},{1,17},{... | collective-permute-start | bytes 393224 | tf_op jit(solution)/shard_map/one_part_1_to_chip_2/ppermute | solution.py:28
  14.3 0.0 collective-permute-done.1.other
  14.3 3.2 %collective-permute-start.12 = (bf16[128,512]{1,0:T(8,128)(2,1)S(1)}, bf16[128,512]{1,0:T(8,128)(2,1)S(1)}, u32[]{:S(2)}, u32[]{:S(2)}) collective-permute-start(bf16[128,512]{1,0:T(8,128)(2,1)S(1)} %get-tuple-element.45), channel_id=1, source_target_pairs={{0,24},{4,28},{8,16},{12,20},{16,8},{20,12},{24,0},{28,4},{1,25},{... | collective-permute-start | bytes 393224 | tf_op jit(solution)/shard_map/one_part_1_to_chip_3/ppermute | solution.py:28
  17.5 1.3 %pair.1 = (f32[256,512]{1,0:T(8,128)S(1)}, bf16[256,512]{1,0:T(8,128)(2,1)S(1)}, bf16[256,512]{1,0:T(8,128)(2,1)S(1)}, bf16[256,512]{1,0:T(8,128)(2,1)S(1)}) custom-call(bf16[384,2560]{1,0:T(8,128)(2,1)S(1)} %get-tuple-element.32.ahead, bf16[384,2560]{1,0:T(8,128)(2,1)S(1)} %collective-permute-done.1.other, ...), custom_call_target="tpu_custom_call" | custom-call | flops 1 | bytes 1 | tf_op jit(solution)/shard_map/pair/pallas_call | solution.py:247
  18.8 0.0 collective-permute-done.6.refs_0_
  18.8 0.0 collective-permute-done.7.refs_2_
  18.8 0.1 total_0.1
  18.9 2.4 %collective-permute-start.8 = (bf16[128,512]{1,0:T(8,128)(2,1)S(1)}, bf16[128,512]{1,0:T(8,128)(2,1)S(1)}, u32[]{:S(2)}, u32[]{:S(2)}) collective-permute-start(bf16[128,512]{1,0:T(8,128)(2,1)S(1)} %total_0.1), channel_id=1, source_target_pairs={{0,2},{1,3},{2,0},{3,1},{4,6},{5,7},{6,4},{7,5},{8,10},{9,11},{10,... | collective-permute-start | bytes 393224 | tf_op jit(solution)/shard_map/mirror_0/ppermute | solution.py:35
  21.3 0.6 %collective-permute-start.3 = (bf16[256,512]{1,0:T(8,128)(2,1)S(1)}, bf16[256,512]{1,0:T(8,128)(2,1)S(1)}, u32[]{:S(2)}, u32[]{:S(2)}) collective-permute-start(bf16[256,512]{1,0:T(8,128)(2,1)S(1)} %get-tuple-element.35), channel_id=1, source_target_pairs={{0,8},{4,20},{8,0},{12,28},{16,24},{20,4},{24,16},{28,12},{1,9},{5... | collective-permute-start | bytes 786440 | tf_op jit(solution)/shard_map/zero_to_chip_1/ppermute | solution.py:28
  21.9 0.0 collective-permute-done.10.refs_0_
  21.9 1.5 %collective-permute-start.4 = (bf16[256,512]{1,0:T(8,128)(2,1)S(1)}, bf16[256,512]{1,0:T(8,128)(2,1)S(1)}, u32[]{:S(2)}, u32[]{:S(2)}) collective-permute-start(bf16[256,512]{1,0:T(8,128)(2,1)S(1)} %get-tuple-element.36), channel_id=1, source_target_pairs={{0,16},{4,12},{8,24},{12,4},{16,0},{20,28},{24,8},{28,20},{1,17},{... | collective-permute-start | bytes 786440 | tf_op jit(solution)/shard_map/zero_to_chip_2/ppermute | solution.py:28
  23.4 0.0 collective-permute-done.11.refs_1_
  23.4 2.0 %collective-permute-start.5 = (bf16[256,512]{1,0:T(8,128)(2,1)S(1)}, bf16[256,512]{1,0:T(8,128)(2,1)S(1)}, u32[]{:S(2)}, u32[]{:S(2)}) collective-permute-start(bf16[256,512]{1,0:T(8,128)(2,1)S(1)} %get-tuple-element.37), channel_id=1, source_target_pairs={{0,24},{4,28},{8,16},{12,20},{16,8},{20,12},{24,0},{28,4},{1,25},{... | collective-permute-start | bytes 786440 | tf_op jit(solution)/shard_map/zero_to_chip_3/ppermute | solution.py:28
  25.4 0.0 collective-permute-done.12.refs_2_
  25.4 0.0 copy-start
  25.4 0.0 copy-start.1
  25.4 0.1 total_1.1
  25.4 3.0 %collective-permute-start.13 = (bf16[128,512]{1,0:T(8,128)(2,1)S(1)}, bf16[128,512]{1,0:T(8,128)(2,1)S(1)}, u32[]{:S(2)}, u32[]{:S(2)}) collective-permute-start(bf16[128,512]{1,0:T(8,128)(2,1)S(1)} %total_1.1), channel_id=1, source_target_pairs={{0,2},{1,3},{2,0},{3,1},{4,6},{5,7},{6,4},{7,5},{8,10},{9,11},{10,... | collective-permute-start | bytes 393224 | tf_op jit(solution)/shard_map/mirror_1/ppermute | solution.py:35
  28.4 0.0 collective-permute-done.8.refs_3_
  28.5 4.3 %collective-permute-done.13.refs_4_ = bf16[128,512]{1,0:T(8,128)(2,1)S(1)} collective-permute-done((bf16[128,512]{1,0:T(8,128)(2,1)S(1)}, bf16[128,512]{1,0:T(8,128)(2,1)S(1)}, u32[]{:S(2)}, u32[]{:S(2)}) %collective-permute-start.13) | collective-permute-done | bytes 131104 | tf_op jit(solution)/shard_map/mirror_1/ppermute | solution.py:35
  32.8 0.0 collective-permute-done.3.refs_0_
  32.8 0.0 collective-permute-done.4.refs_1_
  32.8 0.4 %collective-permute-done.5.refs_2_ = bf16[256,512]{1,0:T(8,128)(2,1)S(1)} collective-permute-done((bf16[256,512]{1,0:T(8,128)(2,1)S(1)}, bf16[256,512]{1,0:T(8,128)(2,1)S(1)}, u32[]{:S(2)}, u32[]{:S(2)}) %collective-permute-start.5) | collective-permute-done | bytes 262176 | tf_op jit(solution)/shard_map/zero_to_chip_3/ppermute | solution.py:28
  33.2 0.0 copy-done
  33.2 0.0 copy-done.1
  33.2 1.5 %update.1 = (f32[1024,128]{1,0:T(8,128)}, f32[1024,128]{1,0:T(8,128)}, f32[1024,128]{1,0:T(8,128)}, f32[1024,128]{1,0:T(8,128)}) custom-call(f32[256,512]{1,0:T(8,128)S(1)} %get-tuple-element.34.refs_3_.kept, bf16[256,512]{1,0:T(8,128)(2,1)S(1)} %collective-permute-done.3.refs_0_, bf16[256,512]{1,0:T(8,128)(2,1)S(1)} %collective-permute-done.4.refs_1_, ...), custom_call_target="tpu_custom_call" | custom-call | flops 1 | bytes 1 | tf_op jit(solution)/shard_map/update/pallas_call | solution.py:340
Async XLA Ops:
  2.5 2.3 %collective-permute-start = (bf16[4,128,512]{2,1,0:T(8,128)(2,1)S(1)}, bf16[4,128,512]{2,1,0:T(8,128)(2,1)S(1)}, u32[]{:S(2)}, u32[]{:S(2)}) collective-permute-start(bf16[4,128,512]{2,1,0:T(8,128)(2,1)S(1)} %get-tuple-element.30), channel_id=1, source_target_pairs={{0,4},{4,0},{8,12},{12,8},{16,20},{20,16},{24,28},{28,24},{1,5},{5... | collective-permute-start | bytes 1572872 | tf_op jit(solution)/shard_map/sibling_0/ppermute | solution.py:28
  5.0 9.3 %collective-permute-start.1 = (bf16[384,2560]{1,0:T(8,128)(2,1)S(1)}, bf16[384,2560]{1,0:T(8,128)(2,1)S(1)}, u32[]{:S(2)}, u32[]{:S(2)}) collective-permute-start(bf16[384,2560]{1,0:T(8,128)(2,1)S(1)} %get-tuple-element.32.ahead), channel_id=1, source_target_pairs={{0,4},{4,0},{8,12},{12,8},{16,20},{20,16},{24,28},{28,24},{1,5},{5... | collective-permute-start | bytes 5898248 | tf_op jit(solution)/shard_map/operand_exchange/ppermute | solution.py:28
  5.2 4.6 %collective-permute-start.9 = (bf16[4,128,512]{2,1,0:T(8,128)(2,1)S(1)}, bf16[4,128,512]{2,1,0:T(8,128)(2,1)S(1)}, u32[]{:S(2)}, u32[]{:S(2)}) collective-permute-start(bf16[4,128,512]{2,1,0:T(8,128)(2,1)S(1)} %get-tuple-element.41), channel_id=1, source_target_pairs={{0,4},{4,0},{8,12},{12,8},{16,20},{20,16},{24,28},{28,24},{1,5},{5... | collective-permute-start | bytes 1572872 | tf_op jit(solution)/shard_map/sibling_1/ppermute | solution.py:28
  5.6 7.1 %collective-permute-start.2 = (bf16[128,512]{1,0:T(8,128)(2,1)S(1)}, bf16[128,512]{1,0:T(8,128)(2,1)S(1)}, u32[]{:S(2)}, u32[]{:S(2)}) collective-permute-start(bf16[128,512]{1,0:T(8,128)(2,1)S(1)} %get-tuple-element.33), channel_id=1, source_target_pairs={{0,16},{4,12},{8,24},{12,4},{16,0},{20,28},{24,8},{28,20},{1,17},{... | collective-permute-start | bytes 393224 | tf_op jit(solution)/shard_map/one_part_0_to_chip_2/ppermute | solution.py:28
  8.2 10.6 %collective-permute-start.6 = (bf16[128,512]{1,0:T(8,128)(2,1)S(1)}, bf16[128,512]{1,0:T(8,128)(2,1)S(1)}, u32[]{:S(2)}, u32[]{:S(2)}) collective-permute-start(bf16[128,512]{1,0:T(8,128)(2,1)S(1)} %get-tuple-element.39), channel_id=1, source_target_pairs={{0,8},{4,20},{8,0},{12,28},{16,24},{20,4},{24,16},{28,12},{1,9},{5... | collective-permute-start | bytes 393224 | tf_op jit(solution)/shard_map/one_part_0_to_chip_1/ppermute | solution.py:28
  9.7 9.1 %collective-permute-start.7 = (bf16[128,512]{1,0:T(8,128)(2,1)S(1)}, bf16[128,512]{1,0:T(8,128)(2,1)S(1)}, u32[]{:S(2)}, u32[]{:S(2)}) collective-permute-start(bf16[128,512]{1,0:T(8,128)(2,1)S(1)} %get-tuple-element.40), channel_id=1, source_target_pairs={{0,24},{4,28},{8,16},{12,20},{16,8},{20,12},{24,0},{28,4},{1,25},{... | collective-permute-start | bytes 393224 | tf_op jit(solution)/shard_map/one_part_0_to_chip_3/ppermute | solution.py:28
  9.9 12.0 %collective-permute-start.10 = (bf16[128,512]{1,0:T(8,128)(2,1)S(1)}, bf16[128,512]{1,0:T(8,128)(2,1)S(1)}, u32[]{:S(2)}, u32[]{:S(2)}) collective-permute-start(bf16[128,512]{1,0:T(8,128)(2,1)S(1)} %get-tuple-element.43), channel_id=1, source_target_pairs={{0,8},{4,12},{8,0},{12,4},{16,24},{20,28},{24,16},{28,20},{1,9},{5... | collective-permute-start | bytes 393224 | tf_op jit(solution)/shard_map/one_part_1_to_chip_1/ppermute | solution.py:28
  12.6 10.7 %collective-permute-start.11 = (bf16[128,512]{1,0:T(8,128)(2,1)S(1)}, bf16[128,512]{1,0:T(8,128)(2,1)S(1)}, u32[]{:S(2)}, u32[]{:S(2)}) collective-permute-start(bf16[128,512]{1,0:T(8,128)(2,1)S(1)} %get-tuple-element.44), channel_id=1, source_target_pairs={{0,16},{4,20},{8,24},{12,28},{16,0},{20,4},{24,8},{28,12},{1,17},{... | collective-permute-start | bytes 393224 | tf_op jit(solution)/shard_map/one_part_1_to_chip_2/ppermute | solution.py:28
  14.3 11.0 %collective-permute-start.12 = (bf16[128,512]{1,0:T(8,128)(2,1)S(1)}, bf16[128,512]{1,0:T(8,128)(2,1)S(1)}, u32[]{:S(2)}, u32[]{:S(2)}) collective-permute-start(bf16[128,512]{1,0:T(8,128)(2,1)S(1)} %get-tuple-element.45), channel_id=1, source_target_pairs={{0,24},{4,28},{8,16},{12,20},{16,8},{20,12},{24,0},{28,4},{1,25},{... | collective-permute-start | bytes 393224 | tf_op jit(solution)/shard_map/one_part_1_to_chip_3/ppermute | solution.py:28
  18.9 9.6 %collective-permute-start.8 = (bf16[128,512]{1,0:T(8,128)(2,1)S(1)}, bf16[128,512]{1,0:T(8,128)(2,1)S(1)}, u32[]{:S(2)}, u32[]{:S(2)}) collective-permute-start(bf16[128,512]{1,0:T(8,128)(2,1)S(1)} %total_0.1), channel_id=1, source_target_pairs={{0,2},{1,3},{2,0},{3,1},{4,6},{5,7},{6,4},{7,5},{8,10},{9,11},{10,... | collective-permute-start | bytes 393224 | tf_op jit(solution)/shard_map/mirror_0/ppermute | solution.py:35
  21.3 11.5 %collective-permute-start.3 = (bf16[256,512]{1,0:T(8,128)(2,1)S(1)}, bf16[256,512]{1,0:T(8,128)(2,1)S(1)}, u32[]{:S(2)}, u32[]{:S(2)}) collective-permute-start(bf16[256,512]{1,0:T(8,128)(2,1)S(1)} %get-tuple-element.35), channel_id=1, source_target_pairs={{0,8},{4,20},{8,0},{12,28},{16,24},{20,4},{24,16},{28,12},{1,9},{5... | collective-permute-start | bytes 786440 | tf_op jit(solution)/shard_map/zero_to_chip_1/ppermute | solution.py:28
  21.9 10.9 %collective-permute-start.4 = (bf16[256,512]{1,0:T(8,128)(2,1)S(1)}, bf16[256,512]{1,0:T(8,128)(2,1)S(1)}, u32[]{:S(2)}, u32[]{:S(2)}) collective-permute-start(bf16[256,512]{1,0:T(8,128)(2,1)S(1)} %get-tuple-element.36), channel_id=1, source_target_pairs={{0,16},{4,12},{8,24},{12,4},{16,0},{20,28},{24,8},{28,20},{1,17},{... | collective-permute-start | bytes 786440 | tf_op jit(solution)/shard_map/zero_to_chip_2/ppermute | solution.py:28
  23.4 9.8 %collective-permute-start.5 = (bf16[256,512]{1,0:T(8,128)(2,1)S(1)}, bf16[256,512]{1,0:T(8,128)(2,1)S(1)}, u32[]{:S(2)}, u32[]{:S(2)}) collective-permute-start(bf16[256,512]{1,0:T(8,128)(2,1)S(1)} %get-tuple-element.37), channel_id=1, source_target_pairs={{0,24},{4,28},{8,16},{12,20},{16,8},{20,12},{24,0},{28,4},{1,25},{... | collective-permute-start | bytes 786440 | tf_op jit(solution)/shard_map/zero_to_chip_3/ppermute | solution.py:28
  25.4 7.8 %copy-start = (f32[1,256,2,256]{3,2,1,0:T(2,128)S(1)}, f32[1,256,2,256]{3,2,1,0:T(2,128)}, u32[]{:S(2)}) copy-start(f32[1,256,2,256]{3,2,1,0:T(2,128)} %param.10) | copy-start | bytes 1572868
  25.4 7.8 %copy-start.1 = (f32[1,256,2,256]{3,2,1,0:T(2,128)S(1)}, f32[1,256,2,256]{3,2,1,0:T(2,128)}, u32[]{:S(2)}) copy-start(f32[1,256,2,256]{3,2,1,0:T(2,128)} %param.11) | copy-start | bytes 1572868
  25.4 7.4 %collective-permute-start.13 = (bf16[128,512]{1,0:T(8,128)(2,1)S(1)}, bf16[128,512]{1,0:T(8,128)(2,1)S(1)}, u32[]{:S(2)}, u32[]{:S(2)}) collective-permute-start(bf16[128,512]{1,0:T(8,128)(2,1)S(1)} %total_1.1), channel_id=1, source_target_pairs={{0,2},{1,3},{2,0},{3,1},{4,6},{5,7},{6,4},{7,5},{8,10},{9,11},{10,... | collective-permute-start | bytes 393224 | tf_op jit(solution)/shard_map/mirror_1/ppermute | solution.py:35

commit v11 on v10

--- a/solution.py
+++ b/solution.py
@@ -161,14 +161,15 @@
     for copy in copies + column_copies:
         copy.start()
 
-    def step(k, carry):
-        product = contracted(columns[:, owner_columns(k, False, share)], wide[...])
-        out[k] = product.astype(out.dtype)
-        place = owner_columns(k, True, share, slice(share - part, share))
-        later[k] = contracted(columns[:, place], wide[...]).astype(later.dtype)
+    def step(i, carry):
+        for k in (2 * i, 2 * i + 1):
+            product = contracted(columns[:, owner_columns(k, False, share)], wide[...])
+            out[k] = product.astype(out.dtype)
+            place = owner_columns(k, True, share, slice(share - part, share))
+            later[k] = contracted(columns[:, place], wide[...]).astype(later.dtype)
         return carry
 
-    lax.fori_loop(0, chips, step, 0)
+    lax.fori_loop(0, chips // 2, step, 0)
     for copy in copies:
         copy.wait()
     expand_hidden(route_now, counts_now, 0, rows, ahead.at[:, model:], route.shape[1], experts)

time: 34.8 us -> 34.6 us (level)
  Pallas kernels: 6.88 us -> 6.53 us
    ppermute x12, starting transfers between devices: 16.9 us -> 16.5 us  [exchanged(): lax.ppermute(value, axis, [(i, i ^ mask_of(i)) for i in range(count)])]
    ppermute x2, starting transfers between devices: 5.44 us -> 5.81 us  [mirrored(): return lax.ppermute(value, 'section', pairs)]
  transfers between devices with their start and end apart: 14 -> 14, of which waited for: 3 -> 3; matrix products, arithmetic and copies ran while one was open for 0% -> 0% of each run, Pallas kernels for 10% -> 9%
where the time goes in v11:
time: 34.6 us; the launch traced here: 34.4 us
  starting transfers between devices  22.3 us (64%)
  Pallas kernels  6.53 us (19%)
  waiting for transfers between devices  4.85 us (14%)
  between operations  0.7 us (2%)
    ppermute x12, starting transfers between devices, exchanged(): lax.ppermute(value, axis, [(i, i ^ mask_of(i)) for i in range(count)])  16.5 us
    ppermute x2, starting transfers between devices, mirrored(): return lax.ppermute(value, 'section', pairs)  5.81 us
    ppermute x2, waiting for transfers between devices, mirrored(): return lax.ppermute(value, 'section', pairs)  4.35 us
    pallas_call x1, Pallas kernels, sibling_products(): pl.pallas_call(functools.partial(sibling_kernel, experts, cuts[-1].stop),...  1.89 us
    pallas_call x1, Pallas kernels, updated(): pl.pallas_call(functools.partial(update_kernel, first.shape[1], cuts, mes...  1.53 us
    pallas_call x1, Pallas kernels, own_products(): pl.pallas_call(functools.partial(own_kernel, experts), in_specs=[ANYWHERE...  1.47 us
    pallas_call x1, Pallas kernels, paired(): pl.pallas_call(functools.partial(pair_kernel, len(after), messages), in_s...  1.28 us
  transfers between devices with their start and end apart: 14, of which 3 were waited for; matrix products, arithmetic and copies ran while one was open for 0% of the time, Pallas kernels for 9%

profile of v11, /device:TPU:0, one launch (start us, length us, event | category | flops | bytes accessed | tf_op | source)
XLA Modules:
  0.0 34.4 jit_solution(12813294182088410002)
XLA Ops:
  0.6 1.9 %sibling_products.1 = (bf16[4,128,512]{2,1,0:T(8,128)(2,1)S(1)}, bf16[384,2048]{1,0:T(8,128)(2,1)S(1)}, bf16[384,512]{1,0:T(8,128)(2,1)S(1)}) custom-call(s32[2,3]{1,0:T(2,128)} %bitcast.40, s32[2,2]{1,0:T(2,128)} %bitcast.42, bf16[2,384,2048]{2,1,0:T(8,128)(2,1)} %bitcast.36, bf16[2,384,256]{2,1,0:T(8,128)(2,1)} %bitcast.38), custom_call_target="tpu_custom_call" | custom-call | flops 1 | bytes 1 | tf_op jit(solution)/shard_map/sibling_products/pallas_call | solution.py:136
  2.5 0.5 %collective-permute-start = (bf16[4,128,512]{2,1,0:T(8,128)(2,1)S(1)}, bf16[4,128,512]{2,1,0:T(8,128)(2,1)S(1)}, u32[]{:S(2)}, u32[]{:S(2)}) collective-permute-start(bf16[4,128,512]{2,1,0:T(8,128)(2,1)S(1)} %get-tuple-element.30), channel_id=1, source_target_pairs={{0,4},{4,0},{8,12},{12,8},{16,20},{20,16},{24,28},{28,24},{1,5},{5... | collective-permute-start | bytes 1572872 | tf_op jit(solution)/shard_map/sibling_0/ppermute | solution.py:28
  3.0 1.5 %own_products.1 = (bf16[4,256,512]{2,1,0:T(8,128)(2,1)S(1)}, bf16[4,128,512]{2,1,0:T(8,128)(2,1)S(1)}, bf16[384,2560]{1,0:T(8,128)(2,1)S(1)}) custom-call(s32[2,3]{1,0:T(2,128)} %bitcast.41, s32[2,2]{1,0:T(2,128)} %bitcast.43, bf16[2,384,2048]{2,1,0:T(8,128)(2,1)} %bitcast.37, bf16[2,384,256]{2,1,0:T(8,128)(2,1)} %bitcast.39, ...), custom_call_target="tpu_custom_call" | custom-call | flops 1 | bytes 1 | tf_op jit(solution)/shard_map/own_products/pallas_call | solution.py:182
  4.5 0.1 collective-permute-done.received
  4.6 0.1 join_0.1
  4.7 0.4 %collective-permute-start.1 = (bf16[384,2560]{1,0:T(8,128)(2,1)S(1)}, bf16[384,2560]{1,0:T(8,128)(2,1)S(1)}, u32[]{:S(2)}, u32[]{:S(2)}) collective-permute-start(bf16[384,2560]{1,0:T(8,128)(2,1)S(1)} %get-tuple-element.32.ahead), channel_id=1, source_target_pairs={{0,4},{4,0},{8,12},{12,8},{16,20},{20,16},{24,28},{28,24},{1,5},{5... | collective-permute-start | bytes 5898248 | tf_op jit(solution)/shard_map/operand_exchange/ppermute | solution.py:28
  5.1 0.1 collective-permute-start.9
  5.3 2.9 %collective-permute-start.2 = (bf16[128,512]{1,0:T(8,128)(2,1)S(1)}, bf16[128,512]{1,0:T(8,128)(2,1)S(1)}, u32[]{:S(2)}, u32[]{:S(2)}) collective-permute-start(bf16[128,512]{1,0:T(8,128)(2,1)S(1)} %get-tuple-element.33), channel_id=1, source_target_pairs={{0,16},{4,12},{8,24},{12,4},{16,0},{20,28},{24,8},{28,20},{1,17},{... | collective-permute-start | bytes 393224 | tf_op jit(solution)/shard_map/one_part_0_to_chip_2/ppermute | solution.py:28
  8.2 1.5 %collective-permute-start.6 = (bf16[128,512]{1,0:T(8,128)(2,1)S(1)}, bf16[128,512]{1,0:T(8,128)(2,1)S(1)}, u32[]{:S(2)}, u32[]{:S(2)}) collective-permute-start(bf16[128,512]{1,0:T(8,128)(2,1)S(1)} %get-tuple-element.39), channel_id=1, source_target_pairs={{0,8},{4,20},{8,0},{12,28},{16,24},{20,4},{24,16},{28,12},{1,9},{5... | collective-permute-start | bytes 393224 | tf_op jit(solution)/shard_map/one_part_0_to_chip_1/ppermute | solution.py:28
  9.7 0.0 collective-permute-start.7
  9.7 0.0 collective-permute-done.9.received
  9.7 0.1 join_1.1
  9.8 2.7 %collective-permute-start.10 = (bf16[128,512]{1,0:T(8,128)(2,1)S(1)}, bf16[128,512]{1,0:T(8,128)(2,1)S(1)}, u32[]{:S(2)}, u32[]{:S(2)}) collective-permute-start(bf16[128,512]{1,0:T(8,128)(2,1)S(1)} %get-tuple-element.43), channel_id=1, source_target_pairs={{0,8},{4,12},{8,0},{12,4},{16,24},{20,28},{24,16},{28,20},{1,9},{5... | collective-permute-start | bytes 393224 | tf_op jit(solution)/shard_map/one_part_1_to_chip_1/ppermute | solution.py:28
  12.5 0.0 collective-permute-done.2.refs_0_.refs_1_
  12.5 2.7 %collective-permute-start.11 = (bf16[128,512]{1,0:T(8,128)(2,1)S(1)}, bf16[128,512]{1,0:T(8,128)(2,1)S(1)}, u32[]{:S(2)}, u32[]{:S(2)}) collective-permute-start(bf16[128,512]{1,0:T(8,128)(2,1)S(1)} %get-tuple-element.44), channel_id=1, source_target_pairs={{0,16},{4,20},{8,24},{12,28},{16,0},{20,4},{24,8},{28,12},{1,17},{... | collective-permute-start | bytes 393224 | tf_op jit(solution)/shard_map/one_part_1_to_chip_2/ppermute | solution.py:28
  15.3 0.0 collective-permute-done.1.other
  15.3 1.7 %collective-permute-start.12 = (bf16[128,512]{1,0:T(8,128)(2,1)S(1)}, bf16[128,512]{1,0:T(8,128)(2,1)S(1)}, u32[]{:S(2)}, u32[]{:S(2)}) collective-permute-start(bf16[128,512]{1,0:T(8,128)(2,1)S(1)} %get-tuple-element.45), channel_id=1, source_target_pairs={{0,24},{4,28},{8,16},{12,20},{16,8},{20,12},{24,0},{28,4},{1,25},{... | collective-permute-start | bytes 393224 | tf_op jit(solution)/shard_map/one_part_1_to_chip_3/ppermute | solution.py:28
  17.0 1.3 %pair.1 = (f32[256,512]{1,0:T(8,128)S(1)}, bf16[256,512]{1,0:T(8,128)(2,1)S(1)}, bf16[256,512]{1,0:T(8,128)(2,1)S(1)}, bf16[256,512]{1,0:T(8,128)(2,1)S(1)}) custom-call(bf16[384,2560]{1,0:T(8,128)(2,1)S(1)} %get-tuple-element.32.ahead, bf16[384,2560]{1,0:T(8,128)(2,1)S(1)} %collective-permute-done.1.other, ...), custom_call_target="tpu_custom_call" | custom-call | flops 1 | bytes 1 | tf_op jit(solution)/shard_map/pair/pallas_call | solution.py:248
  18.2 0.0 collective-permute-done.6.refs_0_
  18.3 0.0 collective-permute-done.7.refs_2_
  18.3 0.1 total_0.1
  18.3 2.6 %collective-permute-start.8 = (bf16[128,512]{1,0:T(8,128)(2,1)S(1)}, bf16[128,512]{1,0:T(8,128)(2,1)S(1)}, u32[]{:S(2)}, u32[]{:S(2)}) collective-permute-start(bf16[128,512]{1,0:T(8,128)(2,1)S(1)} %total_0.1), channel_id=1, source_target_pairs={{0,2},{1,3},{2,0},{3,1},{4,6},{5,7},{6,4},{7,5},{8,10},{9,11},{10,... | collective-permute-start | bytes 393224 | tf_op jit(solution)/shard_map/mirror_0/ppermute | solution.py:35
  20.9 0.6 %collective-permute-start.3 = (bf16[256,512]{1,0:T(8,128)(2,1)S(1)}, bf16[256,512]{1,0:T(8,128)(2,1)S(1)}, u32[]{:S(2)}, u32[]{:S(2)}) collective-permute-start(bf16[256,512]{1,0:T(8,128)(2,1)S(1)} %get-tuple-element.35), channel_id=1, source_target_pairs={{0,8},{4,20},{8,0},{12,28},{16,24},{20,4},{24,16},{28,12},{1,9},{5... | collective-permute-start | bytes 786440 | tf_op jit(solution)/shard_map/zero_to_chip_1/ppermute | solution.py:28
  21.5 0.0 collective-permute-done.10.refs_0_
  21.5 1.5 %collective-permute-start.4 = (bf16[256,512]{1,0:T(8,128)(2,1)S(1)}, bf16[256,512]{1,0:T(8,128)(2,1)S(1)}, u32[]{:S(2)}, u32[]{:S(2)}) collective-permute-start(bf16[256,512]{1,0:T(8,128)(2,1)S(1)} %get-tuple-element.36), channel_id=1, source_target_pairs={{0,16},{4,12},{8,24},{12,4},{16,0},{20,28},{24,8},{28,20},{1,17},{... | collective-permute-start | bytes 786440 | tf_op jit(solution)/shard_map/zero_to_chip_2/ppermute | solution.py:28
  23.0 0.0 collective-permute-done.11.refs_1_
  23.0 1.8 %collective-permute-start.5 = (bf16[256,512]{1,0:T(8,128)(2,1)S(1)}, bf16[256,512]{1,0:T(8,128)(2,1)S(1)}, u32[]{:S(2)}, u32[]{:S(2)}) collective-permute-start(bf16[256,512]{1,0:T(8,128)(2,1)S(1)} %get-tuple-element.37), channel_id=1, source_target_pairs={{0,24},{4,28},{8,16},{12,20},{16,8},{20,12},{24,0},{28,4},{1,25},{... | collective-permute-start | bytes 786440 | tf_op jit(solution)/shard_map/zero_to_chip_3/ppermute | solution.py:28
  24.8 0.0 collective-permute-done.12.refs_2_
  24.8 0.0 copy-start
  24.8 0.0 copy-start.1
  24.8 0.1 total_1.1
  24.9 3.2 %collective-permute-start.13 = (bf16[128,512]{1,0:T(8,128)(2,1)S(1)}, bf16[128,512]{1,0:T(8,128)(2,1)S(1)}, u32[]{:S(2)}, u32[]{:S(2)}) collective-permute-start(bf16[128,512]{1,0:T(8,128)(2,1)S(1)} %total_1.1), channel_id=1, source_target_pairs={{0,2},{1,3},{2,0},{3,1},{4,6},{5,7},{6,4},{7,5},{8,10},{9,11},{10,... | collective-permute-start | bytes 393224 | tf_op jit(solution)/shard_map/mirror_1/ppermute | solution.py:35
  28.1 0.0 collective-permute-done.8.refs_3_
  28.1 4.3 %collective-permute-done.13.refs_4_ = bf16[128,512]{1,0:T(8,128)(2,1)S(1)} collective-permute-done((bf16[128,512]{1,0:T(8,128)(2,1)S(1)}, bf16[128,512]{1,0:T(8,128)(2,1)S(1)}, u32[]{:S(2)}, u32[]{:S(2)}) %collective-permute-start.13) | collective-permute-done | bytes 131104 | tf_op jit(solution)/shard_map/mirror_1/ppermute | solution.py:35
  32.4 0.0 collective-permute-done.3.refs_0_
  32.4 0.0 collective-permute-done.4.refs_1_
  32.4 0.4 %collective-permute-done.5.refs_2_ = bf16[256,512]{1,0:T(8,128)(2,1)S(1)} collective-permute-done((bf16[256,512]{1,0:T(8,128)(2,1)S(1)}, bf16[256,512]{1,0:T(8,128)(2,1)S(1)}, u32[]{:S(2)}, u32[]{:S(2)}) %collective-permute-start.5) | collective-permute-done | bytes 262176 | tf_op jit(solution)/shard_map/zero_to_chip_3/ppermute | solution.py:28
  32.9 0.0 copy-done
  32.9 0.0 copy-done.1
  32.9 1.5 %update.1 = (f32[1024,128]{1,0:T(8,128)}, f32[1024,128]{1,0:T(8,128)}, f32[1024,128]{1,0:T(8,128)}, f32[1024,128]{1,0:T(8,128)}) custom-call(f32[256,512]{1,0:T(8,128)S(1)} %get-tuple-element.34.refs_3_.kept, bf16[256,512]{1,0:T(8,128)(2,1)S(1)} %collective-permute-done.3.refs_0_, bf16[256,512]{1,0:T(8,128)(2,1)S(1)} %collective-permute-done.4.refs_1_, ...), custom_call_target="tpu_custom_call" | custom-call | flops 1 | bytes 1 | tf_op jit(solution)/shard_map/update/pallas_call | solution.py:341
Async XLA Ops:
  2.5 2.0 %collective-permute-start = (bf16[4,128,512]{2,1,0:T(8,128)(2,1)S(1)}, bf16[4,128,512]{2,1,0:T(8,128)(2,1)S(1)}, u32[]{:S(2)}, u32[]{:S(2)}) collective-permute-start(bf16[4,128,512]{2,1,0:T(8,128)(2,1)S(1)} %get-tuple-element.30), channel_id=1, source_target_pairs={{0,4},{4,0},{8,12},{12,8},{16,20},{20,16},{24,28},{28,24},{1,5},{5... | collective-permute-start | bytes 1572872 | tf_op jit(solution)/shard_map/sibling_0/ppermute | solution.py:28
  4.7 10.6 %collective-permute-start.1 = (bf16[384,2560]{1,0:T(8,128)(2,1)S(1)}, bf16[384,2560]{1,0:T(8,128)(2,1)S(1)}, u32[]{:S(2)}, u32[]{:S(2)}) collective-permute-start(bf16[384,2560]{1,0:T(8,128)(2,1)S(1)} %get-tuple-element.32.ahead), channel_id=1, source_target_pairs={{0,4},{4,0},{8,12},{12,8},{16,20},{20,16},{24,28},{28,24},{1,5},{5... | collective-permute-start | bytes 5898248 | tf_op jit(solution)/shard_map/operand_exchange/ppermute | solution.py:28
  5.1 4.6 %collective-permute-start.9 = (bf16[4,128,512]{2,1,0:T(8,128)(2,1)S(1)}, bf16[4,128,512]{2,1,0:T(8,128)(2,1)S(1)}, u32[]{:S(2)}, u32[]{:S(2)}) collective-permute-start(bf16[4,128,512]{2,1,0:T(8,128)(2,1)S(1)} %get-tuple-element.41), channel_id=1, source_target_pairs={{0,4},{4,0},{8,12},{12,8},{16,20},{20,16},{24,28},{28,24},{1,5},{5... | collective-permute-start | bytes 1572872 | tf_op jit(solution)/shard_map/sibling_1/ppermute | solution.py:28
  5.3 7.3 %collective-permute-start.2 = (bf16[128,512]{1,0:T(8,128)(2,1)S(1)}, bf16[128,512]{1,0:T(8,128)(2,1)S(1)}, u32[]{:S(2)}, u32[]{:S(2)}) collective-permute-start(bf16[128,512]{1,0:T(8,128)(2,1)S(1)} %get-tuple-element.33), channel_id=1, source_target_pairs={{0,16},{4,12},{8,24},{12,4},{16,0},{20,28},{24,8},{28,20},{1,17},{... | collective-permute-start | bytes 393224 | tf_op jit(solution)/shard_map/one_part_0_to_chip_2/ppermute | solution.py:28
  8.2 10.1 %collective-permute-start.6 = (bf16[128,512]{1,0:T(8,128)(2,1)S(1)}, bf16[128,512]{1,0:T(8,128)(2,1)S(1)}, u32[]{:S(2)}, u32[]{:S(2)}) collective-permute-start(bf16[128,512]{1,0:T(8,128)(2,1)S(1)} %get-tuple-element.39), channel_id=1, source_target_pairs={{0,8},{4,20},{8,0},{12,28},{16,24},{20,4},{24,16},{28,12},{1,9},{5... | collective-permute-start | bytes 393224 | tf_op jit(solution)/shard_map/one_part_0_to_chip_1/ppermute | solution.py:28
  9.7 8.6 %collective-permute-start.7 = (bf16[128,512]{1,0:T(8,128)(2,1)S(1)}, bf16[128,512]{1,0:T(8,128)(2,1)S(1)}, u32[]{:S(2)}, u32[]{:S(2)}) collective-permute-start(bf16[128,512]{1,0:T(8,128)(2,1)S(1)} %get-tuple-element.40), channel_id=1, source_target_pairs={{0,24},{4,28},{8,16},{12,20},{16,8},{20,12},{24,0},{28,4},{1,25},{... | collective-permute-start | bytes 393224 | tf_op jit(solution)/shard_map/one_part_0_to_chip_3/ppermute | solution.py:28
  9.8 11.7 %collective-permute-start.10 = (bf16[128,512]{1,0:T(8,128)(2,1)S(1)}, bf16[128,512]{1,0:T(8,128)(2,1)S(1)}, u32[]{:S(2)}, u32[]{:S(2)}) collective-permute-start(bf16[128,512]{1,0:T(8,128)(2,1)S(1)} %get-tuple-element.43), channel_id=1, source_target_pairs={{0,8},{4,12},{8,0},{12,4},{16,24},{20,28},{24,16},{28,20},{1,9},{5... | collective-permute-start | bytes 393224 | tf_op jit(solution)/shard_map/one_part_1_to_chip_1/ppermute | solution.py:28
  12.5 10.4 %collective-permute-start.11 = (bf16[128,512]{1,0:T(8,128)(2,1)S(1)}, bf16[128,512]{1,0:T(8,128)(2,1)S(1)}, u32[]{:S(2)}, u32[]{:S(2)}) collective-permute-start(bf16[128,512]{1,0:T(8,128)(2,1)S(1)} %get-tuple-element.44), channel_id=1, source_target_pairs={{0,16},{4,20},{8,24},{12,28},{16,0},{20,4},{24,8},{28,12},{1,17},{... | collective-permute-start | bytes 393224 | tf_op jit(solution)/shard_map/one_part_1_to_chip_2/ppermute | solution.py:28
  15.3 9.6 %collective-permute-start.12 = (bf16[128,512]{1,0:T(8,128)(2,1)S(1)}, bf16[128,512]{1,0:T(8,128)(2,1)S(1)}, u32[]{:S(2)}, u32[]{:S(2)}) collective-permute-start(bf16[128,512]{1,0:T(8,128)(2,1)S(1)} %get-tuple-element.45), channel_id=1, source_target_pairs={{0,24},{4,28},{8,16},{12,20},{16,8},{20,12},{24,0},{28,4},{1,25},{... | collective-permute-start | bytes 393224 | tf_op jit(solution)/shard_map/one_part_1_to_chip_3/ppermute | solution.py:28
  18.3 9.8 %collective-permute-start.8 = (bf16[128,512]{1,0:T(8,128)(2,1)S(1)}, bf16[128,512]{1,0:T(8,128)(2,1)S(1)}, u32[]{:S(2)}, u32[]{:S(2)}) collective-permute-start(bf16[128,512]{1,0:T(8,128)(2,1)S(1)} %total_0.1), channel_id=1, source_target_pairs={{0,2},{1,3},{2,0},{3,1},{4,6},{5,7},{6,4},{7,5},{8,10},{9,11},{10,... | collective-permute-start | bytes 393224 | tf_op jit(solution)/shard_map/mirror_0/ppermute | solution.py:35
  20.9 11.5 %collective-permute-start.3 = (bf16[256,512]{1,0:T(8,128)(2,1)S(1)}, bf16[256,512]{1,0:T(8,128)(2,1)S(1)}, u32[]{:S(2)}, u32[]{:S(2)}) collective-permute-start(bf16[256,512]{1,0:T(8,128)(2,1)S(1)} %get-tuple-element.35), channel_id=1, source_target_pairs={{0,8},{4,20},{8,0},{12,28},{16,24},{20,4},{24,16},{28,12},{1,9},{5... | collective-permute-start | bytes 786440 | tf_op jit(solution)/shard_map/zero_to_chip_1/ppermute | solution.py:28
  21.5 10.9 %collective-permute-start.4 = (bf16[256,512]{1,0:T(8,128)(2,1)S(1)}, bf16[256,512]{1,0:T(8,128)(2,1)S(1)}, u32[]{:S(2)}, u32[]{:S(2)}) collective-permute-start(bf16[256,512]{1,0:T(8,128)(2,1)S(1)} %get-tuple-element.36), channel_id=1, source_target_pairs={{0,16},{4,12},{8,24},{12,4},{16,0},{20,28},{24,8},{28,20},{1,17},{... | collective-permute-start | bytes 786440 | tf_op jit(solution)/shard_map/zero_to_chip_2/ppermute | solution.py:28
  23.0 9.9 %collective-permute-start.5 = (bf16[256,512]{1,0:T(8,128)(2,1)S(1)}, bf16[256,512]{1,0:T(8,128)(2,1)S(1)}, u32[]{:S(2)}, u32[]{:S(2)}) collective-permute-start(bf16[256,512]{1,0:T(8,128)(2,1)S(1)} %get-tuple-element.37), channel_id=1, source_target_pairs={{0,24},{4,28},{8,16},{12,20},{16,8},{20,12},{24,0},{28,4},{1,25},{... | collective-permute-start | bytes 786440 | tf_op jit(solution)/shard_map/zero_to_chip_3/ppermute | solution.py:28
  24.8 8.0 %copy-start = (f32[1,256,2,256]{3,2,1,0:T(2,128)S(1)}, f32[1,256,2,256]{3,2,1,0:T(2,128)}, u32[]{:S(2)}) copy-start(f32[1,256,2,256]{3,2,1,0:T(2,128)} %param.10) | copy-start | bytes 1572868
  24.8 8.1 %copy-start.1 = (f32[1,256,2,256]{3,2,1,0:T(2,128)S(1)}, f32[1,256,2,256]{3,2,1,0:T(2,128)}, u32[]{:S(2)}) copy-start(f32[1,256,2,256]{3,2,1,0:T(2,128)} %param.11) | copy-start | bytes 1572868
  24.9 7.6 %collective-permute-start.13 = (bf16[128,512]{1,0:T(8,128)(2,1)S(1)}, bf16[128,512]{1,0:T(8,128)(2,1)S(1)}, u32[]{:S(2)}, u32[]{:S(2)}) collective-permute-start(bf16[128,512]{1,0:T(8,128)(2,1)S(1)} %total_1.1), channel_id=1, source_target_pairs={{0,2},{1,3},{2,0},{3,1},{4,6},{5,7},{6,4},{7,5},{8,10},{9,11},{10,... | collective-permute-start | bytes 393224 | tf_op jit(solution)/shard_map/mirror_1/ppermute | solution.py:35

commit v12 on v11

--- a/solution.py
+++ b/solution.py
@@ -55,7 +55,7 @@
 ANYWHERE = pl.BlockSpec(memory_space=pl.ANY)
 IN_VMEM = pl.BlockSpec(memory_space=pltpu.VMEM)
 PARAMS = pltpu.CompilerParams(vmem_limit_bytes=VMEM_BYTES)
-PIECES = 4
+PIECES = 2
 STEPS = 4
 SMALL = pl.CostEstimate(flops=1, bytes_accessed=1, transcendentals=0)
 LARGE = pl.CostEstimate(flops=1 << 33, bytes_accessed=1, transcendentals=0)

time: 34.6 us -> 34.6 us (level)
  no operation moved by 1% of the time
where the time goes in v12:
time: 34.6 us; the launch traced here: 34.4 us
  starting transfers between devices  22.3 us (64%)
  Pallas kernels  6.53 us (19%)
  waiting for transfers between devices  4.85 us (14%)
  between operations  0.7 us (2%)
    ppermute x12, starting transfers between devices, exchanged(): lax.ppermute(value, axis, [(i, i ^ mask_of(i)) for i in range(count)])  16.5 us
    ppermute x2, starting transfers between devices, mirrored(): return lax.ppermute(value, 'section', pairs)  5.81 us
    ppermute x2, waiting for transfers between devices, mirrored(): return lax.ppermute(value, 'section', pairs)  4.35 us
    pallas_call x1, Pallas kernels, sibling_products(): pl.pallas_call(functools.partial(sibling_kernel, experts, cuts[-1].stop),...  1.89 us
    pallas_call x1, Pallas kernels, updated(): pl.pallas_call(functools.partial(update_kernel, first.shape[1], cuts, mes...  1.53 us
    pallas_call x1, Pallas kernels, own_products(): pl.pallas_call(functools.partial(own_kernel, experts), in_specs=[ANYWHERE...  1.47 us
    pallas_call x1, Pallas kernels, paired(): pl.pallas_call(functools.partial(pair_kernel, len(after), messages), in_s...  1.28 us
  transfers between devices with their start and end apart: 14, of which 3 were waited for; matrix products, arithmetic and copies ran while one was open for 0% of the time, Pallas kernels for 9%

profile of v12, /device:TPU:0, one launch (start us, length us, event | category | flops | bytes accessed | tf_op | source)
XLA Modules:
  0.0 34.4 jit_solution(8280939836183501500)
XLA Ops:
  0.6 1.9 %sibling_products.1 = (bf16[4,128,512]{2,1,0:T(8,128)(2,1)S(1)}, bf16[384,2048]{1,0:T(8,128)(2,1)S(1)}, bf16[384,512]{1,0:T(8,128)(2,1)S(1)}) custom-call(s32[2,3]{1,0:T(2,128)} %bitcast.40, s32[2,2]{1,0:T(2,128)} %bitcast.42, bf16[2,384,2048]{2,1,0:T(8,128)(2,1)} %bitcast.36, bf16[2,384,256]{2,1,0:T(8,128)(2,1)} %bitcast.38), custom_call_target="tpu_custom_call" | custom-call | flops 1 | bytes 1 | tf_op jit(solution)/shard_map/sibling_products/pallas_call | solution.py:136
  2.5 0.5 %collective-permute-start = (bf16[4,128,512]{2,1,0:T(8,128)(2,1)S(1)}, bf16[4,128,512]{2,1,0:T(8,128)(2,1)S(1)}, u32[]{:S(2)}, u32[]{:S(2)}) collective-permute-start(bf16[4,128,512]{2,1,0:T(8,128)(2,1)S(1)} %get-tuple-element.30), channel_id=1, source_target_pairs={{0,4},{4,0},{8,12},{12,8},{16,20},{20,16},{24,28},{28,24},{1,5},{5... | collective-permute-start | bytes 1572872 | tf_op jit(solution)/shard_map/sibling_0/ppermute | solution.py:28
  3.0 1.5 %own_products.1 = (bf16[4,256,512]{2,1,0:T(8,128)(2,1)S(1)}, bf16[4,128,512]{2,1,0:T(8,128)(2,1)S(1)}, bf16[384,2560]{1,0:T(8,128)(2,1)S(1)}) custom-call(s32[2,3]{1,0:T(2,128)} %bitcast.41, s32[2,2]{1,0:T(2,128)} %bitcast.43, bf16[2,384,2048]{2,1,0:T(8,128)(2,1)} %bitcast.37, bf16[2,384,256]{2,1,0:T(8,128)(2,1)} %bitcast.39, ...), custom_call_target="tpu_custom_call" | custom-call | flops 1 | bytes 1 | tf_op jit(solution)/shard_map/own_products/pallas_call | solution.py:182
  4.5 0.1 collective-permute-done.received
  4.6 0.1 join_0.1
  4.7 0.4 %collective-permute-start.1 = (bf16[384,2560]{1,0:T(8,128)(2,1)S(1)}, bf16[384,2560]{1,0:T(8,128)(2,1)S(1)}, u32[]{:S(2)}, u32[]{:S(2)}) collective-permute-start(bf16[384,2560]{1,0:T(8,128)(2,1)S(1)} %get-tuple-element.32.ahead), channel_id=1, source_target_pairs={{0,4},{4,0},{8,12},{12,8},{16,20},{20,16},{24,28},{28,24},{1,5},{5... | collective-permute-start | bytes 5898248 | tf_op jit(solution)/shard_map/operand_exchange/ppermute | solution.py:28
  5.1 0.1 collective-permute-start.9
  5.3 2.9 %collective-permute-start.2 = (bf16[128,512]{1,0:T(8,128)(2,1)S(1)}, bf16[128,512]{1,0:T(8,128)(2,1)S(1)}, u32[]{:S(2)}, u32[]{:S(2)}) collective-permute-start(bf16[128,512]{1,0:T(8,128)(2,1)S(1)} %get-tuple-element.33), channel_id=1, source_target_pairs={{0,16},{4,12},{8,24},{12,4},{16,0},{20,28},{24,8},{28,20},{1,17},{... | collective-permute-start | bytes 393224 | tf_op jit(solution)/shard_map/one_part_0_to_chip_2/ppermute | solution.py:28
  8.2 1.5 %collective-permute-start.6 = (bf16[128,512]{1,0:T(8,128)(2,1)S(1)}, bf16[128,512]{1,0:T(8,128)(2,1)S(1)}, u32[]{:S(2)}, u32[]{:S(2)}) collective-permute-start(bf16[128,512]{1,0:T(8,128)(2,1)S(1)} %get-tuple-element.39), channel_id=1, source_target_pairs={{0,8},{4,20},{8,0},{12,28},{16,24},{20,4},{24,16},{28,12},{1,9},{5... | collective-permute-start | bytes 393224 | tf_op jit(solution)/shard_map/one_part_0_to_chip_1/ppermute | solution.py:28
  9.7 0.0 collective-permute-start.7
  9.7 0.0 collective-permute-done.9.received
  9.7 0.1 join_1.1
  9.8 2.7 %collective-permute-start.10 = (bf16[128,512]{1,0:T(8,128)(2,1)S(1)}, bf16[128,512]{1,0:T(8,128)(2,1)S(1)}, u32[]{:S(2)}, u32[]{:S(2)}) collective-permute-start(bf16[128,512]{1,0:T(8,128)(2,1)S(1)} %get-tuple-element.43), channel_id=1, source_target_pairs={{0,8},{4,12},{8,0},{12,4},{16,24},{20,28},{24,16},{28,20},{1,9},{5... | collective-permute-start | bytes 393224 | tf_op jit(solution)/shard_map/one_part_1_to_chip_1/ppermute | solution.py:28
  12.5 0.0 collective-permute-done.2.refs_0_.refs_1_
  12.5 2.7 %collective-permute-start.11 = (bf16[128,512]{1,0:T(8,128)(2,1)S(1)}, bf16[128,512]{1,0:T(8,128)(2,1)S(1)}, u32[]{:S(2)}, u32[]{:S(2)}) collective-permute-start(bf16[128,512]{1,0:T(8,128)(2,1)S(1)} %get-tuple-element.44), channel_id=1, source_target_pairs={{0,16},{4,20},{8,24},{12,28},{16,0},{20,4},{24,8},{28,12},{1,17},{... | collective-permute-start | bytes 393224 | tf_op jit(solution)/shard_map/one_part_1_to_chip_2/ppermute | solution.py:28
  15.3 0.0 collective-permute-done.1.other
  15.3 1.7 %collective-permute-start.12 = (bf16[128,512]{1,0:T(8,128)(2,1)S(1)}, bf16[128,512]{1,0:T(8,128)(2,1)S(1)}, u32[]{:S(2)}, u32[]{:S(2)}) collective-permute-start(bf16[128,512]{1,0:T(8,128)(2,1)S(1)} %get-tuple-element.45), channel_id=1, source_target_pairs={{0,24},{4,28},{8,16},{12,20},{16,8},{20,12},{24,0},{28,4},{1,25},{... | collective-permute-start | bytes 393224 | tf_op jit(solution)/shard_map/one_part_1_to_chip_3/ppermute | solution.py:28
  17.0 1.3 %pair.1 = (f32[256,512]{1,0:T(8,128)S(1)}, bf16[256,512]{1,0:T(8,128)(2,1)S(1)}, bf16[256,512]{1,0:T(8,128)(2,1)S(1)}, bf16[256,512]{1,0:T(8,128)(2,1)S(1)}) custom-call(bf16[384,2560]{1,0:T(8,128)(2,1)S(1)} %get-tuple-element.32.ahead, bf16[384,2560]{1,0:T(8,128)(2,1)S(1)} %collective-permute-done.1.other, ...), custom_call_target="tpu_custom_call" | custom-call | flops 1 | bytes 1 | tf_op jit(solution)/shard_map/pair/pallas_call | solution.py:248
  18.2 0.0 collective-permute-done.6.refs_0_
  18.3 0.0 collective-permute-done.7.refs_2_
  18.3 0.1 total_0.1
  18.3 2.6 %collective-permute-start.8 = (bf16[128,512]{1,0:T(8,128)(2,1)S(1)}, bf16[128,512]{1,0:T(8,128)(2,1)S(1)}, u32[]{:S(2)}, u32[]{:S(2)}) collective-permute-start(bf16[128,512]{1,0:T(8,128)(2,1)S(1)} %total_0.1), channel_id=1, source_target_pairs={{0,2},{1,3},{2,0},{3,1},{4,6},{5,7},{6,4},{7,5},{8,10},{9,11},{10,... | collective-permute-start | bytes 393224 | tf_op jit(solution)/shard_map/mirror_0/ppermute | solution.py:35
  20.9 0.6 %collective-permute-start.3 = (bf16[256,512]{1,0:T(8,128)(2,1)S(1)}, bf16[256,512]{1,0:T(8,128)(2,1)S(1)}, u32[]{:S(2)}, u32[]{:S(2)}) collective-permute-start(bf16[256,512]{1,0:T(8,128)(2,1)S(1)} %get-tuple-element.35), channel_id=1, source_target_pairs={{0,8},{4,20},{8,0},{12,28},{16,24},{20,4},{24,16},{28,12},{1,9},{5... | collective-permute-start | bytes 786440 | tf_op jit(solution)/shard_map/zero_to_chip_1/ppermute | solution.py:28
  21.5 0.0 collective-permute-done.10.refs_0_
  21.5 1.5 %collective-permute-start.4 = (bf16[256,512]{1,0:T(8,128)(2,1)S(1)}, bf16[256,512]{1,0:T(8,128)(2,1)S(1)}, u32[]{:S(2)}, u32[]{:S(2)}) collective-permute-start(bf16[256,512]{1,0:T(8,128)(2,1)S(1)} %get-tuple-element.36), channel_id=1, source_target_pairs={{0,16},{4,12},{8,24},{12,4},{16,0},{20,28},{24,8},{28,20},{1,17},{... | collective-permute-start | bytes 786440 | tf_op jit(solution)/shard_map/zero_to_chip_2/ppermute | solution.py:28
  23.0 0.0 collective-permute-done.11.refs_1_
  23.0 1.8 %collective-permute-start.5 = (bf16[256,512]{1,0:T(8,128)(2,1)S(1)}, bf16[256,512]{1,0:T(8,128)(2,1)S(1)}, u32[]{:S(2)}, u32[]{:S(2)}) collective-permute-start(bf16[256,512]{1,0:T(8,128)(2,1)S(1)} %get-tuple-element.37), channel_id=1, source_target_pairs={{0,24},{4,28},{8,16},{12,20},{16,8},{20,12},{24,0},{28,4},{1,25},{... | collective-permute-start | bytes 786440 | tf_op jit(solution)/shard_map/zero_to_chip_3/ppermute | solution.py:28
  24.8 0.0 collective-permute-done.12.refs_2_
  24.8 0.0 copy-start
  24.8 0.0 copy-start.1
  24.8 0.1 total_1.1
  24.9 3.2 %collective-permute-start.13 = (bf16[128,512]{1,0:T(8,128)(2,1)S(1)}, bf16[128,512]{1,0:T(8,128)(2,1)S(1)}, u32[]{:S(2)}, u32[]{:S(2)}) collective-permute-start(bf16[128,512]{1,0:T(8,128)(2,1)S(1)} %total_1.1), channel_id=1, source_target_pairs={{0,2},{1,3},{2,0},{3,1},{4,6},{5,7},{6,4},{7,5},{8,10},{9,11},{10,... | collective-permute-start | bytes 393224 | tf_op jit(solution)/shard_map/mirror_1/ppermute | solution.py:35
  28.1 0.0 collective-permute-done.8.refs_3_
  28.1 4.3 %collective-permute-done.13.refs_4_ = bf16[128,512]{1,0:T(8,128)(2,1)S(1)} collective-permute-done((bf16[128,512]{1,0:T(8,128)(2,1)S(1)}, bf16[128,512]{1,0:T(8,128)(2,1)S(1)}, u32[]{:S(2)}, u32[]{:S(2)}) %collective-permute-start.13) | collective-permute-done | bytes 131104 | tf_op jit(solution)/shard_map/mirror_1/ppermute | solution.py:35
  32.4 0.0 collective-permute-done.3.refs_0_
  32.4 0.0 collective-permute-done.4.refs_1_
  32.4 0.4 %collective-permute-done.5.refs_2_ = bf16[256,512]{1,0:T(8,128)(2,1)S(1)} collective-permute-done((bf16[256,512]{1,0:T(8,128)(2,1)S(1)}, bf16[256,512]{1,0:T(8,128)(2,1)S(1)}, u32[]{:S(2)}, u32[]{:S(2)}) %collective-permute-start.5) | collective-permute-done | bytes 262176 | tf_op jit(solution)/shard_map/zero_to_chip_3/ppermute | solution.py:28
  32.9 0.0 copy-done
  32.9 0.0 copy-done.1
  32.9 1.5 %update.1 = (f32[1024,128]{1,0:T(8,128)}, f32[1024,128]{1,0:T(8,128)}, f32[1024,128]{1,0:T(8,128)}, f32[1024,128]{1,0:T(8,128)}) custom-call(f32[256,512]{1,0:T(8,128)S(1)} %get-tuple-element.34.refs_3_.kept, bf16[256,512]{1,0:T(8,128)(2,1)S(1)} %collective-permute-done.3.refs_0_, bf16[256,512]{1,0:T(8,128)(2,1)S(1)} %collective-permute-done.4.refs_1_, ...), custom_call_target="tpu_custom_call" | custom-call | flops 1 | bytes 1 | tf_op jit(solution)/shard_map/update/pallas_call | solution.py:341
Async XLA Ops:
  2.5 2.0 %collective-permute-start = (bf16[4,128,512]{2,1,0:T(8,128)(2,1)S(1)}, bf16[4,128,512]{2,1,0:T(8,128)(2,1)S(1)}, u32[]{:S(2)}, u32[]{:S(2)}) collective-permute-start(bf16[4,128,512]{2,1,0:T(8,128)(2,1)S(1)} %get-tuple-element.30), channel_id=1, source_target_pairs={{0,4},{4,0},{8,12},{12,8},{16,20},{20,16},{24,28},{28,24},{1,5},{5... | collective-permute-start | bytes 1572872 | tf_op jit(solution)/shard_map/sibling_0/ppermute | solution.py:28
  4.7 10.6 %collective-permute-start.1 = (bf16[384,2560]{1,0:T(8,128)(2,1)S(1)}, bf16[384,2560]{1,0:T(8,128)(2,1)S(1)}, u32[]{:S(2)}, u32[]{:S(2)}) collective-permute-start(bf16[384,2560]{1,0:T(8,128)(2,1)S(1)} %get-tuple-element.32.ahead), channel_id=1, source_target_pairs={{0,4},{4,0},{8,12},{12,8},{16,20},{20,16},{24,28},{28,24},{1,5},{5... | collective-permute-start | bytes 5898248 | tf_op jit(solution)/shard_map/operand_exchange/ppermute | solution.py:28
  5.1 4.6 %collective-permute-start.9 = (bf16[4,128,512]{2,1,0:T(8,128)(2,1)S(1)}, bf16[4,128,512]{2,1,0:T(8,128)(2,1)S(1)}, u32[]{:S(2)}, u32[]{:S(2)}) collective-permute-start(bf16[4,128,512]{2,1,0:T(8,128)(2,1)S(1)} %get-tuple-element.41), channel_id=1, source_target_pairs={{0,4},{4,0},{8,12},{12,8},{16,20},{20,16},{24,28},{28,24},{1,5},{5... | collective-permute-start | bytes 1572872 | tf_op jit(solution)/shard_map/sibling_1/ppermute | solution.py:28
  5.3 7.3 %collective-permute-start.2 = (bf16[128,512]{1,0:T(8,128)(2,1)S(1)}, bf16[128,512]{1,0:T(8,128)(2,1)S(1)}, u32[]{:S(2)}, u32[]{:S(2)}) collective-permute-start(bf16[128,512]{1,0:T(8,128)(2,1)S(1)} %get-tuple-element.33), channel_id=1, source_target_pairs={{0,16},{4,12},{8,24},{12,4},{16,0},{20,28},{24,8},{28,20},{1,17},{... | collective-permute-start | bytes 393224 | tf_op jit(solution)/shard_map/one_part_0_to_chip_2/ppermute | solution.py:28
  8.2 10.1 %collective-permute-start.6 = (bf16[128,512]{1,0:T(8,128)(2,1)S(1)}, bf16[128,512]{1,0:T(8,128)(2,1)S(1)}, u32[]{:S(2)}, u32[]{:S(2)}) collective-permute-start(bf16[128,512]{1,0:T(8,128)(2,1)S(1)} %get-tuple-element.39), channel_id=1, source_target_pairs={{0,8},{4,20},{8,0},{12,28},{16,24},{20,4},{24,16},{28,12},{1,9},{5... | collective-permute-start | bytes 393224 | tf_op jit(solution)/shard_map/one_part_0_to_chip_1/ppermute | solution.py:28
  9.7 8.6 %collective-permute-start.7 = (bf16[128,512]{1,0:T(8,128)(2,1)S(1)}, bf16[128,512]{1,0:T(8,128)(2,1)S(1)}, u32[]{:S(2)}, u32[]{:S(2)}) collective-permute-start(bf16[128,512]{1,0:T(8,128)(2,1)S(1)} %get-tuple-element.40), channel_id=1, source_target_pairs={{0,24},{4,28},{8,16},{12,20},{16,8},{20,12},{24,0},{28,4},{1,25},{... | collective-permute-start | bytes 393224 | tf_op jit(solution)/shard_map/one_part_0_to_chip_3/ppermute | solution.py:28
  9.8 11.7 %collective-permute-start.10 = (bf16[128,512]{1,0:T(8,128)(2,1)S(1)}, bf16[128,512]{1,0:T(8,128)(2,1)S(1)}, u32[]{:S(2)}, u32[]{:S(2)}) collective-permute-start(bf16[128,512]{1,0:T(8,128)(2,1)S(1)} %get-tuple-element.43), channel_id=1, source_target_pairs={{0,8},{4,12},{8,0},{12,4},{16,24},{20,28},{24,16},{28,20},{1,9},{5... | collective-permute-start | bytes 393224 | tf_op jit(solution)/shard_map/one_part_1_to_chip_1/ppermute | solution.py:28
  12.5 10.4 %collective-permute-start.11 = (bf16[128,512]{1,0:T(8,128)(2,1)S(1)}, bf16[128,512]{1,0:T(8,128)(2,1)S(1)}, u32[]{:S(2)}, u32[]{:S(2)}) collective-permute-start(bf16[128,512]{1,0:T(8,128)(2,1)S(1)} %get-tuple-element.44), channel_id=1, source_target_pairs={{0,16},{4,20},{8,24},{12,28},{16,0},{20,4},{24,8},{28,12},{1,17},{... | collective-permute-start | bytes 393224 | tf_op jit(solution)/shard_map/one_part_1_to_chip_2/ppermute | solution.py:28
  15.3 9.6 %collective-permute-start.12 = (bf16[128,512]{1,0:T(8,128)(2,1)S(1)}, bf16[128,512]{1,0:T(8,128)(2,1)S(1)}, u32[]{:S(2)}, u32[]{:S(2)}) collective-permute-start(bf16[128,512]{1,0:T(8,128)(2,1)S(1)} %get-tuple-element.45), channel_id=1, source_target_pairs={{0,24},{4,28},{8,16},{12,20},{16,8},{20,12},{24,0},{28,4},{1,25},{... | collective-permute-start | bytes 393224 | tf_op jit(solution)/shard_map/one_part_1_to_chip_3/ppermute | solution.py:28
  18.3 9.8 %collective-permute-start.8 = (bf16[128,512]{1,0:T(8,128)(2,1)S(1)}, bf16[128,512]{1,0:T(8,128)(2,1)S(1)}, u32[]{:S(2)}, u32[]{:S(2)}) collective-permute-start(bf16[128,512]{1,0:T(8,128)(2,1)S(1)} %total_0.1), channel_id=1, source_target_pairs={{0,2},{1,3},{2,0},{3,1},{4,6},{5,7},{6,4},{7,5},{8,10},{9,11},{10,... | collective-permute-start | bytes 393224 | tf_op jit(solution)/shard_map/mirror_0/ppermute | solution.py:35
  20.9 11.5 %collective-permute-start.3 = (bf16[256,512]{1,0:T(8,128)(2,1)S(1)}, bf16[256,512]{1,0:T(8,128)(2,1)S(1)}, u32[]{:S(2)}, u32[]{:S(2)}) collective-permute-start(bf16[256,512]{1,0:T(8,128)(2,1)S(1)} %get-tuple-element.35), channel_id=1, source_target_pairs={{0,8},{4,20},{8,0},{12,28},{16,24},{20,4},{24,16},{28,12},{1,9},{5... | collective-permute-start | bytes 786440 | tf_op jit(solution)/shard_map/zero_to_chip_1/ppermute | solution.py:28
  21.5 10.9 %collective-permute-start.4 = (bf16[256,512]{1,0:T(8,128)(2,1)S(1)}, bf16[256,512]{1,0:T(8,128)(2,1)S(1)}, u32[]{:S(2)}, u32[]{:S(2)}) collective-permute-start(bf16[256,512]{1,0:T(8,128)(2,1)S(1)} %get-tuple-element.36), channel_id=1, source_target_pairs={{0,16},{4,12},{8,24},{12,4},{16,0},{20,28},{24,8},{28,20},{1,17},{... | collective-permute-start | bytes 786440 | tf_op jit(solution)/shard_map/zero_to_chip_2/ppermute | solution.py:28
  23.0 9.9 %collective-permute-start.5 = (bf16[256,512]{1,0:T(8,128)(2,1)S(1)}, bf16[256,512]{1,0:T(8,128)(2,1)S(1)}, u32[]{:S(2)}, u32[]{:S(2)}) collective-permute-start(bf16[256,512]{1,0:T(8,128)(2,1)S(1)} %get-tuple-element.37), channel_id=1, source_target_pairs={{0,24},{4,28},{8,16},{12,20},{16,8},{20,12},{24,0},{28,4},{1,25},{... | collective-permute-start | bytes 786440 | tf_op jit(solution)/shard_map/zero_to_chip_3/ppermute | solution.py:28
  24.8 8.0 %copy-start = (f32[1,256,2,256]{3,2,1,0:T(2,128)S(1)}, f32[1,256,2,256]{3,2,1,0:T(2,128)}, u32[]{:S(2)}) copy-start(f32[1,256,2,256]{3,2,1,0:T(2,128)} %param.10) | copy-start | bytes 1572868
  24.8 8.1 %copy-start.1 = (f32[1,256,2,256]{3,2,1,0:T(2,128)S(1)}, f32[1,256,2,256]{3,2,1,0:T(2,128)}, u32[]{:S(2)}) copy-start(f32[1,256,2,256]{3,2,1,0:T(2,128)} %param.11) | copy-start | bytes 1572868
  24.9 7.6 %collective-permute-start.13 = (bf16[128,512]{1,0:T(8,128)(2,1)S(1)}, bf16[128,512]{1,0:T(8,128)(2,1)S(1)}, u32[]{:S(2)}, u32[]{:S(2)}) collective-permute-start(bf16[128,512]{1,0:T(8,128)(2,1)S(1)} %total_1.1), channel_id=1, source_target_pairs={{0,2},{1,3},{2,0},{3,1},{4,6},{5,7},{6,4},{7,5},{8,10},{9,11},{10,... | collective-permute-start | bytes 393224 | tf_op jit(solution)/shard_map/mirror_1/ppermute | solution.py:35

commit v13 on v11

--- a/solution.py
+++ b/solution.py
@@ -230,11 +230,12 @@
     share, columns = kept.shape
     model = ahead.shape[1] - columns
     chips = 1 + max(place for place, _ in messages)
+    wide_both = jnp.concatenate([ahead[:, model:], other[:, model:]], axis=0)
     for k in range(chips):
         chip = neighbour(k, lax.axis_index("dp") % 2, chips, True)
         place = owner_columns(chip, False, share)
-        total = contracted(ahead[:, place], ahead[:, model:])
-        total = total + contracted(other[:, place], other[:, model:])
+        columns_both = jnp.concatenate([ahead[:, place], other[:, place]], axis=0)
+        total = contracted(columns_both, wide_both)
         if k == 0:
             kept[...] = total
         for (chip, some), out in zip(messages, sent):

time: 34.6 us -> 34.6 us (level)
  transfers between devices with their start and end apart: 14 -> 14, of which waited for: 3 -> 3; matrix products, arithmetic and copies ran while one was open for 0% -> 0% of each run, Pallas kernels for 9% -> 8%
where the time goes in v13:
time: 34.6 us; the launch traced here: 34.4 us
  starting transfers between devices  22.6 us (65%)
  Pallas kernels  6.27 us (18%)
  waiting for transfers between devices  4.85 us (14%)
  between operations  0.7 us (2%)
    ppermute x12, starting transfers between devices, exchanged(): lax.ppermute(value, axis, [(i, i ^ mask_of(i)) for i in range(count)])  16.8 us
    ppermute x2, starting transfers between devices, mirrored(): return lax.ppermute(value, 'section', pairs)  5.8 us
    ppermute x2, waiting for transfers between devices, mirrored(): return lax.ppermute(value, 'section', pairs)  4.35 us
    pallas_call x1, Pallas kernels, sibling_products(): pl.pallas_call(functools.partial(sibling_kernel, experts, cuts[-1].stop),...  1.89 us
    pallas_call x1, Pallas kernels, updated(): pl.pallas_call(functools.partial(update_kernel, first.shape[1], cuts, mes...  1.53 us
    pallas_call x1, Pallas kernels, own_products(): pl.pallas_call(functools.partial(own_kernel, experts), in_specs=[ANYWHERE...  1.47 us
    pallas_call x1, Pallas kernels, paired(): pl.pallas_call(functools.partial(pair_kernel, len(after), messages), in_s...  1.02 us
  transfers between devices with their start and end apart: 14, of which 3 were waited for; matrix products, arithmetic and copies ran while one was open for 0% of the time, Pallas kernels for 8%

profile of v13, /device:TPU:0, one launch (start us, length us, event | category | flops | bytes accessed | tf_op | source)
XLA Modules:
  0.0 34.4 jit_solution(1232550951348934736)
XLA Ops:
  0.6 1.9 %sibling_products.1 = (bf16[4,128,512]{2,1,0:T(8,128)(2,1)S(1)}, bf16[384,2048]{1,0:T(8,128)(2,1)S(1)}, bf16[384,512]{1,0:T(8,128)(2,1)S(1)}) custom-call(s32[2,3]{1,0:T(2,128)} %bitcast.40, s32[2,2]{1,0:T(2,128)} %bitcast.42, bf16[2,384,2048]{2,1,0:T(8,128)(2,1)} %bitcast.36, bf16[2,384,256]{2,1,0:T(8,128)(2,1)} %bitcast.38), custom_call_target="tpu_custom_call" | custom-call | flops 1 | bytes 1 | tf_op jit(solution)/shard_map/sibling_products/pallas_call | solution.py:136
  2.5 0.5 %collective-permute-start = (bf16[4,128,512]{2,1,0:T(8,128)(2,1)S(1)}, bf16[4,128,512]{2,1,0:T(8,128)(2,1)S(1)}, u32[]{:S(2)}, u32[]{:S(2)}) collective-permute-start(bf16[4,128,512]{2,1,0:T(8,128)(2,1)S(1)} %get-tuple-element.30), channel_id=1, source_target_pairs={{0,4},{4,0},{8,12},{12,8},{16,20},{20,16},{24,28},{28,24},{1,5},{5... | collective-permute-start | bytes 1572872 | tf_op jit(solution)/shard_map/sibling_0/ppermute | solution.py:28
  3.0 1.5 %own_products.1 = (bf16[4,256,512]{2,1,0:T(8,128)(2,1)S(1)}, bf16[4,128,512]{2,1,0:T(8,128)(2,1)S(1)}, bf16[384,2560]{1,0:T(8,128)(2,1)S(1)}) custom-call(s32[2,3]{1,0:T(2,128)} %bitcast.41, s32[2,2]{1,0:T(2,128)} %bitcast.43, bf16[2,384,2048]{2,1,0:T(8,128)(2,1)} %bitcast.37, bf16[2,384,256]{2,1,0:T(8,128)(2,1)} %bitcast.39, ...), custom_call_target="tpu_custom_call" | custom-call | flops 1 | bytes 1 | tf_op jit(solution)/shard_map/own_products/pallas_call | solution.py:182
  4.5 0.1 collective-permute-done.received
  4.6 0.1 join_0.1
  4.7 0.4 %collective-permute-start.1 = (bf16[384,2560]{1,0:T(8,128)(2,1)S(1)}, bf16[384,2560]{1,0:T(8,128)(2,1)S(1)}, u32[]{:S(2)}, u32[]{:S(2)}) collective-permute-start(bf16[384,2560]{1,0:T(8,128)(2,1)S(1)} %get-tuple-element.32.ahead), channel_id=1, source_target_pairs={{0,4},{4,0},{8,12},{12,8},{16,20},{20,16},{24,28},{28,24},{1,5},{5... | collective-permute-start | bytes 5898248 | tf_op jit(solution)/shard_map/operand_exchange/ppermute | solution.py:28
  5.1 0.1 collective-permute-start.9
  5.3 2.9 %collective-permute-start.2 = (bf16[128,512]{1,0:T(8,128)(2,1)S(1)}, bf16[128,512]{1,0:T(8,128)(2,1)S(1)}, u32[]{:S(2)}, u32[]{:S(2)}) collective-permute-start(bf16[128,512]{1,0:T(8,128)(2,1)S(1)} %get-tuple-element.33), channel_id=1, source_target_pairs={{0,16},{4,12},{8,24},{12,4},{16,0},{20,28},{24,8},{28,20},{1,17},{... | collective-permute-start | bytes 393224 | tf_op jit(solution)/shard_map/one_part_0_to_chip_2/ppermute | solution.py:28
  8.2 1.5 %collective-permute-start.6 = (bf16[128,512]{1,0:T(8,128)(2,1)S(1)}, bf16[128,512]{1,0:T(8,128)(2,1)S(1)}, u32[]{:S(2)}, u32[]{:S(2)}) collective-permute-start(bf16[128,512]{1,0:T(8,128)(2,1)S(1)} %get-tuple-element.39), channel_id=1, source_target_pairs={{0,8},{4,20},{8,0},{12,28},{16,24},{20,4},{24,16},{28,12},{1,9},{5... | collective-permute-start | bytes 393224 | tf_op jit(solution)/shard_map/one_part_0_to_chip_1/ppermute | solution.py:28
  9.7 0.0 collective-permute-start.7
  9.7 0.0 collective-permute-done.9.received
  9.7 0.1 join_1.1
  9.8 2.7 %collective-permute-start.10 = (bf16[128,512]{1,0:T(8,128)(2,1)S(1)}, bf16[128,512]{1,0:T(8,128)(2,1)S(1)}, u32[]{:S(2)}, u32[]{:S(2)}) collective-permute-start(bf16[128,512]{1,0:T(8,128)(2,1)S(1)} %get-tuple-element.43), channel_id=1, source_target_pairs={{0,8},{4,12},{8,0},{12,4},{16,24},{20,28},{24,16},{28,20},{1,9},{5... | collective-permute-start | bytes 393224 | tf_op jit(solution)/shard_map/one_part_1_to_chip_1/ppermute | solution.py:28
  12.5 0.0 collective-permute-done.2.refs_0_.refs_1_
  12.5 2.7 %collective-permute-start.11 = (bf16[128,512]{1,0:T(8,128)(2,1)S(1)}, bf16[128,512]{1,0:T(8,128)(2,1)S(1)}, u32[]{:S(2)}, u32[]{:S(2)}) collective-permute-start(bf16[128,512]{1,0:T(8,128)(2,1)S(1)} %get-tuple-element.44), channel_id=1, source_target_pairs={{0,16},{4,20},{8,24},{12,28},{16,0},{20,4},{24,8},{28,12},{1,17},{... | collective-permute-start | bytes 393224 | tf_op jit(solution)/shard_map/one_part_1_to_chip_2/ppermute | solution.py:28
  15.3 0.0 collective-permute-done.1.other
  15.3 1.7 %collective-permute-start.12 = (bf16[128,512]{1,0:T(8,128)(2,1)S(1)}, bf16[128,512]{1,0:T(8,128)(2,1)S(1)}, u32[]{:S(2)}, u32[]{:S(2)}) collective-permute-start(bf16[128,512]{1,0:T(8,128)(2,1)S(1)} %get-tuple-element.45), channel_id=1, source_target_pairs={{0,24},{4,28},{8,16},{12,20},{16,8},{20,12},{24,0},{28,4},{1,25},{... | collective-permute-start | bytes 393224 | tf_op jit(solution)/shard_map/one_part_1_to_chip_3/ppermute | solution.py:28
  17.0 1.0 %pair.1 = (f32[256,512]{1,0:T(8,128)S(1)}, bf16[256,512]{1,0:T(8,128)(2,1)S(1)}, bf16[256,512]{1,0:T(8,128)(2,1)S(1)}, bf16[256,512]{1,0:T(8,128)(2,1)S(1)}) custom-call(bf16[384,2560]{1,0:T(8,128)(2,1)S(1)} %get-tuple-element.32.ahead, bf16[384,2560]{1,0:T(8,128)(2,1)S(1)} %collective-permute-done.1.other, ...), custom_call_target="tpu_custom_call" | custom-call | flops 1 | bytes 1 | tf_op jit(solution)/shard_map/pair/pallas_call | solution.py:249
  18.0 0.0 collective-permute-done.6.refs_0_
  18.0 0.0 collective-permute-done.7.refs_2_
  18.0 0.1 total_0.1
  18.1 2.6 %collective-permute-start.8 = (bf16[128,512]{1,0:T(8,128)(2,1)S(1)}, bf16[128,512]{1,0:T(8,128)(2,1)S(1)}, u32[]{:S(2)}, u32[]{:S(2)}) collective-permute-start(bf16[128,512]{1,0:T(8,128)(2,1)S(1)} %total_0.1), channel_id=1, source_target_pairs={{0,2},{1,3},{2,0},{3,1},{4,6},{5,7},{6,4},{7,5},{8,10},{9,11},{10,... | collective-permute-start | bytes 393224 | tf_op jit(solution)/shard_map/mirror_0/ppermute | solution.py:35
  20.7 0.6 %collective-permute-start.3 = (bf16[256,512]{1,0:T(8,128)(2,1)S(1)}, bf16[256,512]{1,0:T(8,128)(2,1)S(1)}, u32[]{:S(2)}, u32[]{:S(2)}) collective-permute-start(bf16[256,512]{1,0:T(8,128)(2,1)S(1)} %get-tuple-element.35), channel_id=1, source_target_pairs={{0,8},{4,20},{8,0},{12,28},{16,24},{20,4},{24,16},{28,12},{1,9},{5... | collective-permute-start | bytes 786440 | tf_op jit(solution)/shard_map/zero_to_chip_1/ppermute | solution.py:28
  21.3 0.0 collective-permute-done.10.refs_0_
  21.3 1.4 %collective-permute-start.4 = (bf16[256,512]{1,0:T(8,128)(2,1)S(1)}, bf16[256,512]{1,0:T(8,128)(2,1)S(1)}, u32[]{:S(2)}, u32[]{:S(2)}) collective-permute-start(bf16[256,512]{1,0:T(8,128)(2,1)S(1)} %get-tuple-element.36), channel_id=1, source_target_pairs={{0,16},{4,12},{8,24},{12,4},{16,0},{20,28},{24,8},{28,20},{1,17},{... | collective-permute-start | bytes 786440 | tf_op jit(solution)/shard_map/zero_to_chip_2/ppermute | solution.py:28
  22.7 0.0 collective-permute-done.11.refs_1_
  22.7 2.1 %collective-permute-start.5 = (bf16[256,512]{1,0:T(8,128)(2,1)S(1)}, bf16[256,512]{1,0:T(8,128)(2,1)S(1)}, u32[]{:S(2)}, u32[]{:S(2)}) collective-permute-start(bf16[256,512]{1,0:T(8,128)(2,1)S(1)} %get-tuple-element.37), channel_id=1, source_target_pairs={{0,24},{4,28},{8,16},{12,20},{16,8},{20,12},{24,0},{28,4},{1,25},{... | collective-permute-start | bytes 786440 | tf_op jit(solution)/shard_map/zero_to_chip_3/ppermute | solution.py:28
  24.8 0.0 collective-permute-done.12.refs_2_
  24.8 0.0 copy-start
  24.8 0.0 copy-start.1
  24.8 0.1 total_1.1
  24.9 3.2 %collective-permute-start.13 = (bf16[128,512]{1,0:T(8,128)(2,1)S(1)}, bf16[128,512]{1,0:T(8,128)(2,1)S(1)}, u32[]{:S(2)}, u32[]{:S(2)}) collective-permute-start(bf16[128,512]{1,0:T(8,128)(2,1)S(1)} %total_1.1), channel_id=1, source_target_pairs={{0,2},{1,3},{2,0},{3,1},{4,6},{5,7},{6,4},{7,5},{8,10},{9,11},{10,... | collective-permute-start | bytes 393224 | tf_op jit(solution)/shard_map/mirror_1/ppermute | solution.py:35
  28.1 0.0 collective-permute-done.8.refs_3_
  28.1 4.3 %collective-permute-done.13.refs_4_ = bf16[128,512]{1,0:T(8,128)(2,1)S(1)} collective-permute-done((bf16[128,512]{1,0:T(8,128)(2,1)S(1)}, bf16[128,512]{1,0:T(8,128)(2,1)S(1)}, u32[]{:S(2)}, u32[]{:S(2)}) %collective-permute-start.13) | collective-permute-done | bytes 131104 | tf_op jit(solution)/shard_map/mirror_1/ppermute | solution.py:35
  32.4 0.0 collective-permute-done.3.refs_0_
  32.4 0.0 collective-permute-done.4.refs_1_
  32.4 0.4 %collective-permute-done.5.refs_2_ = bf16[256,512]{1,0:T(8,128)(2,1)S(1)} collective-permute-done((bf16[256,512]{1,0:T(8,128)(2,1)S(1)}, bf16[256,512]{1,0:T(8,128)(2,1)S(1)}, u32[]{:S(2)}, u32[]{:S(2)}) %collective-permute-start.5) | collective-permute-done | bytes 262176 | tf_op jit(solution)/shard_map/zero_to_chip_3/ppermute | solution.py:28
  32.9 0.0 copy-done
  32.9 0.0 copy-done.1
  32.9 1.5 %update.1 = (f32[1024,128]{1,0:T(8,128)}, f32[1024,128]{1,0:T(8,128)}, f32[1024,128]{1,0:T(8,128)}, f32[1024,128]{1,0:T(8,128)}) custom-call(f32[256,512]{1,0:T(8,128)S(1)} %get-tuple-element.34.refs_3_.kept, bf16[256,512]{1,0:T(8,128)(2,1)S(1)} %collective-permute-done.3.refs_0_, bf16[256,512]{1,0:T(8,128)(2,1)S(1)} %collective-permute-done.4.refs_1_, ...), custom_call_target="tpu_custom_call" | custom-call | flops 1 | bytes 1 | tf_op jit(solution)/shard_map/update/pallas_call | solution.py:342
Async XLA Ops:
  2.5 2.0 %collective-permute-start = (bf16[4,128,512]{2,1,0:T(8,128)(2,1)S(1)}, bf16[4,128,512]{2,1,0:T(8,128)(2,1)S(1)}, u32[]{:S(2)}, u32[]{:S(2)}) collective-permute-start(bf16[4,128,512]{2,1,0:T(8,128)(2,1)S(1)} %get-tuple-element.30), channel_id=1, source_target_pairs={{0,4},{4,0},{8,12},{12,8},{16,20},{20,16},{24,28},{28,24},{1,5},{5... | collective-permute-start | bytes 1572872 | tf_op jit(solution)/shard_map/sibling_0/ppermute | solution.py:28
  4.7 10.6 %collective-permute-start.1 = (bf16[384,2560]{1,0:T(8,128)(2,1)S(1)}, bf16[384,2560]{1,0:T(8,128)(2,1)S(1)}, u32[]{:S(2)}, u32[]{:S(2)}) collective-permute-start(bf16[384,2560]{1,0:T(8,128)(2,1)S(1)} %get-tuple-element.32.ahead), channel_id=1, source_target_pairs={{0,4},{4,0},{8,12},{12,8},{16,20},{20,16},{24,28},{28,24},{1,5},{5... | collective-permute-start | bytes 5898248 | tf_op jit(solution)/shard_map/operand_exchange/ppermute | solution.py:28
  5.1 4.6 %collective-permute-start.9 = (bf16[4,128,512]{2,1,0:T(8,128)(2,1)S(1)}, bf16[4,128,512]{2,1,0:T(8,128)(2,1)S(1)}, u32[]{:S(2)}, u32[]{:S(2)}) collective-permute-start(bf16[4,128,512]{2,1,0:T(8,128)(2,1)S(1)} %get-tuple-element.41), channel_id=1, source_target_pairs={{0,4},{4,0},{8,12},{12,8},{16,20},{20,16},{24,28},{28,24},{1,5},{5... | collective-permute-start | bytes 1572872 | tf_op jit(solution)/shard_map/sibling_1/ppermute | solution.py:28
  5.3 7.3 %collective-permute-start.2 = (bf16[128,512]{1,0:T(8,128)(2,1)S(1)}, bf16[128,512]{1,0:T(8,128)(2,1)S(1)}, u32[]{:S(2)}, u32[]{:S(2)}) collective-permute-start(bf16[128,512]{1,0:T(8,128)(2,1)S(1)} %get-tuple-element.33), channel_id=1, source_target_pairs={{0,16},{4,12},{8,24},{12,4},{16,0},{20,28},{24,8},{28,20},{1,17},{... | collective-permute-start | bytes 393224 | tf_op jit(solution)/shard_map/one_part_0_to_chip_2/ppermute | solution.py:28
  8.2 9.8 %collective-permute-start.6 = (bf16[128,512]{1,0:T(8,128)(2,1)S(1)}, bf16[128,512]{1,0:T(8,128)(2,1)S(1)}, u32[]{:S(2)}, u32[]{:S(2)}) collective-permute-start(bf16[128,512]{1,0:T(8,128)(2,1)S(1)} %get-tuple-element.39), channel_id=1, source_target_pairs={{0,8},{4,20},{8,0},{12,28},{16,24},{20,4},{24,16},{28,12},{1,9},{5... | collective-permute-start | bytes 393224 | tf_op jit(solution)/shard_map/one_part_0_to_chip_1/ppermute | solution.py:28
  9.7 8.3 %collective-permute-start.7 = (bf16[128,512]{1,0:T(8,128)(2,1)S(1)}, bf16[128,512]{1,0:T(8,128)(2,1)S(1)}, u32[]{:S(2)}, u32[]{:S(2)}) collective-permute-start(bf16[128,512]{1,0:T(8,128)(2,1)S(1)} %get-tuple-element.40), channel_id=1, source_target_pairs={{0,24},{4,28},{8,16},{12,20},{16,8},{20,12},{24,0},{28,4},{1,25},{... | collective-permute-start | bytes 393224 | tf_op jit(solution)/shard_map/one_part_0_to_chip_3/ppermute | solution.py:28
  9.8 11.5 %collective-permute-start.10 = (bf16[128,512]{1,0:T(8,128)(2,1)S(1)}, bf16[128,512]{1,0:T(8,128)(2,1)S(1)}, u32[]{:S(2)}, u32[]{:S(2)}) collective-permute-start(bf16[128,512]{1,0:T(8,128)(2,1)S(1)} %get-tuple-element.43), channel_id=1, source_target_pairs={{0,8},{4,12},{8,0},{12,4},{16,24},{20,28},{24,16},{28,20},{1,9},{5... | collective-permute-start | bytes 393224 | tf_op jit(solution)/shard_map/one_part_1_to_chip_1/ppermute | solution.py:28
  12.5 10.2 %collective-permute-start.11 = (bf16[128,512]{1,0:T(8,128)(2,1)S(1)}, bf16[128,512]{1,0:T(8,128)(2,1)S(1)}, u32[]{:S(2)}, u32[]{:S(2)}) collective-permute-start(bf16[128,512]{1,0:T(8,128)(2,1)S(1)} %get-tuple-element.44), channel_id=1, source_target_pairs={{0,16},{4,20},{8,24},{12,28},{16,0},{20,4},{24,8},{28,12},{1,17},{... | collective-permute-start | bytes 393224 | tf_op jit(solution)/shard_map/one_part_1_to_chip_2/ppermute | solution.py:28
  15.3 9.6 %collective-permute-start.12 = (bf16[128,512]{1,0:T(8,128)(2,1)S(1)}, bf16[128,512]{1,0:T(8,128)(2,1)S(1)}, u32[]{:S(2)}, u32[]{:S(2)}) collective-permute-start(bf16[128,512]{1,0:T(8,128)(2,1)S(1)} %get-tuple-element.45), channel_id=1, source_target_pairs={{0,24},{4,28},{8,16},{12,20},{16,8},{20,12},{24,0},{28,4},{1,25},{... | collective-permute-start | bytes 393224 | tf_op jit(solution)/shard_map/one_part_1_to_chip_3/ppermute | solution.py:28
  18.1 10.0 %collective-permute-start.8 = (bf16[128,512]{1,0:T(8,128)(2,1)S(1)}, bf16[128,512]{1,0:T(8,128)(2,1)S(1)}, u32[]{:S(2)}, u32[]{:S(2)}) collective-permute-start(bf16[128,512]{1,0:T(8,128)(2,1)S(1)} %total_0.1), channel_id=1, source_target_pairs={{0,2},{1,3},{2,0},{3,1},{4,6},{5,7},{6,4},{7,5},{8,10},{9,11},{10,... | collective-permute-start | bytes 393224 | tf_op jit(solution)/shard_map/mirror_0/ppermute | solution.py:35
  20.7 11.8 %collective-permute-start.3 = (bf16[256,512]{1,0:T(8,128)(2,1)S(1)}, bf16[256,512]{1,0:T(8,128)(2,1)S(1)}, u32[]{:S(2)}, u32[]{:S(2)}) collective-permute-start(bf16[256,512]{1,0:T(8,128)(2,1)S(1)} %get-tuple-element.35), channel_id=1, source_target_pairs={{0,8},{4,20},{8,0},{12,28},{16,24},{20,4},{24,16},{28,12},{1,9},{5... | collective-permute-start | bytes 786440 | tf_op jit(solution)/shard_map/zero_to_chip_1/ppermute | solution.py:28
  21.3 11.1 %collective-permute-start.4 = (bf16[256,512]{1,0:T(8,128)(2,1)S(1)}, bf16[256,512]{1,0:T(8,128)(2,1)S(1)}, u32[]{:S(2)}, u32[]{:S(2)}) collective-permute-start(bf16[256,512]{1,0:T(8,128)(2,1)S(1)} %get-tuple-element.36), channel_id=1, source_target_pairs={{0,16},{4,12},{8,24},{12,4},{16,0},{20,28},{24,8},{28,20},{1,17},{... | collective-permute-start | bytes 786440 | tf_op jit(solution)/shard_map/zero_to_chip_2/ppermute | solution.py:28
  22.7 10.2 %collective-permute-start.5 = (bf16[256,512]{1,0:T(8,128)(2,1)S(1)}, bf16[256,512]{1,0:T(8,128)(2,1)S(1)}, u32[]{:S(2)}, u32[]{:S(2)}) collective-permute-start(bf16[256,512]{1,0:T(8,128)(2,1)S(1)} %get-tuple-element.37), channel_id=1, source_target_pairs={{0,24},{4,28},{8,16},{12,20},{16,8},{20,12},{24,0},{28,4},{1,25},{... | collective-permute-start | bytes 786440 | tf_op jit(solution)/shard_map/zero_to_chip_3/ppermute | solution.py:28
  24.8 8.0 %copy-start = (f32[1,256,2,256]{3,2,1,0:T(2,128)S(1)}, f32[1,256,2,256]{3,2,1,0:T(2,128)}, u32[]{:S(2)}) copy-start(f32[1,256,2,256]{3,2,1,0:T(2,128)} %param.10) | copy-start | bytes 1572868
  24.8 8.1 %copy-start.1 = (f32[1,256,2,256]{3,2,1,0:T(2,128)S(1)}, f32[1,256,2,256]{3,2,1,0:T(2,128)}, u32[]{:S(2)}) copy-start(f32[1,256,2,256]{3,2,1,0:T(2,128)} %param.11) | copy-start | bytes 1572868
  24.9 7.6 %collective-permute-start.13 = (bf16[128,512]{1,0:T(8,128)(2,1)S(1)}, bf16[128,512]{1,0:T(8,128)(2,1)S(1)}, u32[]{:S(2)}, u32[]{:S(2)}) collective-permute-start(bf16[128,512]{1,0:T(8,128)(2,1)S(1)} %total_1.1), channel_id=1, source_target_pairs={{0,2},{1,3},{2,0},{3,1},{4,6},{5,7},{6,4},{7,5},{8,10},{9,11},{10,... | collective-permute-start | bytes 393224 | tf_op jit(solution)/shard_map/mirror_1/ppermute | solution.py:35
